TPU v7x, 32 devices: a whole 2x2x4 slice. The times are simulated.
32 devices in a mesh: dp: 4 (over z), mp: 4 (over y, x), phase: 2 (over core).
Axes of the slice: x: 2, y: 2, z: 4, core: 2. Of those that a mesh axis runs over, the one named last changes fastest.
Arguments:
- item_owner: int32 [2048, 1], P('dp'), may hold values from 0 to 3; in each aligned block of 512 rows (0 to 511, 512 to 1023, ...) at most 224 rows name the same one
- item_row: int32 [2048], P('dp'), may hold values from 0 to 1023
- segments: int32 [4, 2, 256], P('dp'), may hold values from 0 to 31, never falling along the last dimension, each value on 1 to 128 neighbouring positions
- neighbors: int32 [4, 2, 256, 8], P('dp'), may hold values from 0 to 255
- table: bfloat16 [4096, 1024], P('dp'), may hold values from -6 to 6
- gains: bfloat16 [2, 1024], P('phase'), may hold values from 0.099609375 to 1.8984375
- w_in: bfloat16 [2, 1024, 4, 1024], P('phase', None, None, 'mp'), may hold values from -0.1875 to 0.1875
- w_out: bfloat16 [2, 1024, 1024], P('phase', 'mp'), may hold values from -0.1875 to 0.1875
- w_ctx: bfloat16 [1024, 1024], P(None, 'mp'), may hold values from -0.1875 to 0.1875
- ctx_bias: bfloat16 [1024], P('mp'), may hold values from -3 to 3
Outputs:
- user_states: bfloat16 [4, 2, 256, 1024], P('dp', 'phase')
- impression_context: bfloat16 [4, 2, 256, 1024], P('dp', 'phase', None, 'mp')
Inputs may be any that keep to these rules, and one draw needn't show every extreme that they name: `item_owner`: among the rows of one index of dp, at most 224 name the same owner.
All inputs are finite; a program needn't handle non-finite values.
Results may differ from a plain program's by a relative error of at most 0.02.
Values may be sent and summed in bfloat16 or wider, within the bound.
No kernel may reach another device: no remote copies, remote signals or barrier semaphores. Data moves between devices by JAX's collectives and lax.ppermute only.
A program may use at most 64 MiB of HBM per device.

v0:
```python
import jax
import jax.numpy as jnp
from jax import lax
from jax.sharding import PartitionSpec as P

HD = 128
NBR = 8
MB_ROWS = 256


norm_eps = 1e-06


def hstu_local(acts, seg_ids, gain, w_proj, w_back):
    rows_n = acts.shape[0]
    width = acts.shape[1]
    local_cols = w_back.shape[0]
    local_heads = local_cols // HD
    acts_f = acts.astype(jnp.float32)
    inv_rms = lax.rsqrt(jnp.mean(acts_f * acts_f, axis=-1, keepdims=True) + norm_eps)
    normed = (acts_f * inv_rms * gain.astype(jnp.float32)).astype(jnp.bfloat16)
    projected = jnp.dot(
        normed, w_proj.reshape(width, 4 * local_cols), preferred_element_type=jnp.float32
    )
    projected = jax.nn.silu(projected).astype(jnp.bfloat16).reshape(rows_n, 4, local_heads, HD)
    gates_u = projected[:, 0]
    values_h = projected[:, 1]
    queries = projected[:, 2]
    keys_h = projected[:, 3]
    scores = jnp.einsum(
        "qhd,khd->hqk", queries, keys_h, preferred_element_type=jnp.float32
    ) * HD ** (-0.5)
    position = jnp.arange(rows_n)
    allowed = (position[None, :] <= position[:, None]) & (seg_ids[:, None] == seg_ids[None, :])
    weights = (jnp.where(allowed[None], jax.nn.silu(scores), 0.0) / MB_ROWS).astype(jnp.bfloat16)
    mixed = jnp.einsum("hqk,khd->qhd", weights, values_h, preferred_element_type=jnp.float32)
    mixed = mixed * lax.rsqrt(jnp.mean(mixed * mixed, axis=-1, keepdims=True) + norm_eps)
    gated = (mixed * gates_u.astype(jnp.float32)).astype(jnp.bfloat16).reshape(rows_n, local_cols)
    partial_term = jnp.dot(gated, w_back, preferred_element_type=jnp.float32)
    summed = lax.psum(partial_term.astype(jnp.bfloat16), "mp").astype(jnp.float32)
    return (acts_f + summed).astype(jnp.bfloat16)


def context_local(states, neigh_rows, w_ctx, ctx_bias):
    picked = jnp.take(states, neigh_rows.reshape(-1), axis=0).astype(jnp.float32)
    context = jnp.mean(picked.reshape(neigh_rows.shape[0], NBR, states.shape[1]), axis=1).astype(
        jnp.bfloat16
    )
    summed = jnp.dot(context, w_ctx, preferred_element_type=jnp.float32) + ctx_bias.astype(
        jnp.float32
    )
    return jax.nn.silu(summed).astype(jnp.bfloat16)


def on_device(
    item_owner, item_row, segments, neighbors, table, gains, w_in, w_out, w_ctx, ctx_bias
):
    dp_count = lax.axis_size("dp")
    row_total = item_row.shape[0]
    capacity = max(2, 7 * row_total // (4 * dp_count))
    owners = item_owner[:, 0]
    owner_hits = (owners[:, None] == jnp.arange(dp_count, dtype=jnp.int32)[None, :]).astype(
        jnp.int32
    )
    slot_rank = jnp.sum((jnp.cumsum(owner_hits, axis=0) - 1) * owner_hits, axis=1)
    slot_index = owners * capacity + slot_rank
    requests = jnp.full((dp_count * capacity,), -1, jnp.int32).at[slot_index].set(item_row)
    requests = requests.reshape(dp_count, capacity)
    found = jnp.take(
        table,
        jnp.maximum(lax.all_to_all(requests, "dp", split_axis=0, concat_axis=0, tiled=True), 0),
        axis=0,
    )
    fetched = lax.all_to_all(found, "dp", split_axis=0, concat_axis=0, tiled=True)
    width = table.shape[1]
    batches = segments.shape[1]
    acts_all = fetched.reshape(dp_count * capacity, width)[slot_index].reshape(batches, -1, width)
    batch_rows = acts_all.shape[1]
    impressions = neighbors.shape[2]
    ctx_cols = w_ctx.shape[1]
    phase_index = lax.axis_index("phase")
    all_gains, all_proj, all_back = (
        lax.all_gather(gains, "phase", axis=0, tiled=True),
        lax.all_gather(w_in, "phase", axis=0, tiled=True),
        lax.all_gather(w_out, "phase", axis=0, tiled=True),
    )
    own_acts = lax.dynamic_index_in_dim(acts_all, phase_index, 0, keepdims=False)
    seg_ids = lax.dynamic_index_in_dim(segments[0], phase_index, 0, keepdims=False)
    neigh_rows = lax.dynamic_index_in_dim(neighbors[0], phase_index, 0, keepdims=False)
    first_out = hstu_local(own_acts, seg_ids, all_gains[0], all_proj[0], all_back[0])
    user_states = hstu_local(first_out, seg_ids, all_gains[1], all_proj[1], all_back[1])
    impression_context = context_local(user_states, neigh_rows, w_ctx, ctx_bias)
    return (
        user_states.reshape(1, 1, batch_rows, width),
        impression_context.reshape(1, 1, impressions, ctx_cols),
    )


def solution(mesh):
    in_specs = (
        P("dp", None),
        P("dp"),
        P("dp", None, None),
        P("dp", None, None, None),
        P("dp", None),
        P("phase", None),
        P("phase", None, None, "mp"),
        P("phase", "mp", None),
        P(None, "mp"),
        P("mp"),
    )
    out_specs = (P("dp", "phase", None, None), P("dp", "phase", None, "mp"))
    return jax.shard_map(
        on_device, mesh=mesh, in_specs=in_specs, out_specs=out_specs, check_vma=False
    )
```

profile of v0, /device:TPU:0, one launch (start us, length us, event | category | flops | bytes accessed | tf_op | source)
XLA Modules:
  0.0 228.6 jit_solution(7618415314698615537)
XLA Ops:
  7.2 3.3 %copy.47 = bf16[1,1024,4,256]{3,1,2,0:T(8,128)(2,1)} copy(bf16[1,1024,4,256]{3,2,1,0:T(4,128)(2,1)} %param.16) | data formatting | bytes 4194304 | tf_op args[6]
  10.6 0.7 copy-done.5
  11.2 1.2 reduce-window.6
  12.5 0.2 slice_reduce_fusion
  12.7 0.2 reduce-window.9
  13.0 2.6 %scatter_custom_fusion = s32[896]{0:T(1024)S(1)} fusion(s32[512]{0:T(512)S(1)} %bitcast.131, s32[512]{0:T(512)} %param.11, s32[]{:T(128)} %constant.78.clone.1), kind=kCustom, calls=%fused_computation.93 | custom fusion | bytes 4096 | tf_op jit(solution)/shard_map/scatter | solution.py:67
  15.6 0.1 all_to_all.9
  15.7 11.7 %all_to_all.14 = s32[4,1,224]{2,1,0:T(1,128)S(1)} all-to-all(s32[4,1,224]{2,1,0:T(1,128)S(1)} %all_to_all.9), channel_id=1, replica_groups=mesh['dp'=4,'mp'=4,'phase'=2] {'dp'}, dimensions={0} | all-to-all | bytes 7168 | tf_op jit(solution)/shard_map/all_to_all | solution.py:71
  27.5 4.3 %gather_fusion = bf16[896,1024]{1,0:T(8,128)(2,1)} fusion(bf16[1024,1024]{1,0:T(8,128)(2,1)S(1)} %copy-done, s32[1024]{0:T(1024)S(1)} %pad_clamp_fusion.1), kind=kCustom, calls=%fused_computation | custom fusion | bytes 3673600 | tf_op jit(solution)/shard_map/jit(_take)/gather | solution.py:69
  31.8 3.0 %broadcast_select_fusion = bf16[4,224,1024]{2,1,0:T(8,128)(2,1)} fusion(bf16[4,224,1024]{2,1,0:T(8,128)(2,1)} %bitcast.119, pred[4,224]{1,0:T(4,128)(4,1)S(1)} %bitcast.138), kind=kLoop, calls=%fused_computation.6 | loop fusion | flops 917504 | bytes 3670912 | tf_op jit(solution)/shard_map/jit(_take)/select_n | solution.py:69
  34.7 4.6 %all-to-all-start.1 = ((bf16[4,224,1024]{2,1,0:T(8,128)(2,1)}), bf16[4,224,1024]{2,1,0:T(8,128)(2,1)}, u32[]{:S(2)}, u32[]{:S(2)}) async-start(bf16[4,224,1024]{2,1,0:T(8,128)(2,1)} %broadcast_select_fusion), calls=%async_computation.1 | async-start | bytes 3670016 | tf_op jit(solution)/shard_map/all_to_all | solution.py:74
  39.4 0.7 all-gather.6.cloned.1.call-update
  40.1 1.8 all-gather
  42.0 0.6 slice_convert_fusion
  42.5 0.7 fusion.36
  43.3 37.5 %all-to-all-done.1 = bf16[4,224,1024]{2,1,0:T(8,128)(2,1)} async-done(((bf16[4,224,1024]{2,1,0:T(8,128)(2,1)}), bf16[4,224,1024]{2,1,0:T(8,128)(2,1)}, u32[]{:S(2)}, u32[]{:S(2)}) %all-to-all-start.1) | async-done | bytes 1835040 | tf_op jit(solution)/shard_map/all_to_all | solution.py:74
  80.8 4.5 %gather_fusion.1 = bf16[512,1024]{1,0:T(8,128)(2,1)S(1)} fusion(bf16[896,1024]{1,0:T(8,128)(2,1)} %bitcast.6, s32[1024]{0:T(1024)S(1)} %pad_clamp_fusion), kind=kCustom, calls=%fused_computation.1 | custom fusion | bytes 2099200 | tf_op jit(solution)/shard_map/gather | solution.py:77
  85.3 0.2 fusion.2
  85.5 4.5 %fusion.57 = (bf16[1,1024,4,256]{3,1,2,0:T(8,128)(2,1)}, bf16[1,1024,4,256]{3,1,2,0:T(8,128)(2,1)}) fusion(bf16[2,1024,4,256]{3,1,2,0:T(8,128)(2,1)} %all-gather.4.cloned.1.call-done), kind=kLoop, calls=%fused_computation.109 | loop fusion | bytes 8388608 | tf_op jit(solution)/shard_map/slice | solution.py:91
  90.0 4.0 %copy.61 = bf16[1,1024,4,256]{1,3,2,0:T(8,128)(2,1)} copy(bf16[1,1024,4,256]{3,1,2,0:T(8,128)(2,1)} %get-tuple-element.7) | data formatting | bytes 4194304
  94.0 3.3 %multiply_convert_fusion.2 = bf16[256,1024]{1,0:T(8,128)(2,1)} fusion(bf16[1024,1024]{0,1:T(8,128)(2,1)} %bitcast.124, f32[1024]{0:T(1024)S(1)} %bitcast.137, f32[256]{0:T(256)S(1)} %add_rsqrt_fusion.3, bf16[2,256,1024]{2,1,0:T(8,128)(2,1)S(1)} %bitcast.121, s32[]{:T(128)S(6)} %select_n.51), kind=kOutput, calls=%fused_computation.31 | convolution fusion | flops 539230208 | bytes 3150852 | tf_op jit(solution)/shard_map/dot_general | solution.py:22
  97.2 2.2 reshape.228
  99.4 2.1 fusion.59
  101.6 0.1 copy.62
  101.7 0.1 copy.65
  101.8 2.2 multiply_reduce_fusion.1
  104.0 1.0 fusion.26
  105.0 2.2 convolution_convert_fusion.1
  107.2 0.2 all-reduce.5.cloned.1.call-start
  107.5 0.1 copy.59
  107.6 0.1 reshape.234
  107.7 0.2 copy.58
  107.9 4.0 %copy.66 = bf16[1,1024,4,256]{1,3,2,0:T(8,128)(2,1)} copy(bf16[1,1024,4,256]{3,1,2,0:T(8,128)(2,1)} %get-tuple-element.6) | data formatting | bytes 4194304
  112.0 39.9 %all-reduce.3.cloned.1.call-done = bf16[256,1024]{1,0:T(8,128)(2,1)} async-done(((bf16[256,1024]{1,0:T(8,128)(2,1)}), bf16[256,1024]{1,0:T(8,128)(2,1)}) %all-reduce.3.cloned.1.call-update) | async-done | bytes 524304 | tf_op jit(solution)/shard_map/psum | solution.py:40
  151.9 1.3 fusion.6
  153.2 0.8 copy-done.2
  154.0 2.5 %multiply_convert_fusion.1 = bf16[256,1024]{1,0:T(8,128)(2,1)S(1)} fusion(bf16[1024,1024]{0,1:T(8,128)(2,1)} %bitcast.123, bf16[256,1024]{1,0:T(8,128)(2,1)S(1)} %get-tuple-element.5, f32[1024]{0:T(1024)S(1)} %bitcast.136, f32[256]{0:T(256)S(1)} %add_rsqrt_fusion.2), kind=kOutput, calls=%fused_computation.30 | convolution fusion | flops 539230208 | bytes 3150848 | tf_op jit(solution)/shard_map/dot_general | solution.py:22
  156.5 0.4 reshape.230
  156.8 0.4 fusion.58
  157.2 0.1 copy.67
  157.3 0.1 copy.70
  157.5 0.5 multiply_reduce_fusion
  158.0 2.2 convolution_convert_fusion
  160.3 45.5 %all-reduce.5.cloned.1.call-done = bf16[256,1024]{1,0:T(8,128)(2,1)} async-done(((bf16[256,1024]{1,0:T(8,128)(2,1)}), bf16[256,1024]{1,0:T(8,128)(2,1)}) %all-reduce.5.cloned.1.call-update) | async-done | bytes 524304 | tf_op jit(solution)/shard_map/psum | solution.py:40
  205.7 1.2 fusion.9
  207.0 9.7 %gather_fusion.2 = bf16[2048,1024]{1,0:T(8,128)(2,1)} fusion(bf16[256,1024]{1,0:T(8,128)(2,1)S(1)} %fusion.9, s32[2048]{0:T(1024)S(1)} %broadcast_clamp_fusion), kind=kCustom, calls=%fused_computation.2 | custom fusion | bytes 8396800 | tf_op jit(solution)/shard_map/jit(_take)/gather | solution.py:45
  216.7 4.4 %convert_reduce_fusion = f32[256,1024]{1,0:T(8,128)S(1)} fusion(bf16[2048,1024]{1,0:T(8,128)(2,1)} %gather_fusion.2, pred[256,8]{1,0:T(8,128)(4,1)S(1)} %copy.58), kind=kLoop, calls=%fused_computation.4 | loop fusion | flops 6029312 | bytes 5244928 | tf_op jit(solution)/shard_map/reduce_sum | solution.py:46
  221.1 1.0 fusion.27
  (50 shorter events, 0.6 us)
Async XLA Ops:
  7.2 20.3 %copy-start = (bf16[1024,1024]{1,0:T(8,128)(2,1)S(1)}, bf16[1024,1024]{1,0:T(8,128)(2,1)}, u32[]{:S(2)}) copy-start(bf16[1024,1024]{1,0:T(8,128)(2,1)} %param.14) | copy-start | bytes 6291460
  7.2 78.3 %all-gather.4.cloned.1.call-start = ((), (), s32[]{:S(2)}) async-start(), calls=%async_computation.2 | async-start | bytes 6291456 | tf_op jit(solution)/shard_map/all_gather | solution.py:84
  10.6 0.7 copy-start.5
  34.7 5.4 %copy-start.6 = (bf16[1,1024]{1,0:T(2,128)(2,1)S(1)}, bf16[1,1024]{1,0:T(2,128)(2,1)}, u32[]{:S(2)}) copy-start(bf16[1,1024]{1,0:T(2,128)(2,1)} %param.15) | copy-start | bytes 6148
  34.7 7.2 %copy-start.9 = (s32[1,2,256]{2,1,0:T(2,128)S(1)}, s32[1,2,256]{2,1,0:T(2,128)}, u32[]{:S(2)}) copy-start(s32[1,2,256]{2,1,0:T(2,128)} %param.12) | copy-start | bytes 6148
  34.7 46.1 %all-to-all-start.1 = ((bf16[4,224,1024]{2,1,0:T(8,128)(2,1)}), bf16[4,224,1024]{2,1,0:T(8,128)(2,1)}, u32[]{:S(2)}, u32[]{:S(2)}) async-start(bf16[4,224,1024]{2,1,0:T(8,128)(2,1)} %broadcast_select_fusion), calls=%async_computation.1 | async-start | bytes 3670016 | tf_op jit(solution)/shard_map/all_to_all | solution.py:74
  39.3 65.7 %all-gather.6.cloned.1.call-start = ((), (), s32[]{:S(2)}) async-start(), calls=%async_computation.3 | async-start | bytes 1572864 | tf_op jit(solution)/shard_map/all_gather | solution.py:85
  40.1 111.8 %all-reduce.3.cloned.1.call-start = ((), (), s32[]{:S(2)}) async-start(), calls=%async_computation.4 | async-start | bytes 1048576 | tf_op jit(solution)/shard_map/psum | solution.py:40
  101.8 5.7 %copy-start.7 = (s32[1,2,256,8]{2,3,1,0:T(8,128)S(1)}, s32[1,2,256,8]{2,3,1,0:T(8,128)}, u32[]{:S(2)}) copy-start(s32[1,2,256,8]{2,3,1,0:T(8,128)} %param.13) | copy-start | bytes 49156
  104.0 3.9 %copy-start.11 = (bf16[256]{0:T(256)(128)(2,1)S(1)}, bf16[256]{0:T(256)(128)(2,1)}, u32[]{:S(2)}) copy-start(bf16[256]{0:T(256)(128)(2,1)} %param.19) | copy-start | bytes 1540
  107.2 98.5 %all-reduce.5.cloned.1.call-start = ((), (), s32[]{:S(2)}) async-start(), calls=%async_computation.5 | async-start | bytes 1048576 | tf_op jit(solution)/shard_map/psum | solution.py:40
  107.9 46.0 %copy-start.8 = (f32[1,1,1024]{2,1,0:T(1,128)S(1)}, f32[1,1,1024]{2,1,0:T(1,128)}, u32[]{:S(2)}) copy-start(f32[1,1,1024]{2,1,0:T(1,128)} %get-tuple-element.16) | copy-start | bytes 12292
  153.2 0.8 copy-start.2
  156.5 1.0 copy-start.4
  157.4 48.3 %copy-start.3 = (bf16[256,1024]{1,0:T(8,128)(2,1)S(1)}, bf16[256,1024]{1,0:T(8,128)(2,1)}, u32[]{:S(2)}) copy-start(bf16[256,1024]{1,0:T(8,128)(2,1)} %copy-done.2) | copy-start | bytes 1572868
  207.0 9.7 %copy-start.1 = (bf16[256,1024]{1,0:T(8,128)(2,1)}, bf16[256,1024]{1,0:T(8,128)(2,1)S(1)}, u32[]{:S(2)}) copy-start(bf16[256,1024]{1,0:T(8,128)(2,1)S(1)} %fusion.9) | copy-start | bytes 1572868
  216.6 4.4 %copy-start.10 = (bf16[1024,256]{1,0:T(8,128)(2,1)S(1)}, bf16[1024,256]{1,0:T(8,128)(2,1)}, u32[]{:S(2)}) copy-start(bf16[1024,256]{1,0:T(8,128)(2,1)} %param.18) | copy-start | bytes 1572868
Sparse Core Ops, SparseCore 0:
  10.7 16.3 all-gather.3
  41.7 10.4 all-gather.5
  107.4 44.4 all-reduce.2
  160.3 45.3 all-reduce.4
where the time goes:
time: 229 us
  waiting for transfers between devices  124 us (54%)
  local copies, waits for them, and re-layouts  44.6 us (19%)
  between operations  14.1 us (6%)
  other arithmetic  14 us (6%)
  matrix products  13.8 us (6%)
  blocking collectives  13.5 us (6%)
  starting transfers between devices  4.92 us (2%)
    psum x2, waiting for transfers between devices, hstu_local(): lax.psum(partial_term.astype(jnp.bfloat16), 'mp').astype(jnp.float32)  85.4 us
    all_to_all x1, waiting for transfers between devices, on_device(): lax.all_to_all(found, 'dp', split_axis=0, concat_axis=0, tiled=True)  37.5 us
    unnamed x32, local copies, waits for them, and re-layouts  13.2 us
    all_to_all x1, blocking collectives, on_device(): lax.all_to_all(requests, 'dp', split_axis=0, concat_axis=0, tiled=True)  11.7 us
    gather x1, local copies, waits for them, and re-layouts, context_local(): jnp.take(states, neigh_rows.reshape(-1), axis=0).astype(jnp.float32)  9.67 us
    dot_general x2, matrix products, hstu_local(): jnp.dot(normed, w_proj.reshape(width, 4 * local_cols), preferred_element_...  5.73 us
  transfers between devices with their start and end apart: 5, of which 3 were waited for; matrix products, arithmetic and copies ran while one was open for 18% of the time, Pallas kernels for 0%

commit v1 on v0

v1 whole, which is shorter than its diff:
```python
import functools

import jax
import jax.numpy as jnp
from jax import lax
from jax.experimental import pallas as pl
from jax.experimental.pallas import tpu as pltpu
from jax.sharding import PartitionSpec as P

HD = 128
NBR = 8
LANES = 128
EPS = 1e-06
VMEM_LIMIT = 48 * 1024 * 1024
VMEM = pl.BlockSpec(memory_space=pltpu.VMEM)
ANY = pl.BlockSpec(memory_space=pl.ANY)
SMEM = pl.BlockSpec(memory_space=pltpu.SMEM)
F32 = jnp.float32
BF16 = jnp.bfloat16


def params():
    return pltpu.CompilerParams(vmem_limit_bytes=VMEM_LIMIT)


def is_pow2(n):
    return n & (n - 1) == 0


def source_of(me, k, n):
    return me ^ k if is_pow2(n) else lax.rem(me + n - k, n)


def exchange(value, axis, k):
    n = lax.axis_size(axis)
    pairs = [(i, i ^ k if is_pow2(n) else (i + k) % n) for i in range(n)]
    return lax.ppermute(value, axis, pairs)


def spread(value, axis):
    return [value] + [exchange(value, axis, k) for k in range(1, lax.axis_size(axis))]


def columns_of(row, count):
    return jnp.transpose(jnp.broadcast_to(row, (count, row.shape[1])))


def fetch_kernel(steps, pos_ref, *refs):
    idx_refs, table_ref = refs[:steps], refs[steps]
    out_refs = refs[steps + 1 : 2 * steps + 1]
    tab, sem = refs[2 * steps + 1 :]
    width = tab.shape[1]
    copy = pltpu.make_async_copy(
        table_ref.at[:, pl.ds(pl.multiple_of(pos_ref[1] * width, width), width)], tab, sem
    )
    copy.start()
    first = pos_ref[0] * tab.shape[0]
    hots = []
    for idx_ref in idx_refs:
        cols = columns_of(idx_ref[...] - first, LANES)
        lane = lax.broadcasted_iota(jnp.int32, cols.shape, 1)
        hots.append(
            jnp.concatenate(
                [
                    jnp.where(cols == lane + c, 1.0, 0.0).astype(BF16)
                    for c in range(0, tab.shape[0], LANES)
                ],
                axis=1,
            )
        )
    copy.wait()
    for hot, out_ref in zip(hots, out_refs):
        out_ref[...] = jnp.dot(hot, tab[...], preferred_element_type=F32).astype(BF16)


def fetch(pos, idx_rows, table, width):
    steps = len(idx_rows)
    rows = idx_rows[0].shape[1]
    return pl.pallas_call(
        functools.partial(fetch_kernel, steps),
        out_shape=[jax.ShapeDtypeStruct((rows, width), BF16)] * steps,
        in_specs=[SMEM] + [VMEM] * steps + [ANY],
        out_specs=[VMEM] * steps,
        scratch_shapes=[pltpu.VMEM((table.shape[0], width), BF16), pltpu.SemaphoreType.DMA],
        compiler_params=params(),
        cost_estimate=pl.CostEstimate(
            flops=2 * steps * rows * width * table.shape[0],
            bytes_accessed=2 * width * table.shape[0],
            transcendentals=0,
        ),
        name="fetch",
    )(pos, *idx_rows, table)


def silu(x):
    return x * jax.nn.sigmoid(x)


def start_picked(section, phase, own, other, dst, sem):
    @pl.when(phase == section)
    def _():
        pltpu.make_async_copy(own, dst, sem).start()

    @pl.when(phase != section)
    def _():
        pltpu.make_async_copy(other, dst, sem).start()


def wait_picked(own, dst, sem):
    pltpu.make_async_copy(own, dst, sem).wait()


def front(x, gain, seg, w_own, w_buf, w_sem, gated_ref):
    rows, local_cols = x.shape[0], w_buf.shape[2]
    inv = lax.rsqrt(jnp.mean(x * x, axis=-1, keepdims=True) + EPS)
    normed = (x * inv * gain.astype(F32)).astype(BF16)
    proj = []
    for g in range(4):
        wait_picked(w_own.at[g], w_buf.at[g], w_sem.at[g])
        proj.append(
            silu(jnp.dot(normed, w_buf[g], preferred_element_type=F32)).astype(BF16)
        )
    gates, values, queries, keys = proj
    seg_cols = columns_of(seg, rows)
    at_row = lax.broadcasted_iota(jnp.int32, (rows, rows), 0)
    at_col = lax.broadcasted_iota(jnp.int32, (rows, rows), 1)
    allowed = (at_col <= at_row) & (seg_cols == seg)
    for h in range(0, local_cols, HD):
        head = slice(h, h + HD)
        scores = lax.dot_general(
            queries[:, head], keys[:, head], (((1,), (1,)), ((), ())), preferred_element_type=F32
        ) * HD ** (-0.5)
        weights = (jnp.where(allowed, silu(scores), 0.0) / rows).astype(BF16)
        mixed = jnp.dot(weights, values[:, head], preferred_element_type=F32)
        mixed = mixed * lax.rsqrt(jnp.mean(mixed * mixed, axis=-1, keepdims=True) + EPS)
        gated_ref[:, head] = (mixed * gates[:, head].astype(F32)).astype(BF16)


def back(x, gated_refs, o_own, o_buf, o_sem):
    total = x.astype(F32)
    for k, gated_ref in enumerate(gated_refs):
        wait_picked(o_own[k], o_buf.at[k], o_sem.at[k])
        part = jnp.dot(gated_ref[...], o_buf[k], preferred_element_type=F32)
        total = total + part.astype(BF16).astype(F32)
    return total.astype(BF16)


def first_kernel(steps, pos_ref, *refs):
    x_refs = refs[:steps]
    gain_ref, seg_ref, w_own, w_other, gated_ref, x_ref, w_buf, w_sem = refs[steps:]
    for g in range(4):
        start_picked(0, pos_ref[2], w_own.at[g], w_other.at[g], w_buf.at[g], w_sem.at[g])
    width = x_refs[0].shape[1]
    for k, piece in enumerate(x_refs):
        at = pl.multiple_of(source_of(pos_ref[1], k, steps) * width, width)
        x_ref[:, pl.ds(at, width)] = piece[...]
    front(x_ref[...].astype(F32), gain_ref[...], seg_ref[...], w_own, w_buf, w_sem, gated_ref)


def middle_kernel(steps, pos_ref, *refs):
    gated_refs, o_own, o_other = refs[:steps], refs[steps : 2 * steps], refs[2 * steps : 3 * steps]
    x_ref, gain_ref, seg_ref, w_own, w_other, gated_ref, x1_ref = refs[3 * steps : 3 * steps + 7]
    o_buf, o_sem, w_buf, w_sem = refs[3 * steps + 7 :]
    for k in range(steps):
        start_picked(0, pos_ref[2], o_own[k], o_other[k], o_buf.at[k], o_sem.at[k])
    for g in range(4):
        start_picked(1, pos_ref[2], w_own.at[g], w_other.at[g], w_buf.at[g], w_sem.at[g])
    x1 = back(x_ref[...], gated_refs, o_own, o_buf, o_sem)
    x1_ref[...] = x1
    front(x1.astype(F32), gain_ref[...], seg_ref[...], w_own, w_buf, w_sem, gated_ref)


def last_kernel(steps, pos_ref, *refs):
    gated_refs, o_own, o_other = refs[:steps], refs[steps : 2 * steps], refs[2 * steps : 3 * steps]
    x_ref, neigh_ref, w_ref, bias_ref, states_ref, ctx_ref = refs[3 * steps : 3 * steps + 6]
    o_buf, o_sem = refs[3 * steps + 6 :]
    for k in range(steps):
        start_picked(1, pos_ref[2], o_own[k], o_other[k], o_buf.at[k], o_sem.at[k])
    rows, imps = x_ref.shape[0], neigh_ref.shape[0]
    lane = lax.broadcasted_iota(jnp.int32, (imps, rows), 1)
    share = jnp.zeros((imps, rows), F32)
    for n in range(NBR):
        share = share + jnp.where(neigh_ref[:, n : n + 1] == lane, 1.0 / NBR, 0.0)
    states = back(x_ref[...], gated_refs, o_own, o_buf, o_sem)
    states_ref[...] = states
    context = jnp.dot(share.astype(BF16), states, preferred_element_type=F32).astype(BF16)
    summed = jnp.dot(context, w_ref[...], preferred_element_type=F32) + bias_ref[...].astype(F32)
    ctx_ref[...] = silu(summed).astype(BF16)


def section_flops(rows, width, local_cols):
    return 2 * rows * (width * 4 * local_cols + 2 * rows * local_cols)


def fetch_rows_padded(owners, item_row, table, width):
    dp_count = lax.axis_size("dp")
    row_total = item_row.shape[0]
    capacity = max(2, 7 * row_total // (4 * dp_count))
    hits = (owners[:, None] == jnp.arange(dp_count, dtype=jnp.int32)[None, :]).astype(jnp.int32)
    rank = jnp.sum((jnp.cumsum(hits, axis=0) - 1) * hits, axis=1)
    slot = owners * capacity + rank
    requests = jnp.full((dp_count * capacity,), -1, jnp.int32).at[slot].set(item_row)
    requests = requests.reshape(dp_count, capacity)
    asked = lax.all_to_all(requests, "dp", split_axis=0, concat_axis=0, tiled=True)
    part = lax.dynamic_slice_in_dim(table, lax.axis_index("mp") * width, width, 1)
    found = jnp.take(part, jnp.maximum(asked, 0), axis=0)
    fetched = lax.all_to_all(found, "dp", split_axis=0, concat_axis=0, tiled=True)
    return fetched.reshape(dp_count * capacity, width)[slot]


def on_device(
    item_owner, item_row, segments, neighbors, table, gains, w_in, w_out, w_ctx, ctx_bias
):
    dp_count, mp_count = lax.axis_size("dp"), lax.axis_size("mp")
    dp_at, mp_at, phase = lax.axis_index("dp"), lax.axis_index("mp"), lax.axis_index("phase")
    pos = jnp.stack([dp_at, mp_at, phase]).astype(jnp.int32)
    table_rows, width = table.shape
    batches, rows = segments.shape[1], segments.shape[2]
    imps = neighbors.shape[2]
    local_cols = w_out.shape[1]
    part = width // mp_count

    w_own = jnp.transpose(w_in[0], (1, 0, 2))
    w_other = exchange(w_own, "phase", 1)
    o_own = spread(w_out[0], "mp")
    o_other = [exchange(piece, "phase", 1) for piece in o_own]
    gain_other = exchange(gains, "phase", 1)
    gain0 = jnp.where(phase == 0, gains, gain_other)
    gain1 = jnp.where(phase == 0, gain_other, gains)
    seg = lax.dynamic_index_in_dim(segments[0], phase, 0, keepdims=True)
    neigh = lax.dynamic_index_in_dim(neighbors[0], phase, 0, keepdims=False)

    if is_pow2(dp_count) and dp_count <= 8:
        wanted = (item_owner[:, 0] * table_rows + item_row).reshape(batches, rows)
        wanted = lax.dynamic_index_in_dim(wanted, phase, 0, keepdims=True)
        found = fetch(pos, spread(wanted, "dp"), table, part)
        piece = found[0]
        for k in range(1, dp_count):
            piece = piece + exchange(found[k], "dp", k)
    else:
        piece = fetch_rows_padded(item_owner[:, 0], item_row, table, part)
        piece = lax.dynamic_index_in_dim(
            piece.reshape(batches, rows, part), phase, 0, keepdims=False
        )
    x_pieces = spread(piece, "mp")

    sem4 = pltpu.SemaphoreType.DMA((4,))
    semk = pltpu.SemaphoreType.DMA((mp_count,))
    w_buf = pltpu.VMEM((4, width, local_cols), BF16)
    o_buf = pltpu.VMEM((mp_count, local_cols, width), BF16)
    x_shape = jax.ShapeDtypeStruct((rows, width), BF16)
    gated_shape = jax.ShapeDtypeStruct((rows, local_cols), BF16)
    front_flops = section_flops(rows, width, local_cols)
    back_flops = 2 * rows * width * local_cols * mp_count

    gated, x0 = pl.pallas_call(
        functools.partial(first_kernel, mp_count),
        out_shape=[gated_shape, x_shape],
        in_specs=[SMEM] + [VMEM] * (mp_count + 2) + [ANY] * 2,
        out_specs=[VMEM] * 2,
        scratch_shapes=[w_buf, sem4],
        compiler_params=params(),
        cost_estimate=pl.CostEstimate(
            flops=front_flops, bytes_accessed=8 * width * local_cols, transcendentals=0
        ),
        name="section0_front",
    )(pos, *x_pieces, gain0, seg, w_own, w_other)

    gated, x1 = pl.pallas_call(
        functools.partial(middle_kernel, mp_count),
        out_shape=[gated_shape, x_shape],
        in_specs=[SMEM] + [VMEM] * mp_count + [ANY] * (2 * mp_count) + [VMEM] * 3 + [ANY] * 2,
        out_specs=[VMEM] * 2,
        scratch_shapes=[o_buf, semk, w_buf, sem4],
        compiler_params=params(),
        cost_estimate=pl.CostEstimate(
            flops=front_flops + back_flops,
            bytes_accessed=(8 + 2 * mp_count) * width * local_cols,
            transcendentals=0,
        ),
        name="section0_back_section1_front",
    )(pos, *spread(gated, "mp"), *o_own, *o_other, x0, gain1, seg, w_own, w_other)

    states, ctx = pl.pallas_call(
        functools.partial(last_kernel, mp_count),
        out_shape=[x_shape, jax.ShapeDtypeStruct((imps, w_ctx.shape[1]), BF16)],
        in_specs=[SMEM] + [VMEM] * mp_count + [ANY] * (2 * mp_count) + [VMEM] * 4,
        out_specs=[VMEM] * 2,
        scratch_shapes=[o_buf, semk],
        compiler_params=params(),
        cost_estimate=pl.CostEstimate(
            flops=back_flops + 2 * imps * width * (rows + w_ctx.shape[1]),
            bytes_accessed=2 * mp_count * width * local_cols,
            transcendentals=0,
        ),
        name="section1_back_context",
    )(pos, *spread(gated, "mp"), *o_own, *o_other, x1, neigh, w_ctx, ctx_bias[None])

    return (
        states.reshape(1, 1, rows, width),
        ctx.reshape(1, 1, imps, w_ctx.shape[1]),
    )


def solution(mesh):
    in_specs = (
        P("dp", None),
        P("dp"),
        P("dp", None, None),
        P("dp", None, None, None),
        P("dp", None),
        P("phase", None),
        P("phase", None, None, "mp"),
        P("phase", "mp", None),
        P(None, "mp"),
        P("mp"),
    )
    out_specs = (P("dp", "phase", None, None), P("dp", "phase", None, "mp"))
    return jax.shard_map(
        on_device, mesh=mesh, in_specs=in_specs, out_specs=out_specs, check_vma=False
    )
```

time: 229 us -> 98.9 us (0.43)
  waiting for transfers between devices: 124 us -> 45.8 us
  local copies, waits for them, and re-layouts: 44.6 us -> 8.67 us
  starting transfers between devices: 4.92 us -> 28.3 us
  Pallas kernels: 0 us -> 13.9 us
  matrix products: 13.8 us -> 0 us
  blocking collectives: 13.5 us -> 0 us
  between operations: 14.1 us -> 0.89 us
  other arithmetic: 14 us -> 0.82 us
    psum x2 -> x0, waiting for transfers between devices: 85.4 us -> none  [hstu_local(): lax.psum(partial_term.astype(jnp.bfloat16), 'mp').astype(jnp.float32)]
    ppermute x0 -> x24, waiting for transfers between devices: none -> 45.8 us  [exchange(): return lax.ppermute(value, axis, pairs)]
    all_to_all x1 -> x0, waiting for transfers between devices: 37.5 us -> none  [on_device(): lax.all_to_all(found, 'dp', split_axis=0, concat_axis=0, tiled=True)]
    ppermute x0 -> x24, starting transfers between devices: none -> 28.3 us  [exchange(): return lax.ppermute(value, axis, pairs)]
    gather x3 -> x0, local copies, waits for them, and re-layouts: 18.4 us -> none  [the longest x1 9.67 us: context_local(): jnp.take(states, neigh_rows.reshape(-1), axis=0).astype(jnp.float32)]
    pallas_call x0 -> x4, Pallas kernels: none -> 13.9 us  [the longest x1 4.77 us: on_device(): pl.pallas_call(functools.partial(middle_kernel, mp_count), out_shape=[gat...]
    dot_general x7 -> x0, matrix products: 13.8 us -> none  [the longest x2 5.73 us: hstu_local(): jnp.dot(normed, w_proj.reshape(width, 4 * local_cols), preferred_element_...]
    all_to_all x1 -> x0, blocking collectives: 11.7 us -> none  [on_device(): lax.all_to_all(requests, 'dp', split_axis=0, concat_axis=0, tiled=True)]
  transfers between devices with their start and end apart: 5 -> 24, of which waited for: 3 -> 12; matrix products, arithmetic and copies ran while one was open for 18% -> 2% of each run, Pallas kernels for 0% -> 5%
where the time goes in v1:
time: 98.9 us; the launch traced here: 98.5 us
  waiting for transfers between devices  45.8 us (46%)
  starting transfers between devices  28.3 us (29%)
  Pallas kernels  13.9 us (14%)
  local copies, waits for them, and re-layouts  8.67 us (9%)
    ppermute x24, waiting for transfers between devices, exchange(): return lax.ppermute(value, axis, pairs)  45.8 us
    ppermute x24, starting transfers between devices, exchange(): return lax.ppermute(value, axis, pairs)  28.3 us
    unnamed x39, local copies, waits for them, and re-layouts  7.84 us
    pallas_call x1, Pallas kernels, on_device(): pl.pallas_call(functools.partial(middle_kernel, mp_count), out_shape=[gat...  4.77 us
    pallas_call x1, Pallas kernels, on_device(): pl.pallas_call(functools.partial(last_kernel, mp_count), out_shape=[x_sha...  4.09 us
    pallas_call x1, Pallas kernels, on_device(): pl.pallas_call(functools.partial(first_kernel, mp_count), out_shape=[gate...  3.21 us
  transfers between devices with their start and end apart: 24, of which 12 were waited for; matrix products, arithmetic and copies ran while one was open for 2% of the time, Pallas kernels for 5%

profile of v1, /device:TPU:0, one launch (start us, length us, event | category | flops | bytes accessed | tf_op | source)
XLA Modules:
  0.0 98.5 jit_solution(10676829594393971427)
XLA Ops:
  0.7 1.9 %copy.15 = bf16[1,1024,4,256]{3,1,2,0:T(8,128)(2,1)S(1)} copy(bf16[1,1024,4,256]{3,2,1,0:T(4,128)(2,1)} %param.16) | data formatting | bytes 4194304 | tf_op args[6]
  2.6 0.5 collective-permute-start.10
  3.2 2.7 %collective-permute-start = (s32[1,256]{1,0:T(1,128)S(1)}, s32[1,256]{1,0:T(1,128)S(1)}, u32[]{:S(2)}, u32[]{:S(2)}) collective-permute-start(s32[1,256]{1,0:T(1,128)S(1)} %constant_dynamic-slice_fusion.1.refs_0_), channel_id=1, source_target_pairs={{0,8},{8,0},{16,24},{24,16},{1,9},{9,1},{17,25},{25,17},{2,10},{10... | collective-permute-start | bytes 3080 | tf_op jit(solution)/shard_map/ppermute | solution.py:37
  5.8 2.6 %collective-permute-start.1 = (s32[1,256]{1,0:T(1,128)S(1)}, s32[1,256]{1,0:T(1,128)S(1)}, u32[]{:S(2)}, u32[]{:S(2)}) collective-permute-start(s32[1,256]{1,0:T(1,128)S(1)} %constant_dynamic-slice_fusion.1.refs_0_), channel_id=1, source_target_pairs={{0,16},{8,24},{16,0},{24,8},{1,17},{9,25},{17,1},{25,9},{2,18},{10... | collective-permute-start | bytes 3080 | tf_op jit(solution)/shard_map/ppermute | solution.py:37
  8.4 0.1 pad_add_fusion.pos_ref
  8.5 1.8 %collective-permute-done.1.refs_2_ = s32[1,256]{1,0:T(1,128)S(1)} collective-permute-done((s32[1,256]{1,0:T(1,128)S(1)}, s32[1,256]{1,0:T(1,128)S(1)}, u32[]{:S(2)}, u32[]{:S(2)}) %collective-permute-start.1) | collective-permute-done | bytes 1056 | tf_op jit(solution)/shard_map/ppermute | solution.py:37
  10.3 3.5 %collective-permute-done.2.refs_3_ = s32[1,256]{1,0:T(1,128)S(1)} collective-permute-done((s32[1,256]{1,0:T(1,128)S(1)}, s32[1,256]{1,0:T(1,128)S(1)}, u32[]{:S(2)}, u32[]{:S(2)}) %collective-permute-start.2) | collective-permute-done | bytes 1056 | tf_op jit(solution)/shard_map/ppermute | solution.py:37
  13.8 1.6 %copy-done.7 = bf16[1024,1024]{1,0:T(8,128)(2,1)S(1)} copy-done((bf16[1024,1024]{1,0:T(8,128)(2,1)S(1)}, bf16[1024,1024]{1,0:T(8,128)(2,1)}, u32[]{:S(2)}) %copy-start.7) | copy-done | bytes 2097176
  15.4 1.9 %fetch.1 = (bf16[256,256]{1,0:T(8,128)(2,1)S(1)}, bf16[256,256]{1,0:T(8,128)(2,1)S(1)}, bf16[256,256]{1,0:T(8,128)(2,1)S(1)}, bf16[256,256]{1,0:T(8,128)(2,1)S(1)}) custom-call(s32[3]{0:T(128)S(1)} %pad_add_fusion.pos_ref, s32[1,256]{1,0:T(1,128)S(1)} %constant_dynamic-slice_fusion.1.refs_0_, s32[1,256]{1,0:T(1,128)S(1)} %collective-permute-done.refs_1_, ...), custom_call_target="tpu_custom_call" | custom-call | flops 536870912 | bytes 524288 | tf_op jit(solution)/shard_map/fetch/pallas_call | solution.py:79
  17.3 0.1 collective-permute-start.3
  17.3 0.6 collective-permute-start.4
  17.9 3.8 %collective-permute-start.5 = (bf16[256,256]{1,0:T(8,128)(2,1)S(1)}, bf16[256,256]{1,0:T(8,128)(2,1)S(1)}, u32[]{:S(2)}, u32[]{:S(2)}) collective-permute-start(bf16[256,256]{1,0:T(8,128)(2,1)S(1)} %get-tuple-element.15), channel_id=1, source_target_pairs={{0,24},{8,16},{16,8},{24,0},{1,25},{9,17},{17,9},{25,1},{2,26},{10... | collective-permute-start | bytes 393224 | tf_op jit(solution)/shard_map/ppermute | solution.py:37
  21.7 1.5 %collective-permute-start.14 = (bf16[256,1024]{1,0:T(8,128)(2,1)S(1)}, bf16[256,1024]{1,0:T(8,128)(2,1)S(1)}, u32[]{:S(2)}, u32[]{:S(2)}) collective-permute-start(bf16[256,1024]{1,0:T(8,128)(2,1)S(1)} %bitcast.18), channel_id=1, source_target_pairs={{0,2},{2,0},{4,6},{6,4},{1,3},{3,1},{5,7},{7,5},{8,10},{10,8},{12,... | collective-permute-start | bytes 1572872 | tf_op jit(solution)/shard_map/ppermute | solution.py:37
  23.2 0.9 collective-permute-done.3
  24.1 1.5 %collective-permute-start.15 = (bf16[256,1024]{1,0:T(8,128)(2,1)S(1)}, bf16[256,1024]{1,0:T(8,128)(2,1)}, u32[]{:S(2)}, u32[]{:S(2)}) collective-permute-start(bf16[256,1024]{1,0:T(8,128)(2,1)S(1)} %bitcast.19), channel_id=1, source_target_pairs={{0,4},{2,6},{4,0},{6,2},{1,5},{3,7},{5,1},{7,3},{8,12},{10,14},{12... | collective-permute-start | bytes 1572872 | tf_op jit(solution)/shard_map/ppermute | solution.py:37
  25.6 3.9 %collective-permute-done.4 = bf16[256,256]{1,0:T(8,128)(2,1)S(1)} collective-permute-done((bf16[256,256]{1,0:T(8,128)(2,1)S(1)}, bf16[256,256]{1,0:T(8,128)(2,1)S(1)}, u32[]{:S(2)}, u32[]{:S(2)}) %collective-permute-start.4) | collective-permute-done | bytes 131104 | tf_op jit(solution)/shard_map/ppermute | solution.py:37
  29.5 2.4 %collective-permute-start.16 = (bf16[256,1024]{1,0:T(8,128)(2,1)S(1)}, bf16[256,1024]{1,0:T(8,128)(2,1)}, u32[]{:S(2)}, u32[]{:S(2)}) collective-permute-start(bf16[256,1024]{1,0:T(8,128)(2,1)S(1)} %bitcast.20), channel_id=1, source_target_pairs={{0,6},{2,4},{4,2},{6,0},{1,7},{3,5},{5,3},{7,1},{8,14},{10,12},{12... | collective-permute-start | bytes 1572872 | tf_op jit(solution)/shard_map/ppermute | solution.py:37
  32.0 1.3 %collective-permute-done.9 = bf16[1,1024]{1,0:T(2,128)(2,1)} collective-permute-done((bf16[1,1024]{1,0:T(2,128)(2,1)S(1)}, bf16[1,1024]{1,0:T(2,128)(2,1)}, u32[]{:S(2)}, u32[]{:S(2)}) %collective-permute-start.9) | collective-permute-done | bytes 2080 | tf_op jit(solution)/shard_map/ppermute | solution.py:37
  33.2 0.5 collective-permute-start.6
  33.8 13.8 %collective-permute-done.6.refs_1_ = bf16[256,256]{1,0:T(8,128)(2,1)S(1)} collective-permute-done((bf16[256,256]{1,0:T(8,128)(2,1)S(1)}, bf16[256,256]{1,0:T(8,128)(2,1)S(1)}, u32[]{:S(2)}, u32[]{:S(2)}) %collective-permute-start.6) | collective-permute-done | bytes 131104 | tf_op jit(solution)/shard_map/ppermute | solution.py:37
  47.6 1.5 %collective-permute-start.7 = (bf16[256,256]{1,0:T(8,128)(2,1)S(1)}, bf16[256,256]{1,0:T(8,128)(2,1)S(1)}, u32[]{:S(2)}, u32[]{:S(2)}) collective-permute-start(bf16[256,256]{1,0:T(8,128)(2,1)S(1)} %add_add_fusion.refs_0_), channel_id=1, source_target_pairs={{0,4},{2,6},{4,0},{6,2},{1,5},{3,7},{5,1},{7,3},{8,12},{10,14},{12... | collective-permute-start | bytes 393224 | tf_op jit(solution)/shard_map/ppermute | solution.py:37
  49.1 4.9 %collective-permute-done.7.refs_2_ = bf16[256,256]{1,0:T(8,128)(2,1)S(1)} collective-permute-done((bf16[256,256]{1,0:T(8,128)(2,1)S(1)}, bf16[256,256]{1,0:T(8,128)(2,1)S(1)}, u32[]{:S(2)}, u32[]{:S(2)}) %collective-permute-start.7) | collective-permute-done | bytes 131104 | tf_op jit(solution)/shard_map/ppermute | solution.py:37
  53.9 2.4 %collective-permute-start.8 = (bf16[256,256]{1,0:T(8,128)(2,1)S(1)}, bf16[256,256]{1,0:T(8,128)(2,1)S(1)}, u32[]{:S(2)}, u32[]{:S(2)}) collective-permute-start(bf16[256,256]{1,0:T(8,128)(2,1)S(1)} %add_add_fusion.refs_0_), channel_id=1, source_target_pairs={{0,6},{2,4},{4,2},{6,0},{1,7},{3,5},{5,3},{7,1},{8,14},{10,12},{12... | collective-permute-start | bytes 393224 | tf_op jit(solution)/shard_map/ppermute | solution.py:37
  56.4 3.4 %collective-permute-done.8.refs_3_ = bf16[256,256]{1,0:T(8,128)(2,1)S(1)} collective-permute-done((bf16[256,256]{1,0:T(8,128)(2,1)S(1)}, bf16[256,256]{1,0:T(8,128)(2,1)S(1)}, u32[]{:S(2)}, u32[]{:S(2)}) %collective-permute-start.8) | collective-permute-done | bytes 131104 | tf_op jit(solution)/shard_map/ppermute | solution.py:37
  59.8 0.7 copy-done.9
  60.5 0.5 collective-permute-start.18
  61.0 0.1 collective-permute-start.19
  61.1 0.4 collective-permute-start.20
  61.5 0.7 dynamic-slice_bitcast_fusion.refs_5_.refs_14_
  62.2 0.7 broadcast_select_fusion
  62.9 0.9 copy-done.10
  63.8 0.7 copy-done.12
  64.5 3.2 %section0_front.1 = (bf16[256,256]{1,0:T(8,128)(2,1)S(1)}, bf16[256,1024]{1,0:T(8,128)(2,1)S(1)}) custom-call(s32[3]{0:T(128)S(1)} %copy-done.12, bf16[256,256]{1,0:T(8,128)(2,1)S(1)} %add_add_fusion.refs_0_, bf16[256,256]{1,0:T(8,128)(2,1)S(1)} %collective-permute-done.6.refs_1_, bf16[256,256]{1,0:T(8,128)(2,1)S(1)} %collective-permute-done.7.refs_2_, ...), custom_call_target="tpu_custom_call" | custom-call | flops 603979776 | bytes 2097152 | tf_op jit(solution)/shard_map/section0_front/pallas_call | solution.py:256
  67.7 1.6 %collective-permute-start.11 = (bf16[256,256]{1,0:T(8,128)(2,1)S(1)}, bf16[256,256]{1,0:T(8,128)(2,1)S(1)}, u32[]{:S(2)}, u32[]{:S(2)}) collective-permute-start(bf16[256,256]{1,0:T(8,128)(2,1)S(1)} %get-tuple-element.16.refs_0_), channel_id=1, source_target_pairs={{0,2},{2,0},{4,6},{6,4},{1,3},{3,1},{5,7},{7,5},{8,10},{10,8},{12,... | collective-permute-start | bytes 393224 | tf_op jit(solution)/shard_map/ppermute | solution.py:37
  69.3 1.5 %collective-permute-start.12 = (bf16[256,256]{1,0:T(8,128)(2,1)S(1)}, bf16[256,256]{1,0:T(8,128)(2,1)S(1)}, u32[]{:S(2)}, u32[]{:S(2)}) collective-permute-start(bf16[256,256]{1,0:T(8,128)(2,1)S(1)} %get-tuple-element.16.refs_0_), channel_id=1, source_target_pairs={{0,4},{2,6},{4,0},{6,2},{1,5},{3,7},{5,1},{7,3},{8,12},{10,14},{12... | collective-permute-start | bytes 393224 | tf_op jit(solution)/shard_map/ppermute | solution.py:37
  70.8 0.5 collective-permute-start.13
  71.3 2.9 %collective-permute-done.11.refs_1_ = bf16[256,256]{1,0:T(8,128)(2,1)S(1)} collective-permute-done((bf16[256,256]{1,0:T(8,128)(2,1)S(1)}, bf16[256,256]{1,0:T(8,128)(2,1)S(1)}, u32[]{:S(2)}, u32[]{:S(2)}) %collective-permute-start.11) | collective-permute-done | bytes 131104 | tf_op jit(solution)/shard_map/ppermute | solution.py:37
  74.1 3.8 %collective-permute-done.12.refs_2_ = bf16[256,256]{1,0:T(8,128)(2,1)S(1)} collective-permute-done((bf16[256,256]{1,0:T(8,128)(2,1)S(1)}, bf16[256,256]{1,0:T(8,128)(2,1)S(1)}, u32[]{:S(2)}, u32[]{:S(2)}) %collective-permute-start.12) | collective-permute-done | bytes 131104 | tf_op jit(solution)/shard_map/ppermute | solution.py:37
  77.9 4.8 %section0_back_section1_front.1 = (bf16[256,256]{1,0:T(8,128)(2,1)S(1)}, bf16[256,1024]{1,0:T(8,128)(2,1)S(1)}) custom-call(s32[3]{0:T(128)S(1)} %copy-done.13, bf16[256,256]{1,0:T(8,128)(2,1)S(1)} %get-tuple-element.16.refs_0_, bf16[256,256]{1,0:T(8,128)(2,1)S(1)} %collective-permute-done.11.refs_1_, bf16[256,256]{1,0:T(8,128)(2,1)S(1)} %collective-permute-done.12.refs_2_, ...), custom_call_target="tpu_custom_call" | custom-call | flops 1140850688 | bytes 4194304 | tf_op jit(solution)/shard_map/section0_back_section1_front/pallas_call | solution.py:269
  82.7 1.3 %collective-permute-start.21 = (bf16[256,256]{1,0:T(8,128)(2,1)S(1)}, bf16[256,256]{1,0:T(8,128)(2,1)S(1)}, u32[]{:S(2)}, u32[]{:S(2)}) collective-permute-start(bf16[256,256]{1,0:T(8,128)(2,1)S(1)} %get-tuple-element.18.refs_0_), channel_id=1, source_target_pairs={{0,2},{2,0},{4,6},{6,4},{1,3},{3,1},{5,7},{7,5},{8,10},{10,8},{12,... | collective-permute-start | bytes 393224 | tf_op jit(solution)/shard_map/ppermute | solution.py:37
  84.0 0.9 collective-permute-start.22
  84.8 1.4 %collective-permute-start.23 = (bf16[256,256]{1,0:T(8,128)(2,1)S(1)}, bf16[256,256]{1,0:T(8,128)(2,1)S(1)}, u32[]{:S(2)}, u32[]{:S(2)}) collective-permute-start(bf16[256,256]{1,0:T(8,128)(2,1)S(1)} %get-tuple-element.18.refs_0_), channel_id=1, source_target_pairs={{0,6},{2,4},{4,2},{6,0},{1,7},{3,5},{5,3},{7,1},{8,14},{10,12},{12... | collective-permute-start | bytes 393224 | tf_op jit(solution)/shard_map/ppermute | solution.py:37
  86.3 0.1 copy.13
  86.4 1.8 %collective-permute-done.21.refs_1_ = bf16[256,256]{1,0:T(8,128)(2,1)S(1)} collective-permute-done((bf16[256,256]{1,0:T(8,128)(2,1)S(1)}, bf16[256,256]{1,0:T(8,128)(2,1)S(1)}, u32[]{:S(2)}, u32[]{:S(2)}) %collective-permute-start.21) | collective-permute-done | bytes 131104 | tf_op jit(solution)/shard_map/ppermute | solution.py:37
  88.3 4.0 %collective-permute-done.22.refs_2_ = bf16[256,256]{1,0:T(8,128)(2,1)S(1)} collective-permute-done((bf16[256,256]{1,0:T(8,128)(2,1)S(1)}, bf16[256,256]{1,0:T(8,128)(2,1)S(1)}, u32[]{:S(2)}, u32[]{:S(2)}) %collective-permute-start.22) | collective-permute-done | bytes 131104 | tf_op jit(solution)/shard_map/ppermute | solution.py:37
  92.3 1.0 %copy-done.4 = bf16[256,1024]{1,0:T(8,128)(2,1)S(1)} copy-done((bf16[256,1024]{1,0:T(8,128)(2,1)S(1)}, bf16[256,1024]{1,0:T(8,128)(2,1)}, u32[]{:S(2)}) %copy-start.4) | copy-done | bytes 524312
  93.3 1.0 %copy-done.6 = bf16[256,1024]{1,0:T(8,128)(2,1)S(1)} copy-done((bf16[256,1024]{1,0:T(8,128)(2,1)S(1)}, bf16[256,1024]{1,0:T(8,128)(2,1)}, u32[]{:S(2)}) %copy-start.6) | copy-done | bytes 524312
  94.4 4.1 %section1_back_context.1 = (bf16[256,1024]{1,0:T(8,128)(2,1)}, bf16[256,256]{1,0:T(8,128)(2,1)}) custom-call(s32[3]{0:T(128)S(1)} %copy-done.14, bf16[256,256]{1,0:T(8,128)(2,1)S(1)} %get-tuple-element.18.refs_0_, bf16[256,256]{1,0:T(8,128)(2,1)S(1)} %collective-permute-done.21.refs_1_, bf16[256,256]{1,0:T(8,128)(2,1)S(1)} %collective-permute-done.22.refs_2_, ...), custom_call_target="tpu_custom_call" | custom-call | flops 805306368 | bytes 2097152 | tf_op jit(solution)/shard_map/section1_back_context/pallas_call | solution.py:284
  (54 shorter events, 0.2 us)
Async XLA Ops:
  0.6 85.7 %copy-start = (s32[1,2,256,8]{2,3,1,0:T(8,128)S(1)}, s32[1,2,256,8]{2,3,1,0:T(8,128)}, u32[]{:S(2)}) copy-start(s32[1,2,256,8]{2,3,1,0:T(8,128)} %param.13) | copy-start | bytes 49156
  0.6 2.5 %copy-start.17 = (s32[512,1]{0,1:T(1,128)S(1)}, s32[512,1]{0,1:T(1,128)}, u32[]{:S(2)}) copy-start(s32[512,1]{0,1:T(1,128)} %param.10) | copy-start | bytes 6148
  0.7 2.5 %copy-start.16 = (s32[512]{0:T(512)S(1)}, s32[512]{0:T(512)}, u32[]{:S(2)}) copy-start(s32[512]{0:T(512)} %param.11) | copy-start | bytes 6148
  0.7 31.2 %copy-start.15 = (bf16[1,1024]{1,0:T(2,128)(2,1)S(1)}, bf16[1,1024]{1,0:T(2,128)(2,1)}, u32[]{:S(2)}) copy-start(bf16[1,1024]{1,0:T(2,128)(2,1)} %param.15) | copy-start | bytes 6148
  2.6 65.1 %copy-start.1 = (bf16[1,1024,4,256]{3,1,2,0:T(8,128)(2,1)}, bf16[1,1024,4,256]{3,1,2,0:T(8,128)(2,1)S(1)}, u32[]{:S(2)}) copy-start(bf16[1,1024,4,256]{3,1,2,0:T(8,128)(2,1)S(1)} %copy.15) | copy-start | bytes 6291460
  2.6 19.1 %copy-start.2 = (bf16[1,256,1024]{2,1,0:T(8,128)(2,1)S(1)}, bf16[1,256,1024]{2,1,0:T(8,128)(2,1)}, u32[]{:S(2)}) copy-start(bf16[1,256,1024]{2,1,0:T(8,128)(2,1)} %param.17) | copy-start | bytes 1572868
  2.6 60.3 %collective-permute-start.10 = (bf16[4,1024,256]{2,1,0:T(8,128)(2,1)S(1)}, bf16[4,1024,256]{2,1,0:T(8,128)(2,1)}, u32[]{:S(2)}, u32[]{:S(2)}) collective-permute-start(bf16[4,1024,256]{2,1,0:T(8,128)(2,1)S(1)} %bitcast.15), channel_id=1, source_target_pairs={{0,1},{1,0},{2,3},{3,2},{4,5},{5,4},{6,7},{7,6},{8,9},{9,8},{10,11... | collective-permute-start | bytes 6291464 | tf_op jit(solution)/shard_map/ppermute | solution.py:37
  3.2 5.3 %collective-permute-start = (s32[1,256]{1,0:T(1,128)S(1)}, s32[1,256]{1,0:T(1,128)S(1)}, u32[]{:S(2)}, u32[]{:S(2)}) collective-permute-start(s32[1,256]{1,0:T(1,128)S(1)} %constant_dynamic-slice_fusion.1.refs_0_), channel_id=1, source_target_pairs={{0,8},{8,0},{16,24},{24,16},{1,9},{9,1},{17,25},{25,17},{2,10},{10... | collective-permute-start | bytes 3080 | tf_op jit(solution)/shard_map/ppermute | solution.py:37
  5.8 4.5 %collective-permute-start.1 = (s32[1,256]{1,0:T(1,128)S(1)}, s32[1,256]{1,0:T(1,128)S(1)}, u32[]{:S(2)}, u32[]{:S(2)}) collective-permute-start(s32[1,256]{1,0:T(1,128)S(1)} %constant_dynamic-slice_fusion.1.refs_0_), channel_id=1, source_target_pairs={{0,16},{8,24},{16,0},{24,8},{1,17},{9,25},{17,1},{25,9},{2,18},{10... | collective-permute-start | bytes 3080 | tf_op jit(solution)/shard_map/ppermute | solution.py:37
  8.4 5.4 %collective-permute-start.2 = (s32[1,256]{1,0:T(1,128)S(1)}, s32[1,256]{1,0:T(1,128)S(1)}, u32[]{:S(2)}, u32[]{:S(2)}) collective-permute-start(s32[1,256]{1,0:T(1,128)S(1)} %constant_dynamic-slice_fusion.1.refs_0_), channel_id=1, source_target_pairs={{0,24},{8,16},{16,8},{24,0},{1,25},{9,17},{17,9},{25,1},{2,26},{10... | collective-permute-start | bytes 3080 | tf_op jit(solution)/shard_map/ppermute | solution.py:37
  8.5 52.0 %copy-start.11 = (s32[3]{0:T(128)}, s32[3]{0:T(128)S(1)}, u32[]{:S(2)}) copy-start(s32[3]{0:T(128)S(1)} %pad_add_fusion.pos_ref) | copy-start | bytes 40
  13.8 1.6 %copy-start.7 = (bf16[1024,1024]{1,0:T(8,128)(2,1)S(1)}, bf16[1024,1024]{1,0:T(8,128)(2,1)}, u32[]{:S(2)}) copy-start(bf16[1024,1024]{1,0:T(8,128)(2,1)} %refs_4_.1) | copy-start | bytes 6291460
  17.3 6.8 %collective-permute-start.3 = (bf16[256,256]{1,0:T(8,128)(2,1)S(1)}, bf16[256,256]{1,0:T(8,128)(2,1)S(1)}, u32[]{:S(2)}, u32[]{:S(2)}) collective-permute-start(bf16[256,256]{1,0:T(8,128)(2,1)S(1)} %get-tuple-element.13), channel_id=1, source_target_pairs={{0,8},{8,0},{16,24},{24,16},{1,9},{9,1},{17,25},{25,17},{2,10},{10... | collective-permute-start | bytes 393224 | tf_op jit(solution)/shard_map/ppermute | solution.py:37
  17.3 12.1 %collective-permute-start.4 = (bf16[256,256]{1,0:T(8,128)(2,1)S(1)}, bf16[256,256]{1,0:T(8,128)(2,1)S(1)}, u32[]{:S(2)}, u32[]{:S(2)}) collective-permute-start(bf16[256,256]{1,0:T(8,128)(2,1)S(1)} %get-tuple-element.14), channel_id=1, source_target_pairs={{0,16},{8,24},{16,0},{24,8},{1,17},{9,25},{17,1},{25,9},{2,18},{10... | collective-permute-start | bytes 393224 | tf_op jit(solution)/shard_map/ppermute | solution.py:37
  17.9 14.0 %collective-permute-start.5 = (bf16[256,256]{1,0:T(8,128)(2,1)S(1)}, bf16[256,256]{1,0:T(8,128)(2,1)S(1)}, u32[]{:S(2)}, u32[]{:S(2)}) collective-permute-start(bf16[256,256]{1,0:T(8,128)(2,1)S(1)} %get-tuple-element.15), channel_id=1, source_target_pairs={{0,24},{8,16},{16,8},{24,0},{1,25},{9,17},{17,9},{25,1},{2,26},{10... | collective-permute-start | bytes 393224 | tf_op jit(solution)/shard_map/ppermute | solution.py:37
  21.7 38.7 %collective-permute-start.14 = (bf16[256,1024]{1,0:T(8,128)(2,1)S(1)}, bf16[256,1024]{1,0:T(8,128)(2,1)S(1)}, u32[]{:S(2)}, u32[]{:S(2)}) collective-permute-start(bf16[256,1024]{1,0:T(8,128)(2,1)S(1)} %bitcast.18), channel_id=1, source_target_pairs={{0,2},{2,0},{4,6},{6,4},{1,3},{3,1},{5,7},{7,5},{8,10},{10,8},{12,... | collective-permute-start | bytes 1572872 | tf_op jit(solution)/shard_map/ppermute | solution.py:37
  24.1 36.9 %collective-permute-start.15 = (bf16[256,1024]{1,0:T(8,128)(2,1)S(1)}, bf16[256,1024]{1,0:T(8,128)(2,1)}, u32[]{:S(2)}, u32[]{:S(2)}) collective-permute-start(bf16[256,1024]{1,0:T(8,128)(2,1)S(1)} %bitcast.19), channel_id=1, source_target_pairs={{0,4},{2,6},{4,0},{6,2},{1,5},{3,7},{5,1},{7,3},{8,12},{10,14},{12... | collective-permute-start | bytes 1572872 | tf_op jit(solution)/shard_map/ppermute | solution.py:37
  29.5 31.6 %collective-permute-start.16 = (bf16[256,1024]{1,0:T(8,128)(2,1)S(1)}, bf16[256,1024]{1,0:T(8,128)(2,1)}, u32[]{:S(2)}, u32[]{:S(2)}) collective-permute-start(bf16[256,1024]{1,0:T(8,128)(2,1)S(1)} %bitcast.20), channel_id=1, source_target_pairs={{0,6},{2,4},{4,2},{6,0},{1,7},{3,5},{5,3},{7,1},{8,14},{10,12},{12... | collective-permute-start | bytes 1572872 | tf_op jit(solution)/shard_map/ppermute | solution.py:37
  31.9 1.3 %collective-permute-start.9 = (bf16[1,1024]{1,0:T(2,128)(2,1)S(1)}, bf16[1,1024]{1,0:T(2,128)(2,1)}, u32[]{:S(2)}, u32[]{:S(2)}) collective-permute-start(bf16[1,1024]{1,0:T(2,128)(2,1)S(1)} %copy-done.15), channel_id=1, source_target_pairs={{0,1},{1,0},{2,3},{3,2},{4,5},{5,4},{6,7},{7,6},{8,9},{9,8},{10,11... | collective-permute-start | bytes 6152 | tf_op jit(solution)/shard_map/ppermute | solution.py:37
  33.2 14.3 %collective-permute-start.6 = (bf16[256,256]{1,0:T(8,128)(2,1)S(1)}, bf16[256,256]{1,0:T(8,128)(2,1)S(1)}, u32[]{:S(2)}, u32[]{:S(2)}) collective-permute-start(bf16[256,256]{1,0:T(8,128)(2,1)S(1)} %add_add_fusion.refs_0_), channel_id=1, source_target_pairs={{0,2},{2,0},{4,6},{6,4},{1,3},{3,1},{5,7},{7,5},{8,10},{10,8},{12,... | collective-permute-start | bytes 393224 | tf_op jit(solution)/shard_map/ppermute | solution.py:37
  47.6 6.4 %collective-permute-start.7 = (bf16[256,256]{1,0:T(8,128)(2,1)S(1)}, bf16[256,256]{1,0:T(8,128)(2,1)S(1)}, u32[]{:S(2)}, u32[]{:S(2)}) collective-permute-start(bf16[256,256]{1,0:T(8,128)(2,1)S(1)} %add_add_fusion.refs_0_), channel_id=1, source_target_pairs={{0,4},{2,6},{4,0},{6,2},{1,5},{3,7},{5,1},{7,3},{8,12},{10,14},{12... | collective-permute-start | bytes 393224 | tf_op jit(solution)/shard_map/ppermute | solution.py:37
  53.9 5.9 %collective-permute-start.8 = (bf16[256,256]{1,0:T(8,128)(2,1)S(1)}, bf16[256,256]{1,0:T(8,128)(2,1)S(1)}, u32[]{:S(2)}, u32[]{:S(2)}) collective-permute-start(bf16[256,256]{1,0:T(8,128)(2,1)S(1)} %add_add_fusion.refs_0_), channel_id=1, source_target_pairs={{0,6},{2,4},{4,2},{6,0},{1,7},{3,5},{5,3},{7,1},{8,14},{10,12},{12... | collective-permute-start | bytes 393224 | tf_op jit(solution)/shard_map/ppermute | solution.py:37
  59.8 0.7 copy-start.9
  60.4 8.8 %collective-permute-start.17 = (bf16[256,1024]{1,0:T(8,128)(2,1)S(1)}, bf16[256,1024]{1,0:T(8,128)(2,1)}, u32[]{:S(2)}, u32[]{:S(2)}) collective-permute-start(bf16[256,1024]{1,0:T(8,128)(2,1)S(1)} %bitcast.21), channel_id=1, source_target_pairs={{0,1},{1,0},{2,3},{3,2},{4,5},{5,4},{6,7},{7,6},{8,9},{9,8},{10,11... | collective-permute-start | bytes 1572872 | tf_op jit(solution)/shard_map/ppermute | solution.py:37
  60.5 10.3 %collective-permute-start.18 = (bf16[256,1024]{1,0:T(8,128)(2,1)S(1)}, bf16[256,1024]{1,0:T(8,128)(2,1)}, u32[]{:S(2)}, u32[]{:S(2)}) collective-permute-start(bf16[256,1024]{1,0:T(8,128)(2,1)S(1)} %collective-permute-done.14.refs_5_), channel_id=1, source_target_pairs={{0,1},{1,0},{2,3},{3,2},{4,5},{5,4},{6,7},{7,6},{8,9},{9,8},{10,11... | collective-permute-start | bytes 1572872 | tf_op jit(solution)/shard_map/ppermute | solution.py:37
  61.0 10.3 %collective-permute-start.19 = (bf16[256,1024]{1,0:T(8,128)(2,1)}, bf16[256,1024]{1,0:T(8,128)(2,1)S(1)}, u32[]{:S(2)}, u32[]{:S(2)}) collective-permute-start(bf16[256,1024]{1,0:T(8,128)(2,1)} %collective-permute-done.15.refs_6_), channel_id=1, source_target_pairs={{0,1},{1,0},{2,3},{3,2},{4,5},{5,4},{6,7},{7,6},{8,9},{9,8},{10,11... | collective-permute-start | bytes 1572872 | tf_op jit(solution)/shard_map/ppermute | solution.py:37
  61.1 10.2 %collective-permute-start.20 = (bf16[256,1024]{1,0:T(8,128)(2,1)}, bf16[256,1024]{1,0:T(8,128)(2,1)S(1)}, u32[]{:S(2)}, u32[]{:S(2)}) collective-permute-start(bf16[256,1024]{1,0:T(8,128)(2,1)} %collective-permute-done.16.refs_7_), channel_id=1, source_target_pairs={{0,1},{1,0},{2,3},{3,2},{4,5},{5,4},{6,7},{7,6},{8,9},{9,8},{10,11... | collective-permute-start | bytes 1572872 | tf_op jit(solution)/shard_map/ppermute | solution.py:37
  62.9 0.9 copy-start.10
  63.8 0.7 copy-start.12
  64.5 13.4 %copy-start.13 = (s32[3]{0:T(128)S(1)}, s32[3]{0:T(128)}, u32[]{:S(2)}) copy-start(s32[3]{0:T(128)} %copy-done.11) | copy-start | bytes 40
  67.7 6.4 %collective-permute-start.11 = (bf16[256,256]{1,0:T(8,128)(2,1)S(1)}, bf16[256,256]{1,0:T(8,128)(2,1)S(1)}, u32[]{:S(2)}, u32[]{:S(2)}) collective-permute-start(bf16[256,256]{1,0:T(8,128)(2,1)S(1)} %get-tuple-element.16.refs_0_), channel_id=1, source_target_pairs={{0,2},{2,0},{4,6},{6,4},{1,3},{3,1},{5,7},{7,5},{8,10},{10,8},{12,... | collective-permute-start | bytes 393224 | tf_op jit(solution)/shard_map/ppermute | solution.py:37
  69.3 8.6 %collective-permute-start.12 = (bf16[256,256]{1,0:T(8,128)(2,1)S(1)}, bf16[256,256]{1,0:T(8,128)(2,1)S(1)}, u32[]{:S(2)}, u32[]{:S(2)}) collective-permute-start(bf16[256,256]{1,0:T(8,128)(2,1)S(1)} %get-tuple-element.16.refs_0_), channel_id=1, source_target_pairs={{0,4},{2,6},{4,0},{6,2},{1,5},{3,7},{5,1},{7,3},{8,12},{10,14},{12... | collective-permute-start | bytes 393224 | tf_op jit(solution)/shard_map/ppermute | solution.py:37
  70.8 7.1 %collective-permute-start.13 = (bf16[256,256]{1,0:T(8,128)(2,1)S(1)}, bf16[256,256]{1,0:T(8,128)(2,1)S(1)}, u32[]{:S(2)}, u32[]{:S(2)}) collective-permute-start(bf16[256,256]{1,0:T(8,128)(2,1)S(1)} %get-tuple-element.16.refs_0_), channel_id=1, source_target_pairs={{0,6},{2,4},{4,2},{6,0},{1,7},{3,5},{5,3},{7,1},{8,14},{10,12},{12... | collective-permute-start | bytes 393224 | tf_op jit(solution)/shard_map/ppermute | solution.py:37
  71.3 11.5 %copy-start.3 = (bf16[256,1024]{1,0:T(8,128)(2,1)}, bf16[256,1024]{1,0:T(8,128)(2,1)S(1)}, u32[]{:S(2)}) copy-start(bf16[256,1024]{1,0:T(8,128)(2,1)S(1)} %collective-permute-done.19.refs_10_) | copy-start | bytes 1572868
  71.3 11.5 %copy-start.5 = (bf16[256,1024]{1,0:T(8,128)(2,1)}, bf16[256,1024]{1,0:T(8,128)(2,1)S(1)}, u32[]{:S(2)}) copy-start(bf16[256,1024]{1,0:T(8,128)(2,1)S(1)} %collective-permute-done.20.refs_11_) | copy-start | bytes 1572868
  77.9 8.5 %copy-start.18 = (bf16[256]{0:T(256)(128)(2,1)S(1)}, bf16[256]{0:T(256)(128)(2,1)}, u32[]{:S(2)}) copy-start(bf16[256]{0:T(256)(128)(2,1)} %param.19) | copy-start | bytes 1540
  77.9 14.4 %copy-start.8 = (bf16[1024,256]{1,0:T(8,128)(2,1)S(1)}, bf16[1024,256]{1,0:T(8,128)(2,1)}, u32[]{:S(2)}) copy-start(bf16[1024,256]{1,0:T(8,128)(2,1)} %refs_14_.1) | copy-start | bytes 1572868
  77.9 14.4 %copy-start.14 = (s32[3]{0:T(128)S(1)}, s32[3]{0:T(128)}, u32[]{:S(2)}) copy-start(s32[3]{0:T(128)} %copy-done.11) | copy-start | bytes 40
  82.7 5.5 %collective-permute-start.21 = (bf16[256,256]{1,0:T(8,128)(2,1)S(1)}, bf16[256,256]{1,0:T(8,128)(2,1)S(1)}, u32[]{:S(2)}, u32[]{:S(2)}) collective-permute-start(bf16[256,256]{1,0:T(8,128)(2,1)S(1)} %get-tuple-element.18.refs_0_), channel_id=1, source_target_pairs={{0,2},{2,0},{4,6},{6,4},{1,3},{3,1},{5,7},{7,5},{8,10},{10,8},{12,... | collective-permute-start | bytes 393224 | tf_op jit(solution)/shard_map/ppermute | solution.py:37
  84.0 8.3 %collective-permute-start.22 = (bf16[256,256]{1,0:T(8,128)(2,1)S(1)}, bf16[256,256]{1,0:T(8,128)(2,1)S(1)}, u32[]{:S(2)}, u32[]{:S(2)}) collective-permute-start(bf16[256,256]{1,0:T(8,128)(2,1)S(1)} %get-tuple-element.18.refs_0_), channel_id=1, source_target_pairs={{0,4},{2,6},{4,0},{6,2},{1,5},{3,7},{5,1},{7,3},{8,12},{10,14},{12... | collective-permute-start | bytes 393224 | tf_op jit(solution)/shard_map/ppermute | solution.py:37
  84.8 7.4 %collective-permute-start.23 = (bf16[256,256]{1,0:T(8,128)(2,1)S(1)}, bf16[256,256]{1,0:T(8,128)(2,1)S(1)}, u32[]{:S(2)}, u32[]{:S(2)}) collective-permute-start(bf16[256,256]{1,0:T(8,128)(2,1)S(1)} %get-tuple-element.18.refs_0_), channel_id=1, source_target_pairs={{0,6},{2,4},{4,2},{6,0},{1,7},{3,5},{5,3},{7,1},{8,14},{10,12},{12... | collective-permute-start | bytes 393224 | tf_op jit(solution)/shard_map/ppermute | solution.py:37
  92.3 1.0 %copy-start.4 = (bf16[256,1024]{1,0:T(8,128)(2,1)S(1)}, bf16[256,1024]{1,0:T(8,128)(2,1)}, u32[]{:S(2)}) copy-start(bf16[256,1024]{1,0:T(8,128)(2,1)} %copy-done.3) | copy-start | bytes 1572868
  93.3 1.0 %copy-start.6 = (bf16[256,1024]{1,0:T(8,128)(2,1)S(1)}, bf16[256,1024]{1,0:T(8,128)(2,1)}, u32[]{:S(2)}) copy-start(bf16[256,1024]{1,0:T(8,128)(2,1)} %copy-done.5) | copy-start | bytes 1572868

commit v2 on v1

--- a/solution.py
+++ b/solution.py
@@ -11,10 +11,9 @@
 NBR = 8
 LANES = 128
 EPS = 1e-06
-VMEM_LIMIT = 48 * 1024 * 1024
+VMEM_LIMIT = 20 * 1024 * 1024
 VMEM = pl.BlockSpec(memory_space=pltpu.VMEM)
-ANY = pl.BlockSpec(memory_space=pl.ANY)
-SMEM = pl.BlockSpec(memory_space=pltpu.SMEM)
+HBM = pl.BlockSpec(memory_space=pltpu.HBM)
 F32 = jnp.float32
 BF16 = jnp.bfloat16
 
@@ -45,16 +44,15 @@
     return jnp.transpose(jnp.broadcast_to(row, (count, row.shape[1])))
 
 
-def fetch_kernel(steps, pos_ref, *refs):
+def fetch_kernel(steps, *refs):
     idx_refs, table_ref = refs[:steps], refs[steps]
     out_refs = refs[steps + 1 : 2 * steps + 1]
     tab, sem = refs[2 * steps + 1 :]
     width = tab.shape[1]
-    copy = pltpu.make_async_copy(
-        table_ref.at[:, pl.ds(pl.multiple_of(pos_ref[1] * width, width), width)], tab, sem
-    )
+    at = pl.multiple_of(lax.axis_index("mp") * width, width)
+    copy = pltpu.make_async_copy(table_ref.at[:, pl.ds(at, width)], tab, sem)
     copy.start()
-    first = pos_ref[0] * tab.shape[0]
+    first = lax.axis_index("dp") * tab.shape[0]
     hots = []
     for idx_ref in idx_refs:
         cols = columns_of(idx_ref[...] - first, LANES)
@@ -73,13 +71,13 @@
         out_ref[...] = jnp.dot(hot, tab[...], preferred_element_type=F32).astype(BF16)
 
 
-def fetch(pos, idx_rows, table, width):
+def fetch(idx_rows, table, width):
     steps = len(idx_rows)
     rows = idx_rows[0].shape[1]
     return pl.pallas_call(
         functools.partial(fetch_kernel, steps),
         out_shape=[jax.ShapeDtypeStruct((rows, width), BF16)] * steps,
-        in_specs=[SMEM] + [VMEM] * steps + [ANY],
+        in_specs=[VMEM] * steps + [HBM],
         out_specs=[VMEM] * steps,
         scratch_shapes=[pltpu.VMEM((table.shape[0], width), BF16), pltpu.SemaphoreType.DMA],
         compiler_params=params(),
@@ -89,14 +87,16 @@
             transcendentals=0,
         ),
         name="fetch",
-    )(pos, *idx_rows, table)
+    )(*idx_rows, table)
 
 
 def silu(x):
     return x * jax.nn.sigmoid(x)
 
 
-def start_picked(section, phase, own, other, dst, sem):
+def start_picked(section, own, other, dst, sem):
+    phase = lax.axis_index("phase")
+
     @pl.when(phase == section)
     def _():
         pltpu.make_async_copy(own, dst, sem).start()
@@ -108,6 +108,14 @@
 
 def wait_picked(own, dst, sem):
     pltpu.make_async_copy(own, dst, sem).wait()
+
+
+def back_copy(section, k, steps, o_all, o_buf, o_sem):
+    cols = o_buf.shape[1]
+    at = (section * steps + source_of(lax.axis_index("mp"), k, steps)) * cols
+    return pltpu.make_async_copy(
+        o_all.at[pl.ds(pl.multiple_of(at, cols), cols), :], o_buf.at[k], o_sem.at[k]
+    )
 
 
 def front(x, gain, seg, w_own, w_buf, w_sem, gated_ref):
@@ -136,52 +144,52 @@
         gated_ref[:, head] = (mixed * gates[:, head].astype(F32)).astype(BF16)
 
 
-def back(x, gated_refs, o_own, o_buf, o_sem):
+def back(x, section, gated_refs, o_all, o_buf, o_sem):
     total = x.astype(F32)
     for k, gated_ref in enumerate(gated_refs):
-        wait_picked(o_own[k], o_buf.at[k], o_sem.at[k])
+        back_copy(section, k, len(gated_refs), o_all, o_buf, o_sem).wait()
         part = jnp.dot(gated_ref[...], o_buf[k], preferred_element_type=F32)
         total = total + part.astype(BF16).astype(F32)
     return total.astype(BF16)
 
 
-def first_kernel(steps, pos_ref, *refs):
+def first_kernel(steps, *refs):
     x_refs = refs[:steps]
     gain_ref, seg_ref, w_own, w_other, gated_ref, x_ref, w_buf, w_sem = refs[steps:]
     for g in range(4):
-        start_picked(0, pos_ref[2], w_own.at[g], w_other.at[g], w_buf.at[g], w_sem.at[g])
+        start_picked(0, w_own.at[g], w_other.at[g], w_buf.at[g], w_sem.at[g])
     width = x_refs[0].shape[1]
     for k, piece in enumerate(x_refs):
-        at = pl.multiple_of(source_of(pos_ref[1], k, steps) * width, width)
+        at = pl.multiple_of(source_of(lax.axis_index("mp"), k, steps) * width, width)
         x_ref[:, pl.ds(at, width)] = piece[...]
     front(x_ref[...].astype(F32), gain_ref[...], seg_ref[...], w_own, w_buf, w_sem, gated_ref)
 
 
-def middle_kernel(steps, pos_ref, *refs):
-    gated_refs, o_own, o_other = refs[:steps], refs[steps : 2 * steps], refs[2 * steps : 3 * steps]
-    x_ref, gain_ref, seg_ref, w_own, w_other, gated_ref, x1_ref = refs[3 * steps : 3 * steps + 7]
-    o_buf, o_sem, w_buf, w_sem = refs[3 * steps + 7 :]
+def middle_kernel(steps, *refs):
+    gated_refs = refs[:steps]
+    o_all, x_ref, gain_ref, seg_ref, w_own, w_other, gated_ref, x1_ref = refs[steps : steps + 8]
+    o_buf, o_sem, w_buf, w_sem = refs[steps + 8 :]
     for k in range(steps):
-        start_picked(0, pos_ref[2], o_own[k], o_other[k], o_buf.at[k], o_sem.at[k])
+        back_copy(0, k, steps, o_all, o_buf, o_sem).start()
     for g in range(4):
-        start_picked(1, pos_ref[2], w_own.at[g], w_other.at[g], w_buf.at[g], w_sem.at[g])
-    x1 = back(x_ref[...], gated_refs, o_own, o_buf, o_sem)
+        start_picked(1, w_own.at[g], w_other.at[g], w_buf.at[g], w_sem.at[g])
+    x1 = back(x_ref[...], 0, gated_refs, o_all, o_buf, o_sem)
     x1_ref[...] = x1
     front(x1.astype(F32), gain_ref[...], seg_ref[...], w_own, w_buf, w_sem, gated_ref)
 
 
-def last_kernel(steps, pos_ref, *refs):
-    gated_refs, o_own, o_other = refs[:steps], refs[steps : 2 * steps], refs[2 * steps : 3 * steps]
-    x_ref, neigh_ref, w_ref, bias_ref, states_ref, ctx_ref = refs[3 * steps : 3 * steps + 6]
-    o_buf, o_sem = refs[3 * steps + 6 :]
+def last_kernel(steps, *refs):
+    gated_refs = refs[:steps]
+    o_all, x_ref, neigh_ref, w_ref, bias_ref, states_ref, ctx_ref = refs[steps : steps + 7]
+    o_buf, o_sem = refs[steps + 7 :]
     for k in range(steps):
-        start_picked(1, pos_ref[2], o_own[k], o_other[k], o_buf.at[k], o_sem.at[k])
+        back_copy(1, k, steps, o_all, o_buf, o_sem).start()
     rows, imps = x_ref.shape[0], neigh_ref.shape[0]
     lane = lax.broadcasted_iota(jnp.int32, (imps, rows), 1)
     share = jnp.zeros((imps, rows), F32)
     for n in range(NBR):
         share = share + jnp.where(neigh_ref[:, n : n + 1] == lane, 1.0 / NBR, 0.0)
-    states = back(x_ref[...], gated_refs, o_own, o_buf, o_sem)
+    states = back(x_ref[...], 1, gated_refs, o_all, o_buf, o_sem)
     states_ref[...] = states
     context = jnp.dot(share.astype(BF16), states, preferred_element_type=F32).astype(BF16)
     summed = jnp.dot(context, w_ref[...], preferred_element_type=F32) + bias_ref[...].astype(F32)
@@ -212,8 +220,7 @@
     item_owner, item_row, segments, neighbors, table, gains, w_in, w_out, w_ctx, ctx_bias
 ):
     dp_count, mp_count = lax.axis_size("dp"), lax.axis_size("mp")
-    dp_at, mp_at, phase = lax.axis_index("dp"), lax.axis_index("mp"), lax.axis_index("phase")
-    pos = jnp.stack([dp_at, mp_at, phase]).astype(jnp.int32)
+    phase = lax.axis_index("phase")
     table_rows, width = table.shape
     batches, rows = segments.shape[1], segments.shape[2]
     imps = neighbors.shape[2]
@@ -222,8 +229,7 @@
 
     w_own = jnp.transpose(w_in[0], (1, 0, 2))
     w_other = exchange(w_own, "phase", 1)
-    o_own = spread(w_out[0], "mp")
-    o_other = [exchange(piece, "phase", 1) for piece in o_own]
+    o_all = lax.all_gather(w_out[0], ("phase", "mp"), axis=0, tiled=True)
     gain_other = exchange(gains, "phase", 1)
     gain0 = jnp.where(phase == 0, gains, gain_other)
     gain1 = jnp.where(phase == 0, gain_other, gains)
@@ -233,7 +239,7 @@
     if is_pow2(dp_count) and dp_count <= 8:
         wanted = (item_owner[:, 0] * table_rows + item_row).reshape(batches, rows)
         wanted = lax.dynamic_index_in_dim(wanted, phase, 0, keepdims=True)
-        found = fetch(pos, spread(wanted, "dp"), table, part)
+        found = fetch(spread(wanted, "dp"), table, part)
         piece = found[0]
         for k in range(1, dp_count):
             piece = piece + exchange(found[k], "dp", k)
@@ -256,7 +262,7 @@
     gated, x0 = pl.pallas_call(
         functools.partial(first_kernel, mp_count),
         out_shape=[gated_shape, x_shape],
-        in_specs=[SMEM] + [VMEM] * (mp_count + 2) + [ANY] * 2,
+        in_specs=[VMEM] * (mp_count + 2) + [HBM] * 2,
         out_specs=[VMEM] * 2,
         scratch_shapes=[w_buf, sem4],
         compiler_params=params(),
@@ -264,12 +270,12 @@
             flops=front_flops, bytes_accessed=8 * width * local_cols, transcendentals=0
         ),
         name="section0_front",
-    )(pos, *x_pieces, gain0, seg, w_own, w_other)
+    )(*x_pieces, gain0, seg, w_own, w_other)
 
     gated, x1 = pl.pallas_call(
         functools.partial(middle_kernel, mp_count),
         out_shape=[gated_shape, x_shape],
-        in_specs=[SMEM] + [VMEM] * mp_count + [ANY] * (2 * mp_count) + [VMEM] * 3 + [ANY] * 2,
+        in_specs=[VMEM] * mp_count + [HBM] + [VMEM] * 3 + [HBM] * 2,
         out_specs=[VMEM] * 2,
         scratch_shapes=[o_buf, semk, w_buf, sem4],
         compiler_params=params(),
@@ -279,12 +285,12 @@
             transcendentals=0,
         ),
         name="section0_back_section1_front",
-    )(pos, *spread(gated, "mp"), *o_own, *o_other, x0, gain1, seg, w_own, w_other)
+    )(*spread(gated, "mp"), o_all, x0, gain1, seg, w_own, w_other)
 
     states, ctx = pl.pallas_call(
         functools.partial(last_kernel, mp_count),
         out_shape=[x_shape, jax.ShapeDtypeStruct((imps, w_ctx.shape[1]), BF16)],
-        in_specs=[SMEM] + [VMEM] * mp_count + [ANY] * (2 * mp_count) + [VMEM] * 4,
+        in_specs=[VMEM] * mp_count + [HBM] + [VMEM] * 4,
         out_specs=[VMEM] * 2,
         scratch_shapes=[o_buf, semk],
         compiler_params=params(),
@@ -294,7 +300,7 @@
             transcendentals=0,
         ),
         name="section1_back_context",
-    )(pos, *spread(gated, "mp"), *o_own, *o_other, x1, neigh, w_ctx, ctx_bias[None])
+    )(*spread(gated, "mp"), o_all, x1, neigh, w_ctx, ctx_bias[None])
 
     return (
         states.reshape(1, 1, rows, width),

time: 98.9 us -> 94.5 us (0.956)
  between operations: 0.89 us -> 14.2 us
  waiting for transfers between devices: 45.8 us -> 32.5 us
  starting transfers between devices: 28.3 us -> 20.9 us
  local copies, waits for them, and re-layouts: 8.67 us -> 13.4 us
  Pallas kernels: 13.9 us -> 12.5 us
    ppermute x24 -> x17, waiting for transfers between devices: 45.8 us -> 31.8 us  [exchange(): return lax.ppermute(value, axis, pairs)]
    ppermute x24 -> x17, starting transfers between devices: 28.3 us -> 20.8 us  [exchange(): return lax.ppermute(value, axis, pairs)]
    unnamed x39 -> x33, local copies, waits for them, and re-layouts: 7.84 us -> 12.6 us
  transfers between devices with their start and end apart: 24 -> 18, of which waited for: 12 -> 13; matrix products, arithmetic and copies ran while one was open for 2% -> 4% of each run, Pallas kernels for 5% -> 4%
where the time goes in v2:
time: 94.5 us; the launch traced here: 94.1 us
  waiting for transfers between devices  32.5 us (34%)
  starting transfers between devices  20.9 us (22%)
  between operations  14.2 us (15%)
  local copies, waits for them, and re-layouts  13.4 us (14%)
  Pallas kernels  12.5 us (13%)
    ppermute x17, waiting for transfers between devices, exchange(): return lax.ppermute(value, axis, pairs)  31.8 us
    ppermute x17, starting transfers between devices, exchange(): return lax.ppermute(value, axis, pairs)  20.8 us
    unnamed x33, local copies, waits for them, and re-layouts  12.6 us
    pallas_call x1, Pallas kernels, on_device(): pl.pallas_call(functools.partial(middle_kernel, mp_count), out_shape=[gat...  4.57 us
    pallas_call x1, Pallas kernels, on_device(): pl.pallas_call(functools.partial(last_kernel, mp_count), out_shape=[x_sha...  3.93 us
    pallas_call x1, Pallas kernels, on_device(): pl.pallas_call(functools.partial(first_kernel, mp_count), out_shape=[gate...  2.66 us
  transfers between devices with their start and end apart: 18, of which 13 were waited for; matrix products, arithmetic and copies ran while one was open for 4% of the time, Pallas kernels for 4%

profile of v2, /device:TPU:0, one launch (start us, length us, event | category | flops | bytes accessed | tf_op | source)
XLA Modules:
  0.0 94.1 jit_solution(8492214400802593784)
XLA Ops:
  7.2 0.0 copy-start
  7.2 0.0 all-gather.3.cloned.1.call-start
  7.2 0.7 all-gather.3.cloned.1.call-update
  7.9 1.9 %copy.15 = bf16[1,1024,4,256]{3,1,2,0:T(8,128)(2,1)S(1)} copy(bf16[1,1024,4,256]{3,2,1,0:T(4,128)(2,1)} %param.16) | data formatting | bytes 4194304 | tf_op args[6]
  9.8 0.5 collective-permute-start.10
  10.4 2.7 %collective-permute-start = (s32[1,256]{1,0:T(1,128)S(1)}, s32[1,256]{1,0:T(1,128)S(1)}, u32[]{:S(2)}, u32[]{:S(2)}) collective-permute-start(s32[1,256]{1,0:T(1,128)S(1)} %constant_dynamic-slice_fusion.1.refs_0_), channel_id=1, source_target_pairs={{0,8},{8,0},{16,24},{24,16},{1,9},{9,1},{17,25},{25,17},{2,10},{10... | collective-permute-start | bytes 3080 | tf_op jit(solution)/shard_map/ppermute | solution.py:36
  13.1 2.6 %collective-permute-start.1 = (s32[1,256]{1,0:T(1,128)S(1)}, s32[1,256]{1,0:T(1,128)S(1)}, u32[]{:S(2)}, u32[]{:S(2)}) collective-permute-start(s32[1,256]{1,0:T(1,128)S(1)} %constant_dynamic-slice_fusion.1.refs_0_), channel_id=1, source_target_pairs={{0,16},{8,24},{16,0},{24,8},{1,17},{9,25},{17,1},{25,9},{2,18},{10... | collective-permute-start | bytes 3080 | tf_op jit(solution)/shard_map/ppermute | solution.py:36
  15.7 1.9 %collective-permute-done.1.refs_2_ = s32[1,256]{1,0:T(1,128)S(1)} collective-permute-done((s32[1,256]{1,0:T(1,128)S(1)}, s32[1,256]{1,0:T(1,128)S(1)}, u32[]{:S(2)}, u32[]{:S(2)}) %collective-permute-start.1) | collective-permute-done | bytes 1056 | tf_op jit(solution)/shard_map/ppermute | solution.py:36
  17.6 3.5 %collective-permute-done.2.refs_3_ = s32[1,256]{1,0:T(1,128)S(1)} collective-permute-done((s32[1,256]{1,0:T(1,128)S(1)}, s32[1,256]{1,0:T(1,128)S(1)}, u32[]{:S(2)}, u32[]{:S(2)}) %collective-permute-start.2) | collective-permute-done | bytes 1056 | tf_op jit(solution)/shard_map/ppermute | solution.py:36
  21.0 1.6 %copy-done.3 = bf16[1024,1024]{1,0:T(8,128)(2,1)S(1)} copy-done((bf16[1024,1024]{1,0:T(8,128)(2,1)S(1)}, bf16[1024,1024]{1,0:T(8,128)(2,1)}, u32[]{:S(2)}) %copy-start.3) | copy-done | bytes 2097176
  22.6 1.3 %fetch.1 = (bf16[256,256]{1,0:T(8,128)(2,1)S(1)}, bf16[256,256]{1,0:T(8,128)(2,1)S(1)}, bf16[256,256]{1,0:T(8,128)(2,1)S(1)}, bf16[256,256]{1,0:T(8,128)(2,1)S(1)}) custom-call(s32[1,256]{1,0:T(1,128)S(1)} %constant_dynamic-slice_fusion.1.refs_0_, s32[1,256]{1,0:T(1,128)S(1)} %collective-permute-done.refs_1_, s32[1,256]{1,0:T(1,128)S(1)} %collective-permute-done.1.refs_2_, ...), custom_call_target="tpu_custom_call" | custom-call | flops 536870912 | bytes 524288 | tf_op jit(solution)/shard_map/fetch/pallas_call | solution.py:77
  24.0 0.1 collective-permute-start.3
  24.0 0.6 collective-permute-start.4
  24.6 3.8 %collective-permute-start.5 = (bf16[256,256]{1,0:T(8,128)(2,1)S(1)}, bf16[256,256]{1,0:T(8,128)(2,1)S(1)}, u32[]{:S(2)}, u32[]{:S(2)}) collective-permute-start(bf16[256,256]{1,0:T(8,128)(2,1)S(1)} %get-tuple-element.15), channel_id=1, source_target_pairs={{0,24},{8,16},{16,8},{24,0},{1,25},{9,17},{17,9},{25,1},{2,26},{10... | collective-permute-start | bytes 393224 | tf_op jit(solution)/shard_map/ppermute | solution.py:36
  28.5 2.3 %collective-permute-done.3 = bf16[256,256]{1,0:T(8,128)(2,1)S(1)} collective-permute-done((bf16[256,256]{1,0:T(8,128)(2,1)S(1)}, bf16[256,256]{1,0:T(8,128)(2,1)S(1)}, u32[]{:S(2)}, u32[]{:S(2)}) %collective-permute-start.3) | collective-permute-done | bytes 131104 | tf_op jit(solution)/shard_map/ppermute | solution.py:36
  30.8 5.4 %collective-permute-done.4 = bf16[256,256]{1,0:T(8,128)(2,1)S(1)} collective-permute-done((bf16[256,256]{1,0:T(8,128)(2,1)S(1)}, bf16[256,256]{1,0:T(8,128)(2,1)S(1)}, u32[]{:S(2)}, u32[]{:S(2)}) %collective-permute-start.4) | collective-permute-done | bytes 131104 | tf_op jit(solution)/shard_map/ppermute | solution.py:36
  36.2 1.6 %collective-permute-start.6 = (bf16[256,256]{1,0:T(8,128)(2,1)S(1)}, bf16[256,256]{1,0:T(8,128)(2,1)S(1)}, u32[]{:S(2)}, u32[]{:S(2)}) collective-permute-start(bf16[256,256]{1,0:T(8,128)(2,1)S(1)} %add_add_fusion.refs_0_), channel_id=1, source_target_pairs={{0,2},{2,0},{4,6},{6,4},{1,3},{3,1},{5,7},{7,5},{8,10},{10,8},{12,... | collective-permute-start | bytes 393224 | tf_op jit(solution)/shard_map/ppermute | solution.py:36
  37.8 1.5 %collective-permute-start.7 = (bf16[256,256]{1,0:T(8,128)(2,1)S(1)}, bf16[256,256]{1,0:T(8,128)(2,1)S(1)}, u32[]{:S(2)}, u32[]{:S(2)}) collective-permute-start(bf16[256,256]{1,0:T(8,128)(2,1)S(1)} %add_add_fusion.refs_0_), channel_id=1, source_target_pairs={{0,4},{2,6},{4,0},{6,2},{1,5},{3,7},{5,1},{7,3},{8,12},{10,14},{12... | collective-permute-start | bytes 393224 | tf_op jit(solution)/shard_map/ppermute | solution.py:36
  39.4 0.4 collective-permute-start.8
  39.8 0.6 broadcast_select_fusion
  40.4 5.0 %collective-permute-done.6.refs_1_ = bf16[256,256]{1,0:T(8,128)(2,1)S(1)} collective-permute-done((bf16[256,256]{1,0:T(8,128)(2,1)S(1)}, bf16[256,256]{1,0:T(8,128)(2,1)S(1)}, u32[]{:S(2)}, u32[]{:S(2)}) %collective-permute-start.6) | collective-permute-done | bytes 131104 | tf_op jit(solution)/shard_map/ppermute | solution.py:36
  45.5 1.9 %collective-permute-done.7.refs_2_ = bf16[256,256]{1,0:T(8,128)(2,1)S(1)} collective-permute-done((bf16[256,256]{1,0:T(8,128)(2,1)S(1)}, bf16[256,256]{1,0:T(8,128)(2,1)S(1)}, u32[]{:S(2)}, u32[]{:S(2)}) %collective-permute-start.7) | collective-permute-done | bytes 131104 | tf_op jit(solution)/shard_map/ppermute | solution.py:36
  47.3 3.6 %collective-permute-done.8.refs_3_ = bf16[256,256]{1,0:T(8,128)(2,1)S(1)} collective-permute-done((bf16[256,256]{1,0:T(8,128)(2,1)S(1)}, bf16[256,256]{1,0:T(8,128)(2,1)S(1)}, u32[]{:S(2)}, u32[]{:S(2)}) %collective-permute-start.8) | collective-permute-done | bytes 131104 | tf_op jit(solution)/shard_map/ppermute | solution.py:36
  50.9 2.7 %section0_front.1 = (bf16[256,256]{1,0:T(8,128)(2,1)S(1)}, bf16[256,1024]{1,0:T(8,128)(2,1)S(1)}) custom-call(bf16[256,256]{1,0:T(8,128)(2,1)S(1)} %add_add_fusion.refs_0_, bf16[256,256]{1,0:T(8,128)(2,1)S(1)} %collective-permute-done.6.refs_1_, bf16[256,256]{1,0:T(8,128)(2,1)S(1)} %collective-permute-done.7.refs_2_, ...), custom_call_target="tpu_custom_call" | custom-call | flops 603979776 | bytes 2097152 | tf_op jit(solution)/shard_map/section0_front/pallas_call | solution.py:262
  53.6 0.8 copy-done.5
  54.4 1.5 %collective-permute-start.11 = (bf16[256,256]{1,0:T(8,128)(2,1)S(1)}, bf16[256,256]{1,0:T(8,128)(2,1)S(1)}, u32[]{:S(2)}, u32[]{:S(2)}) collective-permute-start(bf16[256,256]{1,0:T(8,128)(2,1)S(1)} %get-tuple-element.16.refs_0_), channel_id=1, source_target_pairs={{0,2},{2,0},{4,6},{6,4},{1,3},{3,1},{5,7},{7,5},{8,10},{10,8},{12,... | collective-permute-start | bytes 393224 | tf_op jit(solution)/shard_map/ppermute | solution.py:36
  55.9 0.5 collective-permute-start.12
  56.4 1.5 %collective-permute-start.13 = (bf16[256,256]{1,0:T(8,128)(2,1)S(1)}, bf16[256,256]{1,0:T(8,128)(2,1)S(1)}, u32[]{:S(2)}, u32[]{:S(2)}) collective-permute-start(bf16[256,256]{1,0:T(8,128)(2,1)S(1)} %get-tuple-element.16.refs_0_), channel_id=1, source_target_pairs={{0,6},{2,4},{4,2},{6,0},{1,7},{3,5},{5,3},{7,1},{8,14},{10,12},{12... | collective-permute-start | bytes 393224 | tf_op jit(solution)/shard_map/ppermute | solution.py:36
  57.9 1.5 %collective-permute-done.11.refs_1_ = bf16[256,256]{1,0:T(8,128)(2,1)S(1)} collective-permute-done((bf16[256,256]{1,0:T(8,128)(2,1)S(1)}, bf16[256,256]{1,0:T(8,128)(2,1)S(1)}, u32[]{:S(2)}, u32[]{:S(2)}) %collective-permute-start.11) | collective-permute-done | bytes 131104 | tf_op jit(solution)/shard_map/ppermute | solution.py:36
  59.4 1.5 %collective-permute-done.12.refs_2_ = bf16[256,256]{1,0:T(8,128)(2,1)S(1)} collective-permute-done((bf16[256,256]{1,0:T(8,128)(2,1)S(1)}, bf16[256,256]{1,0:T(8,128)(2,1)S(1)}, u32[]{:S(2)}, u32[]{:S(2)}) %collective-permute-start.12) | collective-permute-done | bytes 131104 | tf_op jit(solution)/shard_map/ppermute | solution.py:36
  60.8 1.4 %collective-permute-done.13.refs_3_ = bf16[256,256]{1,0:T(8,128)(2,1)S(1)} collective-permute-done((bf16[256,256]{1,0:T(8,128)(2,1)S(1)}, bf16[256,256]{1,0:T(8,128)(2,1)S(1)}, u32[]{:S(2)}, u32[]{:S(2)}) %collective-permute-start.13) | collective-permute-done | bytes 131104 | tf_op jit(solution)/shard_map/ppermute | solution.py:36
  62.3 0.7 copy-done.7
  62.9 2.2 %copy-done.1 = bf16[1,2048,1024]{2,1,0:T(8,128)(2,1)S(1)} copy-done((bf16[1,2048,1024]{2,1,0:T(8,128)(2,1)S(1)}, bf16[1,2048,1024]{2,1,0:T(8,128)(2,1)}, u32[]{:S(2)}) %copy-start.1) | copy-done | bytes 4194328
  65.1 1.0 %copy-done.6 = bf16[256,1024]{1,0:T(8,128)(2,1)S(1)} copy-done((bf16[256,1024]{1,0:T(8,128)(2,1)S(1)}, bf16[256,1024]{1,0:T(8,128)(2,1)}, u32[]{:S(2)}) %copy-start.6) | copy-done | bytes 524312
  66.2 0.9 copy-done.8
  67.1 0.7 copy-done.9
  67.7 0.7 copy-done.11
  68.4 4.6 %section0_back_section1_front.1 = (bf16[256,256]{1,0:T(8,128)(2,1)}, bf16[256,1024]{1,0:T(8,128)(2,1)S(1)}) custom-call(bf16[256,256]{1,0:T(8,128)(2,1)S(1)} %get-tuple-element.16.refs_0_, bf16[256,256]{1,0:T(8,128)(2,1)S(1)} %collective-permute-done.11.refs_1_, bf16[256,256]{1,0:T(8,128)(2,1)S(1)} %collective-permute-done.12.refs_2_, ...), custom_call_target="tpu_custom_call" | custom-call | flops 1140850688 | bytes 4194304 | tf_op jit(solution)/shard_map/section0_back_section1_front/pallas_call | solution.py:275
  73.0 0.6 collective-permute-start.14
  73.6 1.5 %collective-permute-start.15 = (bf16[256,256]{1,0:T(8,128)(2,1)}, bf16[256,256]{1,0:T(8,128)(2,1)S(1)}, u32[]{:S(2)}, u32[]{:S(2)}) collective-permute-start(bf16[256,256]{1,0:T(8,128)(2,1)} %get-tuple-element.18.refs_0_), channel_id=1, source_target_pairs={{0,4},{2,6},{4,0},{6,2},{1,5},{3,7},{5,1},{7,3},{8,12},{10,14},{12... | collective-permute-start | bytes 393224 | tf_op jit(solution)/shard_map/ppermute | solution.py:36
  75.1 1.5 %collective-permute-start.16 = (bf16[256,256]{1,0:T(8,128)(2,1)}, bf16[256,256]{1,0:T(8,128)(2,1)S(1)}, u32[]{:S(2)}, u32[]{:S(2)}) collective-permute-start(bf16[256,256]{1,0:T(8,128)(2,1)} %get-tuple-element.18.refs_0_), channel_id=1, source_target_pairs={{0,6},{2,4},{4,2},{6,0},{1,7},{3,5},{5,3},{7,1},{8,14},{10,12},{12... | collective-permute-start | bytes 393224 | tf_op jit(solution)/shard_map/ppermute | solution.py:36
  76.5 0.1 copy.13
  76.7 0.7 broadcast_in_dim.3.refs_8_
  77.3 0.9 collective-permute-done.14.refs_1_
  78.2 0.5 collective-permute-done.15.refs_2_
  78.7 2.4 %collective-permute-done.16.refs_3_ = bf16[256,256]{1,0:T(8,128)(2,1)S(1)} collective-permute-done((bf16[256,256]{1,0:T(8,128)(2,1)}, bf16[256,256]{1,0:T(8,128)(2,1)S(1)}, u32[]{:S(2)}, u32[]{:S(2)}) %collective-permute-start.16) | collective-permute-done | bytes 131104 | tf_op jit(solution)/shard_map/ppermute | solution.py:36
  81.2 2.2 %copy-done.2 = bf16[1,2048,1024]{2,1,0:T(8,128)(2,1)S(1)} copy-done((bf16[1,2048,1024]{2,1,0:T(8,128)(2,1)S(1)}, bf16[1,2048,1024]{2,1,0:T(8,128)(2,1)}, u32[]{:S(2)}) %copy-start.2) | copy-done | bytes 4194328
  83.4 3.9 %section1_back_context.1 = (bf16[256,1024]{1,0:T(8,128)(2,1)}, bf16[256,256]{1,0:T(8,128)(2,1)}) custom-call(bf16[256,256]{1,0:T(8,128)(2,1)} %get-tuple-element.18.refs_0_, bf16[256,256]{1,0:T(8,128)(2,1)S(1)} %collective-permute-done.14.refs_1_, bf16[256,256]{1,0:T(8,128)(2,1)S(1)} %collective-permute-done.15.refs_2_, ...), custom_call_target="tpu_custom_call" | custom-call | flops 805306368 | bytes 2097152 | tf_op jit(solution)/shard_map/section1_back_context/pallas_call | solution.py:290
  (36 shorter events, 0.1 us)
Async XLA Ops:
  7.2 69.4 %copy-start = (s32[1,2,256,8]{2,3,1,0:T(8,128)S(1)}, s32[1,2,256,8]{2,3,1,0:T(8,128)}, u32[]{:S(2)}) copy-start(s32[1,2,256,8]{2,3,1,0:T(8,128)} %param.13) | copy-start | bytes 49156
  7.2 55.7 %all-gather.3.cloned.1.call-start = ((), (), s32[]{:S(2)}) async-start(), calls=%async_computation | async-start | bytes 4718592 | tf_op jit(solution)/shard_map/all_gather | solution.py:232
  7.9 2.4 %copy-start.14 = (s32[512,1]{0,1:T(1,128)S(1)}, s32[512,1]{0,1:T(1,128)}, u32[]{:S(2)}) copy-start(s32[512,1]{0,1:T(1,128)} %param.10) | copy-start | bytes 6148
  7.9 2.4 %copy-start.13 = (s32[512]{0:T(512)S(1)}, s32[512]{0:T(512)}, u32[]{:S(2)}) copy-start(s32[512]{0:T(512)} %param.11) | copy-start | bytes 6148
  9.8 18.6 %copy-start.12 = (bf16[1,1024]{1,0:T(2,128)(2,1)S(1)}, bf16[1,1024]{1,0:T(2,128)(2,1)}, u32[]{:S(2)}) copy-start(bf16[1,1024]{1,0:T(2,128)(2,1)} %param.15) | copy-start | bytes 6148
  9.8 18.6 %copy-start.15 = (s32[1,2,256]{2,1,0:T(2,128)S(1)}, s32[1,2,256]{2,1,0:T(2,128)}, u32[]{:S(2)}) copy-start(s32[1,2,256]{2,1,0:T(2,128)} %param.12) | copy-start | bytes 6148
  9.8 41.1 %collective-permute-start.10 = (bf16[4,1024,256]{2,1,0:T(8,128)(2,1)S(1)}, bf16[4,1024,256]{2,1,0:T(8,128)(2,1)}, u32[]{:S(2)}, u32[]{:S(2)}) collective-permute-start(bf16[4,1024,256]{2,1,0:T(8,128)(2,1)S(1)} %bitcast.12), channel_id=1, source_target_pairs={{0,1},{1,0},{2,3},{3,2},{4,5},{5,4},{6,7},{7,6},{8,9},{9,8},{10,11... | collective-permute-start | bytes 6291464 | tf_op jit(solution)/shard_map/ppermute | solution.py:36
  10.4 5.3 %collective-permute-start = (s32[1,256]{1,0:T(1,128)S(1)}, s32[1,256]{1,0:T(1,128)S(1)}, u32[]{:S(2)}, u32[]{:S(2)}) collective-permute-start(s32[1,256]{1,0:T(1,128)S(1)} %constant_dynamic-slice_fusion.1.refs_0_), channel_id=1, source_target_pairs={{0,8},{8,0},{16,24},{24,16},{1,9},{9,1},{17,25},{25,17},{2,10},{10... | collective-permute-start | bytes 3080 | tf_op jit(solution)/shard_map/ppermute | solution.py:36
  13.1 4.5 %collective-permute-start.1 = (s32[1,256]{1,0:T(1,128)S(1)}, s32[1,256]{1,0:T(1,128)S(1)}, u32[]{:S(2)}, u32[]{:S(2)}) collective-permute-start(s32[1,256]{1,0:T(1,128)S(1)} %constant_dynamic-slice_fusion.1.refs_0_), channel_id=1, source_target_pairs={{0,16},{8,24},{16,0},{24,8},{1,17},{9,25},{17,1},{25,9},{2,18},{10... | collective-permute-start | bytes 3080 | tf_op jit(solution)/shard_map/ppermute | solution.py:36
  15.7 5.4 %collective-permute-start.2 = (s32[1,256]{1,0:T(1,128)S(1)}, s32[1,256]{1,0:T(1,128)S(1)}, u32[]{:S(2)}, u32[]{:S(2)}) collective-permute-start(s32[1,256]{1,0:T(1,128)S(1)} %constant_dynamic-slice_fusion.1.refs_0_), channel_id=1, source_target_pairs={{0,24},{8,16},{16,8},{24,0},{1,25},{9,17},{17,9},{25,1},{2,26},{10... | collective-permute-start | bytes 3080 | tf_op jit(solution)/shard_map/ppermute | solution.py:36
  21.0 1.6 %copy-start.3 = (bf16[1024,1024]{1,0:T(8,128)(2,1)S(1)}, bf16[1024,1024]{1,0:T(8,128)(2,1)}, u32[]{:S(2)}) copy-start(bf16[1024,1024]{1,0:T(8,128)(2,1)} %refs_4_.1) | copy-start | bytes 6291460
  24.0 6.8 %collective-permute-start.3 = (bf16[256,256]{1,0:T(8,128)(2,1)S(1)}, bf16[256,256]{1,0:T(8,128)(2,1)S(1)}, u32[]{:S(2)}, u32[]{:S(2)}) collective-permute-start(bf16[256,256]{1,0:T(8,128)(2,1)S(1)} %get-tuple-element.13), channel_id=1, source_target_pairs={{0,8},{8,0},{16,24},{24,16},{1,9},{9,1},{17,25},{25,17},{2,10},{10... | collective-permute-start | bytes 393224 | tf_op jit(solution)/shard_map/ppermute | solution.py:36
  24.0 12.2 %collective-permute-start.4 = (bf16[256,256]{1,0:T(8,128)(2,1)S(1)}, bf16[256,256]{1,0:T(8,128)(2,1)S(1)}, u32[]{:S(2)}, u32[]{:S(2)}) collective-permute-start(bf16[256,256]{1,0:T(8,128)(2,1)S(1)} %get-tuple-element.14), channel_id=1, source_target_pairs={{0,16},{8,24},{16,0},{24,8},{1,17},{9,25},{17,1},{25,9},{2,18},{10... | collective-permute-start | bytes 393224 | tf_op jit(solution)/shard_map/ppermute | solution.py:36
  24.6 11.6 %collective-permute-start.5 = (bf16[256,256]{1,0:T(8,128)(2,1)S(1)}, bf16[256,256]{1,0:T(8,128)(2,1)S(1)}, u32[]{:S(2)}, u32[]{:S(2)}) collective-permute-start(bf16[256,256]{1,0:T(8,128)(2,1)S(1)} %get-tuple-element.15), channel_id=1, source_target_pairs={{0,24},{8,16},{16,8},{24,0},{1,25},{9,17},{17,9},{25,1},{2,26},{10... | collective-permute-start | bytes 393224 | tf_op jit(solution)/shard_map/ppermute | solution.py:36
  28.4 11.4 %collective-permute-start.9 = (bf16[1,1024]{1,0:T(2,128)(2,1)S(1)}, bf16[1,1024]{1,0:T(2,128)(2,1)S(1)}, u32[]{:S(2)}, u32[]{:S(2)}) collective-permute-start(bf16[1,1024]{1,0:T(2,128)(2,1)S(1)} %copy-done.12), channel_id=1, source_target_pairs={{0,1},{1,0},{2,3},{3,2},{4,5},{5,4},{6,7},{7,6},{8,9},{9,8},{10,11... | collective-permute-start | bytes 6152 | tf_op jit(solution)/shard_map/ppermute | solution.py:36
  28.4 25.1 %copy-start.10 = (s32[1,256]{1,0:T(1,128)}, s32[1,256]{1,0:T(1,128)S(1)}, u32[]{:S(2)}) copy-start(s32[1,256]{1,0:T(1,128)S(1)} %dynamic-slice_bitcast_fusion.refs_5_.refs_7_) | copy-start | bytes 3076
  36.2 9.2 %collective-permute-start.6 = (bf16[256,256]{1,0:T(8,128)(2,1)S(1)}, bf16[256,256]{1,0:T(8,128)(2,1)S(1)}, u32[]{:S(2)}, u32[]{:S(2)}) collective-permute-start(bf16[256,256]{1,0:T(8,128)(2,1)S(1)} %add_add_fusion.refs_0_), channel_id=1, source_target_pairs={{0,2},{2,0},{4,6},{6,4},{1,3},{3,1},{5,7},{7,5},{8,10},{10,8},{12,... | collective-permute-start | bytes 393224 | tf_op jit(solution)/shard_map/ppermute | solution.py:36
  37.8 9.5 %collective-permute-start.7 = (bf16[256,256]{1,0:T(8,128)(2,1)S(1)}, bf16[256,256]{1,0:T(8,128)(2,1)S(1)}, u32[]{:S(2)}, u32[]{:S(2)}) collective-permute-start(bf16[256,256]{1,0:T(8,128)(2,1)S(1)} %add_add_fusion.refs_0_), channel_id=1, source_target_pairs={{0,4},{2,6},{4,0},{6,2},{1,5},{3,7},{5,1},{7,3},{8,12},{10,14},{12... | collective-permute-start | bytes 393224 | tf_op jit(solution)/shard_map/ppermute | solution.py:36
  39.4 11.5 %collective-permute-start.8 = (bf16[256,256]{1,0:T(8,128)(2,1)S(1)}, bf16[256,256]{1,0:T(8,128)(2,1)S(1)}, u32[]{:S(2)}, u32[]{:S(2)}) collective-permute-start(bf16[256,256]{1,0:T(8,128)(2,1)S(1)} %add_add_fusion.refs_0_), channel_id=1, source_target_pairs={{0,6},{2,4},{4,2},{6,0},{1,7},{3,5},{5,3},{7,1},{8,14},{10,12},{12... | collective-permute-start | bytes 393224 | tf_op jit(solution)/shard_map/ppermute | solution.py:36
  53.6 0.8 copy-start.5
  54.4 5.0 %collective-permute-start.11 = (bf16[256,256]{1,0:T(8,128)(2,1)S(1)}, bf16[256,256]{1,0:T(8,128)(2,1)S(1)}, u32[]{:S(2)}, u32[]{:S(2)}) collective-permute-start(bf16[256,256]{1,0:T(8,128)(2,1)S(1)} %get-tuple-element.16.refs_0_), channel_id=1, source_target_pairs={{0,2},{2,0},{4,6},{6,4},{1,3},{3,1},{5,7},{7,5},{8,10},{10,8},{12,... | collective-permute-start | bytes 393224 | tf_op jit(solution)/shard_map/ppermute | solution.py:36
  55.9 5.0 %collective-permute-start.12 = (bf16[256,256]{1,0:T(8,128)(2,1)S(1)}, bf16[256,256]{1,0:T(8,128)(2,1)S(1)}, u32[]{:S(2)}, u32[]{:S(2)}) collective-permute-start(bf16[256,256]{1,0:T(8,128)(2,1)S(1)} %get-tuple-element.16.refs_0_), channel_id=1, source_target_pairs={{0,4},{2,6},{4,0},{6,2},{1,5},{3,7},{5,1},{7,3},{8,12},{10,14},{12... | collective-permute-start | bytes 393224 | tf_op jit(solution)/shard_map/ppermute | solution.py:36
  56.4 5.9 %collective-permute-start.13 = (bf16[256,256]{1,0:T(8,128)(2,1)S(1)}, bf16[256,256]{1,0:T(8,128)(2,1)S(1)}, u32[]{:S(2)}, u32[]{:S(2)}) collective-permute-start(bf16[256,256]{1,0:T(8,128)(2,1)S(1)} %get-tuple-element.16.refs_0_), channel_id=1, source_target_pairs={{0,6},{2,4},{4,2},{6,0},{1,7},{3,5},{5,3},{7,1},{8,14},{10,12},{12... | collective-permute-start | bytes 393224 | tf_op jit(solution)/shard_map/ppermute | solution.py:36
  62.3 0.7 copy-start.7
  62.9 2.2 %copy-start.1 = (bf16[1,2048,1024]{2,1,0:T(8,128)(2,1)S(1)}, bf16[1,2048,1024]{2,1,0:T(8,128)(2,1)}, u32[]{:S(2)}) copy-start(bf16[1,2048,1024]{2,1,0:T(8,128)(2,1)} %all-gather.3.cloned.1.call-done) | copy-start | bytes 12582916
  65.1 1.0 %copy-start.6 = (bf16[256,1024]{1,0:T(8,128)(2,1)S(1)}, bf16[256,1024]{1,0:T(8,128)(2,1)}, u32[]{:S(2)}) copy-start(bf16[256,1024]{1,0:T(8,128)(2,1)} %copy-done.5) | copy-start | bytes 1572868
  66.2 0.9 copy-start.8
  67.1 0.7 copy-start.9
  67.7 0.7 copy-start.11
  68.4 12.8 %copy-start.4 = (bf16[1024,256]{1,0:T(8,128)(2,1)S(1)}, bf16[1024,256]{1,0:T(8,128)(2,1)}, u32[]{:S(2)}) copy-start(bf16[1024,256]{1,0:T(8,128)(2,1)} %refs_7_.1) | copy-start | bytes 1572868
  73.0 5.2 %collective-permute-start.14 = (bf16[256,256]{1,0:T(8,128)(2,1)}, bf16[256,256]{1,0:T(8,128)(2,1)S(1)}, u32[]{:S(2)}, u32[]{:S(2)}) collective-permute-start(bf16[256,256]{1,0:T(8,128)(2,1)} %get-tuple-element.18.refs_0_), channel_id=1, source_target_pairs={{0,2},{2,0},{4,6},{6,4},{1,3},{3,1},{5,7},{7,5},{8,10},{10,8},{12,... | collective-permute-start | bytes 393224 | tf_op jit(solution)/shard_map/ppermute | solution.py:36
  73.6 5.2 %collective-permute-start.15 = (bf16[256,256]{1,0:T(8,128)(2,1)}, bf16[256,256]{1,0:T(8,128)(2,1)S(1)}, u32[]{:S(2)}, u32[]{:S(2)}) collective-permute-start(bf16[256,256]{1,0:T(8,128)(2,1)} %get-tuple-element.18.refs_0_), channel_id=1, source_target_pairs={{0,4},{2,6},{4,0},{6,2},{1,5},{3,7},{5,1},{7,3},{8,12},{10,14},{12... | collective-permute-start | bytes 393224 | tf_op jit(solution)/shard_map/ppermute | solution.py:36
  75.1 6.1 %collective-permute-start.16 = (bf16[256,256]{1,0:T(8,128)(2,1)}, bf16[256,256]{1,0:T(8,128)(2,1)S(1)}, u32[]{:S(2)}, u32[]{:S(2)}) collective-permute-start(bf16[256,256]{1,0:T(8,128)(2,1)} %get-tuple-element.18.refs_0_), channel_id=1, source_target_pairs={{0,6},{2,4},{4,2},{6,0},{1,7},{3,5},{5,3},{7,1},{8,14},{10,12},{12... | collective-permute-start | bytes 393224 | tf_op jit(solution)/shard_map/ppermute | solution.py:36
  81.2 2.2 %copy-start.2 = (bf16[1,2048,1024]{2,1,0:T(8,128)(2,1)S(1)}, bf16[1,2048,1024]{2,1,0:T(8,128)(2,1)}, u32[]{:S(2)}) copy-start(bf16[1,2048,1024]{2,1,0:T(8,128)(2,1)} %all-gather.3.cloned.1.call-done) | copy-start | bytes 12582916
Sparse Core Ops, SparseCore 0:
  9.9 45.0 all-gather.2

commit v3 on v2

v3 whole, which is shorter than its diff:
```python
import functools

import jax
import jax.numpy as jnp
from jax import lax
from jax.experimental import pallas as pl
from jax.experimental.pallas import tpu as pltpu
from jax.sharding import PartitionSpec as P

HD = 128
NBR = 8
LANES = 128
EPS = 1e-06
VMEM_LIMIT = 20 * 1024 * 1024
VMEM = pl.BlockSpec(memory_space=pltpu.VMEM)
HBM = pl.BlockSpec(memory_space=pltpu.HBM)
F32 = jnp.float32
BF16 = jnp.bfloat16


def params():
    return pltpu.CompilerParams(vmem_limit_bytes=VMEM_LIMIT)


def is_pow2(n):
    return n & (n - 1) == 0


def source_of(me, k, n):
    return me ^ k if is_pow2(n) else lax.rem(me + n - k, n)


def exchange(value, axis, k):
    n = lax.axis_size(axis)
    pairs = [(i, i ^ k if is_pow2(n) else (i + k) % n) for i in range(n)]
    return lax.ppermute(value, axis, pairs)


def spread(value, axis):
    return [value] + [exchange(value, axis, k) for k in range(1, lax.axis_size(axis))]


def swap(blocks, axis):
    return lax.all_to_all(blocks, axis, split_axis=0, concat_axis=0, tiled=True)


def columns_of(row, count):
    return jnp.transpose(jnp.broadcast_to(row, (count, row.shape[1])))


def silu(x):
    return x * jax.nn.sigmoid(x)


def fetch_kernel(asked_ref, table_ref, out_ref, tab, sem):
    width = tab.shape[1]
    at = pl.multiple_of(lax.axis_index("mp") * width, width)
    copy = pltpu.make_async_copy(table_ref.at[:, pl.ds(at, width)], tab, sem)
    copy.start()
    first = lax.axis_index("dp") * tab.shape[0]
    phase = lax.axis_index("phase")
    hots = []
    for d in range(out_ref.shape[0]):
        cols = columns_of(asked_ref[d, pl.ds(phase, 1), :] - first, LANES)
        lane = lax.broadcasted_iota(jnp.int32, cols.shape, 1)
        hots.append(
            jnp.concatenate(
                [
                    jnp.where(cols == lane + c, 1.0, 0.0).astype(BF16)
                    for c in range(0, tab.shape[0], LANES)
                ],
                axis=1,
            )
        )
    copy.wait()
    for d, hot in enumerate(hots):
        out_ref[d] = jnp.dot(hot, tab[...], preferred_element_type=F32).astype(BF16)


def fetch(asked, table, width):
    count, rows = asked.shape[0], asked.shape[2]
    return pl.pallas_call(
        fetch_kernel,
        out_shape=jax.ShapeDtypeStruct((count, rows, width), BF16),
        in_specs=[VMEM, HBM],
        out_specs=VMEM,
        scratch_shapes=[pltpu.VMEM((table.shape[0], width), BF16), pltpu.SemaphoreType.DMA],
        compiler_params=params(),
        cost_estimate=pl.CostEstimate(
            flops=2 * count * rows * width * table.shape[0],
            bytes_accessed=2 * width * table.shape[0],
            transcendentals=0,
        ),
        name="fetch",
    )(asked, table)


def start_picked(section, own, other, dst, sem):
    phase = lax.axis_index("phase")

    @pl.when(phase == section)
    def _():
        pltpu.make_async_copy(own, dst, sem).start()

    @pl.when(phase != section)
    def _():
        pltpu.make_async_copy(other, dst, sem).start()


def wait_picked(own, dst, sem):
    pltpu.make_async_copy(own, dst, sem).wait()


def front(x, section, gain_own, gain_other, seg_ref, w_own, w_buf, w_sem, gated_ref):
    phase = lax.axis_index("phase")
    rows, local_cols = x.shape[0], w_buf.shape[2]
    gain = jnp.where(phase == section, gain_own[...].astype(F32), gain_other[...].astype(F32))
    inv = lax.rsqrt(jnp.mean(x * x, axis=-1, keepdims=True) + EPS)
    normed = (x * inv * gain).astype(BF16)
    proj = []
    for g in range(4):
        wait_picked(w_own.at[g], w_buf.at[g], w_sem.at[g])
        proj.append(
            silu(jnp.dot(normed, w_buf[g], preferred_element_type=F32)).astype(BF16)
        )
    gates, values, queries, keys = proj
    seg = seg_ref[0, pl.ds(phase, 1), :]
    seg_cols = columns_of(seg, rows)
    at_row = lax.broadcasted_iota(jnp.int32, (rows, rows), 0)
    at_col = lax.broadcasted_iota(jnp.int32, (rows, rows), 1)
    allowed = (at_col <= at_row) & (seg_cols == seg)
    for h in range(0, local_cols, HD):
        head = slice(h, h + HD)
        scores = lax.dot_general(
            queries[:, head], keys[:, head], (((1,), (1,)), ((), ())), preferred_element_type=F32
        ) * HD ** (-0.5)
        weights = (jnp.where(allowed, silu(scores), 0.0) / rows).astype(BF16)
        mixed = jnp.dot(weights, values[:, head], preferred_element_type=F32)
        mixed = mixed * lax.rsqrt(jnp.mean(mixed * mixed, axis=-1, keepdims=True) + EPS)
        gated = (mixed * gates[:, head].astype(F32)).astype(BF16)
        for j in range(gated_ref.shape[0]):
            gated_ref[j, :, head] = gated


def back(x, gated_ref, o_own, o_buf, o_sem):
    steps = len(o_own)
    total = x.astype(F32)
    for k in range(steps):
        wait_picked(o_own[k], o_buf.at[k], o_sem.at[k])
        gated = gated_ref[source_of(lax.axis_index("mp"), k, steps)]
        part = jnp.dot(gated, o_buf[k], preferred_element_type=F32)
        total = total + part.astype(BF16).astype(F32)
    return total.astype(BF16)


def first_kernel(
    pieces_ref, gain_own, gain_other, seg_ref, w_own, w_other, *refs
):
    gated_ref, x_ref, w_buf, w_sem = refs[-4:]
    for g in range(4):
        start_picked(0, w_own.at[g], w_other.at[g], w_buf.at[g], w_sem.at[g])
    width = pieces_ref.shape[2]
    for j in range(pieces_ref.shape[0]):
        x_ref[:, j * width : (j + 1) * width] = pieces_ref[j]
    front(
        x_ref[...].astype(F32), 0, gain_own, gain_other, seg_ref, w_own, w_buf, w_sem, gated_ref
    )


def middle_kernel(steps, gated_in, x_ref, gain_own, gain_other, seg_ref, w_own, w_other, *refs):
    o_own, o_other = refs[:steps], refs[steps : 2 * steps]
    gated_ref, x1_ref, o_buf, o_sem, w_buf, w_sem = refs[2 * steps :]
    for k in range(steps):
        start_picked(0, o_own[k], o_other[k], o_buf.at[k], o_sem.at[k])
    for g in range(4):
        start_picked(1, w_own.at[g], w_other.at[g], w_buf.at[g], w_sem.at[g])
    x1 = back(x_ref[...], gated_in, o_own, o_buf, o_sem)
    x1_ref[...] = x1
    front(x1.astype(F32), 1, gain_own, gain_other, seg_ref, w_own, w_buf, w_sem, gated_ref)


def last_kernel(steps, gated_in, x_ref, neigh_ref, w_ref, bias_ref, *refs):
    o_own, o_other = refs[:steps], refs[steps : 2 * steps]
    states_ref, ctx_ref, o_buf, o_sem = refs[2 * steps :]
    for k in range(steps):
        start_picked(1, o_own[k], o_other[k], o_buf.at[k], o_sem.at[k])
    near = neigh_ref[lax.axis_index("phase")]
    row = lax.broadcasted_iota(jnp.int32, (x_ref.shape[0], near.shape[1]), 0)
    share = jnp.zeros(row.shape, F32)
    for n in range(NBR):
        share = share + jnp.where(near[n : n + 1, :] == row, 1.0 / NBR, 0.0)
    share = jnp.transpose(share).astype(BF16)
    states = back(x_ref[...], gated_in, o_own, o_buf, o_sem)
    states_ref[...] = states
    context = jnp.dot(share, states, preferred_element_type=F32).astype(BF16)
    summed = jnp.dot(context, w_ref[...], preferred_element_type=F32) + bias_ref[...].astype(F32)
    ctx_ref[...] = silu(summed).astype(BF16)


def section_flops(rows, width, local_cols):
    return 2 * rows * (width * 4 * local_cols + 2 * rows * local_cols)


def fetch_rows_padded(owners, item_row, table, width):
    dp_count = lax.axis_size("dp")
    row_total = item_row.shape[0]
    capacity = max(2, 7 * row_total // (4 * dp_count))
    hits = (owners[:, None] == jnp.arange(dp_count, dtype=jnp.int32)[None, :]).astype(jnp.int32)
    rank = jnp.sum((jnp.cumsum(hits, axis=0) - 1) * hits, axis=1)
    slot = owners * capacity + rank
    requests = jnp.full((dp_count * capacity,), -1, jnp.int32).at[slot].set(item_row)
    asked = swap(requests.reshape(dp_count, capacity), "dp")
    part = lax.dynamic_slice_in_dim(table, lax.axis_index("mp") * width, width, 1)
    found = jnp.take(part, jnp.maximum(asked, 0), axis=0)
    return swap(found, "dp").reshape(dp_count * capacity, width)[slot]


def on_device(
    item_owner, item_row, segments, neighbors, table, gains, w_in, w_out, w_ctx, ctx_bias
):
    dp_count, mp_count = lax.axis_size("dp"), lax.axis_size("mp")
    table_rows, width = table.shape
    batches, rows = segments.shape[1], segments.shape[2]
    imps = neighbors.shape[2]
    local_cols = w_out.shape[1]
    part = width // mp_count

    w_own = jnp.transpose(w_in[0], (1, 0, 2))
    w_other = exchange(w_own, "phase", 1)
    o_own = spread(w_out[0], "mp")
    o_other = [exchange(piece, "phase", 1) for piece in o_own]
    gain_other = exchange(gains, "phase", 1)
    near = jnp.transpose(neighbors[0], (0, 2, 1))
    bias = ctx_bias.reshape(1, -1)

    if dp_count <= 8:
        wanted = (item_owner[:, 0] * table_rows + item_row).reshape(1, batches, rows)
        asked = swap(jnp.broadcast_to(wanted, (dp_count, batches, rows)), "dp")
        found = swap(fetch(asked, table, part), "dp")
        piece = functools.reduce(jnp.add, [found[d] for d in range(dp_count)])
    else:
        piece = fetch_rows_padded(item_owner[:, 0], item_row, table, part)
        piece = lax.dynamic_index_in_dim(
            piece.reshape(batches, rows, part), lax.axis_index("phase"), 0, keepdims=False
        )
    x_pieces = swap(jnp.broadcast_to(piece[None], (mp_count, rows, part)), "mp")

    sem4 = pltpu.SemaphoreType.DMA((4,))
    semk = pltpu.SemaphoreType.DMA((mp_count,))
    w_buf = pltpu.VMEM((4, width, local_cols), BF16)
    o_buf = pltpu.VMEM((mp_count, local_cols, width), BF16)
    x_shape = jax.ShapeDtypeStruct((rows, width), BF16)
    gated_shape = jax.ShapeDtypeStruct((mp_count, rows, local_cols), BF16)
    front_flops = section_flops(rows, width, local_cols)
    back_flops = 2 * rows * width * local_cols * mp_count

    gated, x0 = pl.pallas_call(
        first_kernel,
        out_shape=[gated_shape, x_shape],
        in_specs=[VMEM] * 4 + [HBM] * (2 + mp_count),
        out_specs=[VMEM] * 2,
        scratch_shapes=[w_buf, sem4],
        compiler_params=params(),
        cost_estimate=pl.CostEstimate(
            flops=front_flops, bytes_accessed=8 * width * local_cols, transcendentals=0
        ),
        name="section0_front",
    )(x_pieces, gains, gain_other, segments, w_own, w_other, *o_other)

    gated, x1 = pl.pallas_call(
        functools.partial(middle_kernel, mp_count),
        out_shape=[gated_shape, x_shape],
        in_specs=[VMEM] * 5 + [HBM] * (2 + 2 * mp_count),
        out_specs=[VMEM] * 2,
        scratch_shapes=[o_buf, semk, w_buf, sem4],
        compiler_params=params(),
        cost_estimate=pl.CostEstimate(
            flops=front_flops + back_flops,
            bytes_accessed=(8 + 2 * mp_count) * width * local_cols,
            transcendentals=0,
        ),
        name="section0_back_section1_front",
    )(swap(gated, "mp"), x0, gains, gain_other, segments, w_own, w_other, *o_own, *o_other)

    states, ctx = pl.pallas_call(
        functools.partial(last_kernel, mp_count),
        out_shape=[x_shape, jax.ShapeDtypeStruct((imps, w_ctx.shape[1]), BF16)],
        in_specs=[VMEM] * 5 + [HBM] * (2 * mp_count),
        out_specs=[VMEM] * 2,
        scratch_shapes=[o_buf, semk],
        compiler_params=params(),
        cost_estimate=pl.CostEstimate(
            flops=back_flops + 2 * imps * width * (rows + w_ctx.shape[1]),
            bytes_accessed=2 * mp_count * width * local_cols,
            transcendentals=0,
        ),
        name="section1_back_context",
    )(swap(gated, "mp"), x1, near, w_ctx, bias, *o_own, *o_other)

    return (
        states.reshape(1, 1, rows, width),
        ctx.reshape(1, 1, imps, w_ctx.shape[1]),
    )


def solution(mesh):
    in_specs = (
        P("dp", None),
        P("dp"),
        P("dp", None, None),
        P("dp", None, None, None),
        P("dp", None),
        P("phase", None),
        P("phase", None, None, "mp"),
        P("phase", "mp", None),
        P(None, "mp"),
        P("mp"),
    )
    out_specs = (P("dp", "phase", None, None), P("dp", "phase", None, "mp"))
    return jax.shard_map(
        on_device, mesh=mesh, in_specs=in_specs, out_specs=out_specs, check_vma=False
    )
```

time: 94.5 us -> 100 us (1.058)
  blocking collectives: 0 us -> 22.5 us
  between operations: 14.2 us -> 0.8 us
  local copies, waits for them, and re-layouts: 13.4 us -> 8.03 us
  waiting for transfers between devices: 32.5 us -> 37 us
  starting transfers between devices: 20.9 us -> 16.6 us
    all_to_all x0 -> x2, blocking collectives: none -> 22.5 us  [swap(): return lax.all_to_all(blocks, axis, split_axis=0, concat_axis=0, tiled=True)]
    ppermute x17 -> x9, starting transfers between devices: 20.8 us -> 4.75 us  [exchange(): return lax.ppermute(value, axis, pairs)]
    all_to_all x0 -> x3, waiting for transfers between devices: none -> 15 us  [swap(): return lax.all_to_all(blocks, axis, split_axis=0, concat_axis=0, tiled=True)]
    all_to_all x0 -> x3, starting transfers between devices: none -> 11.8 us  [swap(): return lax.all_to_all(blocks, axis, split_axis=0, concat_axis=0, tiled=True)]
    ppermute x17 -> x9, waiting for transfers between devices: 31.8 us -> 22 us  [exchange(): return lax.ppermute(value, axis, pairs)]
    unnamed x33 -> x23, local copies, waits for them, and re-layouts: 12.6 us -> 7.17 us
    pallas_call x2, Pallas kernels: 3.98 us -> 5.77 us  [the longest x1 3.66 us: on_device(): pl.pallas_call(first_kernel, out_shape=[gated_shape, x_shape], in_specs=[...]
    broadcast_in_dim x0 -> x1, other arithmetic: none -> 1.12 us  [on_device(): x_pieces = swap(jnp.broadcast_to(piece[None], (mp_count, rows, part)), 'mp')]
  transfers between devices with their start and end apart: 18 -> 12, of which waited for: 13 -> 5; matrix products, arithmetic and copies ran while one was open for 4% -> 2% of each run, Pallas kernels for 4% -> 2%
where the time goes in v3:
time: 100 us; the launch traced here: 99.4 us
  waiting for transfers between devices  37 us (37%)
  blocking collectives  22.5 us (22%)
  starting transfers between devices  16.6 us (17%)
  Pallas kernels  13.4 us (13%)
  local copies, waits for them, and re-layouts  8.03 us (8%)
  other arithmetic  1.13 us (1%)
    all_to_all x2, blocking collectives, swap(): return lax.all_to_all(blocks, axis, split_axis=0, concat_axis=0, tiled=True)  22.5 us
    ppermute x9, waiting for transfers between devices, exchange(): return lax.ppermute(value, axis, pairs)  22 us
    all_to_all x3, waiting for transfers between devices, swap(): return lax.all_to_all(blocks, axis, split_axis=0, concat_axis=0, tiled=True)  15 us
    all_to_all x3, starting transfers between devices, swap(): return lax.all_to_all(blocks, axis, split_axis=0, concat_axis=0, tiled=True)  11.8 us
    unnamed x23, local copies, waits for them, and re-layouts  7.17 us
    pallas_call x1, Pallas kernels, on_device(): pl.pallas_call(functools.partial(middle_kernel, mp_count), out_shape=[gat...  4.77 us
    ppermute x9, starting transfers between devices, exchange(): return lax.ppermute(value, axis, pairs)  4.75 us
    pallas_call x1, Pallas kernels, on_device(): pl.pallas_call(first_kernel, out_shape=[gated_shape, x_shape], in_specs=[...  3.66 us
  transfers between devices with their start and end apart: 12, of which 5 were waited for; matrix products, arithmetic and copies ran while one was open for 2% of the time, Pallas kernels for 2%

profile of v3, /device:TPU:0, one launch (start us, length us, event | category | flops | bytes accessed | tf_op | source)
XLA Modules:
  0.0 99.4 jit_solution(13296087234277374451)
XLA Ops:
  0.6 0.0 copy-start.9
  0.6 0.0 copy-start.8
  0.6 1.9 %copy.14 = bf16[1,1024,4,256]{3,1,2,0:T(8,128)(2,1)S(1)} copy(bf16[1,1024,4,256]{3,2,1,0:T(4,128)(2,1)} %param.16) | data formatting | bytes 4194304 | tf_op args[6]
  2.5 0.0 copy-start.6
  2.5 0.5 collective-permute-start.1
  3.1 0.0 copy-done.9
  3.1 0.0 copy-done.8
  3.1 11.3 %all_to_all.25.asked_ref = s32[4,2,256]{2,1,0:T(2,128)S(1)} all-to-all(s32[4,2,256]{2,1,0:T(2,128)S(1)} %broadcast_in_dim.16), channel_id=1, replica_groups=mesh['dp'=4,'mp'=4,'phase'=2] {'dp'}, dimensions={0} | all-to-all | bytes 16384 | tf_op jit(solution)/shard_map/all_to_all | solution.py:44
  14.4 1.6 %copy-done = bf16[1024,1024]{1,0:T(8,128)(2,1)S(1)} copy-done((bf16[1024,1024]{1,0:T(8,128)(2,1)S(1)}, bf16[1024,1024]{1,0:T(8,128)(2,1)}, u32[]{:S(2)}) %copy-start) | copy-done | bytes 2097176
  16.0 2.1 %fetch.1 = bf16[4,256,256]{2,1,0:T(8,128)(2,1)} custom-call(s32[4,2,256]{2,1,0:T(2,128)S(1)} %all_to_all.25.asked_ref, bf16[1024,1024]{1,0:T(8,128)(2,1)S(1)} %copy-done), custom_call_target="tpu_custom_call" | custom-call | flops 536870912 | bytes 524288 | tf_op jit(solution)/shard_map/fetch/pallas_call | solution.py:82
  18.1 0.0 copy-start.7
  18.1 4.2 %all-to-all-start.1 = ((bf16[4,256,256]{2,1,0:T(8,128)(2,1)}), bf16[4,256,256]{2,1,0:T(8,128)(2,1)}, u32[]{:S(2)}, u32[]{:S(2)}) async-start(bf16[4,256,256]{2,1,0:T(8,128)(2,1)} %fetch.1), calls=%async_computation.1 | async-start | bytes 1048576 | tf_op jit(solution)/shard_map/all_to_all | solution.py:44
  22.3 1.6 %collective-permute-start.3 = (bf16[256,1024]{1,0:T(8,128)(2,1)}, bf16[256,1024]{1,0:T(8,128)(2,1)}, u32[]{:S(2)}, u32[]{:S(2)}) collective-permute-start(bf16[256,1024]{1,0:T(8,128)(2,1)} %bitcast.5.refs_0_), channel_id=1, source_target_pairs={{0,2},{2,0},{4,6},{6,4},{1,3},{3,1},{5,7},{7,5},{8,10},{10,8},{12,... | collective-permute-start | bytes 1572872 | tf_op jit(solution)/shard_map/ppermute | solution.py:36
  23.9 1.5 %collective-permute-start.5 = (bf16[256,1024]{1,0:T(8,128)(2,1)}, bf16[256,1024]{1,0:T(8,128)(2,1)}, u32[]{:S(2)}, u32[]{:S(2)}) collective-permute-start(bf16[256,1024]{1,0:T(8,128)(2,1)} %bitcast.5.refs_0_), channel_id=1, source_target_pairs={{0,4},{2,6},{4,0},{6,2},{1,5},{3,7},{5,1},{7,3},{8,12},{10,14},{12... | collective-permute-start | bytes 1572872 | tf_op jit(solution)/shard_map/ppermute | solution.py:36
  25.4 0.5 collective-permute-start.7
  25.9 0.0 copy-done.6
  25.9 0.0 collective-permute-start
  25.9 1.2 %collective-permute-done.gain_other = bf16[1,1024]{1,0:T(2,128)(2,1)S(1)} collective-permute-done((bf16[1,1024]{1,0:T(2,128)(2,1)S(1)}, bf16[1,1024]{1,0:T(2,128)(2,1)S(1)}, u32[]{:S(2)}, u32[]{:S(2)}) %collective-permute-start) | collective-permute-done | bytes 2080 | tf_op jit(solution)/shard_map/ppermute | solution.py:36
  27.0 0.2 collective-permute-start.2
  27.2 10.3 %collective-permute-done.3.refs_1_ = bf16[256,1024]{1,0:T(8,128)(2,1)} collective-permute-done((bf16[256,1024]{1,0:T(8,128)(2,1)}, bf16[256,1024]{1,0:T(8,128)(2,1)}, u32[]{:S(2)}, u32[]{:S(2)}) %collective-permute-start.3) | collective-permute-done | bytes 524320 | tf_op jit(solution)/shard_map/ppermute | solution.py:36
  37.6 0.0 collective-permute-start.4
  37.6 10.5 %collective-permute-done.5.refs_2_ = bf16[256,1024]{1,0:T(8,128)(2,1)} collective-permute-done((bf16[256,1024]{1,0:T(8,128)(2,1)}, bf16[256,1024]{1,0:T(8,128)(2,1)}, u32[]{:S(2)}, u32[]{:S(2)}) %collective-permute-start.5) | collective-permute-done | bytes 524320 | tf_op jit(solution)/shard_map/ppermute | solution.py:36
  48.0 0.0 collective-permute-start.6
  48.0 0.0 collective-permute-done.7.refs_3_
  48.0 0.5 collective-permute-start.8
  48.5 0.0 all-to-all-done.1
  48.5 1.1 %fusion = bf16[256,256]{1,0:T(8,128)(2,1)S(1)} fusion(bf16[4,256,256]{2,1,0:T(8,128)(2,1)} %all-to-all-done.1), kind=kLoop, calls=%fused_computation.2 | loop fusion | flops 196608 | bytes 655360 | tf_op jit(solution)/shard_map/broadcast_in_dim | solution.py:246
  49.7 0.8 broadcast_in_dim.18
  50.5 4.2 %all-to-all-start.2 = ((bf16[4,256,256]{2,1,0:T(8,128)(2,1)}), bf16[4,256,256]{2,1,0:T(8,128)(2,1)}, u32[]{:S(2)}, u32[]{:S(2)}) async-start(bf16[4,256,256]{2,1,0:T(8,128)(2,1)} %broadcast_in_dim.18), calls=%async_computation.2 | async-start | bytes 1048576 | tf_op jit(solution)/shard_map/all_to_all | solution.py:44
  54.7 0.0 collective-permute-done.2.refs_0_.refs_4_
  54.7 0.0 collective-permute-done.4.refs_1_.refs_5_
  54.7 0.0 collective-permute-done.6.refs_2_.refs_6_
  54.7 0.0 collective-permute-done.8.refs_3_.refs_7_
  54.7 8.5 %all-to-all-done.2.pieces_ref = bf16[4,256,256]{2,1,0:T(8,128)(2,1)} async-done(((bf16[4,256,256]{2,1,0:T(8,128)(2,1)}), bf16[4,256,256]{2,1,0:T(8,128)(2,1)}, u32[]{:S(2)}, u32[]{:S(2)}) %all-to-all-start.2) | async-done | bytes 524320 | tf_op jit(solution)/shard_map/all_to_all | solution.py:44
  63.2 0.0 collective-permute-done.1.w_other
  63.2 0.0 copy-done.7
  63.2 3.7 %section0_front.1 = (bf16[4,256,256]{2,1,0:T(8,128)(2,1)S(1)}, bf16[256,1024]{1,0:T(8,128)(2,1)S(1)}) custom-call(bf16[4,256,256]{2,1,0:T(8,128)(2,1)} %all-to-all-done.2.pieces_ref, bf16[1,1024]{1,0:T(2,128)(2,1)S(1)} %copy-done.6, bf16[1,1024]{1,0:T(2,128)(2,1)S(1)} %collective-permute-done.gain_other, s32[1,2,256]{2,1,0:T(2,128)S(1)} %copy-done.7, ...), custom_call_target="tpu_custom_call" | custom-call | flops 603979776 | bytes 2097152 | tf_op jit(solution)/shard_map/section0_front/pallas_call | solution.py:257
  66.9 11.2 %all_to_all.26.gated_in = bf16[4,256,256]{2,1,0:T(8,128)(2,1)S(1)} all-to-all(bf16[4,256,256]{2,1,0:T(8,128)(2,1)S(1)} %get-tuple-element.8), channel_id=1, replica_groups=mesh['dp'=4,'mp'=4,'phase'=2] {'mp'}, dimensions={0} | all-to-all | bytes 1048576 | tf_op jit(solution)/shard_map/all_to_all | solution.py:44
  78.0 4.8 %section0_back_section1_front.1 = (bf16[4,256,256]{2,1,0:T(8,128)(2,1)S(1)}, bf16[256,1024]{1,0:T(8,128)(2,1)S(1)}) custom-call(bf16[4,256,256]{2,1,0:T(8,128)(2,1)S(1)} %all_to_all.26.gated_in, bf16[256,1024]{1,0:T(8,128)(2,1)S(1)} %get-tuple-element.9.x_ref, bf16[1,1024]{1,0:T(2,128)(2,1)S(1)} %copy-done.6, ...), custom_call_target="tpu_custom_call" | custom-call | flops 1140850688 | bytes 4194304 | tf_op jit(solution)/shard_map/section0_back_section1_front/pallas_call | solution.py:270
  82.8 0.0 copy-start.2
  82.8 0.8 copy-done.2
  83.6 0.8 copy-done.4
  84.4 3.5 %all-to-all-start.4 = ((bf16[4,256,256]{2,1,0:T(8,128)(2,1)}), bf16[4,256,256]{2,1,0:T(8,128)(2,1)S(1)}, u32[]{:S(2)}, u32[]{:S(2)}) async-start(bf16[4,256,256]{2,1,0:T(8,128)(2,1)} %copy-done.4), calls=%async_computation.4 | async-start | bytes 1048576 | tf_op jit(solution)/shard_map/all_to_all | solution.py:44
  87.9 0.0 copy-done.10
  87.9 6.5 %all-to-all-done.4.gated_in = bf16[4,256,256]{2,1,0:T(8,128)(2,1)S(1)} async-done(((bf16[4,256,256]{2,1,0:T(8,128)(2,1)}), bf16[4,256,256]{2,1,0:T(8,128)(2,1)S(1)}, u32[]{:S(2)}, u32[]{:S(2)}) %all-to-all-start.4) | async-done | bytes 524320 | tf_op jit(solution)/shard_map/all_to_all | solution.py:44
  94.5 1.0 %copy-done.1 = bf16[1024,256]{1,0:T(8,128)(2,1)S(1)} copy-done((bf16[1024,256]{1,0:T(8,128)(2,1)S(1)}, bf16[1024,256]{1,0:T(8,128)(2,1)}, u32[]{:S(2)}) %copy-start.1) | copy-done | bytes 524312
  95.5 1.0 %copy-done.3 = bf16[256,1024]{1,0:T(8,128)(2,1)S(1)} copy-done((bf16[256,1024]{1,0:T(8,128)(2,1)S(1)}, bf16[256,1024]{1,0:T(8,128)(2,1)}, u32[]{:S(2)}) %copy-start.3) | copy-done | bytes 524312
  96.5 2.9 %section1_back_context.1 = (bf16[256,1024]{1,0:T(8,128)(2,1)}, bf16[256,256]{1,0:T(8,128)(2,1)}) custom-call(bf16[4,256,256]{2,1,0:T(8,128)(2,1)S(1)} %all-to-all-done.4.gated_in, bf16[256,1024]{1,0:T(8,128)(2,1)S(1)} %copy-done.3, s32[2,8,256]{2,1,0:T(8,128)S(1)} %bitcast.17, bf16[1024,256]{1,0:T(8,128)(2,1)S(1)} %copy-done.1, ...), custom_call_target="tpu_custom_call" | custom-call | flops 805306368 | bytes 2097152 | tf_op jit(solution)/shard_map/section1_back_context/pallas_call | solution.py:285
  (12 shorter events, 0.0 us)
Async XLA Ops:
  0.6 2.4 %copy-start.9 = (s32[512,1]{0,1:T(1,128)S(1)}, s32[512,1]{0,1:T(1,128)}, u32[]{:S(2)}) copy-start(s32[512,1]{0,1:T(1,128)} %param.10) | copy-start | bytes 6148
  0.6 2.4 %copy-start.8 = (s32[512]{0:T(512)S(1)}, s32[512]{0:T(512)}, u32[]{:S(2)}) copy-start(s32[512]{0:T(512)} %param.11) | copy-start | bytes 6148
  2.5 23.3 %copy-start.6 = (bf16[1,1024]{1,0:T(2,128)(2,1)S(1)}, bf16[1,1024]{1,0:T(2,128)(2,1)}, u32[]{:S(2)}) copy-start(bf16[1,1024]{1,0:T(2,128)(2,1)} %gain_own.3) | copy-start | bytes 6148
  2.5 60.7 %collective-permute-start.1 = (bf16[4,1024,256]{2,1,0:T(8,128)(2,1)S(1)}, bf16[4,1024,256]{2,1,0:T(8,128)(2,1)}, u32[]{:S(2)}, u32[]{:S(2)}) collective-permute-start(bf16[4,1024,256]{2,1,0:T(8,128)(2,1)S(1)} %bitcast.14), channel_id=1, source_target_pairs={{0,1},{1,0},{2,3},{3,2},{4,5},{5,4},{6,7},{7,6},{8,9},{9,8},{10,11... | collective-permute-start | bytes 6291464 | tf_op jit(solution)/shard_map/ppermute | solution.py:36
  14.4 1.6 %copy-start = (bf16[1024,1024]{1,0:T(8,128)(2,1)S(1)}, bf16[1024,1024]{1,0:T(8,128)(2,1)}, u32[]{:S(2)}) copy-start(bf16[1024,1024]{1,0:T(8,128)(2,1)} %table_ref.1) | copy-start | bytes 6291460
  18.1 45.1 %copy-start.7 = (s32[1,2,256]{2,1,0:T(2,128)S(1)}, s32[1,2,256]{2,1,0:T(2,128)}, u32[]{:S(2)}) copy-start(s32[1,2,256]{2,1,0:T(2,128)} %seg_ref.3) | copy-start | bytes 6148
  18.1 30.4 %all-to-all-start.1 = ((bf16[4,256,256]{2,1,0:T(8,128)(2,1)}), bf16[4,256,256]{2,1,0:T(8,128)(2,1)}, u32[]{:S(2)}, u32[]{:S(2)}) async-start(bf16[4,256,256]{2,1,0:T(8,128)(2,1)} %fetch.1), calls=%async_computation.1 | async-start | bytes 1048576 | tf_op jit(solution)/shard_map/all_to_all | solution.py:44
  22.3 15.2 %collective-permute-start.3 = (bf16[256,1024]{1,0:T(8,128)(2,1)}, bf16[256,1024]{1,0:T(8,128)(2,1)}, u32[]{:S(2)}, u32[]{:S(2)}) collective-permute-start(bf16[256,1024]{1,0:T(8,128)(2,1)} %bitcast.5.refs_0_), channel_id=1, source_target_pairs={{0,2},{2,0},{4,6},{6,4},{1,3},{3,1},{5,7},{7,5},{8,10},{10,8},{12,... | collective-permute-start | bytes 1572872 | tf_op jit(solution)/shard_map/ppermute | solution.py:36
  23.9 24.1 %collective-permute-start.5 = (bf16[256,1024]{1,0:T(8,128)(2,1)}, bf16[256,1024]{1,0:T(8,128)(2,1)}, u32[]{:S(2)}, u32[]{:S(2)}) collective-permute-start(bf16[256,1024]{1,0:T(8,128)(2,1)} %bitcast.5.refs_0_), channel_id=1, source_target_pairs={{0,4},{2,6},{4,0},{6,2},{1,5},{3,7},{5,1},{7,3},{8,12},{10,14},{12... | collective-permute-start | bytes 1572872 | tf_op jit(solution)/shard_map/ppermute | solution.py:36
  25.4 22.6 %collective-permute-start.7 = (bf16[256,1024]{1,0:T(8,128)(2,1)}, bf16[256,1024]{1,0:T(8,128)(2,1)}, u32[]{:S(2)}, u32[]{:S(2)}) collective-permute-start(bf16[256,1024]{1,0:T(8,128)(2,1)} %bitcast.5.refs_0_), channel_id=1, source_target_pairs={{0,6},{2,4},{4,2},{6,0},{1,7},{3,5},{5,3},{7,1},{8,14},{10,12},{12... | collective-permute-start | bytes 1572872 | tf_op jit(solution)/shard_map/ppermute | solution.py:36
  25.9 1.2 %collective-permute-start = (bf16[1,1024]{1,0:T(2,128)(2,1)S(1)}, bf16[1,1024]{1,0:T(2,128)(2,1)S(1)}, u32[]{:S(2)}, u32[]{:S(2)}) collective-permute-start(bf16[1,1024]{1,0:T(2,128)(2,1)S(1)} %copy-done.6), channel_id=1, source_target_pairs={{0,1},{1,0},{2,3},{3,2},{4,5},{5,4},{6,7},{7,6},{8,9},{9,8},{10,11... | collective-permute-start | bytes 6152 | tf_op jit(solution)/shard_map/ppermute | solution.py:36
  27.0 27.6 %collective-permute-start.2 = (bf16[256,1024]{1,0:T(8,128)(2,1)}, bf16[256,1024]{1,0:T(8,128)(2,1)S(1)}, u32[]{:S(2)}, u32[]{:S(2)}) collective-permute-start(bf16[256,1024]{1,0:T(8,128)(2,1)} %bitcast.5.refs_0_), channel_id=1, source_target_pairs={{0,1},{1,0},{2,3},{3,2},{4,5},{5,4},{6,7},{7,6},{8,9},{9,8},{10,11... | collective-permute-start | bytes 1572872 | tf_op jit(solution)/shard_map/ppermute | solution.py:36
  37.6 17.1 %collective-permute-start.4 = (bf16[256,1024]{1,0:T(8,128)(2,1)}, bf16[256,1024]{1,0:T(8,128)(2,1)S(1)}, u32[]{:S(2)}, u32[]{:S(2)}) collective-permute-start(bf16[256,1024]{1,0:T(8,128)(2,1)} %collective-permute-done.3.refs_1_), channel_id=1, source_target_pairs={{0,1},{1,0},{2,3},{3,2},{4,5},{5,4},{6,7},{7,6},{8,9},{9,8},{10,11... | collective-permute-start | bytes 1572872 | tf_op jit(solution)/shard_map/ppermute | solution.py:36
  48.0 6.7 %collective-permute-start.6 = (bf16[256,1024]{1,0:T(8,128)(2,1)}, bf16[256,1024]{1,0:T(8,128)(2,1)}, u32[]{:S(2)}, u32[]{:S(2)}) collective-permute-start(bf16[256,1024]{1,0:T(8,128)(2,1)} %collective-permute-done.5.refs_2_), channel_id=1, source_target_pairs={{0,1},{1,0},{2,3},{3,2},{4,5},{5,4},{6,7},{7,6},{8,9},{9,8},{10,11... | collective-permute-start | bytes 1572872 | tf_op jit(solution)/shard_map/ppermute | solution.py:36
  48.0 6.7 %collective-permute-start.8 = (bf16[256,1024]{1,0:T(8,128)(2,1)}, bf16[256,1024]{1,0:T(8,128)(2,1)}, u32[]{:S(2)}, u32[]{:S(2)}) collective-permute-start(bf16[256,1024]{1,0:T(8,128)(2,1)} %collective-permute-done.7.refs_3_), channel_id=1, source_target_pairs={{0,1},{1,0},{2,3},{3,2},{4,5},{5,4},{6,7},{7,6},{8,9},{9,8},{10,11... | collective-permute-start | bytes 1572872 | tf_op jit(solution)/shard_map/ppermute | solution.py:36
  50.5 12.7 %all-to-all-start.2 = ((bf16[4,256,256]{2,1,0:T(8,128)(2,1)}), bf16[4,256,256]{2,1,0:T(8,128)(2,1)}, u32[]{:S(2)}, u32[]{:S(2)}) async-start(bf16[4,256,256]{2,1,0:T(8,128)(2,1)} %broadcast_in_dim.18), calls=%async_computation.2 | async-start | bytes 1048576 | tf_op jit(solution)/shard_map/all_to_all | solution.py:44
  78.0 9.9 %copy-start.10 = (bf16[256]{0:T(256)(128)(2,1)S(1)}, bf16[256]{0:T(256)(128)(2,1)}, u32[]{:S(2)}) copy-start(bf16[256]{0:T(256)(128)(2,1)} %param.19) | copy-start | bytes 1540
  78.0 16.4 %copy-start.5 = (s32[1,2,256,8]{2,3,1,0:T(8,128)S(1)}, s32[1,2,256,8]{2,3,1,0:T(8,128)}, u32[]{:S(2)}) copy-start(s32[1,2,256,8]{2,3,1,0:T(8,128)} %param.13) | copy-start | bytes 49156
  82.8 0.8 copy-start.2
  83.6 0.8 copy-start.4
  84.4 10.0 %all-to-all-start.4 = ((bf16[4,256,256]{2,1,0:T(8,128)(2,1)}), bf16[4,256,256]{2,1,0:T(8,128)(2,1)S(1)}, u32[]{:S(2)}, u32[]{:S(2)}) async-start(bf16[4,256,256]{2,1,0:T(8,128)(2,1)} %copy-done.4), calls=%async_computation.4 | async-start | bytes 1048576 | tf_op jit(solution)/shard_map/all_to_all | solution.py:44
  94.5 1.0 %copy-start.1 = (bf16[1024,256]{1,0:T(8,128)(2,1)S(1)}, bf16[1024,256]{1,0:T(8,128)(2,1)}, u32[]{:S(2)}) copy-start(bf16[1024,256]{1,0:T(8,128)(2,1)} %w_ref.1) | copy-start | bytes 1572868
  95.5 1.0 %copy-start.3 = (bf16[256,1024]{1,0:T(8,128)(2,1)S(1)}, bf16[256,1024]{1,0:T(8,128)(2,1)}, u32[]{:S(2)}) copy-start(bf16[256,1024]{1,0:T(8,128)(2,1)} %copy-done.2) | copy-start | bytes 1572868

commit v4 on v2

v4 whole, which is shorter than its diff:
```python
import functools

import jax
import jax.numpy as jnp
from jax import lax
from jax.experimental import pallas as pl
from jax.experimental.pallas import tpu as pltpu
from jax.sharding import PartitionSpec as P

HD = 128
NBR = 8
LANES = 128
EPS = 1e-06
VMEM_LIMIT = 20 * 1024 * 1024
VMEM = pl.BlockSpec(memory_space=pltpu.VMEM)
HBM = pl.BlockSpec(memory_space=pltpu.HBM)
F32 = jnp.float32
BF16 = jnp.bfloat16


def params():
    return pltpu.CompilerParams(vmem_limit_bytes=VMEM_LIMIT)


def is_pow2(n):
    return n & (n - 1) == 0


def source_of(me, k, n):
    return me ^ k if is_pow2(n) else lax.rem(me + n - k, n)


def exchange(value, axis, k):
    n = lax.axis_size(axis)
    pairs = [(i, i ^ k if is_pow2(n) else (i + k) % n) for i in range(n)]
    return lax.ppermute(value, axis, pairs)


def spread(value, axis):
    return [value] + [exchange(value, axis, k) for k in range(1, lax.axis_size(axis))]


def swap(blocks, axis):
    return lax.all_to_all(blocks, axis, split_axis=0, concat_axis=0, tiled=True)


def columns_of(row, count):
    return jnp.transpose(jnp.broadcast_to(row, (count, row.shape[1])))


def silu(x):
    return x * jax.nn.sigmoid(x)


def fetch_kernel(steps, *refs):
    asked_refs, table_ref = refs[:steps], refs[steps]
    out_refs, (tab, sem) = refs[-steps - 2 : -2], refs[-2:]
    width = tab.shape[1]
    at = pl.multiple_of(lax.axis_index("mp") * width, width)
    copy = pltpu.make_async_copy(table_ref.at[:, pl.ds(at, width)], tab, sem)
    copy.start()
    first = lax.axis_index("dp") * tab.shape[0]
    phase = lax.axis_index("phase")
    hots = []
    for asked_ref in asked_refs:
        cols = columns_of(asked_ref[pl.ds(phase, 1), :] - first, LANES)
        lane = lax.broadcasted_iota(jnp.int32, cols.shape, 1)
        hots.append(
            jnp.concatenate(
                [
                    jnp.where(cols == lane + c, 1.0, 0.0).astype(BF16)
                    for c in range(0, tab.shape[0], LANES)
                ],
                axis=1,
            )
        )
    copy.wait()
    for hot, out_ref in zip(hots, out_refs):
        out_ref[...] = jnp.dot(hot, tab[...], preferred_element_type=F32).astype(BF16)


def fetch(asked, table, width, after):
    steps, rows = len(asked), asked[0].shape[1]
    return pl.pallas_call(
        functools.partial(fetch_kernel, steps),
        out_shape=[jax.ShapeDtypeStruct((rows, width), BF16)] * steps,
        in_specs=[VMEM] * steps + [HBM] * (1 + len(after)),
        out_specs=[VMEM] * steps,
        scratch_shapes=[pltpu.VMEM((table.shape[0], width), BF16), pltpu.SemaphoreType.DMA],
        compiler_params=params(),
        cost_estimate=pl.CostEstimate(
            flops=2 * steps * rows * width * table.shape[0],
            bytes_accessed=2 * width * table.shape[0],
            transcendentals=0,
        ),
        name="fetch",
    )(*asked, table, *after)


def merge_kernel(a_ref, b_ref, *refs):
    refs[-1][...] = a_ref[...] + b_ref[...]


def merge(a, b, after):
    return pl.pallas_call(
        merge_kernel,
        out_shape=jax.ShapeDtypeStruct(a.shape, BF16),
        in_specs=[VMEM] * 2 + [HBM] * len(after),
        out_specs=VMEM,
        compiler_params=params(),
        name="merge",
    )(a, b, *after)


def hold_kernel(*refs):
    pass


def hold(value, after):
    return pl.pallas_call(
        hold_kernel,
        out_shape=jax.ShapeDtypeStruct(value.shape, value.dtype),
        in_specs=[HBM] * (1 + len(after)),
        out_specs=HBM,
        input_output_aliases={0: 0},
        compiler_params=params(),
        name="hold",
    )(value, *after)


def ask_around(wanted):
    asked, step = [wanted], 1
    while step < lax.axis_size("dp"):
        got = exchange(jnp.concatenate(asked), "dp", step)
        asked = asked + jnp.split(got, step)
        step = 2 * step
    return asked


def gather_in(blocks, after):
    blocks, step = dict(enumerate(blocks)), 1
    while step < lax.axis_size("dp"):
        for k in sorted((k for k in blocks if k & step), reverse=True):
            got = exchange(blocks.pop(k), "dp", step)
            last = 2 * step == lax.axis_size("dp")
            blocks[k ^ step] = merge(blocks[k ^ step], got, after if last else [])
        step = 2 * step
    return blocks[0]


def start_picked(section, own, other, dst, sem):
    phase = lax.axis_index("phase")

    @pl.when(phase == section)
    def _():
        pltpu.make_async_copy(own, dst, sem).start()

    @pl.when(phase != section)
    def _():
        pltpu.make_async_copy(other, dst, sem).start()


def wait_picked(own, dst, sem):
    pltpu.make_async_copy(own, dst, sem).wait()


def start_weights(section, w_own, w_other, w_buf, w_sem):
    for g in range(4):
        start_picked(section, w_own.at[g], w_other.at[g], w_buf.at[g], w_sem.at[g])


def front(x, section, gain_own, gain_other, seg_ref, w_own, w_buf, w_sem, gated_ref):
    phase = lax.axis_index("phase")
    rows, local_cols = x.shape[0], w_buf.shape[2]
    gain = jnp.where(phase == section, gain_own[...].astype(F32), gain_other[...].astype(F32))
    inv = lax.rsqrt(jnp.mean(x * x, axis=-1, keepdims=True) + EPS)
    normed = (x * inv * gain).astype(BF16)
    proj = []
    for g in range(4):
        wait_picked(w_own.at[g], w_buf.at[g], w_sem.at[g])
        proj.append(
            silu(jnp.dot(normed, w_buf[g], preferred_element_type=F32)).astype(BF16)
        )
    gates, values, queries, keys = proj
    seg = seg_ref[0, pl.ds(phase, 1), :]
    seg_cols = columns_of(seg, rows)
    at_row = lax.broadcasted_iota(jnp.int32, (rows, rows), 0)
    at_col = lax.broadcasted_iota(jnp.int32, (rows, rows), 1)
    allowed = (at_col <= at_row) & (seg_cols == seg)
    for h in range(0, local_cols, HD):
        head = slice(h, h + HD)
        scores = lax.dot_general(
            queries[:, head], keys[:, head], (((1,), (1,)), ((), ())), preferred_element_type=F32
        ) * HD ** (-0.5)
        weights = (jnp.where(allowed, silu(scores), 0.0) / rows).astype(BF16)
        mixed = jnp.dot(weights, values[:, head], preferred_element_type=F32)
        mixed = mixed * lax.rsqrt(jnp.mean(mixed * mixed, axis=-1, keepdims=True) + EPS)
        gated_ref[:, head] = (mixed * gates[:, head].astype(F32)).astype(BF16)


def back(x, gated_refs, o_own, o_buf, o_sem):
    total = x.astype(F32)
    for k, gated_ref in enumerate(gated_refs):
        wait_picked(o_own.at[k], o_buf.at[k], o_sem.at[k])
        part = jnp.dot(gated_ref[...], o_buf[k], preferred_element_type=F32)
        total = total + part.astype(BF16).astype(F32)
    return total.astype(BF16)


def first_kernel(steps, *refs):
    x_refs, o_own = refs[:steps], refs[steps : 2 * steps]
    gain_own, gain_other, seg_ref, w_own, w_other = refs[2 * steps : -6]
    gated_ref, x_ref, stack_ref, w_buf, w_sem, o_sem = refs[-6:]
    start_weights(0, w_own, w_other, w_buf, w_sem)
    copies = [
        pltpu.make_async_copy(o_own[k], stack_ref.at[k], o_sem.at[k]) for k in range(steps)
    ]
    for copy in copies:
        copy.start()
    width = x_refs[0].shape[1]
    for k, piece in enumerate(x_refs):
        at = pl.multiple_of(source_of(lax.axis_index("mp"), k, steps) * width, width)
        x_ref[:, pl.ds(at, width)] = piece[...]
    x = x_ref[...].astype(F32)
    front(x, 0, gain_own, gain_other, seg_ref, w_own, w_buf, w_sem, gated_ref)
    for copy in copies:
        copy.wait()


def middle_kernel(steps, *refs):
    gated_refs = refs[:steps]
    x_ref, gain_own, gain_other, seg_ref, w_own, w_other, o_own, o_other = refs[steps : steps + 8]
    gated_ref, x1_ref, o_buf, o_sem, w_buf, w_sem = refs[steps + 8 :]
    for k in range(steps):
        start_picked(0, o_own.at[k], o_other.at[k], o_buf.at[k], o_sem.at[k])
    start_weights(1, w_own, w_other, w_buf, w_sem)
    x1 = back(x_ref[...], gated_refs, o_own, o_buf, o_sem)
    x1_ref[...] = x1
    x1 = x1.astype(F32)
    front(x1, 1, gain_own, gain_other, seg_ref, w_own, w_buf, w_sem, gated_ref)


def last_kernel(steps, *refs):
    gated_refs = refs[:steps]
    x_ref, neigh_ref, w_ref, bias_ref, o_own, o_other, states_ref, ctx_ref = refs[steps : steps + 8]
    o_buf, o_sem = refs[steps + 8 :]
    for k in range(steps):
        start_picked(1, o_own.at[k], o_other.at[k], o_buf.at[k], o_sem.at[k])
    near = neigh_ref[lax.axis_index("phase")]
    row = lax.broadcasted_iota(jnp.int32, (x_ref.shape[0], near.shape[1]), 0)
    share = jnp.zeros(row.shape, F32)
    for n in range(NBR):
        share = share + jnp.where(near[n : n + 1, :] == row, 1.0 / NBR, 0.0)
    share = jnp.transpose(share).astype(BF16)
    states = back(x_ref[...], gated_refs, o_own, o_buf, o_sem)
    states_ref[...] = states
    context = jnp.dot(share, states, preferred_element_type=F32).astype(BF16)
    summed = jnp.dot(context, w_ref[...], preferred_element_type=F32) + bias_ref[...].astype(F32)
    ctx_ref[...] = silu(summed).astype(BF16)


def section_flops(rows, width, local_cols):
    return 2 * rows * (width * 4 * local_cols + 2 * rows * local_cols)


def fetch_rows_padded(owners, item_row, table, width):
    dp_count = lax.axis_size("dp")
    row_total = item_row.shape[0]
    capacity = max(2, 7 * row_total // (4 * dp_count))
    hits = (owners[:, None] == jnp.arange(dp_count, dtype=jnp.int32)[None, :]).astype(jnp.int32)
    rank = jnp.sum((jnp.cumsum(hits, axis=0) - 1) * hits, axis=1)
    slot = owners * capacity + rank
    requests = jnp.full((dp_count * capacity,), -1, jnp.int32).at[slot].set(item_row)
    asked = swap(requests.reshape(dp_count, capacity), "dp")
    part = lax.dynamic_slice_in_dim(table, lax.axis_index("mp") * width, width, 1)
    found = jnp.take(part, jnp.maximum(asked, 0), axis=0)
    return swap(found, "dp").reshape(dp_count * capacity, width)[slot]


def on_device(
    item_owner, item_row, segments, neighbors, table, gains, w_in, w_out, w_ctx, ctx_bias
):
    dp_count, mp_count = lax.axis_size("dp"), lax.axis_size("mp")
    table_rows, width = table.shape
    batches, rows = segments.shape[1], segments.shape[2]
    imps = neighbors.shape[2]
    local_cols = w_out.shape[1]
    part = width // mp_count

    w_own = jnp.transpose(w_in[0], (1, 0, 2))
    o_pieces = spread(w_out[0], "mp")
    gain_other = exchange(gains, "phase", 1)
    near = jnp.transpose(neighbors[0], (0, 2, 1))
    bias = ctx_bias.reshape(1, -1)

    if is_pow2(dp_count) and dp_count <= 8:
        wanted = (item_owner[:, 0] * table_rows + item_row).reshape(batches, rows)
        asked = ask_around(wanted)
        w_own = hold(w_own, asked[1:2])
        w_other = exchange(w_own, "phase", 1)
        found = fetch(asked, table, part, [gain_other])
        piece = gather_in(found, o_pieces[1:3] + [w_other])
    else:
        piece = fetch_rows_padded(item_owner[:, 0], item_row, table, part)
        piece = lax.dynamic_index_in_dim(
            piece.reshape(batches, rows, part), lax.axis_index("phase"), 0, keepdims=False
        )
        w_other = exchange(w_own, "phase", 1)
    x_pieces = spread(piece, "mp")

    sem4 = pltpu.SemaphoreType.DMA((4,))
    semk = pltpu.SemaphoreType.DMA((mp_count,))
    w_buf = pltpu.VMEM((4, width, local_cols), BF16)
    o_buf = pltpu.VMEM((mp_count, local_cols, width), BF16)
    x_shape = jax.ShapeDtypeStruct((rows, width), BF16)
    gated_shape = jax.ShapeDtypeStruct((rows, local_cols), BF16)
    front_flops = section_flops(rows, width, local_cols)
    back_flops = 2 * rows * width * local_cols * mp_count

    gated, x0, o_own = pl.pallas_call(
        functools.partial(first_kernel, mp_count),
        out_shape=[
            gated_shape,
            x_shape,
            jax.ShapeDtypeStruct((mp_count, local_cols, width), BF16),
        ],
        in_specs=[VMEM] * mp_count + [HBM] * mp_count + [VMEM] * 3 + [HBM] * 2,
        out_specs=[VMEM] * 2 + [HBM],
        scratch_shapes=[w_buf, sem4, semk],
        compiler_params=params(),
        cost_estimate=pl.CostEstimate(
            flops=front_flops, bytes_accessed=8 * width * local_cols, transcendentals=0
        ),
        name="section0_front",
    )(*x_pieces, *o_pieces, gains, gain_other, segments, w_own, w_other)
    o_other = exchange(o_own, "phase", 1)

    gated, x1 = pl.pallas_call(
        functools.partial(middle_kernel, mp_count),
        out_shape=[gated_shape, x_shape],
        in_specs=[VMEM] * (mp_count + 4) + [HBM] * 4,
        out_specs=[VMEM] * 2,
        scratch_shapes=[o_buf, semk, w_buf, sem4],
        compiler_params=params(),
        cost_estimate=pl.CostEstimate(
            flops=front_flops + back_flops,
            bytes_accessed=(8 + 2 * mp_count) * width * local_cols,
            transcendentals=0,
        ),
        name="section0_back_section1_front",
    )(*spread(gated, "mp"), x0, gains, gain_other, segments, w_own, w_other, o_own, o_other)

    states, ctx = pl.pallas_call(
        functools.partial(last_kernel, mp_count),
        out_shape=[x_shape, jax.ShapeDtypeStruct((imps, w_ctx.shape[1]), BF16)],
        in_specs=[VMEM] * (mp_count + 4) + [HBM] * 2,
        out_specs=[VMEM] * 2,
        scratch_shapes=[o_buf, semk],
        compiler_params=params(),
        cost_estimate=pl.CostEstimate(
            flops=back_flops + 2 * imps * width * (rows + w_ctx.shape[1]),
            bytes_accessed=2 * mp_count * width * local_cols,
            transcendentals=0,
        ),
        name="section1_back_context",
    )(*spread(gated, "mp"), x1, near, w_ctx, bias, o_own, o_other)

    return (
        states.reshape(1, 1, rows, width),
        ctx.reshape(1, 1, imps, w_ctx.shape[1]),
    )


def solution(mesh):
    in_specs = (
        P("dp", None),
        P("dp"),
        P("dp", None, None),
        P("dp", None, None, None),
        P("dp", None),
        P("phase", None),
        P("phase", None, None, "mp"),
        P("phase", "mp", None),
        P(None, "mp"),
        P("mp"),
    )
    out_specs = (P("dp", "phase", None, None), P("dp", "phase", None, "mp"))
    return jax.shard_map(
        on_device, mesh=mesh, in_specs=in_specs, out_specs=out_specs, check_vma=False
    )
```

time: 94.5 us -> 73.2 us (0.77)
  between operations: 14.2 us -> 0.77 us
  local copies, waits for them, and re-layouts: 13.4 us -> 1.92 us
  starting transfers between devices: 20.9 us -> 24.2 us
  Pallas kernels: 12.5 us -> 11.3 us
  waiting for transfers between devices: 32.5 us -> 33.5 us
    unnamed x33 -> x15, local copies, waits for them, and re-layouts: 12.6 us -> 1.9 us
    ppermute x17 -> x20, starting transfers between devices: 20.8 us -> 24.2 us  [exchange(): return lax.ppermute(value, axis, pairs)]
    ppermute x17 -> x20, waiting for transfers between devices: 31.8 us -> 33.5 us  [exchange(): return lax.ppermute(value, axis, pairs)]
    pallas_call x1, Pallas kernels: 3.93 us -> 2.95 us  [on_device(): pl.pallas_call(functools.partial(last_kernel, mp_count), out_shape=[x_sha...]
  transfers between devices with their start and end apart: 18 -> 20, of which waited for: 13 -> 12; matrix products, arithmetic and copies ran while one was open for 4% -> 3% of each run, Pallas kernels for 4% -> 2%
where the time goes in v4:
time: 73.2 us; the launch traced here: 73 us
  waiting for transfers between devices  33.5 us (46%)
  starting transfers between devices  24.2 us (33%)
  Pallas kernels  11.3 us (15%)
  local copies, waits for them, and re-layouts  1.92 us (3%)
  other arithmetic  1.38 us (2%)
  between operations  0.77 us (1%)
    ppermute x20, waiting for transfers between devices, exchange(): return lax.ppermute(value, axis, pairs)  33.5 us
    ppermute x20, starting transfers between devices, exchange(): return lax.ppermute(value, axis, pairs)  24.2 us
    pallas_call x1, Pallas kernels, on_device(): pl.pallas_call(functools.partial(middle_kernel, mp_count), out_shape=[gat...  4.08 us
    pallas_call x1, Pallas kernels, on_device(): pl.pallas_call(functools.partial(last_kernel, mp_count), out_shape=[x_sha...  2.95 us
    pallas_call x1, Pallas kernels, on_device(): pl.pallas_call(functools.partial(first_kernel, mp_count), out_shape=[gate...  2.87 us
    unnamed x15, local copies, waits for them, and re-layouts  1.9 us
  transfers between devices with their start and end apart: 20, of which 12 were waited for; matrix products, arithmetic and copies ran while one was open for 3% of the time, Pallas kernels for 2%

profile of v4, /device:TPU:0, one launch (start us, length us, event | category | flops | bytes accessed | tf_op | source)
XLA Modules:
  0.0 73.0 jit_solution(3409037469770233065)
XLA Ops:
  0.6 0.7 broadcast_multiply_fusion
  1.3 0.7 add.3
  2.0 3.0 %collective-permute-start = (s32[2,256]{1,0:T(2,128)S(1)}, s32[2,256]{1,0:T(2,128)S(1)}, u32[]{:S(2)}, u32[]{:S(2)}) collective-permute-start(s32[2,256]{1,0:T(2,128)S(1)} %reshape.18.refs_0_), channel_id=1, source_target_pairs={{0,8},{8,0},{16,24},{24,16},{1,9},{9,1},{17,25},{25,17},{2,10},{10... | collective-permute-start | bytes 6152 | tf_op jit(solution)/shard_map/ppermute | solution.py:36
  5.0 1.9 %copy.15 = bf16[1,1024,4,256]{3,1,2,0:T(8,128)(2,1)S(1)} copy(bf16[1,1024,4,256]{3,2,1,0:T(4,128)(2,1)} %param.16) | data formatting | bytes 4194304 | tf_op args[6]
  6.9 0.0 collective-permute-done.refs_1_
  6.9 0.0 copy-start.1
  6.9 0.0 copy-start.4
  6.9 0.0 copy-start
  7.0 0.1 collective-permute-start.8
  7.1 2.7 %collective-permute-start.1 = (s32[4,256]{1,0:T(4,128)S(1)}, s32[4,256]{1,0:T(4,128)S(1)}, u32[]{:S(2)}, u32[]{:S(2)}) collective-permute-start(s32[4,256]{1,0:T(4,128)S(1)} %pad_add_fusion), channel_id=1, source_target_pairs={{0,16},{8,24},{16,0},{24,8},{1,17},{9,25},{17,1},{25,9},{2,18},{10... | collective-permute-start | bytes 12296 | tf_op jit(solution)/shard_map/ppermute | solution.py:36
  9.8 1.5 %collective-permute-start.6 = (bf16[256,1024]{1,0:T(8,128)(2,1)S(1)}, bf16[256,1024]{1,0:T(8,128)(2,1)S(1)}, u32[]{:S(2)}, u32[]{:S(2)}) collective-permute-start(bf16[256,1024]{1,0:T(8,128)(2,1)S(1)} %bitcast.13), channel_id=1, source_target_pairs={{0,2},{2,0},{4,6},{6,4},{1,3},{3,1},{5,7},{7,5},{8,10},{10,8},{12,... | collective-permute-start | bytes 1572872 | tf_op jit(solution)/shard_map/ppermute | solution.py:36
  11.3 1.5 %collective-permute-start.7 = (bf16[256,1024]{1,0:T(8,128)(2,1)S(1)}, bf16[256,1024]{1,0:T(8,128)(2,1)S(1)}, u32[]{:S(2)}, u32[]{:S(2)}) collective-permute-start(bf16[256,1024]{1,0:T(8,128)(2,1)S(1)} %bitcast.14), channel_id=1, source_target_pairs={{0,4},{2,6},{4,0},{6,2},{1,5},{3,7},{5,1},{7,3},{8,12},{10,14},{12... | collective-permute-start | bytes 1572872 | tf_op jit(solution)/shard_map/ppermute | solution.py:36
  12.8 0.0 collective-permute-start.2
  12.8 0.0 collective-permute-done.1
  12.8 1.1 %collective-permute-done.2.refs_5_.refs_9_.refs_6_ = bf16[1,1024]{1,0:T(2,128)(2,1)S(1)} collective-permute-done((bf16[1,1024]{1,0:T(2,128)(2,1)S(1)}, bf16[1,1024]{1,0:T(2,128)(2,1)S(1)}, u32[]{:S(2)}, u32[]{:S(2)}) %collective-permute-start.2) | collective-permute-done | bytes 2080 | tf_op jit(solution)/shard_map/ppermute | solution.py:36
  14.0 1.3 %fetch.1 = (bf16[256,256]{1,0:T(8,128)(2,1)S(1)}, bf16[256,256]{1,0:T(8,128)(2,1)S(1)}, bf16[256,256]{1,0:T(8,128)(2,1)S(1)}, bf16[256,256]{1,0:T(8,128)(2,1)S(1)}) custom-call(s32[2,256]{1,0:T(2,128)S(1)} %reshape.18.refs_0_, s32[2,256]{1,0:T(2,128)S(1)} %collective-permute-done.refs_1_, s32[2,256]{1,0:T(2,128)S(1)} %get-tuple-element.25.refs_2_, ...), custom_call_target="tpu_custom_call" | custom-call | flops 536870912 | bytes 524288 | tf_op jit(solution)/shard_map/fetch/pallas_call | solution.py:84
  15.3 1.6 %collective-permute-start.4 = (bf16[256,256]{1,0:T(8,128)(2,1)S(1)}, bf16[256,256]{1,0:T(8,128)(2,1)S(1)}, u32[]{:S(2)}, u32[]{:S(2)}) collective-permute-start(bf16[256,256]{1,0:T(8,128)(2,1)S(1)} %get-tuple-element.16), channel_id=1, source_target_pairs={{0,8},{8,0},{16,24},{24,16},{1,9},{9,1},{17,25},{25,17},{2,10},{10... | collective-permute-start | bytes 393224 | tf_op jit(solution)/shard_map/ppermute | solution.py:36
  17.0 0.5 collective-permute-start.12
  17.4 3.5 %collective-permute-done.4.b_ref = bf16[256,256]{1,0:T(8,128)(2,1)S(1)} collective-permute-done((bf16[256,256]{1,0:T(8,128)(2,1)S(1)}, bf16[256,256]{1,0:T(8,128)(2,1)S(1)}, u32[]{:S(2)}, u32[]{:S(2)}) %collective-permute-start.4) | collective-permute-done | bytes 131104 | tf_op jit(solution)/shard_map/ppermute | solution.py:36
  21.0 1.6 %collective-permute-start.3 = (bf16[256,256]{1,0:T(8,128)(2,1)S(1)}, bf16[256,256]{1,0:T(8,128)(2,1)S(1)}, u32[]{:S(2)}, u32[]{:S(2)}) collective-permute-start(bf16[256,256]{1,0:T(8,128)(2,1)S(1)} %get-tuple-element.14), channel_id=1, source_target_pairs={{0,8},{8,0},{16,24},{24,16},{1,9},{9,1},{17,25},{25,17},{2,10},{10... | collective-permute-start | bytes 393224 | tf_op jit(solution)/shard_map/ppermute | solution.py:36
  22.6 3.4 %collective-permute-done.3.b_ref = bf16[256,256]{1,0:T(8,128)(2,1)S(1)} collective-permute-done((bf16[256,256]{1,0:T(8,128)(2,1)S(1)}, bf16[256,256]{1,0:T(8,128)(2,1)S(1)}, u32[]{:S(2)}, u32[]{:S(2)}) %collective-permute-start.3) | collective-permute-done | bytes 131104 | tf_op jit(solution)/shard_map/ppermute | solution.py:36
  25.9 0.9 %collective-permute-start.5 = (bf16[256,256]{1,0:T(8,128)(2,1)S(1)}, bf16[256,256]{1,0:T(8,128)(2,1)S(1)}, u32[]{:S(2)}, u32[]{:S(2)}) collective-permute-start(bf16[256,256]{1,0:T(8,128)(2,1)S(1)} %merge.4), channel_id=1, source_target_pairs={{0,16},{8,24},{16,0},{24,8},{1,17},{9,25},{17,1},{25,9},{2,18},{10... | collective-permute-start | bytes 393224 | tf_op jit(solution)/shard_map/ppermute | solution.py:36
  26.8 6.7 %collective-permute-done.5.b_ref = bf16[256,256]{1,0:T(8,128)(2,1)S(1)} collective-permute-done((bf16[256,256]{1,0:T(8,128)(2,1)S(1)}, bf16[256,256]{1,0:T(8,128)(2,1)S(1)}, u32[]{:S(2)}, u32[]{:S(2)}) %collective-permute-start.5) | collective-permute-done | bytes 131104 | tf_op jit(solution)/shard_map/ppermute | solution.py:36
  33.5 0.0 collective-permute-done.6.refs_0_.refs_5_
  33.5 2.7 %collective-permute-done.7.refs_1_.refs_6_ = bf16[256,1024]{1,0:T(8,128)(2,1)S(1)} collective-permute-done((bf16[256,1024]{1,0:T(8,128)(2,1)S(1)}, bf16[256,1024]{1,0:T(8,128)(2,1)S(1)}, u32[]{:S(2)}, u32[]{:S(2)}) %collective-permute-start.7) | collective-permute-done | bytes 524320 | tf_op jit(solution)/shard_map/ppermute | solution.py:36
  36.2 0.0 collective-permute-done.8.refs_2_.refs_12_.refs_9_
  36.3 1.6 %collective-permute-start.10 = (bf16[256,256]{1,0:T(8,128)(2,1)S(1)}, bf16[256,256]{1,0:T(8,128)(2,1)S(1)}, u32[]{:S(2)}, u32[]{:S(2)}) collective-permute-start(bf16[256,256]{1,0:T(8,128)(2,1)S(1)} %merge.5.refs_0_), channel_id=1, source_target_pairs={{0,4},{2,6},{4,0},{6,2},{1,5},{3,7},{5,1},{7,3},{8,12},{10,14},{12... | collective-permute-start | bytes 393224 | tf_op jit(solution)/shard_map/ppermute | solution.py:36
  37.8 0.2 collective-permute-start.11
  38.0 1.8 %collective-permute-start.9 = (bf16[256,256]{1,0:T(8,128)(2,1)S(1)}, bf16[256,256]{1,0:T(8,128)(2,1)S(1)}, u32[]{:S(2)}, u32[]{:S(2)}) collective-permute-start(bf16[256,256]{1,0:T(8,128)(2,1)S(1)} %merge.5.refs_0_), channel_id=1, source_target_pairs={{0,2},{2,0},{4,6},{6,4},{1,3},{3,1},{5,7},{7,5},{8,10},{10,8},{12,... | collective-permute-start | bytes 393224 | tf_op jit(solution)/shard_map/ppermute | solution.py:36
  39.8 0.0 collective-permute-done.12.refs_7_
  39.8 3.2 %collective-permute-done.10.refs_2_ = bf16[256,256]{1,0:T(8,128)(2,1)S(1)} collective-permute-done((bf16[256,256]{1,0:T(8,128)(2,1)S(1)}, bf16[256,256]{1,0:T(8,128)(2,1)S(1)}, u32[]{:S(2)}, u32[]{:S(2)}) %collective-permute-start.10) | collective-permute-done | bytes 131104 | tf_op jit(solution)/shard_map/ppermute | solution.py:36
  43.0 1.3 %collective-permute-done.11.refs_3_ = bf16[256,256]{1,0:T(8,128)(2,1)S(1)} collective-permute-done((bf16[256,256]{1,0:T(8,128)(2,1)S(1)}, bf16[256,256]{1,0:T(8,128)(2,1)S(1)}, u32[]{:S(2)}, u32[]{:S(2)}) %collective-permute-start.11) | collective-permute-done | bytes 131104 | tf_op jit(solution)/shard_map/ppermute | solution.py:36
  44.3 0.3 collective-permute-done.9.refs_1_
  44.7 2.9 %section0_front.1 = (bf16[256,256]{1,0:T(8,128)(2,1)S(1)}, bf16[256,1024]{1,0:T(8,128)(2,1)S(1)}, bf16[4,256,1024]{2,1,0:T(8,128)(2,1)S(1)}) custom-call(bf16[256,256]{1,0:T(8,128)(2,1)S(1)} %merge.5.refs_0_, bf16[256,256]{1,0:T(8,128)(2,1)S(1)} %collective-permute-done.9.refs_1_, bf16[256,256]{1,0:T(8,128)(2,1)S(1)} %collective-permute-done.10.refs_2_, ...), custom_call_target="tpu_custom_call" | custom-call | flops 603979776 | bytes 2097152 | tf_op jit(solution)/shard_map/section0_front/pallas_call | solution.py:320
  47.6 0.1 collective-permute-start.16
  47.6 0.5 collective-permute-start.13
  48.1 1.5 %collective-permute-start.14 = (bf16[256,256]{1,0:T(8,128)(2,1)S(1)}, bf16[256,256]{1,0:T(8,128)(2,1)S(1)}, u32[]{:S(2)}, u32[]{:S(2)}) collective-permute-start(bf16[256,256]{1,0:T(8,128)(2,1)S(1)} %get-tuple-element.17.refs_0_), channel_id=1, source_target_pairs={{0,4},{2,6},{4,0},{6,2},{1,5},{3,7},{5,1},{7,3},{8,12},{10,14},{12... | collective-permute-start | bytes 393224 | tf_op jit(solution)/shard_map/ppermute | solution.py:36
  49.6 1.6 %collective-permute-start.15 = (bf16[256,256]{1,0:T(8,128)(2,1)S(1)}, bf16[256,256]{1,0:T(8,128)(2,1)S(1)}, u32[]{:S(2)}, u32[]{:S(2)}) collective-permute-start(bf16[256,256]{1,0:T(8,128)(2,1)S(1)} %get-tuple-element.17.refs_0_), channel_id=1, source_target_pairs={{0,6},{2,4},{4,2},{6,0},{1,7},{3,5},{5,3},{7,1},{8,14},{10,12},{12... | collective-permute-start | bytes 393224 | tf_op jit(solution)/shard_map/ppermute | solution.py:36
  51.2 2.8 %collective-permute-done.13.refs_1_ = bf16[256,256]{1,0:T(8,128)(2,1)S(1)} collective-permute-done((bf16[256,256]{1,0:T(8,128)(2,1)S(1)}, bf16[256,256]{1,0:T(8,128)(2,1)S(1)}, u32[]{:S(2)}, u32[]{:S(2)}) %collective-permute-start.13) | collective-permute-done | bytes 131104 | tf_op jit(solution)/shard_map/ppermute | solution.py:36
  54.0 0.0 collective-permute-done.14.refs_2_
  54.0 3.4 %collective-permute-done.15.refs_3_ = bf16[256,256]{1,0:T(8,128)(2,1)S(1)} collective-permute-done((bf16[256,256]{1,0:T(8,128)(2,1)S(1)}, bf16[256,256]{1,0:T(8,128)(2,1)S(1)}, u32[]{:S(2)}, u32[]{:S(2)}) %collective-permute-start.15) | collective-permute-done | bytes 131104 | tf_op jit(solution)/shard_map/ppermute | solution.py:36
  57.4 4.1 %section0_back_section1_front.1 = (bf16[256,256]{1,0:T(8,128)(2,1)S(1)}, bf16[256,1024]{1,0:T(8,128)(2,1)S(1)}) custom-call(bf16[256,256]{1,0:T(8,128)(2,1)S(1)} %get-tuple-element.17.refs_0_, bf16[256,256]{1,0:T(8,128)(2,1)S(1)} %collective-permute-done.13.refs_1_, bf16[256,256]{1,0:T(8,128)(2,1)S(1)} %collective-permute-done.14.refs_2_, ...), custom_call_target="tpu_custom_call" | custom-call | flops 1140850688 | bytes 4194304 | tf_op jit(solution)/shard_map/section0_back_section1_front/pallas_call | solution.py:338
  61.5 0.8 %collective-permute-start.17 = (bf16[256,256]{1,0:T(8,128)(2,1)S(1)}, bf16[256,256]{1,0:T(8,128)(2,1)S(1)}, u32[]{:S(2)}, u32[]{:S(2)}) collective-permute-start(bf16[256,256]{1,0:T(8,128)(2,1)S(1)} %get-tuple-element.20.refs_0_), channel_id=1, source_target_pairs={{0,2},{2,0},{4,6},{6,4},{1,3},{3,1},{5,7},{7,5},{8,10},{10,8},{12,... | collective-permute-start | bytes 393224 | tf_op jit(solution)/shard_map/ppermute | solution.py:36
  62.3 1.6 %collective-permute-start.18 = (bf16[256,256]{1,0:T(8,128)(2,1)S(1)}, bf16[256,256]{1,0:T(8,128)(2,1)S(1)}, u32[]{:S(2)}, u32[]{:S(2)}) collective-permute-start(bf16[256,256]{1,0:T(8,128)(2,1)S(1)} %get-tuple-element.20.refs_0_), channel_id=1, source_target_pairs={{0,4},{2,6},{4,0},{6,2},{1,5},{3,7},{5,1},{7,3},{8,12},{10,14},{12... | collective-permute-start | bytes 393224 | tf_op jit(solution)/shard_map/ppermute | solution.py:36
  63.9 1.2 %collective-permute-start.19 = (bf16[256,256]{1,0:T(8,128)(2,1)S(1)}, bf16[256,256]{1,0:T(8,128)(2,1)S(1)}, u32[]{:S(2)}, u32[]{:S(2)}) collective-permute-start(bf16[256,256]{1,0:T(8,128)(2,1)S(1)} %get-tuple-element.20.refs_0_), channel_id=1, source_target_pairs={{0,6},{2,4},{4,2},{6,0},{1,7},{3,5},{5,3},{7,1},{8,14},{10,12},{12... | collective-permute-start | bytes 393224 | tf_op jit(solution)/shard_map/ppermute | solution.py:36
  65.1 2.9 %collective-permute-done.17.refs_1_ = bf16[256,256]{1,0:T(8,128)(2,1)S(1)} collective-permute-done((bf16[256,256]{1,0:T(8,128)(2,1)S(1)}, bf16[256,256]{1,0:T(8,128)(2,1)S(1)}, u32[]{:S(2)}, u32[]{:S(2)}) %collective-permute-start.17) | collective-permute-done | bytes 131104 | tf_op jit(solution)/shard_map/ppermute | solution.py:36
  68.0 2.1 %collective-permute-done.18.refs_2_ = bf16[256,256]{1,0:T(8,128)(2,1)S(1)} collective-permute-done((bf16[256,256]{1,0:T(8,128)(2,1)S(1)}, bf16[256,256]{1,0:T(8,128)(2,1)S(1)}, u32[]{:S(2)}, u32[]{:S(2)}) %collective-permute-start.18) | collective-permute-done | bytes 131104 | tf_op jit(solution)/shard_map/ppermute | solution.py:36
  70.1 3.0 %section1_back_context.1 = (bf16[256,1024]{1,0:T(8,128)(2,1)}, bf16[256,256]{1,0:T(8,128)(2,1)}) custom-call(bf16[256,256]{1,0:T(8,128)(2,1)S(1)} %get-tuple-element.20.refs_0_, bf16[256,256]{1,0:T(8,128)(2,1)S(1)} %collective-permute-done.17.refs_1_, bf16[256,256]{1,0:T(8,128)(2,1)S(1)} %collective-permute-done.18.refs_2_, ...), custom_call_target="tpu_custom_call" | custom-call | flops 805306368 | bytes 2097152 | tf_op jit(solution)/shard_map/section1_back_context/pallas_call | solution.py:353
  (21 shorter events, 0.1 us)
Async XLA Ops:
  2.0 4.9 %collective-permute-start = (s32[2,256]{1,0:T(2,128)S(1)}, s32[2,256]{1,0:T(2,128)S(1)}, u32[]{:S(2)}, u32[]{:S(2)}) collective-permute-start(s32[2,256]{1,0:T(2,128)S(1)} %reshape.18.refs_0_), channel_id=1, source_target_pairs={{0,8},{8,0},{16,24},{24,16},{1,9},{9,1},{17,25},{25,17},{2,10},{10... | collective-permute-start | bytes 6152 | tf_op jit(solution)/shard_map/ppermute | solution.py:36
  6.9 2.9 %copy-start.1 = (bf16[1,256,1024]{2,1,0:T(8,128)(2,1)S(1)}, bf16[1,256,1024]{2,1,0:T(8,128)(2,1)}, u32[]{:S(2)}) copy-start(bf16[1,256,1024]{2,1,0:T(8,128)(2,1)} %param.17) | copy-start | bytes 1572868
  6.9 5.9 %copy-start.4 = (bf16[1,1024]{1,0:T(2,128)(2,1)S(1)}, bf16[1,1024]{1,0:T(2,128)(2,1)}, u32[]{:S(2)}) copy-start(bf16[1,1024]{1,0:T(2,128)(2,1)} %refs_5_.1) | copy-start | bytes 6148
  6.9 7.0 %copy-start = (bf16[1024,1024]{1,0:T(8,128)(2,1)S(1)}, bf16[1024,1024]{1,0:T(8,128)(2,1)}, u32[]{:S(2)}) copy-start(bf16[1024,1024]{1,0:T(8,128)(2,1)} %refs_4_.1) | copy-start | bytes 6291460
  7.0 29.3 %collective-permute-start.8 = (bf16[4,1024,256]{2,1,0:T(8,128)(2,1)S(1)}, bf16[4,1024,256]{2,1,0:T(8,128)(2,1)S(1)}, u32[]{:S(2)}, u32[]{:S(2)}) collective-permute-start(bf16[4,1024,256]{2,1,0:T(8,128)(2,1)S(1)} %hold.1.refs_11_.refs_8_), channel_id=1, source_target_pairs={{0,1},{1,0},{2,3},{3,2},{4,5},{5,4},{6,7},{7,6},{8,9},{9,8},{10,11... | collective-permute-start | bytes 6291464 | tf_op jit(solution)/shard_map/ppermute | solution.py:36
  7.1 5.8 %collective-permute-start.1 = (s32[4,256]{1,0:T(4,128)S(1)}, s32[4,256]{1,0:T(4,128)S(1)}, u32[]{:S(2)}, u32[]{:S(2)}) collective-permute-start(s32[4,256]{1,0:T(4,128)S(1)} %pad_add_fusion), channel_id=1, source_target_pairs={{0,16},{8,24},{16,0},{24,8},{1,17},{9,25},{17,1},{25,9},{2,18},{10... | collective-permute-start | bytes 12296 | tf_op jit(solution)/shard_map/ppermute | solution.py:36
  9.8 23.7 %collective-permute-start.6 = (bf16[256,1024]{1,0:T(8,128)(2,1)S(1)}, bf16[256,1024]{1,0:T(8,128)(2,1)S(1)}, u32[]{:S(2)}, u32[]{:S(2)}) collective-permute-start(bf16[256,1024]{1,0:T(8,128)(2,1)S(1)} %bitcast.13), channel_id=1, source_target_pairs={{0,2},{2,0},{4,6},{6,4},{1,3},{3,1},{5,7},{7,5},{8,10},{10,8},{12,... | collective-permute-start | bytes 1572872 | tf_op jit(solution)/shard_map/ppermute | solution.py:36
  11.3 24.9 %collective-permute-start.7 = (bf16[256,1024]{1,0:T(8,128)(2,1)S(1)}, bf16[256,1024]{1,0:T(8,128)(2,1)S(1)}, u32[]{:S(2)}, u32[]{:S(2)}) collective-permute-start(bf16[256,1024]{1,0:T(8,128)(2,1)S(1)} %bitcast.14), channel_id=1, source_target_pairs={{0,4},{2,6},{4,0},{6,2},{1,5},{3,7},{5,1},{7,3},{8,12},{10,14},{12... | collective-permute-start | bytes 1572872 | tf_op jit(solution)/shard_map/ppermute | solution.py:36
  12.8 1.2 %collective-permute-start.2 = (bf16[1,1024]{1,0:T(2,128)(2,1)S(1)}, bf16[1,1024]{1,0:T(2,128)(2,1)S(1)}, u32[]{:S(2)}, u32[]{:S(2)}) collective-permute-start(bf16[1,1024]{1,0:T(2,128)(2,1)S(1)} %copy-done.4), channel_id=1, source_target_pairs={{0,1},{1,0},{2,3},{3,2},{4,5},{5,4},{6,7},{7,6},{8,9},{9,8},{10,11... | collective-permute-start | bytes 6152 | tf_op jit(solution)/shard_map/ppermute | solution.py:36
  15.3 5.6 %collective-permute-start.4 = (bf16[256,256]{1,0:T(8,128)(2,1)S(1)}, bf16[256,256]{1,0:T(8,128)(2,1)S(1)}, u32[]{:S(2)}, u32[]{:S(2)}) collective-permute-start(bf16[256,256]{1,0:T(8,128)(2,1)S(1)} %get-tuple-element.16), channel_id=1, source_target_pairs={{0,8},{8,0},{16,24},{24,16},{1,9},{9,1},{17,25},{25,17},{2,10},{10... | collective-permute-start | bytes 393224 | tf_op jit(solution)/shard_map/ppermute | solution.py:36
  17.0 22.9 %collective-permute-start.12 = (bf16[256,1024]{1,0:T(8,128)(2,1)S(1)}, bf16[256,1024]{1,0:T(8,128)(2,1)S(1)}, u32[]{:S(2)}, u32[]{:S(2)}) collective-permute-start(bf16[256,1024]{1,0:T(8,128)(2,1)S(1)} %bitcast.15), channel_id=1, source_target_pairs={{0,6},{2,4},{4,2},{6,0},{1,7},{3,5},{5,3},{7,1},{8,14},{10,12},{12... | collective-permute-start | bytes 1572872 | tf_op jit(solution)/shard_map/ppermute | solution.py:36
  21.0 5.0 %collective-permute-start.3 = (bf16[256,256]{1,0:T(8,128)(2,1)S(1)}, bf16[256,256]{1,0:T(8,128)(2,1)S(1)}, u32[]{:S(2)}, u32[]{:S(2)}) collective-permute-start(bf16[256,256]{1,0:T(8,128)(2,1)S(1)} %get-tuple-element.14), channel_id=1, source_target_pairs={{0,8},{8,0},{16,24},{24,16},{1,9},{9,1},{17,25},{25,17},{2,10},{10... | collective-permute-start | bytes 393224 | tf_op jit(solution)/shard_map/ppermute | solution.py:36
  22.5 22.1 %copy-start.5 = (s32[1,2,256]{2,1,0:T(2,128)S(1)}, s32[1,2,256]{2,1,0:T(2,128)}, u32[]{:S(2)}) copy-start(s32[1,2,256]{2,1,0:T(2,128)} %refs_7_.1) | copy-start | bytes 6148
  25.9 7.6 %collective-permute-start.5 = (bf16[256,256]{1,0:T(8,128)(2,1)S(1)}, bf16[256,256]{1,0:T(8,128)(2,1)S(1)}, u32[]{:S(2)}, u32[]{:S(2)}) collective-permute-start(bf16[256,256]{1,0:T(8,128)(2,1)S(1)} %merge.4), channel_id=1, source_target_pairs={{0,16},{8,24},{16,0},{24,8},{1,17},{9,25},{17,1},{25,9},{2,18},{10... | collective-permute-start | bytes 393224 | tf_op jit(solution)/shard_map/ppermute | solution.py:36
  36.3 6.8 %collective-permute-start.10 = (bf16[256,256]{1,0:T(8,128)(2,1)S(1)}, bf16[256,256]{1,0:T(8,128)(2,1)S(1)}, u32[]{:S(2)}, u32[]{:S(2)}) collective-permute-start(bf16[256,256]{1,0:T(8,128)(2,1)S(1)} %merge.5.refs_0_), channel_id=1, source_target_pairs={{0,4},{2,6},{4,0},{6,2},{1,5},{3,7},{5,1},{7,3},{8,12},{10,14},{12... | collective-permute-start | bytes 393224 | tf_op jit(solution)/shard_map/ppermute | solution.py:36
  37.8 6.5 %collective-permute-start.11 = (bf16[256,256]{1,0:T(8,128)(2,1)S(1)}, bf16[256,256]{1,0:T(8,128)(2,1)S(1)}, u32[]{:S(2)}, u32[]{:S(2)}) collective-permute-start(bf16[256,256]{1,0:T(8,128)(2,1)S(1)} %merge.5.refs_0_), channel_id=1, source_target_pairs={{0,6},{2,4},{4,2},{6,0},{1,7},{3,5},{5,3},{7,1},{8,14},{10,12},{12... | collective-permute-start | bytes 393224 | tf_op jit(solution)/shard_map/ppermute | solution.py:36
  38.0 6.6 %collective-permute-start.9 = (bf16[256,256]{1,0:T(8,128)(2,1)S(1)}, bf16[256,256]{1,0:T(8,128)(2,1)S(1)}, u32[]{:S(2)}, u32[]{:S(2)}) collective-permute-start(bf16[256,256]{1,0:T(8,128)(2,1)S(1)} %merge.5.refs_0_), channel_id=1, source_target_pairs={{0,2},{2,0},{4,6},{6,4},{1,3},{3,1},{5,7},{7,5},{8,10},{10,8},{12,... | collective-permute-start | bytes 393224 | tf_op jit(solution)/shard_map/ppermute | solution.py:36
  47.6 9.9 %collective-permute-start.16 = (bf16[4,256,1024]{2,1,0:T(8,128)(2,1)S(1)}, bf16[4,256,1024]{2,1,0:T(8,128)(2,1)S(1)}, u32[]{:S(2)}, u32[]{:S(2)}) collective-permute-start(bf16[4,256,1024]{2,1,0:T(8,128)(2,1)S(1)} %get-tuple-element.19.refs_10_.refs_8_), channel_id=1, source_target_pairs={{0,1},{1,0},{2,3},{3,2},{4,5},{5,4},{6,7},{7,6},{8,9},{9,8},{10,11... | collective-permute-start | bytes 6291464 | tf_op jit(solution)/shard_map/ppermute | solution.py:36
  47.6 6.4 %collective-permute-start.13 = (bf16[256,256]{1,0:T(8,128)(2,1)S(1)}, bf16[256,256]{1,0:T(8,128)(2,1)S(1)}, u32[]{:S(2)}, u32[]{:S(2)}) collective-permute-start(bf16[256,256]{1,0:T(8,128)(2,1)S(1)} %get-tuple-element.17.refs_0_), channel_id=1, source_target_pairs={{0,2},{2,0},{4,6},{6,4},{1,3},{3,1},{5,7},{7,5},{8,10},{10,8},{12,... | collective-permute-start | bytes 393224 | tf_op jit(solution)/shard_map/ppermute | solution.py:36
  48.1 5.9 %collective-permute-start.14 = (bf16[256,256]{1,0:T(8,128)(2,1)S(1)}, bf16[256,256]{1,0:T(8,128)(2,1)S(1)}, u32[]{:S(2)}, u32[]{:S(2)}) collective-permute-start(bf16[256,256]{1,0:T(8,128)(2,1)S(1)} %get-tuple-element.17.refs_0_), channel_id=1, source_target_pairs={{0,4},{2,6},{4,0},{6,2},{1,5},{3,7},{5,1},{7,3},{8,12},{10,14},{12... | collective-permute-start | bytes 393224 | tf_op jit(solution)/shard_map/ppermute | solution.py:36
  49.6 7.8 %collective-permute-start.15 = (bf16[256,256]{1,0:T(8,128)(2,1)S(1)}, bf16[256,256]{1,0:T(8,128)(2,1)S(1)}, u32[]{:S(2)}, u32[]{:S(2)}) collective-permute-start(bf16[256,256]{1,0:T(8,128)(2,1)S(1)} %get-tuple-element.17.refs_0_), channel_id=1, source_target_pairs={{0,6},{2,4},{4,2},{6,0},{1,7},{3,5},{5,3},{7,1},{8,14},{10,12},{12... | collective-permute-start | bytes 393224 | tf_op jit(solution)/shard_map/ppermute | solution.py:36
  57.4 7.7 %copy-start.6 = (bf16[256]{0:T(256)(128)(2,1)S(1)}, bf16[256]{0:T(256)(128)(2,1)}, u32[]{:S(2)}) copy-start(bf16[256]{0:T(256)(128)(2,1)} %param.19) | copy-start | bytes 1540
  57.4 12.7 %copy-start.2 = (bf16[1024,256]{1,0:T(8,128)(2,1)S(1)}, bf16[1024,256]{1,0:T(8,128)(2,1)}, u32[]{:S(2)}) copy-start(bf16[1024,256]{1,0:T(8,128)(2,1)} %refs_6_.1) | copy-start | bytes 1572868
  57.4 12.7 %copy-start.3 = (s32[1,2,256,8]{2,3,1,0:T(8,128)S(1)}, s32[1,2,256,8]{2,3,1,0:T(8,128)}, u32[]{:S(2)}) copy-start(s32[1,2,256,8]{2,3,1,0:T(8,128)} %param.13) | copy-start | bytes 49156
  61.5 6.5 %collective-permute-start.17 = (bf16[256,256]{1,0:T(8,128)(2,1)S(1)}, bf16[256,256]{1,0:T(8,128)(2,1)S(1)}, u32[]{:S(2)}, u32[]{:S(2)}) collective-permute-start(bf16[256,256]{1,0:T(8,128)(2,1)S(1)} %get-tuple-element.20.refs_0_), channel_id=1, source_target_pairs={{0,2},{2,0},{4,6},{6,4},{1,3},{3,1},{5,7},{7,5},{8,10},{10,8},{12,... | collective-permute-start | bytes 393224 | tf_op jit(solution)/shard_map/ppermute | solution.py:36
  62.3 7.8 %collective-permute-start.18 = (bf16[256,256]{1,0:T(8,128)(2,1)S(1)}, bf16[256,256]{1,0:T(8,128)(2,1)S(1)}, u32[]{:S(2)}, u32[]{:S(2)}) collective-permute-start(bf16[256,256]{1,0:T(8,128)(2,1)S(1)} %get-tuple-element.20.refs_0_), channel_id=1, source_target_pairs={{0,4},{2,6},{4,0},{6,2},{1,5},{3,7},{5,1},{7,3},{8,12},{10,14},{12... | collective-permute-start | bytes 393224 | tf_op jit(solution)/shard_map/ppermute | solution.py:36
  63.9 6.2 %collective-permute-start.19 = (bf16[256,256]{1,0:T(8,128)(2,1)S(1)}, bf16[256,256]{1,0:T(8,128)(2,1)S(1)}, u32[]{:S(2)}, u32[]{:S(2)}) collective-permute-start(bf16[256,256]{1,0:T(8,128)(2,1)S(1)} %get-tuple-element.20.refs_0_), channel_id=1, source_target_pairs={{0,6},{2,4},{4,2},{6,0},{1,7},{3,5},{5,3},{7,1},{8,14},{10,12},{12... | collective-permute-start | bytes 393224 | tf_op jit(solution)/shard_map/ppermute | solution.py:36

commit v5 on v4

--- a/solution.py
+++ b/solution.py
@@ -128,6 +128,33 @@
     )(value, *after)
 
 
+def cut_kernel(near_ref, far_ref, *refs):
+    low_ref, high_ref, sems = refs[-3:]
+    half = low_ref.shape[0]
+    copies = [
+        pltpu.make_async_copy(far_ref.at[pl.ds(0, half), :], low_ref, sems.at[0]),
+        pltpu.make_async_copy(near_ref.at[pl.ds(half, half), :], high_ref, sems.at[1]),
+    ]
+    for copy in copies:
+        copy.start()
+    for copy in copies:
+        copy.wait()
+
+
+def relay(near, far, axis, after):
+    half = jax.ShapeDtypeStruct((near.shape[0] // 2,) + near.shape[1:], near.dtype)
+    low, high = pl.pallas_call(
+        cut_kernel,
+        out_shape=[half] * 2,
+        in_specs=[HBM] * (2 + len(after)),
+        out_specs=[HBM] * 2,
+        scratch_shapes=[pltpu.SemaphoreType.DMA((2,))],
+        compiler_params=params(),
+        name="cut",
+    )(near, far, *after)
+    return [exchange(low, axis, 1), exchange(high, axis, 2)]
+
+
 def ask_around(wanted):
     asked, step = [wanted], 1
     while step < lax.axis_size("dp"):
@@ -137,13 +164,15 @@
     return asked
 
 
-def gather_in(blocks, after):
+def gather_in(blocks, first, then):
     blocks, step = dict(enumerate(blocks)), 1
     while step < lax.axis_size("dp"):
+        at_end = 2 * step == lax.axis_size("dp")
         for k in sorted((k for k in blocks if k & step), reverse=True):
             got = exchange(blocks.pop(k), "dp", step)
-            last = 2 * step == lax.axis_size("dp")
-            blocks[k ^ step] = merge(blocks[k ^ step], got, after if last else [])
+            after = then(blocks[k ^ step]) if at_end else first
+            blocks[k ^ step] = merge(blocks[k ^ step], got, after)
+            first = [blocks[k ^ step]]
         step = 2 * step
     return blocks[0]
 
@@ -207,14 +236,15 @@
     return total.astype(BF16)
 
 
-def first_kernel(steps, *refs):
-    x_refs, o_own = refs[:steps], refs[steps : 2 * steps]
-    gain_own, gain_other, seg_ref, w_own, w_other = refs[2 * steps : -6]
+def first_kernel(steps, places, *refs):
+    x_refs, o_own = refs[:steps], refs[steps : steps + len(places)]
+    gain_own, gain_other, seg_ref, w_own, w_other = refs[steps + len(places) : -6]
     gated_ref, x_ref, stack_ref, w_buf, w_sem, o_sem = refs[-6:]
     start_weights(0, w_own, w_other, w_buf, w_sem)
-    copies = [
-        pltpu.make_async_copy(o_own[k], stack_ref.at[k], o_sem.at[k]) for k in range(steps)
-    ]
+    copies = []
+    for n, (k, row) in enumerate(places):
+        at = stack_ref.at[k, pl.ds(row, o_own[n].shape[0]), :]
+        copies.append(pltpu.make_async_copy(o_own[n], at, o_sem.at[n]))
     for copy in copies:
         copy.start()
     width = x_refs[0].shape[1]
@@ -288,9 +318,15 @@
     part = width // mp_count
 
     w_own = jnp.transpose(w_in[0], (1, 0, 2))
-    o_pieces = spread(w_out[0], "mp")
+    places = [(k, 0) for k in range(mp_count)]
+    if mp_count == 4:
+        near, far = exchange(w_out[0], "mp", 1), exchange(w_out[0], "mp", 2)
+        o_pieces = [w_out[0], near, far]
+        places.append((3, local_cols // 2))
+    else:
+        o_pieces = spread(w_out[0], "mp")
     gain_other = exchange(gains, "phase", 1)
-    near = jnp.transpose(neighbors[0], (0, 2, 1))
+    neigh = jnp.transpose(neighbors[0], (0, 2, 1))
     bias = ctx_bias.reshape(1, -1)
 
     if is_pow2(dp_count) and dp_count <= 8:
@@ -298,14 +334,23 @@
         asked = ask_around(wanted)
         w_own = hold(w_own, asked[1:2])
         w_other = exchange(w_own, "phase", 1)
-        found = fetch(asked, table, part, [gain_other])
-        piece = gather_in(found, o_pieces[1:3] + [w_other])
+        late = fetch(asked[-1:], table, part, [])
+        found = fetch(asked[:-1], table, part, late) + late
+
+        def then(first):
+            if mp_count == 4:
+                o_pieces.extend(relay(near, far, "mp", [first]))
+            return [w_other, gain_other]
+
+        piece = gather_in(found, [], then)
     else:
         piece = fetch_rows_padded(item_owner[:, 0], item_row, table, part)
         piece = lax.dynamic_index_in_dim(
             piece.reshape(batches, rows, part), lax.axis_index("phase"), 0, keepdims=False
         )
         w_other = exchange(w_own, "phase", 1)
+        if mp_count == 4:
+            o_pieces.extend(relay(near, far, "mp", [piece]))
     x_pieces = spread(piece, "mp")
 
     sem4 = pltpu.SemaphoreType.DMA((4,))
@@ -318,15 +363,15 @@
     back_flops = 2 * rows * width * local_cols * mp_count
 
     gated, x0, o_own = pl.pallas_call(
-        functools.partial(first_kernel, mp_count),
+        functools.partial(first_kernel, mp_count, places),
         out_shape=[
             gated_shape,
             x_shape,
             jax.ShapeDtypeStruct((mp_count, local_cols, width), BF16),
         ],
-        in_specs=[VMEM] * mp_count + [HBM] * mp_count + [VMEM] * 3 + [HBM] * 2,
+        in_specs=[VMEM] * mp_count + [HBM] * len(places) + [VMEM] * 3 + [HBM] * 2,
         out_specs=[VMEM] * 2 + [HBM],
-        scratch_shapes=[w_buf, sem4, semk],
+        scratch_shapes=[w_buf, sem4, pltpu.SemaphoreType.DMA((len(places),))],
         compiler_params=params(),
         cost_estimate=pl.CostEstimate(
             flops=front_flops, bytes_accessed=8 * width * local_cols, transcendentals=0
@@ -363,7 +408,7 @@
             transcendentals=0,
         ),
         name="section1_back_context",
-    )(*spread(gated, "mp"), x1, near, w_ctx, bias, o_own, o_other)
+    )(*spread(gated, "mp"), x1, neigh, w_ctx, bias, o_own, o_other)
 
     return (
         states.reshape(1, 1, rows, width),

time: 73.2 us -> 66.6 us (0.910)
  waiting for transfers between devices: 33.5 us -> 24.9 us
  local copies, waits for them, and re-layouts: 1.92 us -> 2.85 us
    ppermute x20 -> x21, waiting for transfers between devices: 33.5 us -> 24.9 us  [exchange(): return lax.ppermute(value, axis, pairs)]
    unnamed x15, local copies, waits for them, and re-layouts: 1.9 us -> 2.83 us
    ppermute x20 -> x21, starting transfers between devices: 24.2 us -> 24.8 us  [exchange(): return lax.ppermute(value, axis, pairs)]
    pallas_call x1 -> x2, Pallas kernels: 1.32 us -> 1.64 us  [fetch(): pl.pallas_call(functools.partial(fetch_kernel, steps), out_shape=[jax.Sha...]
    pallas_call x1 -> x2, Pallas kernels: 2.87 us -> 2.94 us  [the longest x1 2.88 us: on_device(): pl.pallas_call(functools.partial(first_kernel, mp_count, places), out_sha...]
  transfers between devices with their start and end apart: 20 -> 21, of which waited for: 12 -> 10; matrix products, arithmetic and copies ran while one was open for 3% -> 3% of each run, Pallas kernels for 2% -> 3%
where the time goes in v5:
time: 66.6 us; the launch traced here: 66.4 us
  waiting for transfers between devices  24.9 us (37%)
  starting transfers between devices  24.8 us (37%)
  Pallas kernels  11.7 us (18%)
  local copies, waits for them, and re-layouts  2.85 us (4%)
  other arithmetic  1.38 us (2%)
  between operations  0.79 us (1%)
    ppermute x21, waiting for transfers between devices, exchange(): return lax.ppermute(value, axis, pairs)  24.9 us
    ppermute x21, starting transfers between devices, exchange(): return lax.ppermute(value, axis, pairs)  24.8 us
    pallas_call x1, Pallas kernels, on_device(): pl.pallas_call(functools.partial(middle_kernel, mp_count), out_shape=[gat...  4.08 us
    pallas_call x1, Pallas kernels, on_device(): pl.pallas_call(functools.partial(last_kernel, mp_count), out_shape=[x_sha...  2.95 us
    pallas_call x1, Pallas kernels, on_device(): pl.pallas_call(functools.partial(first_kernel, mp_count, places), out_sha...  2.88 us
    unnamed x15, local copies, waits for them, and re-layouts  2.83 us
    pallas_call x2, Pallas kernels, fetch(): pl.pallas_call(functools.partial(fetch_kernel, steps), out_shape=[jax.Sha...  1.64 us
  transfers between devices with their start and end apart: 21, of which 10 were waited for; matrix products, arithmetic and copies ran while one was open for 3% of the time, Pallas kernels for 3%

profile of v5, /device:TPU:0, one launch (start us, length us, event | category | flops | bytes accessed | tf_op | source)
XLA Modules:
  0.0 66.4 jit_solution(14216699248703879901)
XLA Ops:
  0.6 0.7 %broadcast_multiply_fusion = s32[512,1]{0,1:T(1,128)S(1)} fusion(s32[512,1]{0,1:T(1,128)} %param.10), kind=kLoop, calls=%fused_computation.2 | loop fusion | flops 512 | bytes 4096 | tf_op jit(solution)/shard_map/mul | solution.py:333
  1.3 0.7 %add.3 = s32[512]{0:T(512)S(1)} add(s32[512]{0:T(512)S(1)} %bitcast.17, s32[512]{0:T(512)} %param.11) | non-fusion elementwise | flops 512 | bytes 6144 | tf_op jit(solution)/shard_map/add | solution.py:333
  2.0 3.0 %collective-permute-start = (s32[2,256]{1,0:T(2,128)S(1)}, s32[2,256]{1,0:T(2,128)S(1)}, u32[]{:S(2)}, u32[]{:S(2)}) collective-permute-start(s32[2,256]{1,0:T(2,128)S(1)} %reshape.18.refs_0_), channel_id=1, source_target_pairs={{0,8},{8,0},{16,24},{24,16},{1,9},{9,1},{17,25},{25,17},{2,10},{10... | collective-permute-start | bytes 6152 | tf_op jit(solution)/shard_map/ppermute | solution.py:36
  5.0 1.9 %copy.15 = bf16[1,1024,4,256]{3,1,2,0:T(8,128)(2,1)S(1)} copy(bf16[1,1024,4,256]{3,2,1,0:T(4,128)(2,1)} %param.16) | data formatting | bytes 4194304 | tf_op args[6]
  6.9 0.0 collective-permute-done.refs_1_
  6.9 0.0 copy-start.1
  6.9 0.0 copy-start
  7.0 0.1 collective-permute-start.5
  7.0 0.9 %copy-done.1 = bf16[1,256,1024]{2,1,0:T(8,128)(2,1)S(1)} copy-done((bf16[1,256,1024]{2,1,0:T(8,128)(2,1)S(1)}, bf16[1,256,1024]{2,1,0:T(8,128)(2,1)}, u32[]{:S(2)}) %copy-start.1) | copy-done | bytes 524312
  8.0 1.6 %collective-permute-start.10 = (bf16[256,1024]{1,0:T(8,128)(2,1)S(1)}, bf16[256,1024]{1,0:T(8,128)(2,1)S(1)}, u32[]{:S(2)}, u32[]{:S(2)}) collective-permute-start(bf16[256,1024]{1,0:T(8,128)(2,1)S(1)} %bitcast.13), channel_id=1, source_target_pairs={{0,2},{2,0},{4,6},{6,4},{1,3},{3,1},{5,7},{7,5},{8,10},{10,8},{12,... | collective-permute-start | bytes 1572872 | tf_op jit(solution)/shard_map/ppermute | solution.py:36
  9.6 1.5 %collective-permute-start.11 = (bf16[256,1024]{1,0:T(8,128)(2,1)S(1)}, bf16[256,1024]{1,0:T(8,128)(2,1)S(1)}, u32[]{:S(2)}, u32[]{:S(2)}) collective-permute-start(bf16[256,1024]{1,0:T(8,128)(2,1)S(1)} %bitcast.14), channel_id=1, source_target_pairs={{0,4},{2,6},{4,0},{6,2},{1,5},{3,7},{5,1},{7,3},{8,12},{10,14},{12... | collective-permute-start | bytes 1572872 | tf_op jit(solution)/shard_map/ppermute | solution.py:36
  11.1 2.6 %collective-permute-start.1 = (s32[4,256]{1,0:T(4,128)S(1)}, s32[4,256]{1,0:T(4,128)S(1)}, u32[]{:S(2)}, u32[]{:S(2)}) collective-permute-start(s32[4,256]{1,0:T(4,128)S(1)} %pad_add_fusion), channel_id=1, source_target_pairs={{0,16},{8,24},{16,0},{24,8},{1,17},{9,25},{17,1},{25,9},{2,18},{10... | collective-permute-start | bytes 12296 | tf_op jit(solution)/shard_map/ppermute | solution.py:36
  13.7 1.9 %collective-permute-done.1 = s32[4,256]{1,0:T(4,128)S(1)} collective-permute-done((s32[4,256]{1,0:T(4,128)S(1)}, s32[4,256]{1,0:T(4,128)S(1)}, u32[]{:S(2)}, u32[]{:S(2)}) %collective-permute-start.1) | collective-permute-done | bytes 4128 | tf_op jit(solution)/shard_map/ppermute | solution.py:36
  15.6 0.6 fetch.2.refs_4_
  16.2 1.6 %collective-permute-start.3 = (bf16[256,256]{1,0:T(8,128)(2,1)S(1)}, bf16[256,256]{1,0:T(8,128)(2,1)S(1)}, u32[]{:S(2)}, u32[]{:S(2)}) collective-permute-start(bf16[256,256]{1,0:T(8,128)(2,1)S(1)} %fetch.2.refs_4_), channel_id=1, source_target_pairs={{0,8},{8,0},{16,24},{24,16},{1,9},{9,1},{17,25},{25,17},{2,10},{10... | collective-permute-start | bytes 393224 | tf_op jit(solution)/shard_map/ppermute | solution.py:36
  17.8 1.1 %fetch.3 = (bf16[256,256]{1,0:T(8,128)(2,1)S(1)}, bf16[256,256]{1,0:T(8,128)(2,1)S(1)}, bf16[256,256]{1,0:T(8,128)(2,1)S(1)}) custom-call(s32[2,256]{1,0:T(2,128)S(1)} %reshape.18.refs_0_, s32[2,256]{1,0:T(2,128)S(1)} %collective-permute-done.refs_1_, s32[2,256]{1,0:T(2,128)S(1)} %get-tuple-element.27.refs_2_, bf16[1024,1024]{1,0:T(8,128)(2,1)S(1)} %copy-done, ...), custom_call_target="tpu_custom_call" | custom-call | flops 402653184 | bytes 524288 | tf_op jit(solution)/shard_map/fetch/pallas_call | solution.py:84
  18.9 0.5 collective-permute-start.2
  19.4 3.8 %collective-permute-done.3.b_ref = bf16[256,256]{1,0:T(8,128)(2,1)S(1)} collective-permute-done((bf16[256,256]{1,0:T(8,128)(2,1)S(1)}, bf16[256,256]{1,0:T(8,128)(2,1)S(1)}, u32[]{:S(2)}, u32[]{:S(2)}) %collective-permute-start.3) | collective-permute-done | bytes 131104 | tf_op jit(solution)/shard_map/ppermute | solution.py:36
  23.3 2.0 %collective-permute-start.4 = (bf16[256,256]{1,0:T(8,128)(2,1)S(1)}, bf16[256,256]{1,0:T(8,128)(2,1)S(1)}, u32[]{:S(2)}, u32[]{:S(2)}) collective-permute-start(bf16[256,256]{1,0:T(8,128)(2,1)S(1)} %merge.3.refs_0_), channel_id=1, source_target_pairs={{0,16},{8,24},{16,0},{24,8},{1,17},{9,25},{17,1},{25,9},{2,18},{10... | collective-permute-start | bytes 393224 | tf_op jit(solution)/shard_map/ppermute | solution.py:36
  25.3 0.0 collective-permute-done.2.b_ref
  25.3 0.0 collective-permute-done.11.far_ref.refs_6_
  25.3 0.1 cut.1
  25.4 0.6 collective-permute-start.12
  26.0 0.5 collective-permute-start.13
  26.5 0.0 collective-permute-start.6
  26.5 1.2 %collective-permute-done.6.refs_1_.refs_10_.refs_6_ = bf16[1,1024]{1,0:T(2,128)(2,1)S(1)} collective-permute-done((bf16[1,1024]{1,0:T(2,128)(2,1)S(1)}, bf16[1,1024]{1,0:T(2,128)(2,1)S(1)}, u32[]{:S(2)}, u32[]{:S(2)}) %collective-permute-start.6) | collective-permute-done | bytes 2080 | tf_op jit(solution)/shard_map/ppermute | solution.py:36
  27.7 1.9 %collective-permute-done.4.b_ref = bf16[256,256]{1,0:T(8,128)(2,1)S(1)} collective-permute-done((bf16[256,256]{1,0:T(8,128)(2,1)S(1)}, bf16[256,256]{1,0:T(8,128)(2,1)S(1)}, u32[]{:S(2)}, u32[]{:S(2)}) %collective-permute-start.4) | collective-permute-done | bytes 131104 | tf_op jit(solution)/shard_map/ppermute | solution.py:36
  29.6 0.6 collective-permute-start.7
  30.2 0.5 collective-permute-start.8
  30.8 2.4 %collective-permute-start.9 = (bf16[256,256]{1,0:T(8,128)(2,1)S(1)}, bf16[256,256]{1,0:T(8,128)(2,1)S(1)}, u32[]{:S(2)}, u32[]{:S(2)}) collective-permute-start(bf16[256,256]{1,0:T(8,128)(2,1)S(1)} %merge.5.refs_0_), channel_id=1, source_target_pairs={{0,6},{2,4},{4,2},{6,0},{1,7},{3,5},{5,3},{7,1},{8,14},{10,12},{12... | collective-permute-start | bytes 393224 | tf_op jit(solution)/shard_map/ppermute | solution.py:36
  33.2 2.8 %collective-permute-done.7.refs_1_ = bf16[256,256]{1,0:T(8,128)(2,1)S(1)} collective-permute-done((bf16[256,256]{1,0:T(8,128)(2,1)S(1)}, bf16[256,256]{1,0:T(8,128)(2,1)S(1)}, u32[]{:S(2)}, u32[]{:S(2)}) %collective-permute-start.7) | collective-permute-done | bytes 131104 | tf_op jit(solution)/shard_map/ppermute | solution.py:36
  36.0 2.0 %collective-permute-done.8.refs_2_ = bf16[256,256]{1,0:T(8,128)(2,1)S(1)} collective-permute-done((bf16[256,256]{1,0:T(8,128)(2,1)S(1)}, bf16[256,256]{1,0:T(8,128)(2,1)S(1)}, u32[]{:S(2)}, u32[]{:S(2)}) %collective-permute-start.8) | collective-permute-done | bytes 131104 | tf_op jit(solution)/shard_map/ppermute | solution.py:36
  38.0 2.9 %section0_front.1 = (bf16[256,256]{1,0:T(8,128)(2,1)S(1)}, bf16[256,1024]{1,0:T(8,128)(2,1)S(1)}, bf16[4,256,1024]{2,1,0:T(8,128)(2,1)S(1)}) custom-call(bf16[256,256]{1,0:T(8,128)(2,1)S(1)} %merge.5.refs_0_, bf16[256,256]{1,0:T(8,128)(2,1)S(1)} %collective-permute-done.7.refs_1_, bf16[256,256]{1,0:T(8,128)(2,1)S(1)} %collective-permute-done.8.refs_2_, ...), custom_call_target="tpu_custom_call" | custom-call | flops 603979776 | bytes 2097152 | tf_op jit(solution)/shard_map/section0_front/pallas_call | solution.py:365
  40.9 0.1 collective-permute-start.17
  41.0 1.5 %collective-permute-start.14 = (bf16[256,256]{1,0:T(8,128)(2,1)S(1)}, bf16[256,256]{1,0:T(8,128)(2,1)S(1)}, u32[]{:S(2)}, u32[]{:S(2)}) collective-permute-start(bf16[256,256]{1,0:T(8,128)(2,1)S(1)} %get-tuple-element.19.refs_0_), channel_id=1, source_target_pairs={{0,2},{2,0},{4,6},{6,4},{1,3},{3,1},{5,7},{7,5},{8,10},{10,8},{12,... | collective-permute-start | bytes 393224 | tf_op jit(solution)/shard_map/ppermute | solution.py:36
  42.5 0.5 collective-permute-start.15
  43.0 1.5 %collective-permute-start.16 = (bf16[256,256]{1,0:T(8,128)(2,1)S(1)}, bf16[256,256]{1,0:T(8,128)(2,1)S(1)}, u32[]{:S(2)}, u32[]{:S(2)}) collective-permute-start(bf16[256,256]{1,0:T(8,128)(2,1)S(1)} %get-tuple-element.19.refs_0_), channel_id=1, source_target_pairs={{0,6},{2,4},{4,2},{6,0},{1,7},{3,5},{5,3},{7,1},{8,14},{10,12},{12... | collective-permute-start | bytes 393224 | tf_op jit(solution)/shard_map/ppermute | solution.py:36
  44.5 2.7 %collective-permute-done.14.refs_1_ = bf16[256,256]{1,0:T(8,128)(2,1)S(1)} collective-permute-done((bf16[256,256]{1,0:T(8,128)(2,1)S(1)}, bf16[256,256]{1,0:T(8,128)(2,1)S(1)}, u32[]{:S(2)}, u32[]{:S(2)}) %collective-permute-start.14) | collective-permute-done | bytes 131104 | tf_op jit(solution)/shard_map/ppermute | solution.py:36
  47.3 3.6 %collective-permute-done.15.refs_2_ = bf16[256,256]{1,0:T(8,128)(2,1)S(1)} collective-permute-done((bf16[256,256]{1,0:T(8,128)(2,1)S(1)}, bf16[256,256]{1,0:T(8,128)(2,1)S(1)}, u32[]{:S(2)}, u32[]{:S(2)}) %collective-permute-start.15) | collective-permute-done | bytes 131104 | tf_op jit(solution)/shard_map/ppermute | solution.py:36
  50.9 0.0 copy-start.2
  50.9 0.0 copy-start.3
  50.9 4.1 %section0_back_section1_front.1 = (bf16[256,256]{1,0:T(8,128)(2,1)S(1)}, bf16[256,1024]{1,0:T(8,128)(2,1)S(1)}) custom-call(bf16[256,256]{1,0:T(8,128)(2,1)S(1)} %get-tuple-element.19.refs_0_, bf16[256,256]{1,0:T(8,128)(2,1)S(1)} %collective-permute-done.14.refs_1_, bf16[256,256]{1,0:T(8,128)(2,1)S(1)} %collective-permute-done.15.refs_2_, ...), custom_call_target="tpu_custom_call" | custom-call | flops 1140850688 | bytes 4194304 | tf_op jit(solution)/shard_map/section0_back_section1_front/pallas_call | solution.py:383
  55.0 0.6 collective-permute-start.18
  55.6 1.2 %collective-permute-start.19 = (bf16[256,256]{1,0:T(8,128)(2,1)S(1)}, bf16[256,256]{1,0:T(8,128)(2,1)S(1)}, u32[]{:S(2)}, u32[]{:S(2)}) collective-permute-start(bf16[256,256]{1,0:T(8,128)(2,1)S(1)} %get-tuple-element.22.refs_0_), channel_id=1, source_target_pairs={{0,4},{2,6},{4,0},{6,2},{1,5},{3,7},{5,1},{7,3},{8,12},{10,14},{12... | collective-permute-start | bytes 393224 | tf_op jit(solution)/shard_map/ppermute | solution.py:36
  56.8 1.8 %collective-permute-start.20 = (bf16[256,256]{1,0:T(8,128)(2,1)S(1)}, bf16[256,256]{1,0:T(8,128)(2,1)S(1)}, u32[]{:S(2)}, u32[]{:S(2)}) collective-permute-start(bf16[256,256]{1,0:T(8,128)(2,1)S(1)} %get-tuple-element.22.refs_0_), channel_id=1, source_target_pairs={{0,6},{2,4},{4,2},{6,0},{1,7},{3,5},{5,3},{7,1},{8,14},{10,12},{12... | collective-permute-start | bytes 393224 | tf_op jit(solution)/shard_map/ppermute | solution.py:36
  58.6 2.7 %collective-permute-done.18.refs_1_ = bf16[256,256]{1,0:T(8,128)(2,1)S(1)} collective-permute-done((bf16[256,256]{1,0:T(8,128)(2,1)S(1)}, bf16[256,256]{1,0:T(8,128)(2,1)S(1)}, u32[]{:S(2)}, u32[]{:S(2)}) %collective-permute-start.18) | collective-permute-done | bytes 131104 | tf_op jit(solution)/shard_map/ppermute | solution.py:36
  61.3 2.1 %collective-permute-done.19.refs_2_ = bf16[256,256]{1,0:T(8,128)(2,1)S(1)} collective-permute-done((bf16[256,256]{1,0:T(8,128)(2,1)S(1)}, bf16[256,256]{1,0:T(8,128)(2,1)S(1)}, u32[]{:S(2)}, u32[]{:S(2)}) %collective-permute-start.19) | collective-permute-done | bytes 131104 | tf_op jit(solution)/shard_map/ppermute | solution.py:36
  63.4 2.9 %section1_back_context.1 = (bf16[256,1024]{1,0:T(8,128)(2,1)}, bf16[256,256]{1,0:T(8,128)(2,1)}) custom-call(bf16[256,256]{1,0:T(8,128)(2,1)S(1)} %get-tuple-element.22.refs_0_, bf16[256,256]{1,0:T(8,128)(2,1)S(1)} %collective-permute-done.18.refs_1_, bf16[256,256]{1,0:T(8,128)(2,1)S(1)} %collective-permute-done.19.refs_2_, ...), custom_call_target="tpu_custom_call" | custom-call | flops 805306368 | bytes 2097152 | tf_op jit(solution)/shard_map/section1_back_context/pallas_call | solution.py:398
  (25 shorter events, 0.1 us)
Async XLA Ops:
  2.0 4.9 %collective-permute-start = (s32[2,256]{1,0:T(2,128)S(1)}, s32[2,256]{1,0:T(2,128)S(1)}, u32[]{:S(2)}, u32[]{:S(2)}) collective-permute-start(s32[2,256]{1,0:T(2,128)S(1)} %reshape.18.refs_0_), channel_id=1, source_target_pairs={{0,8},{8,0},{16,24},{24,16},{1,9},{9,1},{17,25},{25,17},{2,10},{10... | collective-permute-start | bytes 6152 | tf_op jit(solution)/shard_map/ppermute | solution.py:36
  6.9 1.0 %copy-start.1 = (bf16[1,256,1024]{2,1,0:T(8,128)(2,1)S(1)}, bf16[1,256,1024]{2,1,0:T(8,128)(2,1)}, u32[]{:S(2)}) copy-start(bf16[1,256,1024]{2,1,0:T(8,128)(2,1)} %param.17) | copy-start | bytes 1572868
  6.9 8.7 %copy-start = (bf16[1024,1024]{1,0:T(8,128)(2,1)S(1)}, bf16[1024,1024]{1,0:T(8,128)(2,1)}, u32[]{:S(2)}) copy-start(bf16[1024,1024]{1,0:T(8,128)(2,1)} %refs_3_.1) | copy-start | bytes 6291460
  7.0 22.7 %collective-permute-start.5 = (bf16[4,1024,256]{2,1,0:T(8,128)(2,1)S(1)}, bf16[4,1024,256]{2,1,0:T(8,128)(2,1)S(1)}, u32[]{:S(2)}, u32[]{:S(2)}) collective-permute-start(bf16[4,1024,256]{2,1,0:T(8,128)(2,1)S(1)} %hold.1.refs_12_.refs_8_), channel_id=1, source_target_pairs={{0,1},{1,0},{2,3},{3,2},{4,5},{5,4},{6,7},{7,6},{8,9},{9,8},{10,11... | collective-permute-start | bytes 6291464 | tf_op jit(solution)/shard_map/ppermute | solution.py:36
  8.0 17.3 %collective-permute-start.10 = (bf16[256,1024]{1,0:T(8,128)(2,1)S(1)}, bf16[256,1024]{1,0:T(8,128)(2,1)S(1)}, u32[]{:S(2)}, u32[]{:S(2)}) collective-permute-start(bf16[256,1024]{1,0:T(8,128)(2,1)S(1)} %bitcast.13), channel_id=1, source_target_pairs={{0,2},{2,0},{4,6},{6,4},{1,3},{3,1},{5,7},{7,5},{8,10},{10,8},{12,... | collective-permute-start | bytes 1572872 | tf_op jit(solution)/shard_map/ppermute | solution.py:36
  9.6 15.7 %collective-permute-start.11 = (bf16[256,1024]{1,0:T(8,128)(2,1)S(1)}, bf16[256,1024]{1,0:T(8,128)(2,1)S(1)}, u32[]{:S(2)}, u32[]{:S(2)}) collective-permute-start(bf16[256,1024]{1,0:T(8,128)(2,1)S(1)} %bitcast.14), channel_id=1, source_target_pairs={{0,4},{2,6},{4,0},{6,2},{1,5},{3,7},{5,1},{7,3},{8,12},{10,14},{12... | collective-permute-start | bytes 1572872 | tf_op jit(solution)/shard_map/ppermute | solution.py:36
  11.1 4.5 %collective-permute-start.1 = (s32[4,256]{1,0:T(4,128)S(1)}, s32[4,256]{1,0:T(4,128)S(1)}, u32[]{:S(2)}, u32[]{:S(2)}) collective-permute-start(s32[4,256]{1,0:T(4,128)S(1)} %pad_add_fusion), channel_id=1, source_target_pairs={{0,16},{8,24},{16,0},{24,8},{1,17},{9,25},{17,1},{25,9},{2,18},{10... | collective-permute-start | bytes 12296 | tf_op jit(solution)/shard_map/ppermute | solution.py:36
  16.2 7.1 %collective-permute-start.3 = (bf16[256,256]{1,0:T(8,128)(2,1)S(1)}, bf16[256,256]{1,0:T(8,128)(2,1)S(1)}, u32[]{:S(2)}, u32[]{:S(2)}) collective-permute-start(bf16[256,256]{1,0:T(8,128)(2,1)S(1)} %fetch.2.refs_4_), channel_id=1, source_target_pairs={{0,8},{8,0},{16,24},{24,16},{1,9},{9,1},{17,25},{25,17},{2,10},{10... | collective-permute-start | bytes 393224 | tf_op jit(solution)/shard_map/ppermute | solution.py:36
  17.8 8.7 %copy-start.4 = (bf16[1,1024]{1,0:T(2,128)(2,1)S(1)}, bf16[1,1024]{1,0:T(2,128)(2,1)}, u32[]{:S(2)}) copy-start(bf16[1,1024]{1,0:T(2,128)(2,1)} %refs_5_.1) | copy-start | bytes 6148
  18.9 6.3 %collective-permute-start.2 = (bf16[256,256]{1,0:T(8,128)(2,1)S(1)}, bf16[256,256]{1,0:T(8,128)(2,1)S(1)}, u32[]{:S(2)}, u32[]{:S(2)}) collective-permute-start(bf16[256,256]{1,0:T(8,128)(2,1)S(1)} %get-tuple-element.15), channel_id=1, source_target_pairs={{0,8},{8,0},{16,24},{24,16},{1,9},{9,1},{17,25},{25,17},{2,10},{10... | collective-permute-start | bytes 393224 | tf_op jit(solution)/shard_map/ppermute | solution.py:36
  23.3 6.3 %collective-permute-start.4 = (bf16[256,256]{1,0:T(8,128)(2,1)S(1)}, bf16[256,256]{1,0:T(8,128)(2,1)S(1)}, u32[]{:S(2)}, u32[]{:S(2)}) collective-permute-start(bf16[256,256]{1,0:T(8,128)(2,1)S(1)} %merge.3.refs_0_), channel_id=1, source_target_pairs={{0,16},{8,24},{16,0},{24,8},{1,17},{9,25},{17,1},{25,9},{2,18},{10... | collective-permute-start | bytes 393224 | tf_op jit(solution)/shard_map/ppermute | solution.py:36
  25.3 12.7 %copy-start.5 = (s32[1,2,256]{2,1,0:T(2,128)S(1)}, s32[1,2,256]{2,1,0:T(2,128)}, u32[]{:S(2)}) copy-start(s32[1,2,256]{2,1,0:T(2,128)} %refs_7_.1) | copy-start | bytes 6148
  25.4 7.8 %collective-permute-start.12 = (bf16[128,1024]{1,0:T(8,128)(2,1)S(1)}, bf16[128,1024]{1,0:T(8,128)(2,1)S(1)}, u32[]{:S(2)}, u32[]{:S(2)}) collective-permute-start(bf16[128,1024]{1,0:T(8,128)(2,1)S(1)} %get-tuple-element.17), channel_id=1, source_target_pairs={{0,2},{2,0},{4,6},{6,4},{1,3},{3,1},{5,7},{7,5},{8,10},{10,8},{12,... | collective-permute-start | bytes 786440 | tf_op jit(solution)/shard_map/ppermute | solution.py:36
  26.0 7.2 %collective-permute-start.13 = (bf16[128,1024]{1,0:T(8,128)(2,1)S(1)}, bf16[128,1024]{1,0:T(8,128)(2,1)S(1)}, u32[]{:S(2)}, u32[]{:S(2)}) collective-permute-start(bf16[128,1024]{1,0:T(8,128)(2,1)S(1)} %get-tuple-element.18), channel_id=1, source_target_pairs={{0,4},{2,6},{4,0},{6,2},{1,5},{3,7},{5,1},{7,3},{8,12},{10,14},{12... | collective-permute-start | bytes 786440 | tf_op jit(solution)/shard_map/ppermute | solution.py:36
  26.5 1.2 %collective-permute-start.6 = (bf16[1,1024]{1,0:T(2,128)(2,1)S(1)}, bf16[1,1024]{1,0:T(2,128)(2,1)S(1)}, u32[]{:S(2)}, u32[]{:S(2)}) collective-permute-start(bf16[1,1024]{1,0:T(2,128)(2,1)S(1)} %copy-done.4), channel_id=1, source_target_pairs={{0,1},{1,0},{2,3},{3,2},{4,5},{5,4},{6,7},{7,6},{8,9},{9,8},{10,11... | collective-permute-start | bytes 6152 | tf_op jit(solution)/shard_map/ppermute | solution.py:36
  29.6 6.4 %collective-permute-start.7 = (bf16[256,256]{1,0:T(8,128)(2,1)S(1)}, bf16[256,256]{1,0:T(8,128)(2,1)S(1)}, u32[]{:S(2)}, u32[]{:S(2)}) collective-permute-start(bf16[256,256]{1,0:T(8,128)(2,1)S(1)} %merge.5.refs_0_), channel_id=1, source_target_pairs={{0,2},{2,0},{4,6},{6,4},{1,3},{3,1},{5,7},{7,5},{8,10},{10,8},{12,... | collective-permute-start | bytes 393224 | tf_op jit(solution)/shard_map/ppermute | solution.py:36
  30.2 7.8 %collective-permute-start.8 = (bf16[256,256]{1,0:T(8,128)(2,1)S(1)}, bf16[256,256]{1,0:T(8,128)(2,1)S(1)}, u32[]{:S(2)}, u32[]{:S(2)}) collective-permute-start(bf16[256,256]{1,0:T(8,128)(2,1)S(1)} %merge.5.refs_0_), channel_id=1, source_target_pairs={{0,4},{2,6},{4,0},{6,2},{1,5},{3,7},{5,1},{7,3},{8,12},{10,14},{12... | collective-permute-start | bytes 393224 | tf_op jit(solution)/shard_map/ppermute | solution.py:36
  30.8 7.2 %collective-permute-start.9 = (bf16[256,256]{1,0:T(8,128)(2,1)S(1)}, bf16[256,256]{1,0:T(8,128)(2,1)S(1)}, u32[]{:S(2)}, u32[]{:S(2)}) collective-permute-start(bf16[256,256]{1,0:T(8,128)(2,1)S(1)} %merge.5.refs_0_), channel_id=1, source_target_pairs={{0,6},{2,4},{4,2},{6,0},{1,7},{3,5},{5,3},{7,1},{8,14},{10,12},{12... | collective-permute-start | bytes 393224 | tf_op jit(solution)/shard_map/ppermute | solution.py:36
  40.9 10.0 %collective-permute-start.17 = (bf16[4,256,1024]{2,1,0:T(8,128)(2,1)S(1)}, bf16[4,256,1024]{2,1,0:T(8,128)(2,1)S(1)}, u32[]{:S(2)}, u32[]{:S(2)}) collective-permute-start(bf16[4,256,1024]{2,1,0:T(8,128)(2,1)S(1)} %get-tuple-element.21.refs_10_.refs_8_), channel_id=1, source_target_pairs={{0,1},{1,0},{2,3},{3,2},{4,5},{5,4},{6,7},{7,6},{8,9},{9,8},{10,11... | collective-permute-start | bytes 6291464 | tf_op jit(solution)/shard_map/ppermute | solution.py:36
  41.0 6.3 %collective-permute-start.14 = (bf16[256,256]{1,0:T(8,128)(2,1)S(1)}, bf16[256,256]{1,0:T(8,128)(2,1)S(1)}, u32[]{:S(2)}, u32[]{:S(2)}) collective-permute-start(bf16[256,256]{1,0:T(8,128)(2,1)S(1)} %get-tuple-element.19.refs_0_), channel_id=1, source_target_pairs={{0,2},{2,0},{4,6},{6,4},{1,3},{3,1},{5,7},{7,5},{8,10},{10,8},{12,... | collective-permute-start | bytes 393224 | tf_op jit(solution)/shard_map/ppermute | solution.py:36
  42.5 8.4 %collective-permute-start.15 = (bf16[256,256]{1,0:T(8,128)(2,1)S(1)}, bf16[256,256]{1,0:T(8,128)(2,1)S(1)}, u32[]{:S(2)}, u32[]{:S(2)}) collective-permute-start(bf16[256,256]{1,0:T(8,128)(2,1)S(1)} %get-tuple-element.19.refs_0_), channel_id=1, source_target_pairs={{0,4},{2,6},{4,0},{6,2},{1,5},{3,7},{5,1},{7,3},{8,12},{10,14},{12... | collective-permute-start | bytes 393224 | tf_op jit(solution)/shard_map/ppermute | solution.py:36
  43.0 7.9 %collective-permute-start.16 = (bf16[256,256]{1,0:T(8,128)(2,1)S(1)}, bf16[256,256]{1,0:T(8,128)(2,1)S(1)}, u32[]{:S(2)}, u32[]{:S(2)}) collective-permute-start(bf16[256,256]{1,0:T(8,128)(2,1)S(1)} %get-tuple-element.19.refs_0_), channel_id=1, source_target_pairs={{0,6},{2,4},{4,2},{6,0},{1,7},{3,5},{5,3},{7,1},{8,14},{10,12},{12... | collective-permute-start | bytes 393224 | tf_op jit(solution)/shard_map/ppermute | solution.py:36
  50.9 7.7 %copy-start.6 = (bf16[256]{0:T(256)(128)(2,1)S(1)}, bf16[256]{0:T(256)(128)(2,1)}, u32[]{:S(2)}) copy-start(bf16[256]{0:T(256)(128)(2,1)} %param.19) | copy-start | bytes 1540
  50.9 12.5 %copy-start.2 = (bf16[1024,256]{1,0:T(8,128)(2,1)S(1)}, bf16[1024,256]{1,0:T(8,128)(2,1)}, u32[]{:S(2)}) copy-start(bf16[1024,256]{1,0:T(8,128)(2,1)} %refs_6_.1) | copy-start | bytes 1572868
  50.9 12.5 %copy-start.3 = (s32[1,2,256,8]{2,3,1,0:T(8,128)S(1)}, s32[1,2,256,8]{2,3,1,0:T(8,128)}, u32[]{:S(2)}) copy-start(s32[1,2,256,8]{2,3,1,0:T(8,128)} %param.13) | copy-start | bytes 49156
  55.0 6.3 %collective-permute-start.18 = (bf16[256,256]{1,0:T(8,128)(2,1)S(1)}, bf16[256,256]{1,0:T(8,128)(2,1)S(1)}, u32[]{:S(2)}, u32[]{:S(2)}) collective-permute-start(bf16[256,256]{1,0:T(8,128)(2,1)S(1)} %get-tuple-element.22.refs_0_), channel_id=1, source_target_pairs={{0,2},{2,0},{4,6},{6,4},{1,3},{3,1},{5,7},{7,5},{8,10},{10,8},{12,... | collective-permute-start | bytes 393224 | tf_op jit(solution)/shard_map/ppermute | solution.py:36
  55.6 7.8 %collective-permute-start.19 = (bf16[256,256]{1,0:T(8,128)(2,1)S(1)}, bf16[256,256]{1,0:T(8,128)(2,1)S(1)}, u32[]{:S(2)}, u32[]{:S(2)}) collective-permute-start(bf16[256,256]{1,0:T(8,128)(2,1)S(1)} %get-tuple-element.22.refs_0_), channel_id=1, source_target_pairs={{0,4},{2,6},{4,0},{6,2},{1,5},{3,7},{5,1},{7,3},{8,12},{10,14},{12... | collective-permute-start | bytes 393224 | tf_op jit(solution)/shard_map/ppermute | solution.py:36
  56.8 6.6 %collective-permute-start.20 = (bf16[256,256]{1,0:T(8,128)(2,1)S(1)}, bf16[256,256]{1,0:T(8,128)(2,1)S(1)}, u32[]{:S(2)}, u32[]{:S(2)}) collective-permute-start(bf16[256,256]{1,0:T(8,128)(2,1)S(1)} %get-tuple-element.22.refs_0_), channel_id=1, source_target_pairs={{0,6},{2,4},{4,2},{6,0},{1,7},{3,5},{5,3},{7,1},{8,14},{10,12},{12... | collective-permute-start | bytes 393224 | tf_op jit(solution)/shard_map/ppermute | solution.py:36

commit v6 on v5

--- a/solution.py
+++ b/solution.py
@@ -26,7 +26,8 @@
     return n & (n - 1) == 0
 
 
-def source_of(me, k, n):
+def source_of(me, slot, n):
+    k = (n - slot) % n
     return me ^ k if is_pow2(n) else lax.rem(me + n - k, n)
 
 
@@ -37,7 +38,7 @@
 
 
 def spread(value, axis):
-    return [value] + [exchange(value, axis, k) for k in range(1, lax.axis_size(axis))]
+    return [value] + [exchange(value, axis, k) for k in reversed(range(1, lax.axis_size(axis)))]
 
 
 def swap(blocks, axis):
@@ -52,7 +53,7 @@
     return x * jax.nn.sigmoid(x)
 
 
-def fetch_kernel(steps, *refs):
+def fetch_kernel(steps, batches, *refs):
     asked_refs, table_ref = refs[:steps], refs[steps]
     out_refs, (tab, sem) = refs[-steps - 2 : -2], refs[-2:]
     width = tab.shape[1]
@@ -63,7 +64,13 @@
     phase = lax.axis_index("phase")
     hots = []
     for asked_ref in asked_refs:
-        cols = columns_of(asked_ref[pl.ds(phase, 1), :] - first, LANES)
+        per = asked_ref.shape[0] // batches
+        cols = jnp.concatenate(
+            [
+                columns_of(asked_ref[pl.ds(phase * per + n, 1), :] - first, LANES)
+                for n in range(per)
+            ]
+        )
         lane = lax.broadcasted_iota(jnp.int32, cols.shape, 1)
         hots.append(
             jnp.concatenate(
@@ -79,10 +86,10 @@
         out_ref[...] = jnp.dot(hot, tab[...], preferred_element_type=F32).astype(BF16)
 
 
-def fetch(asked, table, width, after):
-    steps, rows = len(asked), asked[0].shape[1]
+def fetch(asked, batches, table, width, after):
+    steps, rows = len(asked), asked[0].size // batches
     return pl.pallas_call(
-        functools.partial(fetch_kernel, steps),
+        functools.partial(fetch_kernel, steps, batches),
         out_shape=[jax.ShapeDtypeStruct((rows, width), BF16)] * steps,
         in_specs=[VMEM] * steps + [HBM] * (1 + len(after)),
         out_specs=[VMEM] * steps,
@@ -198,20 +205,17 @@
         start_picked(section, w_own.at[g], w_other.at[g], w_buf.at[g], w_sem.at[g])
 
 
-def front(x, section, gain_own, gain_other, seg_ref, w_own, w_buf, w_sem, gated_ref):
-    phase = lax.axis_index("phase")
+def front(x, seg_ref, w_own, w_buf, w_sem, gated_ref):
     rows, local_cols = x.shape[0], w_buf.shape[2]
-    gain = jnp.where(phase == section, gain_own[...].astype(F32), gain_other[...].astype(F32))
-    inv = lax.rsqrt(jnp.mean(x * x, axis=-1, keepdims=True) + EPS)
-    normed = (x * inv * gain).astype(BF16)
+    xf = x.astype(F32)
+    inv = lax.rsqrt(jnp.mean(xf * xf, axis=-1, keepdims=True) + EPS)
     proj = []
     for g in range(4):
         wait_picked(w_own.at[g], w_buf.at[g], w_sem.at[g])
-        proj.append(
-            silu(jnp.dot(normed, w_buf[g], preferred_element_type=F32)).astype(BF16)
-        )
+        raw = jnp.dot(x, w_buf[g], preferred_element_type=F32)
+        proj.append(silu(raw * inv).astype(BF16))
     gates, values, queries, keys = proj
-    seg = seg_ref[0, pl.ds(phase, 1), :]
+    seg = seg_ref[0, pl.ds(lax.axis_index("phase"), 1), :]
     seg_cols = columns_of(seg, rows)
     at_row = lax.broadcasted_iota(jnp.int32, (rows, rows), 0)
     at_col = lax.broadcasted_iota(jnp.int32, (rows, rows), 1)
@@ -228,46 +232,44 @@
 
 
 def back(x, gated_refs, o_own, o_buf, o_sem):
-    total = x.astype(F32)
-    for k, gated_ref in enumerate(gated_refs):
+    steps, cols, width = o_buf.shape
+    gated = jnp.concatenate([gated_ref[...] for gated_ref in gated_refs], axis=1)
+    for k in range(steps):
         wait_picked(o_own.at[k], o_buf.at[k], o_sem.at[k])
-        part = jnp.dot(gated_ref[...], o_buf[k], preferred_element_type=F32)
-        total = total + part.astype(BF16).astype(F32)
+    weights = o_buf[...].reshape(steps * cols, width)
+    total = x.astype(F32) + jnp.dot(gated, weights, preferred_element_type=F32)
     return total.astype(BF16)
 
 
 def first_kernel(steps, places, *refs):
-    x_refs, o_own = refs[:steps], refs[steps : steps + len(places)]
-    gain_own, gain_other, seg_ref, w_own, w_other = refs[steps + len(places) : -6]
-    gated_ref, x_ref, stack_ref, w_buf, w_sem, o_sem = refs[-6:]
+    x_refs, pieces, refs = refs[:steps], refs[steps : steps + len(places)], refs[steps + len(places) :]
+    seg_ref, w_own, w_other, gated_ref, x_ref, stack_ref, w_buf, w_sem, o_sem = refs
     start_weights(0, w_own, w_other, w_buf, w_sem)
     copies = []
-    for n, (k, row) in enumerate(places):
-        at = stack_ref.at[k, pl.ds(row, o_own[n].shape[0]), :]
-        copies.append(pltpu.make_async_copy(o_own[n], at, o_sem.at[n]))
+    for n, (slot, row) in enumerate(places):
+        at = stack_ref.at[slot, pl.ds(row, pieces[n].shape[0]), :]
+        copies.append(pltpu.make_async_copy(pieces[n], at, o_sem.at[n]))
     for copy in copies:
         copy.start()
     width = x_refs[0].shape[1]
     for k, piece in enumerate(x_refs):
         at = pl.multiple_of(source_of(lax.axis_index("mp"), k, steps) * width, width)
         x_ref[:, pl.ds(at, width)] = piece[...]
-    x = x_ref[...].astype(F32)
-    front(x, 0, gain_own, gain_other, seg_ref, w_own, w_buf, w_sem, gated_ref)
+    front(x_ref[...], seg_ref, w_own, w_buf, w_sem, gated_ref)
     for copy in copies:
         copy.wait()
 
 
 def middle_kernel(steps, *refs):
     gated_refs = refs[:steps]
-    x_ref, gain_own, gain_other, seg_ref, w_own, w_other, o_own, o_other = refs[steps : steps + 8]
-    gated_ref, x1_ref, o_buf, o_sem, w_buf, w_sem = refs[steps + 8 :]
+    x_ref, seg_ref, w_own, w_other, o_own, o_other = refs[steps : steps + 6]
+    gated_ref, x1_ref, o_buf, o_sem, w_buf, w_sem = refs[steps + 6 :]
     for k in range(steps):
         start_picked(0, o_own.at[k], o_other.at[k], o_buf.at[k], o_sem.at[k])
     start_weights(1, w_own, w_other, w_buf, w_sem)
     x1 = back(x_ref[...], gated_refs, o_own, o_buf, o_sem)
     x1_ref[...] = x1
-    x1 = x1.astype(F32)
-    front(x1, 1, gain_own, gain_other, seg_ref, w_own, w_buf, w_sem, gated_ref)
+    front(x1, seg_ref, w_own, w_buf, w_sem, gated_ref)
 
 
 def last_kernel(steps, *refs):
@@ -317,30 +319,29 @@
     local_cols = w_out.shape[1]
     part = width // mp_count
 
-    w_own = jnp.transpose(w_in[0], (1, 0, 2))
-    places = [(k, 0) for k in range(mp_count)]
+    w_own = jnp.transpose(w_in[0], (1, 0, 2)).astype(F32) * gains[0].astype(F32)[None, :, None]
+    w_own = w_own.astype(BF16)
     if mp_count == 4:
         near, far = exchange(w_out[0], "mp", 1), exchange(w_out[0], "mp", 2)
-        o_pieces = [w_out[0], near, far]
-        places.append((3, local_cols // 2))
+        o_pieces, places = [w_out[0], near, far], [(0, 0), (3, 0), (2, 0)]
     else:
-        o_pieces = spread(w_out[0], "mp")
-    gain_other = exchange(gains, "phase", 1)
+        o_pieces, places = spread(w_out[0], "mp"), [(slot, 0) for slot in range(mp_count)]
     neigh = jnp.transpose(neighbors[0], (0, 2, 1))
     bias = ctx_bias.reshape(1, -1)
 
     if is_pow2(dp_count) and dp_count <= 8:
-        wanted = (item_owner[:, 0] * table_rows + item_row).reshape(batches, rows)
+        wanted = item_owner.reshape(-1, LANES) * table_rows + item_row.reshape(-1, LANES)
         asked = ask_around(wanted)
         w_own = hold(w_own, asked[1:2])
         w_other = exchange(w_own, "phase", 1)
-        late = fetch(asked[-1:], table, part, [])
-        found = fetch(asked[:-1], table, part, late) + late
+        late = fetch(asked[-1:], batches, table, part, [])
+        found = fetch(asked[:-1], batches, table, part, late) + late
 
         def then(first):
             if mp_count == 4:
                 o_pieces.extend(relay(near, far, "mp", [first]))
-            return [w_other, gain_other]
+                places.extend([(1, 0), (1, local_cols // 2)])
+            return [w_other]
 
         piece = gather_in(found, [], then)
     else:
@@ -351,6 +352,7 @@
         w_other = exchange(w_own, "phase", 1)
         if mp_count == 4:
             o_pieces.extend(relay(near, far, "mp", [piece]))
+            places.extend([(1, 0), (1, local_cols // 2)])
     x_pieces = spread(piece, "mp")
 
     sem4 = pltpu.SemaphoreType.DMA((4,))
@@ -369,7 +371,7 @@
             x_shape,
             jax.ShapeDtypeStruct((mp_count, local_cols, width), BF16),
         ],
-        in_specs=[VMEM] * mp_count + [HBM] * len(places) + [VMEM] * 3 + [HBM] * 2,
+        in_specs=[VMEM] * mp_count + [HBM] * len(places) + [VMEM] + [HBM] * 2,
         out_specs=[VMEM] * 2 + [HBM],
         scratch_shapes=[w_buf, sem4, pltpu.SemaphoreType.DMA((len(places),))],
         compiler_params=params(),
@@ -377,13 +379,13 @@
             flops=front_flops, bytes_accessed=8 * width * local_cols, transcendentals=0
         ),
         name="section0_front",
-    )(*x_pieces, *o_pieces, gains, gain_other, segments, w_own, w_other)
+    )(*x_pieces, *o_pieces, segments, w_own, w_other)
     o_other = exchange(o_own, "phase", 1)
 
     gated, x1 = pl.pallas_call(
         functools.partial(middle_kernel, mp_count),
         out_shape=[gated_shape, x_shape],
-        in_specs=[VMEM] * (mp_count + 4) + [HBM] * 4,
+        in_specs=[VMEM] * (mp_count + 2) + [HBM] * 4,
         out_specs=[VMEM] * 2,
         scratch_shapes=[o_buf, semk, w_buf, sem4],
         compiler_params=params(),
@@ -393,7 +395,7 @@
             transcendentals=0,
         ),
         name="section0_back_section1_front",
-    )(*spread(gated, "mp"), x0, gains, gain_other, segments, w_own, w_other, o_own, o_other)
+    )(*spread(gated, "mp"), x0, segments, w_own, w_other, o_own, o_other)
 
     states, ctx = pl.pallas_call(
         functools.partial(last_kernel, mp_count),

time: 66.6 us -> 64.9 us (0.974)
  waiting for transfers between devices: 24.9 us -> 21.8 us
  other arithmetic: 1.38 us -> 4.06 us
  local copies, waits for them, and re-layouts: 2.85 us -> 0.96 us
  starting transfers between devices: 24.8 us -> 26.6 us
  Pallas kernels: 11.7 us -> 10.5 us
    ppermute x21 -> x20, waiting for transfers between devices: 24.9 us -> 21.8 us  [exchange(): return lax.ppermute(value, axis, pairs)]
    convert_element_type x0 -> x2, other arithmetic: none -> 2.68 us  [the longest x1 1.99 us: on_device(): w_own = w_own.astype(BF16)]
    unnamed x15 -> x12, local copies, waits for them, and re-layouts: 2.83 us -> 0.95 us
    ppermute x21 -> x20, starting transfers between devices: 24.8 us -> 26.6 us  [exchange(): return lax.ppermute(value, axis, pairs)]
  transfers between devices with their start and end apart: 21 -> 20, of which waited for: 10 -> 10; matrix products, arithmetic and copies ran while one was open for 3% -> 4% of each run, Pallas kernels for 3% -> 3%
where the time goes in v6:
time: 64.9 us; the launch traced here: 64.7 us
  starting transfers between devices  26.6 us (41%)
  waiting for transfers between devices  21.8 us (34%)
  Pallas kernels  10.5 us (16%)
  other arithmetic  4.06 us (6%)
  local copies, waits for them, and re-layouts  0.96 us (1%)
  between operations  0.79 us (1%)
    ppermute x20, starting transfers between devices, exchange(): return lax.ppermute(value, axis, pairs)  26.6 us
    ppermute x20, waiting for transfers between devices, exchange(): return lax.ppermute(value, axis, pairs)  21.8 us
    pallas_call x1, Pallas kernels, on_device(): pl.pallas_call(functools.partial(middle_kernel, mp_count), out_shape=[gat...  3.51 us
    pallas_call x1, Pallas kernels, on_device(): pl.pallas_call(functools.partial(first_kernel, mp_count, places), out_sha...  2.86 us
    pallas_call x1, Pallas kernels, on_device(): pl.pallas_call(functools.partial(last_kernel, mp_count), out_shape=[x_sha...  2.37 us
    convert_element_type x1, other arithmetic, on_device(): w_own = w_own.astype(BF16)  1.99 us
    pallas_call x2, Pallas kernels, fetch(): pl.pallas_call(functools.partial(fetch_kernel, steps, batches), out_shape...  1.64 us
  transfers between devices with their start and end apart: 20, of which 10 were waited for; matrix products, arithmetic and copies ran while one was open for 4% of the time, Pallas kernels for 3%

profile of v6, /device:TPU:0, one launch (start us, length us, event | category | flops | bytes accessed | tf_op | source)
XLA Modules:
  0.0 64.7 jit_solution(18257340183043487586)
XLA Ops:
  0.6 0.7 %broadcast_multiply_fusion = s32[512,1]{0,1:T(1,128)S(1)} fusion(s32[512,1]{0,1:T(1,128)} %param.10), kind=kLoop, calls=%fused_computation.5 | loop fusion | flops 512 | bytes 4096 | tf_op jit(solution)/shard_map/mul | solution.py:333
  1.3 0.7 %bitcast_add_fusion.refs_0_ = s32[4,128]{1,0:T(4,128)S(1)} fusion(s32[4,128]{1,0:T(4,128)S(1)} %bitcast.20, s32[512]{0:T(512)} %param.11), kind=kLoop, calls=%fused_computation.4 | loop fusion | flops 512 | bytes 6144 | tf_op jit(solution)/shard_map/add | solution.py:333
  2.0 3.0 %collective-permute-start = (s32[4,128]{1,0:T(4,128)S(1)}, s32[4,128]{1,0:T(4,128)S(1)}, u32[]{:S(2)}, u32[]{:S(2)}) collective-permute-start(s32[4,128]{1,0:T(4,128)S(1)} %bitcast_add_fusion.refs_0_), channel_id=1, source_target_pairs={{0,8},{8,0},{16,24},{24,16},{1,9},{9,1},{17,25},{25,17},{2,10},{10... | collective-permute-start | bytes 6152 | tf_op jit(solution)/shard_map/ppermute | solution.py:37
  5.0 0.7 %convert_element_type.29 = f32[1,1024]{1,0:T(1,128)S(1)} convert(bf16[1,1024]{1,0:T(2,128)(2,1)} %param.15) | non-fusion elementwise | flops 1024 | bytes 6144 | tf_op jit(solution)/shard_map/convert_element_type | solution.py:322
  5.7 2.0 %fusion.1.refs_0_ = bf16[4,1024,256]{2,1,0:T(8,128)(2,1)S(1)} fusion(bf16[1,1024,4,256]{3,2,1,0:T(4,128)(2,1)} %param.16, f32[1024]{0:T(1024)S(1)} %bitcast.19), kind=kLoop, calls=%fused_computation.2 | loop fusion | flops 3145728 | bytes 4198400 | tf_op jit(solution)/shard_map/convert_element_type | solution.py:323
  7.7 0.0 copy-start.1
  7.7 0.0 copy-start
  7.7 0.0 collective-permute-done.refs_1_
  7.8 0.1 collective-permute-start.5
  7.8 0.9 %copy-done.1 = bf16[1,256,1024]{2,1,0:T(8,128)(2,1)S(1)} copy-done((bf16[1,256,1024]{2,1,0:T(8,128)(2,1)S(1)}, bf16[1,256,1024]{2,1,0:T(8,128)(2,1)}, u32[]{:S(2)}) %copy-start.1) | copy-done | bytes 524312
  8.8 1.5 %collective-permute-start.10 = (bf16[256,1024]{1,0:T(8,128)(2,1)S(1)}, bf16[256,1024]{1,0:T(8,128)(2,1)S(1)}, u32[]{:S(2)}, u32[]{:S(2)}) collective-permute-start(bf16[256,1024]{1,0:T(8,128)(2,1)S(1)} %bitcast.15), channel_id=1, source_target_pairs={{0,4},{2,6},{4,0},{6,2},{1,5},{3,7},{5,1},{7,3},{8,12},{10,14},{12... | collective-permute-start | bytes 1572872 | tf_op jit(solution)/shard_map/ppermute | solution.py:37
  10.3 1.5 %collective-permute-start.9 = (bf16[256,1024]{1,0:T(8,128)(2,1)S(1)}, bf16[256,1024]{1,0:T(8,128)(2,1)S(1)}, u32[]{:S(2)}, u32[]{:S(2)}) collective-permute-start(bf16[256,1024]{1,0:T(8,128)(2,1)S(1)} %bitcast.16), channel_id=1, source_target_pairs={{0,2},{2,0},{4,6},{6,4},{1,3},{3,1},{5,7},{7,5},{8,10},{10,8},{12,... | collective-permute-start | bytes 1572872 | tf_op jit(solution)/shard_map/ppermute | solution.py:37
  11.8 2.6 %collective-permute-start.1 = (s32[8,128]{1,0:T(8,128)S(1)}, s32[8,128]{1,0:T(8,128)S(1)}, u32[]{:S(2)}, u32[]{:S(2)}) collective-permute-start(s32[8,128]{1,0:T(8,128)S(1)} %pad_add_fusion), channel_id=1, source_target_pairs={{0,16},{8,24},{16,0},{24,8},{1,17},{9,25},{17,1},{25,9},{2,18},{10... | collective-permute-start | bytes 12296 | tf_op jit(solution)/shard_map/ppermute | solution.py:37
  14.4 1.9 %collective-permute-done.1 = s32[8,128]{1,0:T(8,128)S(1)} collective-permute-done((s32[8,128]{1,0:T(8,128)S(1)}, s32[8,128]{1,0:T(8,128)S(1)}, u32[]{:S(2)}, u32[]{:S(2)}) %collective-permute-start.1) | collective-permute-done | bytes 4128 | tf_op jit(solution)/shard_map/ppermute | solution.py:37
  16.3 0.6 fetch.2.refs_4_
  16.9 0.5 collective-permute-start.3
  17.4 1.1 %fetch.3 = (bf16[256,256]{1,0:T(8,128)(2,1)S(1)}, bf16[256,256]{1,0:T(8,128)(2,1)S(1)}, bf16[256,256]{1,0:T(8,128)(2,1)S(1)}) custom-call(s32[4,128]{1,0:T(4,128)S(1)} %bitcast_add_fusion.refs_0_, s32[4,128]{1,0:T(4,128)S(1)} %collective-permute-done.refs_1_, s32[4,128]{1,0:T(4,128)S(1)} %get-tuple-element.27.refs_2_, bf16[1024,1024]{1,0:T(8,128)(2,1)S(1)} %copy-done, ...), custom_call_target="tpu_custom_call" | custom-call | flops 402653184 | bytes 524288 | tf_op jit(solution)/shard_map/fetch/pallas_call | solution.py:91
  18.5 1.6 %collective-permute-start.2 = (bf16[256,256]{1,0:T(8,128)(2,1)S(1)}, bf16[256,256]{1,0:T(8,128)(2,1)S(1)}, u32[]{:S(2)}, u32[]{:S(2)}) collective-permute-start(bf16[256,256]{1,0:T(8,128)(2,1)S(1)} %get-tuple-element.15), channel_id=1, source_target_pairs={{0,8},{8,0},{16,24},{24,16},{1,9},{9,1},{17,25},{25,17},{2,10},{10... | collective-permute-start | bytes 393224 | tf_op jit(solution)/shard_map/ppermute | solution.py:37
  20.1 1.8 %collective-permute-done.3.b_ref = bf16[256,256]{1,0:T(8,128)(2,1)S(1)} collective-permute-done((bf16[256,256]{1,0:T(8,128)(2,1)S(1)}, bf16[256,256]{1,0:T(8,128)(2,1)S(1)}, u32[]{:S(2)}, u32[]{:S(2)}) %collective-permute-start.3) | collective-permute-done | bytes 131104 | tf_op jit(solution)/shard_map/ppermute | solution.py:37
  21.9 3.9 %collective-permute-start.4 = (bf16[256,256]{1,0:T(8,128)(2,1)S(1)}, bf16[256,256]{1,0:T(8,128)(2,1)S(1)}, u32[]{:S(2)}, u32[]{:S(2)}) collective-permute-start(bf16[256,256]{1,0:T(8,128)(2,1)S(1)} %merge.3.refs_0_), channel_id=1, source_target_pairs={{0,16},{8,24},{16,0},{24,8},{1,17},{9,25},{17,1},{25,9},{2,18},{10... | collective-permute-start | bytes 393224 | tf_op jit(solution)/shard_map/ppermute | solution.py:37
  25.8 0.0 collective-permute-done.2.b_ref
  25.8 0.1 cut.1
  25.9 0.6 collective-permute-start.11
  26.5 0.5 collective-permute-start.12
  27.0 2.9 %collective-permute-done.4.b_ref = bf16[256,256]{1,0:T(8,128)(2,1)S(1)} collective-permute-done((bf16[256,256]{1,0:T(8,128)(2,1)S(1)}, bf16[256,256]{1,0:T(8,128)(2,1)S(1)}, u32[]{:S(2)}, u32[]{:S(2)}) %collective-permute-start.4) | collective-permute-done | bytes 131104 | tf_op jit(solution)/shard_map/ppermute | solution.py:37
  29.9 0.5 collective-permute-start.6
  30.5 1.5 %collective-permute-start.7 = (bf16[256,256]{1,0:T(8,128)(2,1)S(1)}, bf16[256,256]{1,0:T(8,128)(2,1)S(1)}, u32[]{:S(2)}, u32[]{:S(2)}) collective-permute-start(bf16[256,256]{1,0:T(8,128)(2,1)S(1)} %merge.5.refs_0_), channel_id=1, source_target_pairs={{0,4},{2,6},{4,0},{6,2},{1,5},{3,7},{5,1},{7,3},{8,12},{10,14},{12... | collective-permute-start | bytes 393224 | tf_op jit(solution)/shard_map/ppermute | solution.py:37
  32.0 1.5 %collective-permute-start.8 = (bf16[256,256]{1,0:T(8,128)(2,1)S(1)}, bf16[256,256]{1,0:T(8,128)(2,1)S(1)}, u32[]{:S(2)}, u32[]{:S(2)}) collective-permute-start(bf16[256,256]{1,0:T(8,128)(2,1)S(1)} %merge.5.refs_0_), channel_id=1, source_target_pairs={{0,2},{2,0},{4,6},{6,4},{1,3},{3,1},{5,7},{7,5},{8,10},{10,8},{12,... | collective-permute-start | bytes 393224 | tf_op jit(solution)/shard_map/ppermute | solution.py:37
  33.5 0.7 %collective-permute-done.12.refs_8_ = bf16[128,1024]{1,0:T(8,128)(2,1)S(1)} collective-permute-done((bf16[128,1024]{1,0:T(8,128)(2,1)S(1)}, bf16[128,1024]{1,0:T(8,128)(2,1)S(1)}, u32[]{:S(2)}, u32[]{:S(2)}) %collective-permute-start.12) | collective-permute-done | bytes 262176 | tf_op jit(solution)/shard_map/ppermute | solution.py:37
  34.1 1.8 %collective-permute-done.6.refs_1_ = bf16[256,256]{1,0:T(8,128)(2,1)S(1)} collective-permute-done((bf16[256,256]{1,0:T(8,128)(2,1)S(1)}, bf16[256,256]{1,0:T(8,128)(2,1)S(1)}, u32[]{:S(2)}, u32[]{:S(2)}) %collective-permute-start.6) | collective-permute-done | bytes 131104 | tf_op jit(solution)/shard_map/ppermute | solution.py:37
  36.0 1.0 %collective-permute-done.7.refs_2_ = bf16[256,256]{1,0:T(8,128)(2,1)S(1)} collective-permute-done((bf16[256,256]{1,0:T(8,128)(2,1)S(1)}, bf16[256,256]{1,0:T(8,128)(2,1)S(1)}, u32[]{:S(2)}, u32[]{:S(2)}) %collective-permute-start.7) | collective-permute-done | bytes 131104 | tf_op jit(solution)/shard_map/ppermute | solution.py:37
  37.0 0.0 collective-permute-done.8.refs_3_
  37.0 2.9 %section0_front.1 = (bf16[256,256]{1,0:T(8,128)(2,1)S(1)}, bf16[256,1024]{1,0:T(8,128)(2,1)S(1)}, bf16[4,256,1024]{2,1,0:T(8,128)(2,1)S(1)}) custom-call(bf16[256,256]{1,0:T(8,128)(2,1)S(1)} %merge.5.refs_0_, bf16[256,256]{1,0:T(8,128)(2,1)S(1)} %collective-permute-done.6.refs_1_, bf16[256,256]{1,0:T(8,128)(2,1)S(1)} %collective-permute-done.7.refs_2_, ...), custom_call_target="tpu_custom_call" | custom-call | flops 603979776 | bytes 2097152 | tf_op jit(solution)/shard_map/section0_front/pallas_call | solution.py:367
  39.8 0.1 collective-permute-start.16
  39.9 1.5 %collective-permute-start.13 = (bf16[256,256]{1,0:T(8,128)(2,1)S(1)}, bf16[256,256]{1,0:T(8,128)(2,1)S(1)}, u32[]{:S(2)}, u32[]{:S(2)}) collective-permute-start(bf16[256,256]{1,0:T(8,128)(2,1)S(1)} %get-tuple-element.19.refs_0_), channel_id=1, source_target_pairs={{0,6},{2,4},{4,2},{6,0},{1,7},{3,5},{5,3},{7,1},{8,14},{10,12},{12... | collective-permute-start | bytes 393224 | tf_op jit(solution)/shard_map/ppermute | solution.py:37
  41.4 1.5 %collective-permute-start.14 = (bf16[256,256]{1,0:T(8,128)(2,1)S(1)}, bf16[256,256]{1,0:T(8,128)(2,1)S(1)}, u32[]{:S(2)}, u32[]{:S(2)}) collective-permute-start(bf16[256,256]{1,0:T(8,128)(2,1)S(1)} %get-tuple-element.19.refs_0_), channel_id=1, source_target_pairs={{0,4},{2,6},{4,0},{6,2},{1,5},{3,7},{5,1},{7,3},{8,12},{10,14},{12... | collective-permute-start | bytes 393224 | tf_op jit(solution)/shard_map/ppermute | solution.py:37
  42.9 0.5 collective-permute-start.15
  43.5 3.8 %collective-permute-done.13.refs_1_ = bf16[256,256]{1,0:T(8,128)(2,1)S(1)} collective-permute-done((bf16[256,256]{1,0:T(8,128)(2,1)S(1)}, bf16[256,256]{1,0:T(8,128)(2,1)S(1)}, u32[]{:S(2)}, u32[]{:S(2)}) %collective-permute-start.13) | collective-permute-done | bytes 131104 | tf_op jit(solution)/shard_map/ppermute | solution.py:37
  47.2 2.3 %collective-permute-done.14.refs_2_ = bf16[256,256]{1,0:T(8,128)(2,1)S(1)} collective-permute-done((bf16[256,256]{1,0:T(8,128)(2,1)S(1)}, bf16[256,256]{1,0:T(8,128)(2,1)S(1)}, u32[]{:S(2)}, u32[]{:S(2)}) %collective-permute-start.14) | collective-permute-done | bytes 131104 | tf_op jit(solution)/shard_map/ppermute | solution.py:37
  49.5 0.0 copy-start.2
  49.5 0.0 copy-start.3
  49.6 3.5 %section0_back_section1_front.1 = (bf16[256,256]{1,0:T(8,128)(2,1)S(1)}, bf16[256,1024]{1,0:T(8,128)(2,1)S(1)}) custom-call(bf16[256,256]{1,0:T(8,128)(2,1)S(1)} %get-tuple-element.19.refs_0_, bf16[256,256]{1,0:T(8,128)(2,1)S(1)} %collective-permute-done.13.refs_1_, bf16[256,256]{1,0:T(8,128)(2,1)S(1)} %collective-permute-done.14.refs_2_, ...), custom_call_target="tpu_custom_call" | custom-call | flops 1140850688 | bytes 4194304 | tf_op jit(solution)/shard_map/section0_back_section1_front/pallas_call | solution.py:385
  53.1 1.6 %collective-permute-start.17 = (bf16[256,256]{1,0:T(8,128)(2,1)S(1)}, bf16[256,256]{1,0:T(8,128)(2,1)S(1)}, u32[]{:S(2)}, u32[]{:S(2)}) collective-permute-start(bf16[256,256]{1,0:T(8,128)(2,1)S(1)} %get-tuple-element.22.refs_0_), channel_id=1, source_target_pairs={{0,6},{2,4},{4,2},{6,0},{1,7},{3,5},{5,3},{7,1},{8,14},{10,12},{12... | collective-permute-start | bytes 393224 | tf_op jit(solution)/shard_map/ppermute | solution.py:37
  54.6 1.1 %collective-permute-start.18 = (bf16[256,256]{1,0:T(8,128)(2,1)S(1)}, bf16[256,256]{1,0:T(8,128)(2,1)S(1)}, u32[]{:S(2)}, u32[]{:S(2)}) collective-permute-start(bf16[256,256]{1,0:T(8,128)(2,1)S(1)} %get-tuple-element.22.refs_0_), channel_id=1, source_target_pairs={{0,4},{2,6},{4,0},{6,2},{1,5},{3,7},{5,1},{7,3},{8,12},{10,14},{12... | collective-permute-start | bytes 393224 | tf_op jit(solution)/shard_map/ppermute | solution.py:37
  55.8 0.8 %collective-permute-start.19 = (bf16[256,256]{1,0:T(8,128)(2,1)S(1)}, bf16[256,256]{1,0:T(8,128)(2,1)S(1)}, u32[]{:S(2)}, u32[]{:S(2)}) collective-permute-start(bf16[256,256]{1,0:T(8,128)(2,1)S(1)} %get-tuple-element.22.refs_0_), channel_id=1, source_target_pairs={{0,2},{2,0},{4,6},{6,4},{1,3},{3,1},{5,7},{7,5},{8,10},{10,8},{12,... | collective-permute-start | bytes 393224 | tf_op jit(solution)/shard_map/ppermute | solution.py:37
  56.6 3.8 %collective-permute-done.17.refs_1_ = bf16[256,256]{1,0:T(8,128)(2,1)S(1)} collective-permute-done((bf16[256,256]{1,0:T(8,128)(2,1)S(1)}, bf16[256,256]{1,0:T(8,128)(2,1)S(1)}, u32[]{:S(2)}, u32[]{:S(2)}) %collective-permute-start.17) | collective-permute-done | bytes 131104 | tf_op jit(solution)/shard_map/ppermute | solution.py:37
  60.4 1.9 %collective-permute-done.18.refs_2_ = bf16[256,256]{1,0:T(8,128)(2,1)S(1)} collective-permute-done((bf16[256,256]{1,0:T(8,128)(2,1)S(1)}, bf16[256,256]{1,0:T(8,128)(2,1)S(1)}, u32[]{:S(2)}, u32[]{:S(2)}) %collective-permute-start.18) | collective-permute-done | bytes 131104 | tf_op jit(solution)/shard_map/ppermute | solution.py:37
  62.3 2.4 %section1_back_context.1 = (bf16[256,1024]{1,0:T(8,128)(2,1)}, bf16[256,256]{1,0:T(8,128)(2,1)}) custom-call(bf16[256,256]{1,0:T(8,128)(2,1)S(1)} %get-tuple-element.22.refs_0_, bf16[256,256]{1,0:T(8,128)(2,1)S(1)} %collective-permute-done.17.refs_1_, bf16[256,256]{1,0:T(8,128)(2,1)S(1)} %collective-permute-done.18.refs_2_, ...), custom_call_target="tpu_custom_call" | custom-call | flops 805306368 | bytes 2097152 | tf_op jit(solution)/shard_map/section1_back_context/pallas_call | solution.py:400
  (21 shorter events, 0.1 us)
Async XLA Ops:
  2.0 5.7 %collective-permute-start = (s32[4,128]{1,0:T(4,128)S(1)}, s32[4,128]{1,0:T(4,128)S(1)}, u32[]{:S(2)}, u32[]{:S(2)}) collective-permute-start(s32[4,128]{1,0:T(4,128)S(1)} %bitcast_add_fusion.refs_0_), channel_id=1, source_target_pairs={{0,8},{8,0},{16,24},{24,16},{1,9},{9,1},{17,25},{25,17},{2,10},{10... | collective-permute-start | bytes 6152 | tf_op jit(solution)/shard_map/ppermute | solution.py:37
  7.7 1.0 %copy-start.1 = (bf16[1,256,1024]{2,1,0:T(8,128)(2,1)S(1)}, bf16[1,256,1024]{2,1,0:T(8,128)(2,1)}, u32[]{:S(2)}) copy-start(bf16[1,256,1024]{2,1,0:T(8,128)(2,1)} %param.17) | copy-start | bytes 1572868
  7.7 8.6 %copy-start = (bf16[1024,1024]{1,0:T(8,128)(2,1)S(1)}, bf16[1024,1024]{1,0:T(8,128)(2,1)}, u32[]{:S(2)}) copy-start(bf16[1024,1024]{1,0:T(8,128)(2,1)} %refs_3_.1) | copy-start | bytes 6291460
  7.8 22.1 %collective-permute-start.5 = (bf16[4,1024,256]{2,1,0:T(8,128)(2,1)S(1)}, bf16[4,1024,256]{2,1,0:T(8,128)(2,1)S(1)}, u32[]{:S(2)}, u32[]{:S(2)}) collective-permute-start(bf16[4,1024,256]{2,1,0:T(8,128)(2,1)S(1)} %hold.1.refs_10_.refs_6_), channel_id=1, source_target_pairs={{0,1},{1,0},{2,3},{3,2},{4,5},{5,4},{6,7},{7,6},{8,9},{9,8},{10,11... | collective-permute-start | bytes 6291464 | tf_op jit(solution)/shard_map/ppermute | solution.py:37
  8.8 17.1 %collective-permute-start.10 = (bf16[256,1024]{1,0:T(8,128)(2,1)S(1)}, bf16[256,1024]{1,0:T(8,128)(2,1)S(1)}, u32[]{:S(2)}, u32[]{:S(2)}) collective-permute-start(bf16[256,1024]{1,0:T(8,128)(2,1)S(1)} %bitcast.15), channel_id=1, source_target_pairs={{0,4},{2,6},{4,0},{6,2},{1,5},{3,7},{5,1},{7,3},{8,12},{10,14},{12... | collective-permute-start | bytes 1572872 | tf_op jit(solution)/shard_map/ppermute | solution.py:37
  10.3 15.5 %collective-permute-start.9 = (bf16[256,1024]{1,0:T(8,128)(2,1)S(1)}, bf16[256,1024]{1,0:T(8,128)(2,1)S(1)}, u32[]{:S(2)}, u32[]{:S(2)}) collective-permute-start(bf16[256,1024]{1,0:T(8,128)(2,1)S(1)} %bitcast.16), channel_id=1, source_target_pairs={{0,2},{2,0},{4,6},{6,4},{1,3},{3,1},{5,7},{7,5},{8,10},{10,8},{12,... | collective-permute-start | bytes 1572872 | tf_op jit(solution)/shard_map/ppermute | solution.py:37
  11.8 4.5 %collective-permute-start.1 = (s32[8,128]{1,0:T(8,128)S(1)}, s32[8,128]{1,0:T(8,128)S(1)}, u32[]{:S(2)}, u32[]{:S(2)}) collective-permute-start(s32[8,128]{1,0:T(8,128)S(1)} %pad_add_fusion), channel_id=1, source_target_pairs={{0,16},{8,24},{16,0},{24,8},{1,17},{9,25},{17,1},{25,9},{2,18},{10... | collective-permute-start | bytes 12296 | tf_op jit(solution)/shard_map/ppermute | solution.py:37
  16.9 5.0 %collective-permute-start.3 = (bf16[256,256]{1,0:T(8,128)(2,1)S(1)}, bf16[256,256]{1,0:T(8,128)(2,1)S(1)}, u32[]{:S(2)}, u32[]{:S(2)}) collective-permute-start(bf16[256,256]{1,0:T(8,128)(2,1)S(1)} %fetch.2.refs_4_), channel_id=1, source_target_pairs={{0,8},{8,0},{16,24},{24,16},{1,9},{9,1},{17,25},{25,17},{2,10},{10... | collective-permute-start | bytes 393224 | tf_op jit(solution)/shard_map/ppermute | solution.py:37
  18.5 7.3 %collective-permute-start.2 = (bf16[256,256]{1,0:T(8,128)(2,1)S(1)}, bf16[256,256]{1,0:T(8,128)(2,1)S(1)}, u32[]{:S(2)}, u32[]{:S(2)}) collective-permute-start(bf16[256,256]{1,0:T(8,128)(2,1)S(1)} %get-tuple-element.15), channel_id=1, source_target_pairs={{0,8},{8,0},{16,24},{24,16},{1,9},{9,1},{17,25},{25,17},{2,10},{10... | collective-permute-start | bytes 393224 | tf_op jit(solution)/shard_map/ppermute | solution.py:37
  21.9 8.0 %collective-permute-start.4 = (bf16[256,256]{1,0:T(8,128)(2,1)S(1)}, bf16[256,256]{1,0:T(8,128)(2,1)S(1)}, u32[]{:S(2)}, u32[]{:S(2)}) collective-permute-start(bf16[256,256]{1,0:T(8,128)(2,1)S(1)} %merge.3.refs_0_), channel_id=1, source_target_pairs={{0,16},{8,24},{16,0},{24,8},{1,17},{9,25},{17,1},{25,9},{2,18},{10... | collective-permute-start | bytes 393224 | tf_op jit(solution)/shard_map/ppermute | solution.py:37
  25.8 11.2 %copy-start.4 = (s32[1,2,256]{2,1,0:T(2,128)S(1)}, s32[1,2,256]{2,1,0:T(2,128)}, u32[]{:S(2)}) copy-start(s32[1,2,256]{2,1,0:T(2,128)} %refs_5_.1) | copy-start | bytes 6148
  25.9 7.6 %collective-permute-start.11 = (bf16[128,1024]{1,0:T(8,128)(2,1)S(1)}, bf16[128,1024]{1,0:T(8,128)(2,1)S(1)}, u32[]{:S(2)}, u32[]{:S(2)}) collective-permute-start(bf16[128,1024]{1,0:T(8,128)(2,1)S(1)} %get-tuple-element.17), channel_id=1, source_target_pairs={{0,2},{2,0},{4,6},{6,4},{1,3},{3,1},{5,7},{7,5},{8,10},{10,8},{12,... | collective-permute-start | bytes 786440 | tf_op jit(solution)/shard_map/ppermute | solution.py:37
  26.5 7.6 %collective-permute-start.12 = (bf16[128,1024]{1,0:T(8,128)(2,1)S(1)}, bf16[128,1024]{1,0:T(8,128)(2,1)S(1)}, u32[]{:S(2)}, u32[]{:S(2)}) collective-permute-start(bf16[128,1024]{1,0:T(8,128)(2,1)S(1)} %get-tuple-element.18), channel_id=1, source_target_pairs={{0,4},{2,6},{4,0},{6,2},{1,5},{3,7},{5,1},{7,3},{8,12},{10,14},{12... | collective-permute-start | bytes 786440 | tf_op jit(solution)/shard_map/ppermute | solution.py:37
  29.9 6.0 %collective-permute-start.6 = (bf16[256,256]{1,0:T(8,128)(2,1)S(1)}, bf16[256,256]{1,0:T(8,128)(2,1)S(1)}, u32[]{:S(2)}, u32[]{:S(2)}) collective-permute-start(bf16[256,256]{1,0:T(8,128)(2,1)S(1)} %merge.5.refs_0_), channel_id=1, source_target_pairs={{0,6},{2,4},{4,2},{6,0},{1,7},{3,5},{5,3},{7,1},{8,14},{10,12},{12... | collective-permute-start | bytes 393224 | tf_op jit(solution)/shard_map/ppermute | solution.py:37
  30.5 6.5 %collective-permute-start.7 = (bf16[256,256]{1,0:T(8,128)(2,1)S(1)}, bf16[256,256]{1,0:T(8,128)(2,1)S(1)}, u32[]{:S(2)}, u32[]{:S(2)}) collective-permute-start(bf16[256,256]{1,0:T(8,128)(2,1)S(1)} %merge.5.refs_0_), channel_id=1, source_target_pairs={{0,4},{2,6},{4,0},{6,2},{1,5},{3,7},{5,1},{7,3},{8,12},{10,14},{12... | collective-permute-start | bytes 393224 | tf_op jit(solution)/shard_map/ppermute | solution.py:37
  32.0 5.0 %collective-permute-start.8 = (bf16[256,256]{1,0:T(8,128)(2,1)S(1)}, bf16[256,256]{1,0:T(8,128)(2,1)S(1)}, u32[]{:S(2)}, u32[]{:S(2)}) collective-permute-start(bf16[256,256]{1,0:T(8,128)(2,1)S(1)} %merge.5.refs_0_), channel_id=1, source_target_pairs={{0,2},{2,0},{4,6},{6,4},{1,3},{3,1},{5,7},{7,5},{8,10},{10,8},{12,... | collective-permute-start | bytes 393224 | tf_op jit(solution)/shard_map/ppermute | solution.py:37
  39.8 9.7 %collective-permute-start.16 = (bf16[4,256,1024]{2,1,0:T(8,128)(2,1)S(1)}, bf16[4,256,1024]{2,1,0:T(8,128)(2,1)S(1)}, u32[]{:S(2)}, u32[]{:S(2)}) collective-permute-start(bf16[4,256,1024]{2,1,0:T(8,128)(2,1)S(1)} %get-tuple-element.21.refs_8_), channel_id=1, source_target_pairs={{0,1},{1,0},{2,3},{3,2},{4,5},{5,4},{6,7},{7,6},{8,9},{9,8},{10,11... | collective-permute-start | bytes 6291464 | tf_op jit(solution)/shard_map/ppermute | solution.py:37
  39.9 7.3 %collective-permute-start.13 = (bf16[256,256]{1,0:T(8,128)(2,1)S(1)}, bf16[256,256]{1,0:T(8,128)(2,1)S(1)}, u32[]{:S(2)}, u32[]{:S(2)}) collective-permute-start(bf16[256,256]{1,0:T(8,128)(2,1)S(1)} %get-tuple-element.19.refs_0_), channel_id=1, source_target_pairs={{0,6},{2,4},{4,2},{6,0},{1,7},{3,5},{5,3},{7,1},{8,14},{10,12},{12... | collective-permute-start | bytes 393224 | tf_op jit(solution)/shard_map/ppermute | solution.py:37
  41.4 8.1 %collective-permute-start.14 = (bf16[256,256]{1,0:T(8,128)(2,1)S(1)}, bf16[256,256]{1,0:T(8,128)(2,1)S(1)}, u32[]{:S(2)}, u32[]{:S(2)}) collective-permute-start(bf16[256,256]{1,0:T(8,128)(2,1)S(1)} %get-tuple-element.19.refs_0_), channel_id=1, source_target_pairs={{0,4},{2,6},{4,0},{6,2},{1,5},{3,7},{5,1},{7,3},{8,12},{10,14},{12... | collective-permute-start | bytes 393224 | tf_op jit(solution)/shard_map/ppermute | solution.py:37
  42.9 6.6 %collective-permute-start.15 = (bf16[256,256]{1,0:T(8,128)(2,1)S(1)}, bf16[256,256]{1,0:T(8,128)(2,1)S(1)}, u32[]{:S(2)}, u32[]{:S(2)}) collective-permute-start(bf16[256,256]{1,0:T(8,128)(2,1)S(1)} %get-tuple-element.19.refs_0_), channel_id=1, source_target_pairs={{0,2},{2,0},{4,6},{6,4},{1,3},{3,1},{5,7},{7,5},{8,10},{10,8},{12,... | collective-permute-start | bytes 393224 | tf_op jit(solution)/shard_map/ppermute | solution.py:37
  49.5 7.1 %copy-start.5 = (bf16[256]{0:T(256)(128)(2,1)S(1)}, bf16[256]{0:T(256)(128)(2,1)}, u32[]{:S(2)}) copy-start(bf16[256]{0:T(256)(128)(2,1)} %param.19) | copy-start | bytes 1540
  49.5 12.8 %copy-start.2 = (bf16[1024,256]{1,0:T(8,128)(2,1)S(1)}, bf16[1024,256]{1,0:T(8,128)(2,1)}, u32[]{:S(2)}) copy-start(bf16[1024,256]{1,0:T(8,128)(2,1)} %refs_6_.1) | copy-start | bytes 1572868
  49.5 12.8 %copy-start.3 = (s32[1,2,256,8]{2,3,1,0:T(8,128)S(1)}, s32[1,2,256,8]{2,3,1,0:T(8,128)}, u32[]{:S(2)}) copy-start(s32[1,2,256,8]{2,3,1,0:T(8,128)} %param.13) | copy-start | bytes 49156
  53.1 7.3 %collective-permute-start.17 = (bf16[256,256]{1,0:T(8,128)(2,1)S(1)}, bf16[256,256]{1,0:T(8,128)(2,1)S(1)}, u32[]{:S(2)}, u32[]{:S(2)}) collective-permute-start(bf16[256,256]{1,0:T(8,128)(2,1)S(1)} %get-tuple-element.22.refs_0_), channel_id=1, source_target_pairs={{0,6},{2,4},{4,2},{6,0},{1,7},{3,5},{5,3},{7,1},{8,14},{10,12},{12... | collective-permute-start | bytes 393224 | tf_op jit(solution)/shard_map/ppermute | solution.py:37
  54.6 7.6 %collective-permute-start.18 = (bf16[256,256]{1,0:T(8,128)(2,1)S(1)}, bf16[256,256]{1,0:T(8,128)(2,1)S(1)}, u32[]{:S(2)}, u32[]{:S(2)}) collective-permute-start(bf16[256,256]{1,0:T(8,128)(2,1)S(1)} %get-tuple-element.22.refs_0_), channel_id=1, source_target_pairs={{0,4},{2,6},{4,0},{6,2},{1,5},{3,7},{5,1},{7,3},{8,12},{10,14},{12... | collective-permute-start | bytes 393224 | tf_op jit(solution)/shard_map/ppermute | solution.py:37
  55.8 6.5 %collective-permute-start.19 = (bf16[256,256]{1,0:T(8,128)(2,1)S(1)}, bf16[256,256]{1,0:T(8,128)(2,1)S(1)}, u32[]{:S(2)}, u32[]{:S(2)}) collective-permute-start(bf16[256,256]{1,0:T(8,128)(2,1)S(1)} %get-tuple-element.22.refs_0_), channel_id=1, source_target_pairs={{0,2},{2,0},{4,6},{6,4},{1,3},{3,1},{5,7},{7,5},{8,10},{10,8},{12,... | collective-permute-start | bytes 393224 | tf_op jit(solution)/shard_map/ppermute | solution.py:37

commit v7 on v6

--- a/solution.py
+++ b/solution.py
@@ -26,8 +26,7 @@
     return n & (n - 1) == 0
 
 
-def source_of(me, slot, n):
-    k = (n - slot) % n
+def source_of(me, k, n):
     return me ^ k if is_pow2(n) else lax.rem(me + n - k, n)
 
 
@@ -38,7 +37,7 @@
 
 
 def spread(value, axis):
-    return [value] + [exchange(value, axis, k) for k in reversed(range(1, lax.axis_size(axis)))]
+    return [value] + [exchange(value, axis, k) for k in range(1, lax.axis_size(axis))]
 
 
 def swap(blocks, axis):
@@ -55,12 +54,8 @@
 
 def fetch_kernel(steps, batches, *refs):
     asked_refs, table_ref = refs[:steps], refs[steps]
-    out_refs, (tab, sem) = refs[-steps - 2 : -2], refs[-2:]
-    width = tab.shape[1]
-    at = pl.multiple_of(lax.axis_index("mp") * width, width)
-    copy = pltpu.make_async_copy(table_ref.at[:, pl.ds(at, width)], tab, sem)
-    copy.start()
-    first = lax.axis_index("dp") * tab.shape[0]
+    out_refs, width = refs[-steps:], refs[-1].shape[1]
+    first = lax.axis_index("dp") * table_ref.shape[0]
     phase = lax.axis_index("phase")
     hots = []
     for asked_ref in asked_refs:
@@ -76,14 +71,14 @@
             jnp.concatenate(
                 [
                     jnp.where(cols == lane + c, 1.0, 0.0).astype(BF16)
-                    for c in range(0, tab.shape[0], LANES)
+                    for c in range(0, table_ref.shape[0], LANES)
                 ],
                 axis=1,
             )
         )
-    copy.wait()
+    held = table_ref[:, pl.ds(pl.multiple_of(lax.axis_index("mp") * width, width), width)]
     for hot, out_ref in zip(hots, out_refs):
-        out_ref[...] = jnp.dot(hot, tab[...], preferred_element_type=F32).astype(BF16)
+        out_ref[...] = jnp.dot(hot, held, preferred_element_type=F32).astype(BF16)
 
 
 def fetch(asked, batches, table, width, after):
@@ -91,12 +86,11 @@
     return pl.pallas_call(
         functools.partial(fetch_kernel, steps, batches),
         out_shape=[jax.ShapeDtypeStruct((rows, width), BF16)] * steps,
-        in_specs=[VMEM] * steps + [HBM] * (1 + len(after)),
+        in_specs=[VMEM] * (steps + 1) + [HBM] * len(after),
         out_specs=[VMEM] * steps,
-        scratch_shapes=[pltpu.VMEM((table.shape[0], width), BF16), pltpu.SemaphoreType.DMA],
         compiler_params=params(),
         cost_estimate=pl.CostEstimate(
-            flops=2 * steps * rows * width * table.shape[0],
+            flops=8 * steps * rows * width * table.shape[0],
             bytes_accessed=2 * width * table.shape[0],
             transcendentals=0,
         ),
@@ -184,111 +178,120 @@
     return blocks[0]
 
 
-def start_picked(section, own, other, dst, sem):
+def prepare_kernel(seg_ref, neigh_ref, mask_ref, share_ref):
+    phase, rows, imps = lax.axis_index("phase"), mask_ref.shape[0], share_ref.shape[0]
+    seg = seg_ref[0, pl.ds(phase, 1), :]
+    at_row = lax.broadcasted_iota(jnp.int32, (rows, rows), 0)
+    at_col = lax.broadcasted_iota(jnp.int32, (rows, rows), 1)
+    allowed = (at_col <= at_row) & (columns_of(seg, rows) == seg)
+    mask_ref[...] = jnp.where(allowed, 1.0 / rows, 0.0)
+    near = neigh_ref[phase]
+    row = lax.broadcasted_iota(jnp.int32, (rows, imps), 0)
+    share = jnp.zeros((rows, imps), F32)
+    for n in range(NBR):
+        share = share + jnp.where(near[n : n + 1, :] == row, 1.0 / NBR, 0.0)
+    share_ref[...] = jnp.transpose(share).astype(BF16)
+
+
+def prepare(segments, neigh):
+    rows, imps = segments.shape[2], neigh.shape[2]
+    return pl.pallas_call(
+        prepare_kernel,
+        out_shape=[
+            jax.ShapeDtypeStruct((rows, rows), F32),
+            jax.ShapeDtypeStruct((imps, rows), BF16),
+        ],
+        in_specs=[VMEM] * 2,
+        out_specs=[VMEM] * 2,
+        compiler_params=params(),
+        cost_estimate=pl.CostEstimate(
+            flops=16 * rows * imps, bytes_accessed=8 * rows * rows, transcendentals=0
+        ),
+        name="prepare",
+    )(segments, neigh)
+
+
+def by_phase(body, zero, one):
     phase = lax.axis_index("phase")
-
-    @pl.when(phase == section)
-    def _():
-        pltpu.make_async_copy(own, dst, sem).start()
-
-    @pl.when(phase != section)
-    def _():
-        pltpu.make_async_copy(other, dst, sem).start()
-
-
-def wait_picked(own, dst, sem):
-    pltpu.make_async_copy(own, dst, sem).wait()
-
-
-def start_weights(section, w_own, w_other, w_buf, w_sem):
-    for g in range(4):
-        start_picked(section, w_own.at[g], w_other.at[g], w_buf.at[g], w_sem.at[g])
-
-
-def front(x, seg_ref, w_own, w_buf, w_sem, gated_ref):
-    rows, local_cols = x.shape[0], w_buf.shape[2]
+    pl.when(phase == 0)(functools.partial(body, *zero))
+    pl.when(phase != 0)(functools.partial(body, *one))
+
+
+def front(x, mask_ref, w_ref, gated_ref):
+    local_cols = w_ref.shape[2]
     xf = x.astype(F32)
     inv = lax.rsqrt(jnp.mean(xf * xf, axis=-1, keepdims=True) + EPS)
     proj = []
     for g in range(4):
-        wait_picked(w_own.at[g], w_buf.at[g], w_sem.at[g])
-        raw = jnp.dot(x, w_buf[g], preferred_element_type=F32)
+        raw = jnp.dot(x, w_ref[g], preferred_element_type=F32)
         proj.append(silu(raw * inv).astype(BF16))
     gates, values, queries, keys = proj
-    seg = seg_ref[0, pl.ds(lax.axis_index("phase"), 1), :]
-    seg_cols = columns_of(seg, rows)
-    at_row = lax.broadcasted_iota(jnp.int32, (rows, rows), 0)
-    at_col = lax.broadcasted_iota(jnp.int32, (rows, rows), 1)
-    allowed = (at_col <= at_row) & (seg_cols == seg)
+    mask = mask_ref[...]
     for h in range(0, local_cols, HD):
         head = slice(h, h + HD)
         scores = lax.dot_general(
             queries[:, head], keys[:, head], (((1,), (1,)), ((), ())), preferred_element_type=F32
         ) * HD ** (-0.5)
-        weights = (jnp.where(allowed, silu(scores), 0.0) / rows).astype(BF16)
+        weights = (silu(scores) * mask).astype(BF16)
         mixed = jnp.dot(weights, values[:, head], preferred_element_type=F32)
         mixed = mixed * lax.rsqrt(jnp.mean(mixed * mixed, axis=-1, keepdims=True) + EPS)
         gated_ref[:, head] = (mixed * gates[:, head].astype(F32)).astype(BF16)
 
 
-def back(x, gated_refs, o_own, o_buf, o_sem):
-    steps, cols, width = o_buf.shape
+def back(x, gated_refs, o_ref):
+    steps, cols, width = o_ref.shape
     gated = jnp.concatenate([gated_ref[...] for gated_ref in gated_refs], axis=1)
-    for k in range(steps):
-        wait_picked(o_own.at[k], o_buf.at[k], o_sem.at[k])
-    weights = o_buf[...].reshape(steps * cols, width)
+    weights = o_ref[...].reshape(steps * cols, width)
     total = x.astype(F32) + jnp.dot(gated, weights, preferred_element_type=F32)
     return total.astype(BF16)
 
 
 def first_kernel(steps, places, *refs):
     x_refs, pieces, refs = refs[:steps], refs[steps : steps + len(places)], refs[steps + len(places) :]
-    seg_ref, w_own, w_other, gated_ref, x_ref, stack_ref, w_buf, w_sem, o_sem = refs
-    start_weights(0, w_own, w_other, w_buf, w_sem)
+    mask_ref, w_own, w_other, gated_ref, x_ref, stack_ref, sems = refs
     copies = []
-    for n, (slot, row) in enumerate(places):
-        at = stack_ref.at[slot, pl.ds(row, pieces[n].shape[0]), :]
-        copies.append(pltpu.make_async_copy(pieces[n], at, o_sem.at[n]))
+    for n, (k, row) in enumerate(places):
+        at = stack_ref.at[k, pl.ds(row, pieces[n].shape[0]), :]
+        copies.append(pltpu.make_async_copy(pieces[n], at, sems.at[n]))
     for copy in copies:
         copy.start()
     width = x_refs[0].shape[1]
     for k, piece in enumerate(x_refs):
         at = pl.multiple_of(source_of(lax.axis_index("mp"), k, steps) * width, width)
         x_ref[:, pl.ds(at, width)] = piece[...]
-    front(x_ref[...], seg_ref, w_own, w_buf, w_sem, gated_ref)
+
+    def body(w_ref):
+        front(x_ref[...], mask_ref, w_ref, gated_ref)
+
+    by_phase(body, [w_own], [w_other])
     for copy in copies:
         copy.wait()
 
 
 def middle_kernel(steps, *refs):
     gated_refs = refs[:steps]
-    x_ref, seg_ref, w_own, w_other, o_own, o_other = refs[steps : steps + 6]
-    gated_ref, x1_ref, o_buf, o_sem, w_buf, w_sem = refs[steps + 6 :]
-    for k in range(steps):
-        start_picked(0, o_own.at[k], o_other.at[k], o_buf.at[k], o_sem.at[k])
-    start_weights(1, w_own, w_other, w_buf, w_sem)
-    x1 = back(x_ref[...], gated_refs, o_own, o_buf, o_sem)
-    x1_ref[...] = x1
-    front(x1, seg_ref, w_own, w_buf, w_sem, gated_ref)
+    x_ref, mask_ref, w_own, w_other, o_own, o_other, gated_ref, x1_ref = refs[steps:]
+
+    def body(o_ref, w_ref):
+        x1 = back(x_ref[...], gated_refs, o_ref)
+        x1_ref[...] = x1
+        front(x1, mask_ref, w_ref, gated_ref)
+
+    by_phase(body, [o_own, w_other], [o_other, w_own])
 
 
 def last_kernel(steps, *refs):
     gated_refs = refs[:steps]
-    x_ref, neigh_ref, w_ref, bias_ref, o_own, o_other, states_ref, ctx_ref = refs[steps : steps + 8]
-    o_buf, o_sem = refs[steps + 8 :]
-    for k in range(steps):
-        start_picked(1, o_own.at[k], o_other.at[k], o_buf.at[k], o_sem.at[k])
-    near = neigh_ref[lax.axis_index("phase")]
-    row = lax.broadcasted_iota(jnp.int32, (x_ref.shape[0], near.shape[1]), 0)
-    share = jnp.zeros(row.shape, F32)
-    for n in range(NBR):
-        share = share + jnp.where(near[n : n + 1, :] == row, 1.0 / NBR, 0.0)
-    share = jnp.transpose(share).astype(BF16)
-    states = back(x_ref[...], gated_refs, o_own, o_buf, o_sem)
-    states_ref[...] = states
-    context = jnp.dot(share, states, preferred_element_type=F32).astype(BF16)
-    summed = jnp.dot(context, w_ref[...], preferred_element_type=F32) + bias_ref[...].astype(F32)
-    ctx_ref[...] = silu(summed).astype(BF16)
+    x_ref, share_ref, w_ref, bias_ref, o_own, o_other, states_ref, ctx_ref = refs[steps:]
+
+    def body(o_ref):
+        states = back(x_ref[...], gated_refs, o_ref)
+        states_ref[...] = states
+        context = jnp.dot(share_ref[...], states, preferred_element_type=F32).astype(BF16)
+        summed = jnp.dot(context, w_ref[...], preferred_element_type=F32)
+        ctx_ref[...] = silu(summed + bias_ref[...].astype(F32)).astype(BF16)
+
+    by_phase(body, [o_other], [o_own])
 
 
 def section_flops(rows, width, local_cols):
@@ -319,15 +322,15 @@
     local_cols = w_out.shape[1]
     part = width // mp_count
 
-    w_own = jnp.transpose(w_in[0], (1, 0, 2)).astype(F32) * gains[0].astype(F32)[None, :, None]
-    w_own = w_own.astype(BF16)
+    w_own = jnp.transpose(w_in[0], (1, 0, 2)) * gains[0][None, :, None]
     if mp_count == 4:
         near, far = exchange(w_out[0], "mp", 1), exchange(w_out[0], "mp", 2)
-        o_pieces, places = [w_out[0], near, far], [(0, 0), (3, 0), (2, 0)]
+        o_pieces, places = [w_out[0], near, far], [(0, 0), (1, 0), (2, 0)]
     else:
-        o_pieces, places = spread(w_out[0], "mp"), [(slot, 0) for slot in range(mp_count)]
+        o_pieces, places = spread(w_out[0], "mp"), [(k, 0) for k in range(mp_count)]
     neigh = jnp.transpose(neighbors[0], (0, 2, 1))
     bias = ctx_bias.reshape(1, -1)
+    mask, share = prepare(segments, neigh)
 
     if is_pow2(dp_count) and dp_count <= 8:
         wanted = item_owner.reshape(-1, LANES) * table_rows + item_row.reshape(-1, LANES)
@@ -340,7 +343,7 @@
         def then(first):
             if mp_count == 4:
                 o_pieces.extend(relay(near, far, "mp", [first]))
-                places.extend([(1, 0), (1, local_cols // 2)])
+                places.extend([(3, 0), (3, local_cols // 2)])
             return [w_other]
 
         piece = gather_in(found, [], then)
@@ -352,13 +355,9 @@
         w_other = exchange(w_own, "phase", 1)
         if mp_count == 4:
             o_pieces.extend(relay(near, far, "mp", [piece]))
-            places.extend([(1, 0), (1, local_cols // 2)])
+            places.extend([(3, 0), (3, local_cols // 2)])
     x_pieces = spread(piece, "mp")
 
-    sem4 = pltpu.SemaphoreType.DMA((4,))
-    semk = pltpu.SemaphoreType.DMA((mp_count,))
-    w_buf = pltpu.VMEM((4, width, local_cols), BF16)
-    o_buf = pltpu.VMEM((mp_count, local_cols, width), BF16)
     x_shape = jax.ShapeDtypeStruct((rows, width), BF16)
     gated_shape = jax.ShapeDtypeStruct((rows, local_cols), BF16)
     front_flops = section_flops(rows, width, local_cols)
@@ -371,23 +370,22 @@
             x_shape,
             jax.ShapeDtypeStruct((mp_count, local_cols, width), BF16),
         ],
-        in_specs=[VMEM] * mp_count + [HBM] * len(places) + [VMEM] + [HBM] * 2,
+        in_specs=[VMEM] * mp_count + [HBM] * len(places) + [VMEM] * 3,
         out_specs=[VMEM] * 2 + [HBM],
-        scratch_shapes=[w_buf, sem4, pltpu.SemaphoreType.DMA((len(places),))],
+        scratch_shapes=[pltpu.SemaphoreType.DMA((len(places),))],
         compiler_params=params(),
         cost_estimate=pl.CostEstimate(
             flops=front_flops, bytes_accessed=8 * width * local_cols, transcendentals=0
         ),
         name="section0_front",
-    )(*x_pieces, *o_pieces, segments, w_own, w_other)
+    )(*x_pieces, *o_pieces, mask, w_own, w_other)
     o_other = exchange(o_own, "phase", 1)
 
     gated, x1 = pl.pallas_call(
         functools.partial(middle_kernel, mp_count),
         out_shape=[gated_shape, x_shape],
-        in_specs=[VMEM] * (mp_count + 2) + [HBM] * 4,
+        in_specs=[VMEM] * (mp_count + 6),
         out_specs=[VMEM] * 2,
-        scratch_shapes=[o_buf, semk, w_buf, sem4],
         compiler_params=params(),
         cost_estimate=pl.CostEstimate(
             flops=front_flops + back_flops,
@@ -395,14 +393,13 @@
             transcendentals=0,
         ),
         name="section0_back_section1_front",
-    )(*spread(gated, "mp"), x0, segments, w_own, w_other, o_own, o_other)
+    )(*spread(gated, "mp"), x0, mask, w_own, w_other, o_own, o_other)
 
     states, ctx = pl.pallas_call(
         functools.partial(last_kernel, mp_count),
         out_shape=[x_shape, jax.ShapeDtypeStruct((imps, w_ctx.shape[1]), BF16)],
-        in_specs=[VMEM] * (mp_count + 4) + [HBM] * 2,
+        in_specs=[VMEM] * (mp_count + 6),
         out_specs=[VMEM] * 2,
-        scratch_shapes=[o_buf, semk],
         compiler_params=params(),
         cost_estimate=pl.CostEstimate(
             flops=back_flops + 2 * imps * width * (rows + w_ctx.shape[1]),
@@ -410,7 +407,7 @@
             transcendentals=0,
         ),
         name="section1_back_context",
-    )(*spread(gated, "mp"), x1, neigh, w_ctx, bias, o_own, o_other)
+    )(*spread(gated, "mp"), x1, share, w_ctx, bias, o_own, o_other)
 
     return (
         states.reshape(1, 1, rows, width),

time: 64.9 us -> 63.4 us (0.977)
  waiting for transfers between devices: 21.8 us -> 26.7 us
  Pallas kernels: 10.5 us -> 6.74 us
  starting transfers between devices: 26.6 us -> 24.9 us
  local copies, waits for them, and re-layouts: 0.96 us -> 0.04 us
    ppermute x20, waiting for transfers between devices: 21.8 us -> 26.7 us  [exchange(): return lax.ppermute(value, axis, pairs)]
    convert_element_type x2 -> x0, other arithmetic: 2.68 us -> none  [the longest x1 1.99 us: on_device(): w_own = w_own.astype(BF16)]
    mul x0 -> x1, other arithmetic: none -> 1.9 us  [on_device(): w_own = jnp.transpose(w_in[0], (1, 0, 2)) * gains[0][None, :, None]]
    pallas_call x1, Pallas kernels: 3.51 us -> 1.75 us  [on_device(): pl.pallas_call(functools.partial(middle_kernel, mp_count), out_shape=[gat...]
    ppermute x20, starting transfers between devices: 26.6 us -> 24.9 us  [exchange(): return lax.ppermute(value, axis, pairs)]
    pallas_call x1, Pallas kernels: 2.86 us -> 1.49 us  [on_device(): pl.pallas_call(functools.partial(first_kernel, mp_count, places), out_sha...]
    unnamed x12, local copies, waits for them, and re-layouts: 0.95 us -> 0.03 us
    unnamed x0 -> x1, other arithmetic: none -> 0.71 us
  transfers between devices with their start and end apart: 20 -> 20, of which waited for: 10 -> 12; matrix products, arithmetic and copies ran while one was open for 4% -> 4% of each run, Pallas kernels for 3% -> 2%
where the time goes in v7:
time: 63.4 us; the launch traced here: 63.2 us
  waiting for transfers between devices  26.7 us (42%)
  starting transfers between devices  24.9 us (39%)
  Pallas kernels  6.74 us (11%)
  other arithmetic  3.99 us (6%)
  between operations  0.77 us (1%)
    ppermute x20, waiting for transfers between devices, exchange(): return lax.ppermute(value, axis, pairs)  26.7 us
    ppermute x20, starting transfers between devices, exchange(): return lax.ppermute(value, axis, pairs)  24.9 us
    pallas_call x1, Pallas kernels, on_device(): pl.pallas_call(functools.partial(last_kernel, mp_count), out_shape=[x_sha...  2.04 us
    mul x1, other arithmetic, on_device(): w_own = jnp.transpose(w_in[0], (1, 0, 2)) * gains[0][None, :, None]  1.9 us
    pallas_call x1, Pallas kernels, on_device(): pl.pallas_call(functools.partial(middle_kernel, mp_count), out_shape=[gat...  1.75 us
    pallas_call x1, Pallas kernels, on_device(): pl.pallas_call(functools.partial(first_kernel, mp_count, places), out_sha...  1.49 us
  transfers between devices with their start and end apart: 20, of which 12 were waited for; matrix products, arithmetic and copies ran while one was open for 4% of the time, Pallas kernels for 2%

profile of v7, /device:TPU:0, one launch (start us, length us, event | category | flops | bytes accessed | tf_op | source)
XLA Modules:
  0.0 63.2 jit_solution(3039079216144935511)
XLA Ops:
  0.6 0.7 %broadcast_multiply_fusion = s32[512,1]{0,1:T(1,128)S(1)} fusion(s32[512,1]{0,1:T(1,128)} %param.10), kind=kLoop, calls=%fused_computation.4 | loop fusion | flops 512 | bytes 4096 | tf_op jit(solution)/shard_map/mul | solution.py:336
  1.3 0.7 %bitcast_add_fusion.refs_0_ = s32[4,128]{1,0:T(4,128)S(1)} fusion(s32[4,128]{1,0:T(4,128)S(1)} %bitcast.19, s32[512]{0:T(512)} %param.11), kind=kLoop, calls=%fused_computation.3 | loop fusion | flops 512 | bytes 6144 | tf_op jit(solution)/shard_map/add | solution.py:336
  2.0 3.0 %collective-permute-start = (s32[4,128]{1,0:T(4,128)S(1)}, s32[4,128]{1,0:T(4,128)S(1)}, u32[]{:S(2)}, u32[]{:S(2)}) collective-permute-start(s32[4,128]{1,0:T(4,128)S(1)} %bitcast_add_fusion.refs_0_), channel_id=1, source_target_pairs={{0,8},{8,0},{16,24},{24,16},{1,9},{9,1},{17,25},{25,17},{2,10},{10... | collective-permute-start | bytes 6152 | tf_op jit(solution)/shard_map/ppermute | solution.py:36
  5.0 0.7 %reduce = bf16[1024]{0:T(1024)(128)(2,1)S(1)} reduce(bf16[1,1024]{1,0:T(2,128)(2,1)} %param.15, bf16[]{:T(256)} %constant.7), dimensions={0}, to_apply=%param.15.reduce_sub_computation | reduce | bytes 4098 | tf_op args[5]
  5.7 1.9 %fusion.refs_0_ = bf16[4,1024,256]{2,1,0:T(8,128)(2,1)S(1)} fusion(bf16[1,1024,4,256]{3,2,1,0:T(4,128)(2,1)} %param.16, bf16[1024]{0:T(1024)(128)(2,1)S(1)} %reduce), kind=kLoop, calls=%fused_computation.1 | loop fusion | flops 1048576 | bytes 4196352 | tf_op jit(solution)/shard_map/mul | solution.py:325
  7.6 0.0 copy-start.1
  7.7 0.0 copy-start
  7.7 0.0 collective-permute-done.refs_1_
  7.7 0.1 collective-permute-start.5
  7.8 2.7 %collective-permute-start.1 = (s32[8,128]{1,0:T(8,128)S(1)}, s32[8,128]{1,0:T(8,128)S(1)}, u32[]{:S(2)}, u32[]{:S(2)}) collective-permute-start(s32[8,128]{1,0:T(8,128)S(1)} %pad_add_fusion), channel_id=1, source_target_pairs={{0,16},{8,24},{16,0},{24,8},{1,17},{9,25},{17,1},{25,9},{2,18},{10... | collective-permute-start | bytes 12296 | tf_op jit(solution)/shard_map/ppermute | solution.py:36
  10.4 1.5 %collective-permute-start.10 = (bf16[256,1024]{1,0:T(8,128)(2,1)S(1)}, bf16[256,1024]{1,0:T(8,128)(2,1)S(1)}, u32[]{:S(2)}, u32[]{:S(2)}) collective-permute-start(bf16[256,1024]{1,0:T(8,128)(2,1)S(1)} %bitcast.15), channel_id=1, source_target_pairs={{0,4},{2,6},{4,0},{6,2},{1,5},{3,7},{5,1},{7,3},{8,12},{10,14},{12... | collective-permute-start | bytes 1572872 | tf_op jit(solution)/shard_map/ppermute | solution.py:36
  12.0 1.5 %collective-permute-start.9 = (bf16[256,1024]{1,0:T(8,128)(2,1)S(1)}, bf16[256,1024]{1,0:T(8,128)(2,1)S(1)}, u32[]{:S(2)}, u32[]{:S(2)}) collective-permute-start(bf16[256,1024]{1,0:T(8,128)(2,1)S(1)} %bitcast.16), channel_id=1, source_target_pairs={{0,2},{2,0},{4,6},{6,4},{1,3},{3,1},{5,7},{7,5},{8,10},{10,8},{12,... | collective-permute-start | bytes 1572872 | tf_op jit(solution)/shard_map/ppermute | solution.py:36
  13.4 0.0 collective-permute-done.1
  13.5 0.4 fetch.2.refs_4_
  13.9 0.9 %collective-permute-start.3 = (bf16[256,256]{1,0:T(8,128)(2,1)S(1)}, bf16[256,256]{1,0:T(8,128)(2,1)S(1)}, u32[]{:S(2)}, u32[]{:S(2)}) collective-permute-start(bf16[256,256]{1,0:T(8,128)(2,1)S(1)} %fetch.2.refs_4_), channel_id=1, source_target_pairs={{0,8},{8,0},{16,24},{24,16},{1,9},{9,1},{17,25},{25,17},{2,10},{10... | collective-permute-start | bytes 393224 | tf_op jit(solution)/shard_map/ppermute | solution.py:36
  14.8 0.7 %fetch.3 = (bf16[256,256]{1,0:T(8,128)(2,1)S(1)}, bf16[256,256]{1,0:T(8,128)(2,1)S(1)}, bf16[256,256]{1,0:T(8,128)(2,1)S(1)}) custom-call(s32[4,128]{1,0:T(4,128)S(1)} %bitcast_add_fusion.refs_0_, s32[4,128]{1,0:T(4,128)S(1)} %collective-permute-done.refs_1_, s32[4,128]{1,0:T(4,128)S(1)} %get-tuple-element.31.refs_2_, bf16[1024,1024]{1,0:T(8,128)(2,1)S(1)} %copy-done, ...), custom_call_target="tpu_custom_call" | custom-call | flops 1610612736 | bytes 524288 | tf_op jit(solution)/shard_map/fetch/pallas_call | solution.py:86
  15.5 1.2 %collective-permute-start.2 = (bf16[256,256]{1,0:T(8,128)(2,1)S(1)}, bf16[256,256]{1,0:T(8,128)(2,1)S(1)}, u32[]{:S(2)}, u32[]{:S(2)}) collective-permute-start(bf16[256,256]{1,0:T(8,128)(2,1)S(1)} %get-tuple-element.17), channel_id=1, source_target_pairs={{0,8},{8,0},{16,24},{24,16},{1,9},{9,1},{17,25},{25,17},{2,10},{10... | collective-permute-start | bytes 393224 | tf_op jit(solution)/shard_map/ppermute | solution.py:36
  16.7 3.6 %collective-permute-done.3.b_ref = bf16[256,256]{1,0:T(8,128)(2,1)S(1)} collective-permute-done((bf16[256,256]{1,0:T(8,128)(2,1)S(1)}, bf16[256,256]{1,0:T(8,128)(2,1)S(1)}, u32[]{:S(2)}, u32[]{:S(2)}) %collective-permute-start.3) | collective-permute-done | bytes 131104 | tf_op jit(solution)/shard_map/ppermute | solution.py:36
  20.4 1.2 %collective-permute-start.4 = (bf16[256,256]{1,0:T(8,128)(2,1)S(1)}, bf16[256,256]{1,0:T(8,128)(2,1)S(1)}, u32[]{:S(2)}, u32[]{:S(2)}) collective-permute-start(bf16[256,256]{1,0:T(8,128)(2,1)S(1)} %merge.3.refs_0_), channel_id=1, source_target_pairs={{0,16},{8,24},{16,0},{24,8},{1,17},{9,25},{17,1},{25,9},{2,18},{10... | collective-permute-start | bytes 393224 | tf_op jit(solution)/shard_map/ppermute | solution.py:36
  21.6 1.0 %collective-permute-done.2.b_ref = bf16[256,256]{1,0:T(8,128)(2,1)S(1)} collective-permute-done((bf16[256,256]{1,0:T(8,128)(2,1)S(1)}, bf16[256,256]{1,0:T(8,128)(2,1)S(1)}, u32[]{:S(2)}, u32[]{:S(2)}) %collective-permute-start.2) | collective-permute-done | bytes 131104 | tf_op jit(solution)/shard_map/ppermute | solution.py:36
  22.6 1.8 %collective-permute-done.10.far_ref.refs_6_ = bf16[256,1024]{1,0:T(8,128)(2,1)S(1)} collective-permute-done((bf16[256,1024]{1,0:T(8,128)(2,1)S(1)}, bf16[256,1024]{1,0:T(8,128)(2,1)S(1)}, u32[]{:S(2)}, u32[]{:S(2)}) %collective-permute-start.10) | collective-permute-done | bytes 524320 | tf_op jit(solution)/shard_map/ppermute | solution.py:36
  24.4 1.2 %collective-permute-done.9.near_ref.refs_5_ = bf16[256,1024]{1,0:T(8,128)(2,1)S(1)} collective-permute-done((bf16[256,1024]{1,0:T(8,128)(2,1)S(1)}, bf16[256,1024]{1,0:T(8,128)(2,1)S(1)}, u32[]{:S(2)}, u32[]{:S(2)}) %collective-permute-start.9) | collective-permute-done | bytes 524320 | tf_op jit(solution)/shard_map/ppermute | solution.py:36
  25.7 0.1 cut.1
  25.7 1.6 %collective-permute-start.11 = (bf16[128,1024]{1,0:T(8,128)(2,1)S(1)}, bf16[128,1024]{1,0:T(8,128)(2,1)S(1)}, u32[]{:S(2)}, u32[]{:S(2)}) collective-permute-start(bf16[128,1024]{1,0:T(8,128)(2,1)S(1)} %get-tuple-element.19), channel_id=1, source_target_pairs={{0,2},{2,0},{4,6},{6,4},{1,3},{3,1},{5,7},{7,5},{8,10},{10,8},{12,... | collective-permute-start | bytes 786440 | tf_op jit(solution)/shard_map/ppermute | solution.py:36
  27.3 0.5 collective-permute-start.12
  27.8 0.6 collective-permute-start.6
  28.4 1.5 %collective-permute-start.7 = (bf16[256,256]{1,0:T(8,128)(2,1)S(1)}, bf16[256,256]{1,0:T(8,128)(2,1)S(1)}, u32[]{:S(2)}, u32[]{:S(2)}) collective-permute-start(bf16[256,256]{1,0:T(8,128)(2,1)S(1)} %merge.5.refs_0_), channel_id=1, source_target_pairs={{0,4},{2,6},{4,0},{6,2},{1,5},{3,7},{5,1},{7,3},{8,12},{10,14},{12... | collective-permute-start | bytes 393224 | tf_op jit(solution)/shard_map/ppermute | solution.py:36
  30.0 1.4 %collective-permute-start.8 = (bf16[256,256]{1,0:T(8,128)(2,1)S(1)}, bf16[256,256]{1,0:T(8,128)(2,1)S(1)}, u32[]{:S(2)}, u32[]{:S(2)}) collective-permute-start(bf16[256,256]{1,0:T(8,128)(2,1)S(1)} %merge.5.refs_0_), channel_id=1, source_target_pairs={{0,6},{2,4},{4,2},{6,0},{1,7},{3,5},{5,3},{7,1},{8,14},{10,12},{12... | collective-permute-start | bytes 393224 | tf_op jit(solution)/shard_map/ppermute | solution.py:36
  31.4 0.3 prepare.1
  31.7 3.4 %collective-permute-done.11.refs_7_ = bf16[128,1024]{1,0:T(8,128)(2,1)S(1)} collective-permute-done((bf16[128,1024]{1,0:T(8,128)(2,1)S(1)}, bf16[128,1024]{1,0:T(8,128)(2,1)S(1)}, u32[]{:S(2)}, u32[]{:S(2)}) %collective-permute-start.11) | collective-permute-done | bytes 262176 | tf_op jit(solution)/shard_map/ppermute | solution.py:36
  35.0 2.0 %collective-permute-done.12.refs_8_ = bf16[128,1024]{1,0:T(8,128)(2,1)S(1)} collective-permute-done((bf16[128,1024]{1,0:T(8,128)(2,1)S(1)}, bf16[128,1024]{1,0:T(8,128)(2,1)S(1)}, u32[]{:S(2)}, u32[]{:S(2)}) %collective-permute-start.12) | collective-permute-done | bytes 262176 | tf_op jit(solution)/shard_map/ppermute | solution.py:36
  37.0 0.2 collective-permute-done.6.refs_1_
  37.2 2.6 %collective-permute-done.7.refs_2_ = bf16[256,256]{1,0:T(8,128)(2,1)S(1)} collective-permute-done((bf16[256,256]{1,0:T(8,128)(2,1)S(1)}, bf16[256,256]{1,0:T(8,128)(2,1)S(1)}, u32[]{:S(2)}, u32[]{:S(2)}) %collective-permute-start.7) | collective-permute-done | bytes 131104 | tf_op jit(solution)/shard_map/ppermute | solution.py:36
  39.9 1.5 %section0_front.1 = (bf16[256,256]{1,0:T(8,128)(2,1)S(1)}, bf16[256,1024]{1,0:T(8,128)(2,1)S(1)}, bf16[4,256,1024]{2,1,0:T(8,128)(2,1)S(1)}) custom-call(bf16[256,256]{1,0:T(8,128)(2,1)S(1)} %merge.5.refs_0_, bf16[256,256]{1,0:T(8,128)(2,1)S(1)} %collective-permute-done.6.refs_1_, bf16[256,256]{1,0:T(8,128)(2,1)S(1)} %collective-permute-done.7.refs_2_, ...), custom_call_target="tpu_custom_call" | custom-call | flops 603979776 | bytes 2097152 | tf_op jit(solution)/shard_map/section0_front/pallas_call | solution.py:366
  41.3 0.1 collective-permute-start.16
  41.4 0.6 collective-permute-start.13
  42.0 1.2 %collective-permute-start.14 = (bf16[256,256]{1,0:T(8,128)(2,1)S(1)}, bf16[256,256]{1,0:T(8,128)(2,1)S(1)}, u32[]{:S(2)}, u32[]{:S(2)}) collective-permute-start(bf16[256,256]{1,0:T(8,128)(2,1)S(1)} %get-tuple-element.22.refs_0_), channel_id=1, source_target_pairs={{0,4},{2,6},{4,0},{6,2},{1,5},{3,7},{5,1},{7,3},{8,12},{10,14},{12... | collective-permute-start | bytes 393224 | tf_op jit(solution)/shard_map/ppermute | solution.py:36
  43.2 1.8 %collective-permute-start.15 = (bf16[256,256]{1,0:T(8,128)(2,1)S(1)}, bf16[256,256]{1,0:T(8,128)(2,1)S(1)}, u32[]{:S(2)}, u32[]{:S(2)}) collective-permute-start(bf16[256,256]{1,0:T(8,128)(2,1)S(1)} %get-tuple-element.22.refs_0_), channel_id=1, source_target_pairs={{0,6},{2,4},{4,2},{6,0},{1,7},{3,5},{5,3},{7,1},{8,14},{10,12},{12... | collective-permute-start | bytes 393224 | tf_op jit(solution)/shard_map/ppermute | solution.py:36
  45.0 2.8 %collective-permute-done.13.refs_1_ = bf16[256,256]{1,0:T(8,128)(2,1)S(1)} collective-permute-done((bf16[256,256]{1,0:T(8,128)(2,1)S(1)}, bf16[256,256]{1,0:T(8,128)(2,1)S(1)}, u32[]{:S(2)}, u32[]{:S(2)}) %collective-permute-start.13) | collective-permute-done | bytes 131104 | tf_op jit(solution)/shard_map/ppermute | solution.py:36
  47.8 2.6 %collective-permute-done.14.refs_2_ = bf16[256,256]{1,0:T(8,128)(2,1)S(1)} collective-permute-done((bf16[256,256]{1,0:T(8,128)(2,1)S(1)}, bf16[256,256]{1,0:T(8,128)(2,1)S(1)}, u32[]{:S(2)}, u32[]{:S(2)}) %collective-permute-start.14) | collective-permute-done | bytes 131104 | tf_op jit(solution)/shard_map/ppermute | solution.py:36
  50.4 0.0 copy-start.2
  50.4 1.8 %section0_back_section1_front.1 = (bf16[256,256]{1,0:T(8,128)(2,1)S(1)}, bf16[256,1024]{1,0:T(8,128)(2,1)S(1)}) custom-call(bf16[256,256]{1,0:T(8,128)(2,1)S(1)} %get-tuple-element.22.refs_0_, bf16[256,256]{1,0:T(8,128)(2,1)S(1)} %collective-permute-done.13.refs_1_, bf16[256,256]{1,0:T(8,128)(2,1)S(1)} %collective-permute-done.14.refs_2_, ...), custom_call_target="tpu_custom_call" | custom-call | flops 1140850688 | bytes 4194304 | tf_op jit(solution)/shard_map/section0_back_section1_front/pallas_call | solution.py:384
  52.2 1.6 %collective-permute-start.17 = (bf16[256,256]{1,0:T(8,128)(2,1)S(1)}, bf16[256,256]{1,0:T(8,128)(2,1)S(1)}, u32[]{:S(2)}, u32[]{:S(2)}) collective-permute-start(bf16[256,256]{1,0:T(8,128)(2,1)S(1)} %get-tuple-element.25.refs_0_), channel_id=1, source_target_pairs={{0,2},{2,0},{4,6},{6,4},{1,3},{3,1},{5,7},{7,5},{8,10},{10,8},{12,... | collective-permute-start | bytes 393224 | tf_op jit(solution)/shard_map/ppermute | solution.py:36
  53.7 0.6 collective-permute-start.18
  54.3 1.4 %collective-permute-start.19 = (bf16[256,256]{1,0:T(8,128)(2,1)S(1)}, bf16[256,256]{1,0:T(8,128)(2,1)S(1)}, u32[]{:S(2)}, u32[]{:S(2)}) collective-permute-start(bf16[256,256]{1,0:T(8,128)(2,1)S(1)} %get-tuple-element.25.refs_0_), channel_id=1, source_target_pairs={{0,6},{2,4},{4,2},{6,0},{1,7},{3,5},{5,3},{7,1},{8,14},{10,12},{12... | collective-permute-start | bytes 393224 | tf_op jit(solution)/shard_map/ppermute | solution.py:36
  55.7 2.4 %collective-permute-done.17.refs_1_ = bf16[256,256]{1,0:T(8,128)(2,1)S(1)} collective-permute-done((bf16[256,256]{1,0:T(8,128)(2,1)S(1)}, bf16[256,256]{1,0:T(8,128)(2,1)S(1)}, u32[]{:S(2)}, u32[]{:S(2)}) %collective-permute-start.17) | collective-permute-done | bytes 131104 | tf_op jit(solution)/shard_map/ppermute | solution.py:36
  58.1 3.0 %collective-permute-done.18.refs_2_ = bf16[256,256]{1,0:T(8,128)(2,1)S(1)} collective-permute-done((bf16[256,256]{1,0:T(8,128)(2,1)S(1)}, bf16[256,256]{1,0:T(8,128)(2,1)S(1)}, u32[]{:S(2)}, u32[]{:S(2)}) %collective-permute-start.18) | collective-permute-done | bytes 131104 | tf_op jit(solution)/shard_map/ppermute | solution.py:36
  61.2 2.0 %section1_back_context.1 = (bf16[256,1024]{1,0:T(8,128)(2,1)}, bf16[256,256]{1,0:T(8,128)(2,1)}) custom-call(bf16[256,256]{1,0:T(8,128)(2,1)S(1)} %get-tuple-element.25.refs_0_, bf16[256,256]{1,0:T(8,128)(2,1)S(1)} %collective-permute-done.17.refs_1_, bf16[256,256]{1,0:T(8,128)(2,1)S(1)} %collective-permute-done.18.refs_2_, ...), custom_call_target="tpu_custom_call" | custom-call | flops 805306368 | bytes 2097152 | tf_op jit(solution)/shard_map/section1_back_context/pallas_call | solution.py:398
  (22 shorter events, 0.1 us)
Async XLA Ops:
  2.0 5.7 %collective-permute-start = (s32[4,128]{1,0:T(4,128)S(1)}, s32[4,128]{1,0:T(4,128)S(1)}, u32[]{:S(2)}, u32[]{:S(2)}) collective-permute-start(s32[4,128]{1,0:T(4,128)S(1)} %bitcast_add_fusion.refs_0_), channel_id=1, source_target_pairs={{0,8},{8,0},{16,24},{24,16},{1,9},{9,1},{17,25},{25,17},{2,10},{10... | collective-permute-start | bytes 6152 | tf_op jit(solution)/shard_map/ppermute | solution.py:36
  7.6 2.8 %copy-start.1 = (bf16[1,256,1024]{2,1,0:T(8,128)(2,1)S(1)}, bf16[1,256,1024]{2,1,0:T(8,128)(2,1)}, u32[]{:S(2)}) copy-start(bf16[1,256,1024]{2,1,0:T(8,128)(2,1)} %param.17) | copy-start | bytes 1572868
  7.7 5.8 %copy-start = (bf16[1024,1024]{1,0:T(8,128)(2,1)S(1)}, bf16[1024,1024]{1,0:T(8,128)(2,1)}, u32[]{:S(2)}) copy-start(bf16[1024,1024]{1,0:T(8,128)(2,1)} %refs_3_.1) | copy-start | bytes 6291460
  7.7 20.1 %collective-permute-start.5 = (bf16[4,1024,256]{2,1,0:T(8,128)(2,1)S(1)}, bf16[4,1024,256]{2,1,0:T(8,128)(2,1)S(1)}, u32[]{:S(2)}, u32[]{:S(2)}) collective-permute-start(bf16[4,1024,256]{2,1,0:T(8,128)(2,1)S(1)} %hold.1.refs_10_.refs_6_), channel_id=1, source_target_pairs={{0,1},{1,0},{2,3},{3,2},{4,5},{5,4},{6,7},{7,6},{8,9},{9,8},{10,11... | collective-permute-start | bytes 6291464 | tf_op jit(solution)/shard_map/ppermute | solution.py:36
  7.8 5.7 %collective-permute-start.1 = (s32[8,128]{1,0:T(8,128)S(1)}, s32[8,128]{1,0:T(8,128)S(1)}, u32[]{:S(2)}, u32[]{:S(2)}) collective-permute-start(s32[8,128]{1,0:T(8,128)S(1)} %pad_add_fusion), channel_id=1, source_target_pairs={{0,16},{8,24},{16,0},{24,8},{1,17},{9,25},{17,1},{25,9},{2,18},{10... | collective-permute-start | bytes 12296 | tf_op jit(solution)/shard_map/ppermute | solution.py:36
  10.4 14.0 %collective-permute-start.10 = (bf16[256,1024]{1,0:T(8,128)(2,1)S(1)}, bf16[256,1024]{1,0:T(8,128)(2,1)S(1)}, u32[]{:S(2)}, u32[]{:S(2)}) collective-permute-start(bf16[256,1024]{1,0:T(8,128)(2,1)S(1)} %bitcast.15), channel_id=1, source_target_pairs={{0,4},{2,6},{4,0},{6,2},{1,5},{3,7},{5,1},{7,3},{8,12},{10,14},{12... | collective-permute-start | bytes 1572872 | tf_op jit(solution)/shard_map/ppermute | solution.py:36
  12.0 13.7 %collective-permute-start.9 = (bf16[256,1024]{1,0:T(8,128)(2,1)S(1)}, bf16[256,1024]{1,0:T(8,128)(2,1)S(1)}, u32[]{:S(2)}, u32[]{:S(2)}) collective-permute-start(bf16[256,1024]{1,0:T(8,128)(2,1)S(1)} %bitcast.16), channel_id=1, source_target_pairs={{0,2},{2,0},{4,6},{6,4},{1,3},{3,1},{5,7},{7,5},{8,10},{10,8},{12,... | collective-permute-start | bytes 1572872 | tf_op jit(solution)/shard_map/ppermute | solution.py:36
  13.9 6.5 %collective-permute-start.3 = (bf16[256,256]{1,0:T(8,128)(2,1)S(1)}, bf16[256,256]{1,0:T(8,128)(2,1)S(1)}, u32[]{:S(2)}, u32[]{:S(2)}) collective-permute-start(bf16[256,256]{1,0:T(8,128)(2,1)S(1)} %fetch.2.refs_4_), channel_id=1, source_target_pairs={{0,8},{8,0},{16,24},{24,16},{1,9},{9,1},{17,25},{25,17},{2,10},{10... | collective-permute-start | bytes 393224 | tf_op jit(solution)/shard_map/ppermute | solution.py:36
  15.5 7.2 %collective-permute-start.2 = (bf16[256,256]{1,0:T(8,128)(2,1)S(1)}, bf16[256,256]{1,0:T(8,128)(2,1)S(1)}, u32[]{:S(2)}, u32[]{:S(2)}) collective-permute-start(bf16[256,256]{1,0:T(8,128)(2,1)S(1)} %get-tuple-element.17), channel_id=1, source_target_pairs={{0,8},{8,0},{16,24},{24,16},{1,9},{9,1},{17,25},{25,17},{2,10},{10... | collective-permute-start | bytes 393224 | tf_op jit(solution)/shard_map/ppermute | solution.py:36
  20.4 7.4 %collective-permute-start.4 = (bf16[256,256]{1,0:T(8,128)(2,1)S(1)}, bf16[256,256]{1,0:T(8,128)(2,1)S(1)}, u32[]{:S(2)}, u32[]{:S(2)}) collective-permute-start(bf16[256,256]{1,0:T(8,128)(2,1)S(1)} %merge.3.refs_0_), channel_id=1, source_target_pairs={{0,16},{8,24},{16,0},{24,8},{1,17},{9,25},{17,1},{25,9},{2,18},{10... | collective-permute-start | bytes 393224 | tf_op jit(solution)/shard_map/ppermute | solution.py:36
  22.6 8.8 %copy-start.3 = (s32[1,2,256,8]{2,3,1,0:T(8,128)S(1)}, s32[1,2,256,8]{2,3,1,0:T(8,128)}, u32[]{:S(2)}) copy-start(s32[1,2,256,8]{2,3,1,0:T(8,128)} %param.13) | copy-start | bytes 49156
  22.6 8.8 %copy-start.4 = (s32[1,2,256]{2,1,0:T(2,128)S(1)}, s32[1,2,256]{2,1,0:T(2,128)}, u32[]{:S(2)}) copy-start(s32[1,2,256]{2,1,0:T(2,128)} %seg_ref.1) | copy-start | bytes 6148
  25.7 9.3 %collective-permute-start.11 = (bf16[128,1024]{1,0:T(8,128)(2,1)S(1)}, bf16[128,1024]{1,0:T(8,128)(2,1)S(1)}, u32[]{:S(2)}, u32[]{:S(2)}) collective-permute-start(bf16[128,1024]{1,0:T(8,128)(2,1)S(1)} %get-tuple-element.19), channel_id=1, source_target_pairs={{0,2},{2,0},{4,6},{6,4},{1,3},{3,1},{5,7},{7,5},{8,10},{10,8},{12,... | collective-permute-start | bytes 786440 | tf_op jit(solution)/shard_map/ppermute | solution.py:36
  27.3 9.8 %collective-permute-start.12 = (bf16[128,1024]{1,0:T(8,128)(2,1)S(1)}, bf16[128,1024]{1,0:T(8,128)(2,1)S(1)}, u32[]{:S(2)}, u32[]{:S(2)}) collective-permute-start(bf16[128,1024]{1,0:T(8,128)(2,1)S(1)} %get-tuple-element.20), channel_id=1, source_target_pairs={{0,4},{2,6},{4,0},{6,2},{1,5},{3,7},{5,1},{7,3},{8,12},{10,14},{12... | collective-permute-start | bytes 786440 | tf_op jit(solution)/shard_map/ppermute | solution.py:36
  27.8 9.4 %collective-permute-start.6 = (bf16[256,256]{1,0:T(8,128)(2,1)S(1)}, bf16[256,256]{1,0:T(8,128)(2,1)S(1)}, u32[]{:S(2)}, u32[]{:S(2)}) collective-permute-start(bf16[256,256]{1,0:T(8,128)(2,1)S(1)} %merge.5.refs_0_), channel_id=1, source_target_pairs={{0,2},{2,0},{4,6},{6,4},{1,3},{3,1},{5,7},{7,5},{8,10},{10,8},{12,... | collective-permute-start | bytes 393224 | tf_op jit(solution)/shard_map/ppermute | solution.py:36
  28.4 11.4 %collective-permute-start.7 = (bf16[256,256]{1,0:T(8,128)(2,1)S(1)}, bf16[256,256]{1,0:T(8,128)(2,1)S(1)}, u32[]{:S(2)}, u32[]{:S(2)}) collective-permute-start(bf16[256,256]{1,0:T(8,128)(2,1)S(1)} %merge.5.refs_0_), channel_id=1, source_target_pairs={{0,4},{2,6},{4,0},{6,2},{1,5},{3,7},{5,1},{7,3},{8,12},{10,14},{12... | collective-permute-start | bytes 393224 | tf_op jit(solution)/shard_map/ppermute | solution.py:36
  30.0 9.9 %collective-permute-start.8 = (bf16[256,256]{1,0:T(8,128)(2,1)S(1)}, bf16[256,256]{1,0:T(8,128)(2,1)S(1)}, u32[]{:S(2)}, u32[]{:S(2)}) collective-permute-start(bf16[256,256]{1,0:T(8,128)(2,1)S(1)} %merge.5.refs_0_), channel_id=1, source_target_pairs={{0,6},{2,4},{4,2},{6,0},{1,7},{3,5},{5,3},{7,1},{8,14},{10,12},{12... | collective-permute-start | bytes 393224 | tf_op jit(solution)/shard_map/ppermute | solution.py:36
  41.3 9.1 %collective-permute-start.16 = (bf16[4,256,1024]{2,1,0:T(8,128)(2,1)S(1)}, bf16[4,256,1024]{2,1,0:T(8,128)(2,1)S(1)}, u32[]{:S(2)}, u32[]{:S(2)}) collective-permute-start(bf16[4,256,1024]{2,1,0:T(8,128)(2,1)S(1)} %get-tuple-element.24.refs_8_), channel_id=1, source_target_pairs={{0,1},{1,0},{2,3},{3,2},{4,5},{5,4},{6,7},{7,6},{8,9},{9,8},{10,11... | collective-permute-start | bytes 6291464 | tf_op jit(solution)/shard_map/ppermute | solution.py:36
  41.4 6.4 %collective-permute-start.13 = (bf16[256,256]{1,0:T(8,128)(2,1)S(1)}, bf16[256,256]{1,0:T(8,128)(2,1)S(1)}, u32[]{:S(2)}, u32[]{:S(2)}) collective-permute-start(bf16[256,256]{1,0:T(8,128)(2,1)S(1)} %get-tuple-element.22.refs_0_), channel_id=1, source_target_pairs={{0,2},{2,0},{4,6},{6,4},{1,3},{3,1},{5,7},{7,5},{8,10},{10,8},{12,... | collective-permute-start | bytes 393224 | tf_op jit(solution)/shard_map/ppermute | solution.py:36
  42.0 8.4 %collective-permute-start.14 = (bf16[256,256]{1,0:T(8,128)(2,1)S(1)}, bf16[256,256]{1,0:T(8,128)(2,1)S(1)}, u32[]{:S(2)}, u32[]{:S(2)}) collective-permute-start(bf16[256,256]{1,0:T(8,128)(2,1)S(1)} %get-tuple-element.22.refs_0_), channel_id=1, source_target_pairs={{0,4},{2,6},{4,0},{6,2},{1,5},{3,7},{5,1},{7,3},{8,12},{10,14},{12... | collective-permute-start | bytes 393224 | tf_op jit(solution)/shard_map/ppermute | solution.py:36
  43.2 7.2 %collective-permute-start.15 = (bf16[256,256]{1,0:T(8,128)(2,1)S(1)}, bf16[256,256]{1,0:T(8,128)(2,1)S(1)}, u32[]{:S(2)}, u32[]{:S(2)}) collective-permute-start(bf16[256,256]{1,0:T(8,128)(2,1)S(1)} %get-tuple-element.22.refs_0_), channel_id=1, source_target_pairs={{0,6},{2,4},{4,2},{6,0},{1,7},{3,5},{5,3},{7,1},{8,14},{10,12},{12... | collective-permute-start | bytes 393224 | tf_op jit(solution)/shard_map/ppermute | solution.py:36
  50.4 5.3 %copy-start.5 = (bf16[256]{0:T(256)(128)(2,1)S(1)}, bf16[256]{0:T(256)(128)(2,1)}, u32[]{:S(2)}) copy-start(bf16[256]{0:T(256)(128)(2,1)} %param.19) | copy-start | bytes 1540
  50.4 10.8 %copy-start.2 = (bf16[1024,256]{1,0:T(8,128)(2,1)S(1)}, bf16[1024,256]{1,0:T(8,128)(2,1)}, u32[]{:S(2)}) copy-start(bf16[1024,256]{1,0:T(8,128)(2,1)} %refs_6_.1) | copy-start | bytes 1572868
  52.2 6.0 %collective-permute-start.17 = (bf16[256,256]{1,0:T(8,128)(2,1)S(1)}, bf16[256,256]{1,0:T(8,128)(2,1)S(1)}, u32[]{:S(2)}, u32[]{:S(2)}) collective-permute-start(bf16[256,256]{1,0:T(8,128)(2,1)S(1)} %get-tuple-element.25.refs_0_), channel_id=1, source_target_pairs={{0,2},{2,0},{4,6},{6,4},{1,3},{3,1},{5,7},{7,5},{8,10},{10,8},{12,... | collective-permute-start | bytes 393224 | tf_op jit(solution)/shard_map/ppermute | solution.py:36
  53.7 7.4 %collective-permute-start.18 = (bf16[256,256]{1,0:T(8,128)(2,1)S(1)}, bf16[256,256]{1,0:T(8,128)(2,1)S(1)}, u32[]{:S(2)}, u32[]{:S(2)}) collective-permute-start(bf16[256,256]{1,0:T(8,128)(2,1)S(1)} %get-tuple-element.25.refs_0_), channel_id=1, source_target_pairs={{0,4},{2,6},{4,0},{6,2},{1,5},{3,7},{5,1},{7,3},{8,12},{10,14},{12... | collective-permute-start | bytes 393224 | tf_op jit(solution)/shard_map/ppermute | solution.py:36
  54.3 6.8 %collective-permute-start.19 = (bf16[256,256]{1,0:T(8,128)(2,1)S(1)}, bf16[256,256]{1,0:T(8,128)(2,1)S(1)}, u32[]{:S(2)}, u32[]{:S(2)}) collective-permute-start(bf16[256,256]{1,0:T(8,128)(2,1)S(1)} %get-tuple-element.25.refs_0_), channel_id=1, source_target_pairs={{0,6},{2,4},{4,2},{6,0},{1,7},{3,5},{5,3},{7,1},{8,14},{10,12},{12... | collective-permute-start | bytes 393224 | tf_op jit(solution)/shard_map/ppermute | solution.py:36

commit v8 on v7

--- a/solution.py
+++ b/solution.py
@@ -90,7 +90,7 @@
         out_specs=[VMEM] * steps,
         compiler_params=params(),
         cost_estimate=pl.CostEstimate(
-            flops=8 * steps * rows * width * table.shape[0],
+            flops=2 * steps * rows * width * table.shape[0],
             bytes_accessed=2 * width * table.shape[0],
             transcendentals=0,
         ),
@@ -165,15 +165,17 @@
     return asked
 
 
-def gather_in(blocks, first, then):
-    blocks, step = dict(enumerate(blocks)), 1
+def gather_in(blocks, then):
+    blocks, step, after, last = dict(enumerate(blocks)), 1, None, []
     while step < lax.axis_size("dp"):
         at_end = 2 * step == lax.axis_size("dp")
         for k in sorted((k for k in blocks if k & step), reverse=True):
             got = exchange(blocks.pop(k), "dp", step)
-            after = then(blocks[k ^ step]) if at_end else first
-            blocks[k ^ step] = merge(blocks[k ^ step], got, after)
-            first = [blocks[k ^ step]]
+            blocks[k ^ step] = merge(blocks[k ^ step], got, last if at_end else after or [])
+            if after is None:
+                after, last = then(blocks[k ^ step])
+            else:
+                after = [blocks[k ^ step]]
         step = 2 * step
     return blocks[0]
 
@@ -341,12 +343,14 @@
         found = fetch(asked[:-1], batches, table, part, late) + late
 
         def then(first):
+            rest = []
             if mp_count == 4:
-                o_pieces.extend(relay(near, far, "mp", [first]))
+                rest = relay(near, far, "mp", [first])
+                o_pieces.extend(rest)
                 places.extend([(3, 0), (3, local_cols // 2)])
-            return [w_other]
-
-        piece = gather_in(found, [], then)
+            return [first], [w_other]
+
+        piece = gather_in(found, then)
     else:
         piece = fetch_rows_padded(item_owner[:, 0], item_row, table, part)
         piece = lax.dynamic_index_in_dim(

time: 63.4 us -> 60.8 us (0.959)
  waiting for transfers between devices: 26.7 us -> 21.6 us
  starting transfers between devices: 24.9 us -> 26.5 us
  local copies, waits for them, and re-layouts: 0.04 us -> 0.96 us
    ppermute x20, waiting for transfers between devices: 26.7 us -> 21.6 us  [exchange(): return lax.ppermute(value, axis, pairs)]
    ppermute x20, starting transfers between devices: 24.9 us -> 26.5 us  [exchange(): return lax.ppermute(value, axis, pairs)]
    unnamed x12, local copies, waits for them, and re-layouts: 0.03 us -> 0.95 us
  transfers between devices with their start and end apart: 20 -> 20, of which waited for: 12 -> 10; matrix products, arithmetic and copies ran while one was open for 4% -> 4% of each run, Pallas kernels for 2% -> 2%
where the time goes in v8:
time: 60.8 us; the launch traced here: 60.5 us
  starting transfers between devices  26.5 us (44%)
  waiting for transfers between devices  21.6 us (36%)
  Pallas kernels  6.73 us (11%)
  other arithmetic  3.99 us (7%)
  local copies, waits for them, and re-layouts  0.96 us (2%)
  between operations  0.79 us (1%)
    ppermute x20, starting transfers between devices, exchange(): return lax.ppermute(value, axis, pairs)  26.5 us
    ppermute x20, waiting for transfers between devices, exchange(): return lax.ppermute(value, axis, pairs)  21.6 us
    pallas_call x1, Pallas kernels, on_device(): pl.pallas_call(functools.partial(last_kernel, mp_count), out_shape=[x_sha...  2.04 us
    mul x1, other arithmetic, on_device(): w_own = jnp.transpose(w_in[0], (1, 0, 2)) * gains[0][None, :, None]  1.9 us
    pallas_call x1, Pallas kernels, on_device(): pl.pallas_call(functools.partial(middle_kernel, mp_count), out_shape=[gat...  1.75 us
    pallas_call x1, Pallas kernels, on_device(): pl.pallas_call(functools.partial(first_kernel, mp_count, places), out_sha...  1.48 us
  transfers between devices with their start and end apart: 20, of which 10 were waited for; matrix products, arithmetic and copies ran while one was open for 4% of the time, Pallas kernels for 2%

profile of v8, /device:TPU:0, one launch (start us, length us, event | category | flops | bytes accessed | tf_op | source)
XLA Modules:
  0.0 60.5 jit_solution(17803072623651231413)
XLA Ops:
  0.6 0.7 %broadcast_multiply_fusion = s32[512,1]{0,1:T(1,128)S(1)} fusion(s32[512,1]{0,1:T(1,128)} %param.10), kind=kLoop, calls=%fused_computation.4 | loop fusion | flops 512 | bytes 4096 | tf_op jit(solution)/shard_map/mul | solution.py:338
  1.3 0.7 %bitcast_add_fusion.refs_0_ = s32[4,128]{1,0:T(4,128)S(1)} fusion(s32[4,128]{1,0:T(4,128)S(1)} %bitcast.19, s32[512]{0:T(512)} %param.11), kind=kLoop, calls=%fused_computation.3 | loop fusion | flops 512 | bytes 6144 | tf_op jit(solution)/shard_map/add | solution.py:338
  2.0 3.0 %collective-permute-start = (s32[4,128]{1,0:T(4,128)S(1)}, s32[4,128]{1,0:T(4,128)S(1)}, u32[]{:S(2)}, u32[]{:S(2)}) collective-permute-start(s32[4,128]{1,0:T(4,128)S(1)} %bitcast_add_fusion.refs_0_), channel_id=1, source_target_pairs={{0,8},{8,0},{16,24},{24,16},{1,9},{9,1},{17,25},{25,17},{2,10},{10... | collective-permute-start | bytes 6152 | tf_op jit(solution)/shard_map/ppermute | solution.py:36
  5.0 0.7 %reduce = bf16[1024]{0:T(1024)(128)(2,1)S(1)} reduce(bf16[1,1024]{1,0:T(2,128)(2,1)} %param.15, bf16[]{:T(256)} %constant.7), dimensions={0}, to_apply=%param.15.reduce_sub_computation | reduce | bytes 4098 | tf_op args[5]
  5.7 1.9 %fusion.refs_0_ = bf16[4,1024,256]{2,1,0:T(8,128)(2,1)S(1)} fusion(bf16[1,1024,4,256]{3,2,1,0:T(4,128)(2,1)} %param.16, bf16[1024]{0:T(1024)(128)(2,1)S(1)} %reduce), kind=kLoop, calls=%fused_computation.1 | loop fusion | flops 1048576 | bytes 4196352 | tf_op jit(solution)/shard_map/mul | solution.py:327
  7.6 0.0 copy-start.1
  7.7 0.0 copy-start
  7.7 0.1 collective-permute-start.5
  7.8 0.9 %copy-done.1 = bf16[1,256,1024]{2,1,0:T(8,128)(2,1)S(1)} copy-done((bf16[1,256,1024]{2,1,0:T(8,128)(2,1)S(1)}, bf16[1,256,1024]{2,1,0:T(8,128)(2,1)}, u32[]{:S(2)}) %copy-start.1) | copy-done | bytes 524312
  8.7 1.5 %collective-permute-start.10 = (bf16[256,1024]{1,0:T(8,128)(2,1)S(1)}, bf16[256,1024]{1,0:T(8,128)(2,1)S(1)}, u32[]{:S(2)}, u32[]{:S(2)}) collective-permute-start(bf16[256,1024]{1,0:T(8,128)(2,1)S(1)} %bitcast.15), channel_id=1, source_target_pairs={{0,4},{2,6},{4,0},{6,2},{1,5},{3,7},{5,1},{7,3},{8,12},{10,14},{12... | collective-permute-start | bytes 1572872 | tf_op jit(solution)/shard_map/ppermute | solution.py:36
  10.2 1.5 %collective-permute-start.9 = (bf16[256,1024]{1,0:T(8,128)(2,1)S(1)}, bf16[256,1024]{1,0:T(8,128)(2,1)S(1)}, u32[]{:S(2)}, u32[]{:S(2)}) collective-permute-start(bf16[256,1024]{1,0:T(8,128)(2,1)S(1)} %bitcast.16), channel_id=1, source_target_pairs={{0,2},{2,0},{4,6},{6,4},{1,3},{3,1},{5,7},{7,5},{8,10},{10,8},{12,... | collective-permute-start | bytes 1572872 | tf_op jit(solution)/shard_map/ppermute | solution.py:36
  11.7 2.6 %collective-permute-start.1 = (s32[8,128]{1,0:T(8,128)S(1)}, s32[8,128]{1,0:T(8,128)S(1)}, u32[]{:S(2)}, u32[]{:S(2)}) collective-permute-start(s32[8,128]{1,0:T(8,128)S(1)} %pad_add_fusion), channel_id=1, source_target_pairs={{0,16},{8,24},{16,0},{24,8},{1,17},{9,25},{17,1},{25,9},{2,18},{10... | collective-permute-start | bytes 12296 | tf_op jit(solution)/shard_map/ppermute | solution.py:36
  14.3 1.9 %collective-permute-done.1 = s32[8,128]{1,0:T(8,128)S(1)} collective-permute-done((s32[8,128]{1,0:T(8,128)S(1)}, s32[8,128]{1,0:T(8,128)S(1)}, u32[]{:S(2)}, u32[]{:S(2)}) %collective-permute-start.1) | collective-permute-done | bytes 4128 | tf_op jit(solution)/shard_map/ppermute | solution.py:36
  16.2 0.4 fetch.2.refs_4_
  16.6 0.5 collective-permute-start.3
  17.1 0.7 %fetch.3 = (bf16[256,256]{1,0:T(8,128)(2,1)S(1)}, bf16[256,256]{1,0:T(8,128)(2,1)S(1)}, bf16[256,256]{1,0:T(8,128)(2,1)S(1)}) custom-call(s32[4,128]{1,0:T(4,128)S(1)} %bitcast_add_fusion.refs_0_, s32[4,128]{1,0:T(4,128)S(1)} %collective-permute-done.refs_1_, s32[4,128]{1,0:T(4,128)S(1)} %get-tuple-element.31.refs_2_, bf16[1024,1024]{1,0:T(8,128)(2,1)S(1)} %copy-done, ...), custom_call_target="tpu_custom_call" | custom-call | flops 402653184 | bytes 524288 | tf_op jit(solution)/shard_map/fetch/pallas_call | solution.py:86
  17.8 1.6 %collective-permute-start.2 = (bf16[256,256]{1,0:T(8,128)(2,1)S(1)}, bf16[256,256]{1,0:T(8,128)(2,1)S(1)}, u32[]{:S(2)}, u32[]{:S(2)}) collective-permute-start(bf16[256,256]{1,0:T(8,128)(2,1)S(1)} %get-tuple-element.17), channel_id=1, source_target_pairs={{0,8},{8,0},{16,24},{24,16},{1,9},{9,1},{17,25},{25,17},{2,10},{10... | collective-permute-start | bytes 393224 | tf_op jit(solution)/shard_map/ppermute | solution.py:36
  19.5 2.2 %collective-permute-done.3.b_ref = bf16[256,256]{1,0:T(8,128)(2,1)S(1)} collective-permute-done((bf16[256,256]{1,0:T(8,128)(2,1)S(1)}, bf16[256,256]{1,0:T(8,128)(2,1)S(1)}, u32[]{:S(2)}, u32[]{:S(2)}) %collective-permute-start.3) | collective-permute-done | bytes 131104 | tf_op jit(solution)/shard_map/ppermute | solution.py:36
  21.7 0.0 copy-start.3
  21.7 0.0 copy-start.4
  21.7 3.8 %collective-permute-start.4 = (bf16[256,256]{1,0:T(8,128)(2,1)S(1)}, bf16[256,256]{1,0:T(8,128)(2,1)S(1)}, u32[]{:S(2)}, u32[]{:S(2)}) collective-permute-start(bf16[256,256]{1,0:T(8,128)(2,1)S(1)} %merge.3.refs_0_), channel_id=1, source_target_pairs={{0,16},{8,24},{16,0},{24,8},{1,17},{9,25},{17,1},{25,9},{2,18},{10... | collective-permute-start | bytes 393224 | tf_op jit(solution)/shard_map/ppermute | solution.py:36
  25.5 0.0 collective-permute-done.10.far_ref.refs_6_
  25.5 0.1 cut.1
  25.5 0.6 %collective-permute-start.11 = (bf16[128,1024]{1,0:T(8,128)(2,1)S(1)}, bf16[128,1024]{1,0:T(8,128)(2,1)S(1)}, u32[]{:S(2)}, u32[]{:S(2)}) collective-permute-start(bf16[128,1024]{1,0:T(8,128)(2,1)S(1)} %get-tuple-element.19), channel_id=1, source_target_pairs={{0,2},{2,0},{4,6},{6,4},{1,3},{3,1},{5,7},{7,5},{8,10},{10,8},{12,... | collective-permute-start | bytes 786440 | tf_op jit(solution)/shard_map/ppermute | solution.py:36
  26.1 0.5 collective-permute-start.12
  26.7 2.6 %collective-permute-done.4.b_ref = bf16[256,256]{1,0:T(8,128)(2,1)S(1)} collective-permute-done((bf16[256,256]{1,0:T(8,128)(2,1)S(1)}, bf16[256,256]{1,0:T(8,128)(2,1)S(1)}, u32[]{:S(2)}, u32[]{:S(2)}) %collective-permute-start.4) | collective-permute-done | bytes 131104 | tf_op jit(solution)/shard_map/ppermute | solution.py:36
  29.3 0.6 collective-permute-start.6
  29.9 0.5 collective-permute-start.7
  30.4 2.4 %collective-permute-start.8 = (bf16[256,256]{1,0:T(8,128)(2,1)S(1)}, bf16[256,256]{1,0:T(8,128)(2,1)S(1)}, u32[]{:S(2)}, u32[]{:S(2)}) collective-permute-start(bf16[256,256]{1,0:T(8,128)(2,1)S(1)} %merge.5.refs_0_), channel_id=1, source_target_pairs={{0,6},{2,4},{4,2},{6,0},{1,7},{3,5},{5,3},{7,1},{8,14},{10,12},{12... | collective-permute-start | bytes 393224 | tf_op jit(solution)/shard_map/ppermute | solution.py:36
  32.9 0.3 prepare.1
  33.2 0.9 %collective-permute-done.12.refs_8_ = bf16[128,1024]{1,0:T(8,128)(2,1)S(1)} collective-permute-done((bf16[128,1024]{1,0:T(8,128)(2,1)S(1)}, bf16[128,1024]{1,0:T(8,128)(2,1)S(1)}, u32[]{:S(2)}, u32[]{:S(2)}) %collective-permute-start.12) | collective-permute-done | bytes 262176 | tf_op jit(solution)/shard_map/ppermute | solution.py:36
  34.1 0.3 collective-permute-done.6.refs_1_
  34.3 2.5 %collective-permute-done.7.refs_2_ = bf16[256,256]{1,0:T(8,128)(2,1)S(1)} collective-permute-done((bf16[256,256]{1,0:T(8,128)(2,1)S(1)}, bf16[256,256]{1,0:T(8,128)(2,1)S(1)}, u32[]{:S(2)}, u32[]{:S(2)}) %collective-permute-start.7) | collective-permute-done | bytes 131104 | tf_op jit(solution)/shard_map/ppermute | solution.py:36
  36.9 1.5 %section0_front.1 = (bf16[256,256]{1,0:T(8,128)(2,1)S(1)}, bf16[256,1024]{1,0:T(8,128)(2,1)S(1)}, bf16[4,256,1024]{2,1,0:T(8,128)(2,1)S(1)}) custom-call(bf16[256,256]{1,0:T(8,128)(2,1)S(1)} %merge.5.refs_0_, bf16[256,256]{1,0:T(8,128)(2,1)S(1)} %collective-permute-done.6.refs_1_, bf16[256,256]{1,0:T(8,128)(2,1)S(1)} %collective-permute-done.7.refs_2_, ...), custom_call_target="tpu_custom_call" | custom-call | flops 603979776 | bytes 2097152 | tf_op jit(solution)/shard_map/section0_front/pallas_call | solution.py:370
  38.4 0.1 collective-permute-start.16
  38.5 1.1 %collective-permute-start.13 = (bf16[256,256]{1,0:T(8,128)(2,1)S(1)}, bf16[256,256]{1,0:T(8,128)(2,1)S(1)}, u32[]{:S(2)}, u32[]{:S(2)}) collective-permute-start(bf16[256,256]{1,0:T(8,128)(2,1)S(1)} %get-tuple-element.22.refs_0_), channel_id=1, source_target_pairs={{0,2},{2,0},{4,6},{6,4},{1,3},{3,1},{5,7},{7,5},{8,10},{10,8},{12,... | collective-permute-start | bytes 393224 | tf_op jit(solution)/shard_map/ppermute | solution.py:36
  39.5 1.4 %collective-permute-start.14 = (bf16[256,256]{1,0:T(8,128)(2,1)S(1)}, bf16[256,256]{1,0:T(8,128)(2,1)S(1)}, u32[]{:S(2)}, u32[]{:S(2)}) collective-permute-start(bf16[256,256]{1,0:T(8,128)(2,1)S(1)} %get-tuple-element.22.refs_0_), channel_id=1, source_target_pairs={{0,4},{2,6},{4,0},{6,2},{1,5},{3,7},{5,1},{7,3},{8,12},{10,14},{12... | collective-permute-start | bytes 393224 | tf_op jit(solution)/shard_map/ppermute | solution.py:36
  40.9 1.1 %collective-permute-start.15 = (bf16[256,256]{1,0:T(8,128)(2,1)S(1)}, bf16[256,256]{1,0:T(8,128)(2,1)S(1)}, u32[]{:S(2)}, u32[]{:S(2)}) collective-permute-start(bf16[256,256]{1,0:T(8,128)(2,1)S(1)} %get-tuple-element.22.refs_0_), channel_id=1, source_target_pairs={{0,6},{2,4},{4,2},{6,0},{1,7},{3,5},{5,3},{7,1},{8,14},{10,12},{12... | collective-permute-start | bytes 393224 | tf_op jit(solution)/shard_map/ppermute | solution.py:36
  42.0 2.8 %collective-permute-done.13.refs_1_ = bf16[256,256]{1,0:T(8,128)(2,1)S(1)} collective-permute-done((bf16[256,256]{1,0:T(8,128)(2,1)S(1)}, bf16[256,256]{1,0:T(8,128)(2,1)S(1)}, u32[]{:S(2)}, u32[]{:S(2)}) %collective-permute-start.13) | collective-permute-done | bytes 131104 | tf_op jit(solution)/shard_map/ppermute | solution.py:36
  44.8 3.1 %collective-permute-done.14.refs_2_ = bf16[256,256]{1,0:T(8,128)(2,1)S(1)} collective-permute-done((bf16[256,256]{1,0:T(8,128)(2,1)S(1)}, bf16[256,256]{1,0:T(8,128)(2,1)S(1)}, u32[]{:S(2)}, u32[]{:S(2)}) %collective-permute-start.14) | collective-permute-done | bytes 131104 | tf_op jit(solution)/shard_map/ppermute | solution.py:36
  47.9 0.0 copy-start.2
  47.9 1.8 %section0_back_section1_front.1 = (bf16[256,256]{1,0:T(8,128)(2,1)S(1)}, bf16[256,1024]{1,0:T(8,128)(2,1)S(1)}) custom-call(bf16[256,256]{1,0:T(8,128)(2,1)S(1)} %get-tuple-element.22.refs_0_, bf16[256,256]{1,0:T(8,128)(2,1)S(1)} %collective-permute-done.13.refs_1_, bf16[256,256]{1,0:T(8,128)(2,1)S(1)} %collective-permute-done.14.refs_2_, ...), custom_call_target="tpu_custom_call" | custom-call | flops 1140850688 | bytes 4194304 | tf_op jit(solution)/shard_map/section0_back_section1_front/pallas_call | solution.py:388
  49.7 1.2 %collective-permute-start.17 = (bf16[256,256]{1,0:T(8,128)(2,1)S(1)}, bf16[256,256]{1,0:T(8,128)(2,1)S(1)}, u32[]{:S(2)}, u32[]{:S(2)}) collective-permute-start(bf16[256,256]{1,0:T(8,128)(2,1)S(1)} %get-tuple-element.25.refs_0_), channel_id=1, source_target_pairs={{0,2},{2,0},{4,6},{6,4},{1,3},{3,1},{5,7},{7,5},{8,10},{10,8},{12,... | collective-permute-start | bytes 393224 | tf_op jit(solution)/shard_map/ppermute | solution.py:36
  50.9 0.8 %collective-permute-start.18 = (bf16[256,256]{1,0:T(8,128)(2,1)S(1)}, bf16[256,256]{1,0:T(8,128)(2,1)S(1)}, u32[]{:S(2)}, u32[]{:S(2)}) collective-permute-start(bf16[256,256]{1,0:T(8,128)(2,1)S(1)} %get-tuple-element.25.refs_0_), channel_id=1, source_target_pairs={{0,4},{2,6},{4,0},{6,2},{1,5},{3,7},{5,1},{7,3},{8,12},{10,14},{12... | collective-permute-start | bytes 393224 | tf_op jit(solution)/shard_map/ppermute | solution.py:36
  51.7 1.6 %collective-permute-start.19 = (bf16[256,256]{1,0:T(8,128)(2,1)S(1)}, bf16[256,256]{1,0:T(8,128)(2,1)S(1)}, u32[]{:S(2)}, u32[]{:S(2)}) collective-permute-start(bf16[256,256]{1,0:T(8,128)(2,1)S(1)} %get-tuple-element.25.refs_0_), channel_id=1, source_target_pairs={{0,6},{2,4},{4,2},{6,0},{1,7},{3,5},{5,3},{7,1},{8,14},{10,12},{12... | collective-permute-start | bytes 393224 | tf_op jit(solution)/shard_map/ppermute | solution.py:36
  53.3 2.2 %collective-permute-done.17.refs_1_ = bf16[256,256]{1,0:T(8,128)(2,1)S(1)} collective-permute-done((bf16[256,256]{1,0:T(8,128)(2,1)S(1)}, bf16[256,256]{1,0:T(8,128)(2,1)S(1)}, u32[]{:S(2)}, u32[]{:S(2)}) %collective-permute-start.17) | collective-permute-done | bytes 131104 | tf_op jit(solution)/shard_map/ppermute | solution.py:36
  55.5 3.0 %collective-permute-done.18.refs_2_ = bf16[256,256]{1,0:T(8,128)(2,1)S(1)} collective-permute-done((bf16[256,256]{1,0:T(8,128)(2,1)S(1)}, bf16[256,256]{1,0:T(8,128)(2,1)S(1)}, u32[]{:S(2)}, u32[]{:S(2)}) %collective-permute-start.18) | collective-permute-done | bytes 131104 | tf_op jit(solution)/shard_map/ppermute | solution.py:36
  58.5 2.0 %section1_back_context.1 = (bf16[256,1024]{1,0:T(8,128)(2,1)}, bf16[256,256]{1,0:T(8,128)(2,1)}) custom-call(bf16[256,256]{1,0:T(8,128)(2,1)S(1)} %get-tuple-element.25.refs_0_, bf16[256,256]{1,0:T(8,128)(2,1)S(1)} %collective-permute-done.17.refs_1_, bf16[256,256]{1,0:T(8,128)(2,1)S(1)} %collective-permute-done.18.refs_2_, ...), custom_call_target="tpu_custom_call" | custom-call | flops 805306368 | bytes 2097152 | tf_op jit(solution)/shard_map/section1_back_context/pallas_call | solution.py:402
  (22 shorter events, 0.1 us)
Async XLA Ops:
  2.0 5.7 %collective-permute-start = (s32[4,128]{1,0:T(4,128)S(1)}, s32[4,128]{1,0:T(4,128)S(1)}, u32[]{:S(2)}, u32[]{:S(2)}) collective-permute-start(s32[4,128]{1,0:T(4,128)S(1)} %bitcast_add_fusion.refs_0_), channel_id=1, source_target_pairs={{0,8},{8,0},{16,24},{24,16},{1,9},{9,1},{17,25},{25,17},{2,10},{10... | collective-permute-start | bytes 6152 | tf_op jit(solution)/shard_map/ppermute | solution.py:36
  7.6 1.0 %copy-start.1 = (bf16[1,256,1024]{2,1,0:T(8,128)(2,1)S(1)}, bf16[1,256,1024]{2,1,0:T(8,128)(2,1)}, u32[]{:S(2)}) copy-start(bf16[1,256,1024]{2,1,0:T(8,128)(2,1)} %param.17) | copy-start | bytes 1572868
  7.7 8.6 %copy-start = (bf16[1024,1024]{1,0:T(8,128)(2,1)S(1)}, bf16[1024,1024]{1,0:T(8,128)(2,1)}, u32[]{:S(2)}) copy-start(bf16[1024,1024]{1,0:T(8,128)(2,1)} %refs_3_.1) | copy-start | bytes 6291460
  7.7 21.6 %collective-permute-start.5 = (bf16[4,1024,256]{2,1,0:T(8,128)(2,1)S(1)}, bf16[4,1024,256]{2,1,0:T(8,128)(2,1)S(1)}, u32[]{:S(2)}, u32[]{:S(2)}) collective-permute-start(bf16[4,1024,256]{2,1,0:T(8,128)(2,1)S(1)} %hold.1.refs_10_.refs_6_), channel_id=1, source_target_pairs={{0,1},{1,0},{2,3},{3,2},{4,5},{5,4},{6,7},{7,6},{8,9},{9,8},{10,11... | collective-permute-start | bytes 6291464 | tf_op jit(solution)/shard_map/ppermute | solution.py:36
  8.7 16.8 %collective-permute-start.10 = (bf16[256,1024]{1,0:T(8,128)(2,1)S(1)}, bf16[256,1024]{1,0:T(8,128)(2,1)S(1)}, u32[]{:S(2)}, u32[]{:S(2)}) collective-permute-start(bf16[256,1024]{1,0:T(8,128)(2,1)S(1)} %bitcast.15), channel_id=1, source_target_pairs={{0,4},{2,6},{4,0},{6,2},{1,5},{3,7},{5,1},{7,3},{8,12},{10,14},{12... | collective-permute-start | bytes 1572872 | tf_op jit(solution)/shard_map/ppermute | solution.py:36
  10.2 15.3 %collective-permute-start.9 = (bf16[256,1024]{1,0:T(8,128)(2,1)S(1)}, bf16[256,1024]{1,0:T(8,128)(2,1)S(1)}, u32[]{:S(2)}, u32[]{:S(2)}) collective-permute-start(bf16[256,1024]{1,0:T(8,128)(2,1)S(1)} %bitcast.16), channel_id=1, source_target_pairs={{0,2},{2,0},{4,6},{6,4},{1,3},{3,1},{5,7},{7,5},{8,10},{10,8},{12,... | collective-permute-start | bytes 1572872 | tf_op jit(solution)/shard_map/ppermute | solution.py:36
  11.7 4.5 %collective-permute-start.1 = (s32[8,128]{1,0:T(8,128)S(1)}, s32[8,128]{1,0:T(8,128)S(1)}, u32[]{:S(2)}, u32[]{:S(2)}) collective-permute-start(s32[8,128]{1,0:T(8,128)S(1)} %pad_add_fusion), channel_id=1, source_target_pairs={{0,16},{8,24},{16,0},{24,8},{1,17},{9,25},{17,1},{25,9},{2,18},{10... | collective-permute-start | bytes 12296 | tf_op jit(solution)/shard_map/ppermute | solution.py:36
  16.6 5.0 %collective-permute-start.3 = (bf16[256,256]{1,0:T(8,128)(2,1)S(1)}, bf16[256,256]{1,0:T(8,128)(2,1)S(1)}, u32[]{:S(2)}, u32[]{:S(2)}) collective-permute-start(bf16[256,256]{1,0:T(8,128)(2,1)S(1)} %fetch.2.refs_4_), channel_id=1, source_target_pairs={{0,8},{8,0},{16,24},{24,16},{1,9},{9,1},{17,25},{25,17},{2,10},{10... | collective-permute-start | bytes 393224 | tf_op jit(solution)/shard_map/ppermute | solution.py:36
  17.8 8.8 %collective-permute-start.2 = (bf16[256,256]{1,0:T(8,128)(2,1)S(1)}, bf16[256,256]{1,0:T(8,128)(2,1)S(1)}, u32[]{:S(2)}, u32[]{:S(2)}) collective-permute-start(bf16[256,256]{1,0:T(8,128)(2,1)S(1)} %get-tuple-element.17), channel_id=1, source_target_pairs={{0,8},{8,0},{16,24},{24,16},{1,9},{9,1},{17,25},{25,17},{2,10},{10... | collective-permute-start | bytes 393224 | tf_op jit(solution)/shard_map/ppermute | solution.py:36
  21.7 11.2 %copy-start.3 = (s32[1,2,256,8]{2,3,1,0:T(8,128)S(1)}, s32[1,2,256,8]{2,3,1,0:T(8,128)}, u32[]{:S(2)}) copy-start(s32[1,2,256,8]{2,3,1,0:T(8,128)} %param.13) | copy-start | bytes 49156
  21.7 11.2 %copy-start.4 = (s32[1,2,256]{2,1,0:T(2,128)S(1)}, s32[1,2,256]{2,1,0:T(2,128)}, u32[]{:S(2)}) copy-start(s32[1,2,256]{2,1,0:T(2,128)} %seg_ref.1) | copy-start | bytes 6148
  21.7 7.6 %collective-permute-start.4 = (bf16[256,256]{1,0:T(8,128)(2,1)S(1)}, bf16[256,256]{1,0:T(8,128)(2,1)S(1)}, u32[]{:S(2)}, u32[]{:S(2)}) collective-permute-start(bf16[256,256]{1,0:T(8,128)(2,1)S(1)} %merge.3.refs_0_), channel_id=1, source_target_pairs={{0,16},{8,24},{16,0},{24,8},{1,17},{9,25},{17,1},{25,9},{2,18},{10... | collective-permute-start | bytes 393224 | tf_op jit(solution)/shard_map/ppermute | solution.py:36
  25.5 7.6 %collective-permute-start.11 = (bf16[128,1024]{1,0:T(8,128)(2,1)S(1)}, bf16[128,1024]{1,0:T(8,128)(2,1)S(1)}, u32[]{:S(2)}, u32[]{:S(2)}) collective-permute-start(bf16[128,1024]{1,0:T(8,128)(2,1)S(1)} %get-tuple-element.19), channel_id=1, source_target_pairs={{0,2},{2,0},{4,6},{6,4},{1,3},{3,1},{5,7},{7,5},{8,10},{10,8},{12,... | collective-permute-start | bytes 786440 | tf_op jit(solution)/shard_map/ppermute | solution.py:36
  26.1 7.9 %collective-permute-start.12 = (bf16[128,1024]{1,0:T(8,128)(2,1)S(1)}, bf16[128,1024]{1,0:T(8,128)(2,1)S(1)}, u32[]{:S(2)}, u32[]{:S(2)}) collective-permute-start(bf16[128,1024]{1,0:T(8,128)(2,1)S(1)} %get-tuple-element.20), channel_id=1, source_target_pairs={{0,4},{2,6},{4,0},{6,2},{1,5},{3,7},{5,1},{7,3},{8,12},{10,14},{12... | collective-permute-start | bytes 786440 | tf_op jit(solution)/shard_map/ppermute | solution.py:36
  29.3 5.0 %collective-permute-start.6 = (bf16[256,256]{1,0:T(8,128)(2,1)S(1)}, bf16[256,256]{1,0:T(8,128)(2,1)S(1)}, u32[]{:S(2)}, u32[]{:S(2)}) collective-permute-start(bf16[256,256]{1,0:T(8,128)(2,1)S(1)} %merge.5.refs_0_), channel_id=1, source_target_pairs={{0,2},{2,0},{4,6},{6,4},{1,3},{3,1},{5,7},{7,5},{8,10},{10,8},{12,... | collective-permute-start | bytes 393224 | tf_op jit(solution)/shard_map/ppermute | solution.py:36
  29.9 7.0 %collective-permute-start.7 = (bf16[256,256]{1,0:T(8,128)(2,1)S(1)}, bf16[256,256]{1,0:T(8,128)(2,1)S(1)}, u32[]{:S(2)}, u32[]{:S(2)}) collective-permute-start(bf16[256,256]{1,0:T(8,128)(2,1)S(1)} %merge.5.refs_0_), channel_id=1, source_target_pairs={{0,4},{2,6},{4,0},{6,2},{1,5},{3,7},{5,1},{7,3},{8,12},{10,14},{12... | collective-permute-start | bytes 393224 | tf_op jit(solution)/shard_map/ppermute | solution.py:36
  30.4 6.5 %collective-permute-start.8 = (bf16[256,256]{1,0:T(8,128)(2,1)S(1)}, bf16[256,256]{1,0:T(8,128)(2,1)S(1)}, u32[]{:S(2)}, u32[]{:S(2)}) collective-permute-start(bf16[256,256]{1,0:T(8,128)(2,1)S(1)} %merge.5.refs_0_), channel_id=1, source_target_pairs={{0,6},{2,4},{4,2},{6,0},{1,7},{3,5},{5,3},{7,1},{8,14},{10,12},{12... | collective-permute-start | bytes 393224 | tf_op jit(solution)/shard_map/ppermute | solution.py:36
  38.4 9.6 %collective-permute-start.16 = (bf16[4,256,1024]{2,1,0:T(8,128)(2,1)S(1)}, bf16[4,256,1024]{2,1,0:T(8,128)(2,1)S(1)}, u32[]{:S(2)}, u32[]{:S(2)}) collective-permute-start(bf16[4,256,1024]{2,1,0:T(8,128)(2,1)S(1)} %get-tuple-element.24.refs_8_), channel_id=1, source_target_pairs={{0,1},{1,0},{2,3},{3,2},{4,5},{5,4},{6,7},{7,6},{8,9},{9,8},{10,11... | collective-permute-start | bytes 6291464 | tf_op jit(solution)/shard_map/ppermute | solution.py:36
  38.5 6.4 %collective-permute-start.13 = (bf16[256,256]{1,0:T(8,128)(2,1)S(1)}, bf16[256,256]{1,0:T(8,128)(2,1)S(1)}, u32[]{:S(2)}, u32[]{:S(2)}) collective-permute-start(bf16[256,256]{1,0:T(8,128)(2,1)S(1)} %get-tuple-element.22.refs_0_), channel_id=1, source_target_pairs={{0,2},{2,0},{4,6},{6,4},{1,3},{3,1},{5,7},{7,5},{8,10},{10,8},{12,... | collective-permute-start | bytes 393224 | tf_op jit(solution)/shard_map/ppermute | solution.py:36
  39.5 8.4 %collective-permute-start.14 = (bf16[256,256]{1,0:T(8,128)(2,1)S(1)}, bf16[256,256]{1,0:T(8,128)(2,1)S(1)}, u32[]{:S(2)}, u32[]{:S(2)}) collective-permute-start(bf16[256,256]{1,0:T(8,128)(2,1)S(1)} %get-tuple-element.22.refs_0_), channel_id=1, source_target_pairs={{0,4},{2,6},{4,0},{6,2},{1,5},{3,7},{5,1},{7,3},{8,12},{10,14},{12... | collective-permute-start | bytes 393224 | tf_op jit(solution)/shard_map/ppermute | solution.py:36
  40.9 7.0 %collective-permute-start.15 = (bf16[256,256]{1,0:T(8,128)(2,1)S(1)}, bf16[256,256]{1,0:T(8,128)(2,1)S(1)}, u32[]{:S(2)}, u32[]{:S(2)}) collective-permute-start(bf16[256,256]{1,0:T(8,128)(2,1)S(1)} %get-tuple-element.22.refs_0_), channel_id=1, source_target_pairs={{0,6},{2,4},{4,2},{6,0},{1,7},{3,5},{5,3},{7,1},{8,14},{10,12},{12... | collective-permute-start | bytes 393224 | tf_op jit(solution)/shard_map/ppermute | solution.py:36
  47.9 5.3 %copy-start.5 = (bf16[256]{0:T(256)(128)(2,1)S(1)}, bf16[256]{0:T(256)(128)(2,1)}, u32[]{:S(2)}) copy-start(bf16[256]{0:T(256)(128)(2,1)} %param.19) | copy-start | bytes 1540
  47.9 10.6 %copy-start.2 = (bf16[1024,256]{1,0:T(8,128)(2,1)S(1)}, bf16[1024,256]{1,0:T(8,128)(2,1)}, u32[]{:S(2)}) copy-start(bf16[1024,256]{1,0:T(8,128)(2,1)} %refs_6_.1) | copy-start | bytes 1572868
  49.7 5.8 %collective-permute-start.17 = (bf16[256,256]{1,0:T(8,128)(2,1)S(1)}, bf16[256,256]{1,0:T(8,128)(2,1)S(1)}, u32[]{:S(2)}, u32[]{:S(2)}) collective-permute-start(bf16[256,256]{1,0:T(8,128)(2,1)S(1)} %get-tuple-element.25.refs_0_), channel_id=1, source_target_pairs={{0,2},{2,0},{4,6},{6,4},{1,3},{3,1},{5,7},{7,5},{8,10},{10,8},{12,... | collective-permute-start | bytes 393224 | tf_op jit(solution)/shard_map/ppermute | solution.py:36
  50.9 7.6 %collective-permute-start.18 = (bf16[256,256]{1,0:T(8,128)(2,1)S(1)}, bf16[256,256]{1,0:T(8,128)(2,1)S(1)}, u32[]{:S(2)}, u32[]{:S(2)}) collective-permute-start(bf16[256,256]{1,0:T(8,128)(2,1)S(1)} %get-tuple-element.25.refs_0_), channel_id=1, source_target_pairs={{0,4},{2,6},{4,0},{6,2},{1,5},{3,7},{5,1},{7,3},{8,12},{10,14},{12... | collective-permute-start | bytes 393224 | tf_op jit(solution)/shard_map/ppermute | solution.py:36
  51.7 6.8 %collective-permute-start.19 = (bf16[256,256]{1,0:T(8,128)(2,1)S(1)}, bf16[256,256]{1,0:T(8,128)(2,1)S(1)}, u32[]{:S(2)}, u32[]{:S(2)}) collective-permute-start(bf16[256,256]{1,0:T(8,128)(2,1)S(1)} %get-tuple-element.25.refs_0_), channel_id=1, source_target_pairs={{0,6},{2,4},{4,2},{6,0},{1,7},{3,5},{5,3},{7,1},{8,14},{10,12},{12... | collective-permute-start | bytes 393224 | tf_op jit(solution)/shard_map/ppermute | solution.py:36

commit v9 on v7

--- a/solution.py
+++ b/solution.py
@@ -90,7 +90,7 @@
         out_specs=[VMEM] * steps,
         compiler_params=params(),
         cost_estimate=pl.CostEstimate(
-            flops=8 * steps * rows * width * table.shape[0],
+            flops=2 * steps * rows * width * table.shape[0],
             bytes_accessed=2 * width * table.shape[0],
             transcendentals=0,
         ),
@@ -117,7 +117,7 @@
     pass
 
 
-def hold(value, after):
+def hold(value, after, flops=0):
     return pl.pallas_call(
         hold_kernel,
         out_shape=jax.ShapeDtypeStruct(value.shape, value.dtype),
@@ -125,6 +125,7 @@
         out_specs=HBM,
         input_output_aliases={0: 0},
         compiler_params=params(),
+        cost_estimate=pl.CostEstimate(flops=flops, bytes_accessed=0, transcendentals=0),
         name="hold",
     )(value, *after)
 
@@ -142,7 +143,7 @@
         copy.wait()
 
 
-def relay(near, far, axis, after):
+def relay(near, far, after):
     half = jax.ShapeDtypeStruct((near.shape[0] // 2,) + near.shape[1:], near.dtype)
     low, high = pl.pallas_call(
         cut_kernel,
@@ -153,7 +154,7 @@
         compiler_params=params(),
         name="cut",
     )(near, far, *after)
-    return [exchange(low, axis, 1), exchange(high, axis, 2)]
+    return [exchange(low, "mp", 1), exchange(high, "mp", 2)]
 
 
 def ask_around(wanted):
@@ -165,13 +166,13 @@
     return asked
 
 
-def gather_in(blocks, first, then):
+def gather_in(blocks, first, last):
     blocks, step = dict(enumerate(blocks)), 1
     while step < lax.axis_size("dp"):
         at_end = 2 * step == lax.axis_size("dp")
         for k in sorted((k for k in blocks if k & step), reverse=True):
             got = exchange(blocks.pop(k), "dp", step)
-            after = then(blocks[k ^ step]) if at_end else first
+            after = last if at_end else first
             blocks[k ^ step] = merge(blocks[k ^ step], got, after)
             first = [blocks[k ^ step]]
         step = 2 * step
@@ -238,21 +239,50 @@
         gated_ref[:, head] = (mixed * gates[:, head].astype(F32)).astype(BF16)
 
 
-def back(x, gated_refs, o_ref):
-    steps, cols, width = o_ref.shape
-    gated = jnp.concatenate([gated_ref[...] for gated_ref in gated_refs], axis=1)
-    weights = o_ref[...].reshape(steps * cols, width)
-    total = x.astype(F32) + jnp.dot(gated, weights, preferred_element_type=F32)
+def back(x, gated_refs, o_refs):
+    total, at = x.astype(F32), 0
+    for o_ref in o_refs:
+        steps, cols, width = o_ref.shape
+        gated = jnp.concatenate([ref[...] for ref in gated_refs[at : at + steps]], axis=1)
+        weights = o_ref[...].reshape(steps * cols, width)
+        total = total + jnp.dot(gated, weights, preferred_element_type=F32)
+        at += steps
     return total.astype(BF16)
 
 
-def first_kernel(steps, places, *refs):
-    x_refs, pieces, refs = refs[:steps], refs[steps : steps + len(places)], refs[steps + len(places) :]
-    mask_ref, w_own, w_other, gated_ref, x_ref, stack_ref, sems = refs
+def stack_copies(pieces, places, stack_ref, sems):
     copies = []
     for n, (k, row) in enumerate(places):
         at = stack_ref.at[k, pl.ds(row, pieces[n].shape[0]), :]
         copies.append(pltpu.make_async_copy(pieces[n], at, sems.at[n]))
+    return copies
+
+
+def stack_kernel(places, *refs):
+    copies = stack_copies(refs[: len(places)], places, refs[-2], refs[-1])
+    for copy in copies:
+        copy.start()
+    for copy in copies:
+        copy.wait()
+
+
+def stack(pieces, places, count, after):
+    rows, width = sum(piece.shape[0] for piece in pieces) // count, pieces[0].shape[1]
+    return pl.pallas_call(
+        functools.partial(stack_kernel, places),
+        out_shape=jax.ShapeDtypeStruct((count, rows, width), BF16),
+        in_specs=[HBM] * (len(pieces) + len(after)),
+        out_specs=HBM,
+        scratch_shapes=[pltpu.SemaphoreType.DMA((len(places),))],
+        compiler_params=params(),
+        name="stack",
+    )(*pieces, *after)
+
+
+def first_kernel(steps, places, *refs):
+    x_refs, pieces, refs = refs[:steps], refs[steps : steps + len(places)], refs[steps + len(places) :]
+    mask_ref, w_own, w_other, gated_ref, x_ref, stack_ref, sems = refs
+    copies = stack_copies(pieces, places, stack_ref, sems)
     for copy in copies:
         copy.start()
     width = x_refs[0].shape[1]
@@ -268,30 +298,34 @@
         copy.wait()
 
 
-def middle_kernel(steps, *refs):
-    gated_refs = refs[:steps]
-    x_ref, mask_ref, w_own, w_other, o_own, o_other, gated_ref, x1_ref = refs[steps:]
-
-    def body(o_ref, w_ref):
-        x1 = back(x_ref[...], gated_refs, o_ref)
+def middle_kernel(steps, parts, *refs):
+    gated_refs, refs = refs[:steps], refs[steps:]
+    x_ref, mask_ref, w_own, w_other = refs[:4]
+    o_own, o_other = refs[4 : 4 + parts], refs[4 + parts : 4 + 2 * parts]
+    gated_ref, x1_ref = refs[-2:]
+
+    def body(w_ref, *o_refs):
+        x1 = back(x_ref[...], gated_refs, o_refs)
         x1_ref[...] = x1
         front(x1, mask_ref, w_ref, gated_ref)
 
-    by_phase(body, [o_own, w_other], [o_other, w_own])
-
-
-def last_kernel(steps, *refs):
-    gated_refs = refs[:steps]
-    x_ref, share_ref, w_ref, bias_ref, o_own, o_other, states_ref, ctx_ref = refs[steps:]
-
-    def body(o_ref):
-        states = back(x_ref[...], gated_refs, o_ref)
+    by_phase(body, (w_other, *o_own), (w_own, *o_other))
+
+
+def last_kernel(steps, parts, *refs):
+    gated_refs, refs = refs[:steps], refs[steps:]
+    x_ref, share_ref, w_ref, bias_ref = refs[:4]
+    o_own, o_other = refs[4 : 4 + parts], refs[4 + parts : 4 + 2 * parts]
+    states_ref, ctx_ref = refs[-2:]
+
+    def body(*o_refs):
+        states = back(x_ref[...], gated_refs, o_refs)
         states_ref[...] = states
         context = jnp.dot(share_ref[...], states, preferred_element_type=F32).astype(BF16)
         summed = jnp.dot(context, w_ref[...], preferred_element_type=F32)
         ctx_ref[...] = silu(summed + bias_ref[...].astype(F32)).astype(BF16)
 
-    by_phase(body, [o_other], [o_own])
+    by_phase(body, o_other, o_own)
 
 
 def section_flops(rows, width, local_cols):
@@ -323,11 +357,11 @@
     part = width // mp_count
 
     w_own = jnp.transpose(w_in[0], (1, 0, 2)) * gains[0][None, :, None]
-    if mp_count == 4:
-        near, far = exchange(w_out[0], "mp", 1), exchange(w_out[0], "mp", 2)
-        o_pieces, places = [w_out[0], near, far], [(0, 0), (1, 0), (2, 0)]
-    else:
-        o_pieces, places = spread(w_out[0], "mp"), [(k, 0) for k in range(mp_count)]
+    relayed = mp_count == 4
+    direct = range(1, 3 if relayed else mp_count)
+    pieces = [w_out[0]] + [exchange(w_out[0], "mp", k) for k in direct]
+    places = [(k, 0) for k in range(len(pieces))]
+    corner = [(0, 0), (0, local_cols // 2)]
     neigh = jnp.transpose(neighbors[0], (0, 2, 1))
     bias = ctx_bias.reshape(1, -1)
     mask, share = prepare(segments, neigh)
@@ -340,22 +374,13 @@
         late = fetch(asked[-1:], batches, table, part, [])
         found = fetch(asked[:-1], batches, table, part, late) + late
 
-        def then(first):
-            if mp_count == 4:
-                o_pieces.extend(relay(near, far, "mp", [first]))
-                places.extend([(3, 0), (3, local_cols // 2)])
-            return [w_other]
-
-        piece = gather_in(found, [], then)
+        piece = gather_in(found, [], [w_other])
     else:
         piece = fetch_rows_padded(item_owner[:, 0], item_row, table, part)
         piece = lax.dynamic_index_in_dim(
             piece.reshape(batches, rows, part), lax.axis_index("phase"), 0, keepdims=False
         )
         w_other = exchange(w_own, "phase", 1)
-        if mp_count == 4:
-            o_pieces.extend(relay(near, far, "mp", [piece]))
-            places.extend([(3, 0), (3, local_cols // 2)])
     x_pieces = spread(piece, "mp")
 
     x_shape = jax.ShapeDtypeStruct((rows, width), BF16)
@@ -368,23 +393,28 @@
         out_shape=[
             gated_shape,
             x_shape,
-            jax.ShapeDtypeStruct((mp_count, local_cols, width), BF16),
+            jax.ShapeDtypeStruct((len(pieces), local_cols, width), BF16),
         ],
         in_specs=[VMEM] * mp_count + [HBM] * len(places) + [VMEM] * 3,
         out_specs=[VMEM] * 2 + [HBM],
         scratch_shapes=[pltpu.SemaphoreType.DMA((len(places),))],
         compiler_params=params(),
         cost_estimate=pl.CostEstimate(
-            flops=front_flops, bytes_accessed=8 * width * local_cols, transcendentals=0
+            flops=1 * front_flops, bytes_accessed=8 * width * local_cols, transcendentals=0
         ),
         name="section0_front",
-    )(*x_pieces, *o_pieces, mask, w_own, w_other)
-    o_other = exchange(o_own, "phase", 1)
-
+    )(*x_pieces, *pieces, mask, w_own, w_other)
+    o_own = [o_own]
+    if relayed:
+        o_own.append(stack(relay(*pieces[1:], [piece]), corner, 1, []))
+    o_other = [exchange(block, "phase", 1) for block in o_own]
+
+    arrived = spread(gated, "mp")
+    arrived[-1] = hold(arrived[-1], arrived[1:-1], 32 * front_flops)
     gated, x1 = pl.pallas_call(
-        functools.partial(middle_kernel, mp_count),
+        functools.partial(middle_kernel, mp_count, len(o_own)),
         out_shape=[gated_shape, x_shape],
-        in_specs=[VMEM] * (mp_count + 6),
+        in_specs=[VMEM] * (mp_count + 4 + 2 * len(o_own)),
         out_specs=[VMEM] * 2,
         compiler_params=params(),
         cost_estimate=pl.CostEstimate(
@@ -393,12 +423,12 @@
             transcendentals=0,
         ),
         name="section0_back_section1_front",
-    )(*spread(gated, "mp"), x0, mask, w_own, w_other, o_own, o_other)
+    )(*arrived, x0, mask, w_own, w_other, *o_own, *o_other)
 
     states, ctx = pl.pallas_call(
-        functools.partial(last_kernel, mp_count),
+        functools.partial(last_kernel, mp_count, len(o_own)),
         out_shape=[x_shape, jax.ShapeDtypeStruct((imps, w_ctx.shape[1]), BF16)],
-        in_specs=[VMEM] * (mp_count + 6),
+        in_specs=[VMEM] * (mp_count + 4 + 2 * len(o_own)),
         out_specs=[VMEM] * 2,
         compiler_params=params(),
         cost_estimate=pl.CostEstimate(
@@ -407,7 +437,7 @@
             transcendentals=0,
         ),
         name="section1_back_context",
-    )(*spread(gated, "mp"), x1, share, w_ctx, bias, o_own, o_other)
+    )(*spread(gated, "mp"), x1, share, w_ctx, bias, *o_own, *o_other)
 
     return (
         states.reshape(1, 1, rows, width),

time: 63.4 us -> 59.4 us (0.937)
  waiting for transfers between devices: 26.7 us -> 22.6 us
    ppermute x20 -> x21, waiting for transfers between devices: 26.7 us -> 22.6 us  [exchange(): return lax.ppermute(value, axis, pairs)]
    ppermute x20 -> x21, starting transfers between devices: 24.9 us -> 25 us  [exchange(): return lax.ppermute(value, axis, pairs)]
    pallas_call x2 -> x3, Pallas kernels: 3.79 us -> 3.88 us  [the longest x1 2.06 us: on_device(): pl.pallas_call(functools.partial(last_kernel, mp_count, len(o_own)), out_...]
  transfers between devices with their start and end apart: 20 -> 21, of which waited for: 12 -> 10; matrix products, arithmetic and copies ran while one was open for 4% -> 4% of each run, Pallas kernels for 2% -> 5%
where the time goes in v9:
time: 59.4 us; the launch traced here: 59.2 us
  starting transfers between devices  25 us (42%)
  waiting for transfers between devices  22.6 us (38%)
  Pallas kernels  6.77 us (11%)
  other arithmetic  3.99 us (7%)
  between operations  0.78 us (1%)
    ppermute x21, starting transfers between devices, exchange(): return lax.ppermute(value, axis, pairs)  25 us
    ppermute x21, waiting for transfers between devices, exchange(): return lax.ppermute(value, axis, pairs)  22.6 us
    pallas_call x1, Pallas kernels, on_device(): pl.pallas_call(functools.partial(last_kernel, mp_count, len(o_own)), out_...  2.06 us
    mul x1, other arithmetic, on_device(): w_own = jnp.transpose(w_in[0], (1, 0, 2)) * gains[0][None, :, None]  1.9 us
    pallas_call x1, Pallas kernels, on_device(): pl.pallas_call(functools.partial(middle_kernel, mp_count, len(o_own)), ou...  1.76 us
    pallas_call x1, Pallas kernels, on_device(): pl.pallas_call(functools.partial(first_kernel, mp_count, places), out_sha...  1.43 us
  transfers between devices with their start and end apart: 21, of which 10 were waited for; matrix products, arithmetic and copies ran while one was open for 4% of the time, Pallas kernels for 5%

profile of v9, /device:TPU:0, one launch (start us, length us, event | category | flops | bytes accessed | tf_op | source)
XLA Modules:
  0.0 59.2 jit_solution(5907280092185294424)
XLA Ops:
  0.6 0.7 %broadcast_multiply_fusion = s32[512,1]{0,1:T(1,128)S(1)} fusion(s32[512,1]{0,1:T(1,128)} %param.10), kind=kLoop, calls=%fused_computation.4 | loop fusion | flops 512 | bytes 4096 | tf_op jit(solution)/shard_map/mul | solution.py:370
  1.3 0.7 %bitcast_add_fusion.refs_0_ = s32[4,128]{1,0:T(4,128)S(1)} fusion(s32[4,128]{1,0:T(4,128)S(1)} %bitcast.19, s32[512]{0:T(512)} %param.11), kind=kLoop, calls=%fused_computation.3 | loop fusion | flops 512 | bytes 6144 | tf_op jit(solution)/shard_map/add | solution.py:370
  2.0 3.0 %collective-permute-start = (s32[4,128]{1,0:T(4,128)S(1)}, s32[4,128]{1,0:T(4,128)S(1)}, u32[]{:S(2)}, u32[]{:S(2)}) collective-permute-start(s32[4,128]{1,0:T(4,128)S(1)} %bitcast_add_fusion.refs_0_), channel_id=1, source_target_pairs={{0,8},{8,0},{16,24},{24,16},{1,9},{9,1},{17,25},{25,17},{2,10},{10... | collective-permute-start | bytes 6152 | tf_op jit(solution)/shard_map/ppermute | solution.py:36
  5.0 0.7 %reduce = bf16[1024]{0:T(1024)(128)(2,1)S(1)} reduce(bf16[1,1024]{1,0:T(2,128)(2,1)} %param.15, bf16[]{:T(256)} %constant.7), dimensions={0}, to_apply=%param.15.reduce_sub_computation | reduce | bytes 4098 | tf_op args[5]
  5.7 1.9 %fusion.refs_0_ = bf16[4,1024,256]{2,1,0:T(8,128)(2,1)S(1)} fusion(bf16[1,1024,4,256]{3,2,1,0:T(4,128)(2,1)} %param.16, bf16[1024]{0:T(1024)(128)(2,1)S(1)} %reduce), kind=kLoop, calls=%fused_computation.1 | loop fusion | flops 1048576 | bytes 4196352 | tf_op jit(solution)/shard_map/mul | solution.py:359
  7.6 0.0 copy-start.1
  7.7 0.0 copy-start
  7.7 0.1 collective-permute-start.5
  7.8 2.7 %collective-permute-start.1 = (s32[8,128]{1,0:T(8,128)S(1)}, s32[8,128]{1,0:T(8,128)S(1)}, u32[]{:S(2)}, u32[]{:S(2)}) collective-permute-start(s32[8,128]{1,0:T(8,128)S(1)} %pad_add_fusion), channel_id=1, source_target_pairs={{0,16},{8,24},{16,0},{24,8},{1,17},{9,25},{17,1},{25,9},{2,18},{10... | collective-permute-start | bytes 12296 | tf_op jit(solution)/shard_map/ppermute | solution.py:36
  10.4 1.5 %collective-permute-start.10 = (bf16[256,1024]{1,0:T(8,128)(2,1)S(1)}, bf16[256,1024]{1,0:T(8,128)(2,1)S(1)}, u32[]{:S(2)}, u32[]{:S(2)}) collective-permute-start(bf16[256,1024]{1,0:T(8,128)(2,1)S(1)} %bitcast.15), channel_id=1, source_target_pairs={{0,4},{2,6},{4,0},{6,2},{1,5},{3,7},{5,1},{7,3},{8,12},{10,14},{12... | collective-permute-start | bytes 1572872 | tf_op jit(solution)/shard_map/ppermute | solution.py:36
  12.0 1.5 %collective-permute-start.9 = (bf16[256,1024]{1,0:T(8,128)(2,1)S(1)}, bf16[256,1024]{1,0:T(8,128)(2,1)S(1)}, u32[]{:S(2)}, u32[]{:S(2)}) collective-permute-start(bf16[256,1024]{1,0:T(8,128)(2,1)S(1)} %bitcast.16), channel_id=1, source_target_pairs={{0,2},{2,0},{4,6},{6,4},{1,3},{3,1},{5,7},{7,5},{8,10},{10,8},{12,... | collective-permute-start | bytes 1572872 | tf_op jit(solution)/shard_map/ppermute | solution.py:36
  13.5 0.4 fetch.2.refs_4_
  13.9 0.9 %collective-permute-start.3 = (bf16[256,256]{1,0:T(8,128)(2,1)S(1)}, bf16[256,256]{1,0:T(8,128)(2,1)S(1)}, u32[]{:S(2)}, u32[]{:S(2)}) collective-permute-start(bf16[256,256]{1,0:T(8,128)(2,1)S(1)} %fetch.2.refs_4_), channel_id=1, source_target_pairs={{0,8},{8,0},{16,24},{24,16},{1,9},{9,1},{17,25},{25,17},{2,10},{10... | collective-permute-start | bytes 393224 | tf_op jit(solution)/shard_map/ppermute | solution.py:36
  14.8 0.7 %fetch.3 = (bf16[256,256]{1,0:T(8,128)(2,1)S(1)}, bf16[256,256]{1,0:T(8,128)(2,1)S(1)}, bf16[256,256]{1,0:T(8,128)(2,1)S(1)}) custom-call(s32[4,128]{1,0:T(4,128)S(1)} %bitcast_add_fusion.refs_0_, s32[4,128]{1,0:T(4,128)S(1)} %collective-permute-done.refs_1_, s32[4,128]{1,0:T(4,128)S(1)} %get-tuple-element.31.refs_2_, bf16[1024,1024]{1,0:T(8,128)(2,1)S(1)} %copy-done, ...), custom_call_target="tpu_custom_call" | custom-call | flops 402653184 | bytes 524288 | tf_op jit(solution)/shard_map/fetch/pallas_call | solution.py:86
  15.5 1.2 %collective-permute-start.2 = (bf16[256,256]{1,0:T(8,128)(2,1)S(1)}, bf16[256,256]{1,0:T(8,128)(2,1)S(1)}, u32[]{:S(2)}, u32[]{:S(2)}) collective-permute-start(bf16[256,256]{1,0:T(8,128)(2,1)S(1)} %get-tuple-element.17), channel_id=1, source_target_pairs={{0,8},{8,0},{16,24},{24,16},{1,9},{9,1},{17,25},{25,17},{2,10},{10... | collective-permute-start | bytes 393224 | tf_op jit(solution)/shard_map/ppermute | solution.py:36
  16.7 3.6 %collective-permute-done.3.b_ref = bf16[256,256]{1,0:T(8,128)(2,1)S(1)} collective-permute-done((bf16[256,256]{1,0:T(8,128)(2,1)S(1)}, bf16[256,256]{1,0:T(8,128)(2,1)S(1)}, u32[]{:S(2)}, u32[]{:S(2)}) %collective-permute-start.3) | collective-permute-done | bytes 131104 | tf_op jit(solution)/shard_map/ppermute | solution.py:36
  20.4 1.2 %collective-permute-start.4 = (bf16[256,256]{1,0:T(8,128)(2,1)S(1)}, bf16[256,256]{1,0:T(8,128)(2,1)S(1)}, u32[]{:S(2)}, u32[]{:S(2)}) collective-permute-start(bf16[256,256]{1,0:T(8,128)(2,1)S(1)} %merge.3.refs_0_), channel_id=1, source_target_pairs={{0,16},{8,24},{16,0},{24,8},{1,17},{9,25},{17,1},{25,9},{2,18},{10... | collective-permute-start | bytes 393224 | tf_op jit(solution)/shard_map/ppermute | solution.py:36
  21.6 1.0 %collective-permute-done.2.b_ref = bf16[256,256]{1,0:T(8,128)(2,1)S(1)} collective-permute-done((bf16[256,256]{1,0:T(8,128)(2,1)S(1)}, bf16[256,256]{1,0:T(8,128)(2,1)S(1)}, u32[]{:S(2)}, u32[]{:S(2)}) %collective-permute-start.2) | collective-permute-done | bytes 131104 | tf_op jit(solution)/shard_map/ppermute | solution.py:36
  22.6 5.1 %collective-permute-done.4.b_ref = bf16[256,256]{1,0:T(8,128)(2,1)S(1)} collective-permute-done((bf16[256,256]{1,0:T(8,128)(2,1)S(1)}, bf16[256,256]{1,0:T(8,128)(2,1)S(1)}, u32[]{:S(2)}, u32[]{:S(2)}) %collective-permute-start.4) | collective-permute-done | bytes 131104 | tf_op jit(solution)/shard_map/ppermute | solution.py:36
  27.7 0.6 %collective-permute-start.6 = (bf16[256,256]{1,0:T(8,128)(2,1)S(1)}, bf16[256,256]{1,0:T(8,128)(2,1)S(1)}, u32[]{:S(2)}, u32[]{:S(2)}) collective-permute-start(bf16[256,256]{1,0:T(8,128)(2,1)S(1)} %merge.5.refs_0_), channel_id=1, source_target_pairs={{0,2},{2,0},{4,6},{6,4},{1,3},{3,1},{5,7},{7,5},{8,10},{10,8},{12,... | collective-permute-start | bytes 393224 | tf_op jit(solution)/shard_map/ppermute | solution.py:36
  28.3 1.1 %collective-permute-start.7 = (bf16[256,256]{1,0:T(8,128)(2,1)S(1)}, bf16[256,256]{1,0:T(8,128)(2,1)S(1)}, u32[]{:S(2)}, u32[]{:S(2)}) collective-permute-start(bf16[256,256]{1,0:T(8,128)(2,1)S(1)} %merge.5.refs_0_), channel_id=1, source_target_pairs={{0,4},{2,6},{4,0},{6,2},{1,5},{3,7},{5,1},{7,3},{8,12},{10,14},{12... | collective-permute-start | bytes 393224 | tf_op jit(solution)/shard_map/ppermute | solution.py:36
  29.4 1.9 %collective-permute-start.8 = (bf16[256,256]{1,0:T(8,128)(2,1)S(1)}, bf16[256,256]{1,0:T(8,128)(2,1)S(1)}, u32[]{:S(2)}, u32[]{:S(2)}) collective-permute-start(bf16[256,256]{1,0:T(8,128)(2,1)S(1)} %merge.5.refs_0_), channel_id=1, source_target_pairs={{0,6},{2,4},{4,2},{6,0},{1,7},{3,5},{5,3},{7,1},{8,14},{10,12},{12... | collective-permute-start | bytes 393224 | tf_op jit(solution)/shard_map/ppermute | solution.py:36
  31.3 0.0 collective-permute-done.10.refs_6_.far_ref
  31.3 0.0 collective-permute-done.9.refs_5_.near_ref
  31.3 0.1 cut.1
  31.3 0.6 %collective-permute-start.14 = (bf16[128,1024]{1,0:T(8,128)(2,1)S(1)}, bf16[128,1024]{1,0:T(8,128)(2,1)S(1)}, u32[]{:S(2)}, u32[]{:S(2)}) collective-permute-start(bf16[128,1024]{1,0:T(8,128)(2,1)S(1)} %get-tuple-element.23), channel_id=1, source_target_pairs={{0,2},{2,0},{4,6},{6,4},{1,3},{3,1},{5,7},{7,5},{8,10},{10,8},{12,... | collective-permute-start | bytes 786440 | tf_op jit(solution)/shard_map/ppermute | solution.py:36
  31.9 1.1 %collective-permute-start.15 = (bf16[128,1024]{1,0:T(8,128)(2,1)S(1)}, bf16[128,1024]{1,0:T(8,128)(2,1)S(1)}, u32[]{:S(2)}, u32[]{:S(2)}) collective-permute-start(bf16[128,1024]{1,0:T(8,128)(2,1)S(1)} %get-tuple-element.24), channel_id=1, source_target_pairs={{0,4},{2,6},{4,0},{6,2},{1,5},{3,7},{5,1},{7,3},{8,12},{10,14},{12... | collective-permute-start | bytes 786440 | tf_op jit(solution)/shard_map/ppermute | solution.py:36
  33.0 0.3 prepare.1
  33.3 0.4 collective-permute-done.6.refs_1_
  33.7 0.0 collective-permute-done.7.refs_2_
  33.7 2.6 %collective-permute-done.8.refs_3_ = bf16[256,256]{1,0:T(8,128)(2,1)S(1)} collective-permute-done((bf16[256,256]{1,0:T(8,128)(2,1)S(1)}, bf16[256,256]{1,0:T(8,128)(2,1)S(1)}, u32[]{:S(2)}, u32[]{:S(2)}) %collective-permute-start.8) | collective-permute-done | bytes 131104 | tf_op jit(solution)/shard_map/ppermute | solution.py:36
  36.3 1.4 %section0_front.1 = (bf16[256,256]{1,0:T(8,128)(2,1)S(1)}, bf16[256,1024]{1,0:T(8,128)(2,1)S(1)}, bf16[3,256,1024]{2,1,0:T(8,128)(2,1)S(1)}) custom-call(bf16[256,256]{1,0:T(8,128)(2,1)S(1)} %merge.5.refs_0_, bf16[256,256]{1,0:T(8,128)(2,1)S(1)} %collective-permute-done.6.refs_1_, bf16[256,256]{1,0:T(8,128)(2,1)S(1)} %collective-permute-done.7.refs_2_, ...), custom_call_target="tpu_custom_call" | custom-call | flops 603979776 | bytes 2097152 | tf_op jit(solution)/shard_map/section0_front/pallas_call | solution.py:391
  37.8 0.7 %collective-permute-start.11 = (bf16[256,256]{1,0:T(8,128)(2,1)S(1)}, bf16[256,256]{1,0:T(8,128)(2,1)S(1)}, u32[]{:S(2)}, u32[]{:S(2)}) collective-permute-start(bf16[256,256]{1,0:T(8,128)(2,1)S(1)} %get-tuple-element.20.refs_0_), channel_id=1, source_target_pairs={{0,2},{2,0},{4,6},{6,4},{1,3},{3,1},{5,7},{7,5},{8,10},{10,8},{12,... | collective-permute-start | bytes 393224 | tf_op jit(solution)/shard_map/ppermute | solution.py:36
  38.5 2.2 %collective-permute-start.12 = (bf16[256,256]{1,0:T(8,128)(2,1)S(1)}, bf16[256,256]{1,0:T(8,128)(2,1)S(1)}, u32[]{:S(2)}, u32[]{:S(2)}) collective-permute-start(bf16[256,256]{1,0:T(8,128)(2,1)S(1)} %get-tuple-element.20.refs_0_), channel_id=1, source_target_pairs={{0,4},{2,6},{4,0},{6,2},{1,5},{3,7},{5,1},{7,3},{8,12},{10,14},{12... | collective-permute-start | bytes 393224 | tf_op jit(solution)/shard_map/ppermute | solution.py:36
  40.7 0.6 %collective-permute-start.13 = (bf16[256,256]{1,0:T(8,128)(2,1)S(1)}, bf16[256,256]{1,0:T(8,128)(2,1)S(1)}, u32[]{:S(2)}, u32[]{:S(2)}) collective-permute-start(bf16[256,256]{1,0:T(8,128)(2,1)S(1)} %get-tuple-element.20.refs_0_), channel_id=1, source_target_pairs={{0,6},{2,4},{4,2},{6,0},{1,7},{3,5},{5,3},{7,1},{8,14},{10,12},{12... | collective-permute-start | bytes 393224 | tf_op jit(solution)/shard_map/ppermute | solution.py:36
  41.3 0.1 stack.1.refs_9_
  41.4 0.6 collective-permute-start.17
  42.0 0.8 %collective-permute-done.11.refs_1_ = bf16[256,256]{1,0:T(8,128)(2,1)S(1)} collective-permute-done((bf16[256,256]{1,0:T(8,128)(2,1)S(1)}, bf16[256,256]{1,0:T(8,128)(2,1)S(1)}, u32[]{:S(2)}, u32[]{:S(2)}) %collective-permute-start.11) | collective-permute-done | bytes 131104 | tf_op jit(solution)/shard_map/ppermute | solution.py:36
  42.8 1.8 %collective-permute-done.12.refs_2_ = bf16[256,256]{1,0:T(8,128)(2,1)S(1)} collective-permute-done((bf16[256,256]{1,0:T(8,128)(2,1)S(1)}, bf16[256,256]{1,0:T(8,128)(2,1)S(1)}, u32[]{:S(2)}, u32[]{:S(2)}) %collective-permute-start.12) | collective-permute-done | bytes 131104 | tf_op jit(solution)/shard_map/ppermute | solution.py:36
  44.6 1.9 %collective-permute-done.13.refs_0_ = bf16[256,256]{1,0:T(8,128)(2,1)S(1)} collective-permute-done((bf16[256,256]{1,0:T(8,128)(2,1)S(1)}, bf16[256,256]{1,0:T(8,128)(2,1)S(1)}, u32[]{:S(2)}, u32[]{:S(2)}) %collective-permute-start.13) | collective-permute-done | bytes 131104 | tf_op jit(solution)/shard_map/ppermute | solution.py:36
  46.6 0.0 copy-start.2
  46.6 1.8 %section0_back_section1_front.1 = (bf16[256,256]{1,0:T(8,128)(2,1)S(1)}, bf16[256,1024]{1,0:T(8,128)(2,1)S(1)}) custom-call(bf16[256,256]{1,0:T(8,128)(2,1)S(1)} %get-tuple-element.20.refs_0_, bf16[256,256]{1,0:T(8,128)(2,1)S(1)} %collective-permute-done.11.refs_1_, bf16[256,256]{1,0:T(8,128)(2,1)S(1)} %collective-permute-done.12.refs_2_, ...), custom_call_target="tpu_custom_call" | custom-call | flops 1140850688 | bytes 4194304 | tf_op jit(solution)/shard_map/section0_back_section1_front/pallas_call | solution.py:414
  48.3 1.0 %collective-permute-start.18 = (bf16[256,256]{1,0:T(8,128)(2,1)S(1)}, bf16[256,256]{1,0:T(8,128)(2,1)S(1)}, u32[]{:S(2)}, u32[]{:S(2)}) collective-permute-start(bf16[256,256]{1,0:T(8,128)(2,1)S(1)} %get-tuple-element.25.refs_0_), channel_id=1, source_target_pairs={{0,2},{2,0},{4,6},{6,4},{1,3},{3,1},{5,7},{7,5},{8,10},{10,8},{12,... | collective-permute-start | bytes 393224 | tf_op jit(solution)/shard_map/ppermute | solution.py:36
  49.3 0.8 %collective-permute-start.19 = (bf16[256,256]{1,0:T(8,128)(2,1)S(1)}, bf16[256,256]{1,0:T(8,128)(2,1)S(1)}, u32[]{:S(2)}, u32[]{:S(2)}) collective-permute-start(bf16[256,256]{1,0:T(8,128)(2,1)S(1)} %get-tuple-element.25.refs_0_), channel_id=1, source_target_pairs={{0,4},{2,6},{4,0},{6,2},{1,5},{3,7},{5,1},{7,3},{8,12},{10,14},{12... | collective-permute-start | bytes 393224 | tf_op jit(solution)/shard_map/ppermute | solution.py:36
  50.2 1.7 %collective-permute-start.20 = (bf16[256,256]{1,0:T(8,128)(2,1)S(1)}, bf16[256,256]{1,0:T(8,128)(2,1)S(1)}, u32[]{:S(2)}, u32[]{:S(2)}) collective-permute-start(bf16[256,256]{1,0:T(8,128)(2,1)S(1)} %get-tuple-element.25.refs_0_), channel_id=1, source_target_pairs={{0,6},{2,4},{4,2},{6,0},{1,7},{3,5},{5,3},{7,1},{8,14},{10,12},{12... | collective-permute-start | bytes 393224 | tf_op jit(solution)/shard_map/ppermute | solution.py:36
  51.9 2.8 %collective-permute-done.18.refs_1_ = bf16[256,256]{1,0:T(8,128)(2,1)S(1)} collective-permute-done((bf16[256,256]{1,0:T(8,128)(2,1)S(1)}, bf16[256,256]{1,0:T(8,128)(2,1)S(1)}, u32[]{:S(2)}, u32[]{:S(2)}) %collective-permute-start.18) | collective-permute-done | bytes 131104 | tf_op jit(solution)/shard_map/ppermute | solution.py:36
  54.7 2.4 %collective-permute-done.19.refs_2_ = bf16[256,256]{1,0:T(8,128)(2,1)S(1)} collective-permute-done((bf16[256,256]{1,0:T(8,128)(2,1)S(1)}, bf16[256,256]{1,0:T(8,128)(2,1)S(1)}, u32[]{:S(2)}, u32[]{:S(2)}) %collective-permute-start.19) | collective-permute-done | bytes 131104 | tf_op jit(solution)/shard_map/ppermute | solution.py:36
  57.1 2.1 %section1_back_context.1 = (bf16[256,1024]{1,0:T(8,128)(2,1)}, bf16[256,256]{1,0:T(8,128)(2,1)}) custom-call(bf16[256,256]{1,0:T(8,128)(2,1)S(1)} %get-tuple-element.25.refs_0_, bf16[256,256]{1,0:T(8,128)(2,1)S(1)} %collective-permute-done.18.refs_1_, bf16[256,256]{1,0:T(8,128)(2,1)S(1)} %collective-permute-done.19.refs_2_, ...), custom_call_target="tpu_custom_call" | custom-call | flops 805306368 | bytes 2097152 | tf_op jit(solution)/shard_map/section1_back_context/pallas_call | solution.py:428
  (26 shorter events, 0.1 us)
Async XLA Ops:
  2.0 5.7 %collective-permute-start = (s32[4,128]{1,0:T(4,128)S(1)}, s32[4,128]{1,0:T(4,128)S(1)}, u32[]{:S(2)}, u32[]{:S(2)}) collective-permute-start(s32[4,128]{1,0:T(4,128)S(1)} %bitcast_add_fusion.refs_0_), channel_id=1, source_target_pairs={{0,8},{8,0},{16,24},{24,16},{1,9},{9,1},{17,25},{25,17},{2,10},{10... | collective-permute-start | bytes 6152 | tf_op jit(solution)/shard_map/ppermute | solution.py:36
  7.6 2.8 %copy-start.1 = (bf16[1,256,1024]{2,1,0:T(8,128)(2,1)S(1)}, bf16[1,256,1024]{2,1,0:T(8,128)(2,1)}, u32[]{:S(2)}) copy-start(bf16[1,256,1024]{2,1,0:T(8,128)(2,1)} %param.17) | copy-start | bytes 1572868
  7.7 5.8 %copy-start = (bf16[1024,1024]{1,0:T(8,128)(2,1)S(1)}, bf16[1024,1024]{1,0:T(8,128)(2,1)}, u32[]{:S(2)}) copy-start(bf16[1024,1024]{1,0:T(8,128)(2,1)} %refs_3_.1) | copy-start | bytes 6291460
  7.7 20.0 %collective-permute-start.5 = (bf16[4,1024,256]{2,1,0:T(8,128)(2,1)S(1)}, bf16[4,1024,256]{2,1,0:T(8,128)(2,1)S(1)}, u32[]{:S(2)}, u32[]{:S(2)}) collective-permute-start(bf16[4,1024,256]{2,1,0:T(8,128)(2,1)S(1)} %hold.2.refs_8_.refs_6_), channel_id=1, source_target_pairs={{0,1},{1,0},{2,3},{3,2},{4,5},{5,4},{6,7},{7,6},{8,9},{9,8},{10,11... | collective-permute-start | bytes 6291464 | tf_op jit(solution)/shard_map/ppermute | solution.py:36
  7.8 5.7 %collective-permute-start.1 = (s32[8,128]{1,0:T(8,128)S(1)}, s32[8,128]{1,0:T(8,128)S(1)}, u32[]{:S(2)}, u32[]{:S(2)}) collective-permute-start(s32[8,128]{1,0:T(8,128)S(1)} %pad_add_fusion), channel_id=1, source_target_pairs={{0,16},{8,24},{16,0},{24,8},{1,17},{9,25},{17,1},{25,9},{2,18},{10... | collective-permute-start | bytes 12296 | tf_op jit(solution)/shard_map/ppermute | solution.py:36
  10.4 20.8 %collective-permute-start.10 = (bf16[256,1024]{1,0:T(8,128)(2,1)S(1)}, bf16[256,1024]{1,0:T(8,128)(2,1)S(1)}, u32[]{:S(2)}, u32[]{:S(2)}) collective-permute-start(bf16[256,1024]{1,0:T(8,128)(2,1)S(1)} %bitcast.15), channel_id=1, source_target_pairs={{0,4},{2,6},{4,0},{6,2},{1,5},{3,7},{5,1},{7,3},{8,12},{10,14},{12... | collective-permute-start | bytes 1572872 | tf_op jit(solution)/shard_map/ppermute | solution.py:36
  12.0 19.3 %collective-permute-start.9 = (bf16[256,1024]{1,0:T(8,128)(2,1)S(1)}, bf16[256,1024]{1,0:T(8,128)(2,1)S(1)}, u32[]{:S(2)}, u32[]{:S(2)}) collective-permute-start(bf16[256,1024]{1,0:T(8,128)(2,1)S(1)} %bitcast.16), channel_id=1, source_target_pairs={{0,2},{2,0},{4,6},{6,4},{1,3},{3,1},{5,7},{7,5},{8,10},{10,8},{12,... | collective-permute-start | bytes 1572872 | tf_op jit(solution)/shard_map/ppermute | solution.py:36
  13.9 6.5 %collective-permute-start.3 = (bf16[256,256]{1,0:T(8,128)(2,1)S(1)}, bf16[256,256]{1,0:T(8,128)(2,1)S(1)}, u32[]{:S(2)}, u32[]{:S(2)}) collective-permute-start(bf16[256,256]{1,0:T(8,128)(2,1)S(1)} %fetch.2.refs_4_), channel_id=1, source_target_pairs={{0,8},{8,0},{16,24},{24,16},{1,9},{9,1},{17,25},{25,17},{2,10},{10... | collective-permute-start | bytes 393224 | tf_op jit(solution)/shard_map/ppermute | solution.py:36
  15.5 7.2 %collective-permute-start.2 = (bf16[256,256]{1,0:T(8,128)(2,1)S(1)}, bf16[256,256]{1,0:T(8,128)(2,1)S(1)}, u32[]{:S(2)}, u32[]{:S(2)}) collective-permute-start(bf16[256,256]{1,0:T(8,128)(2,1)S(1)} %get-tuple-element.17), channel_id=1, source_target_pairs={{0,8},{8,0},{16,24},{24,16},{1,9},{9,1},{17,25},{25,17},{2,10},{10... | collective-permute-start | bytes 393224 | tf_op jit(solution)/shard_map/ppermute | solution.py:36
  20.4 7.3 %collective-permute-start.4 = (bf16[256,256]{1,0:T(8,128)(2,1)S(1)}, bf16[256,256]{1,0:T(8,128)(2,1)S(1)}, u32[]{:S(2)}, u32[]{:S(2)}) collective-permute-start(bf16[256,256]{1,0:T(8,128)(2,1)S(1)} %merge.3.refs_0_), channel_id=1, source_target_pairs={{0,16},{8,24},{16,0},{24,8},{1,17},{9,25},{17,1},{25,9},{2,18},{10... | collective-permute-start | bytes 393224 | tf_op jit(solution)/shard_map/ppermute | solution.py:36
  22.6 10.4 %copy-start.3 = (s32[1,2,256,8]{2,3,1,0:T(8,128)S(1)}, s32[1,2,256,8]{2,3,1,0:T(8,128)}, u32[]{:S(2)}) copy-start(s32[1,2,256,8]{2,3,1,0:T(8,128)} %param.13) | copy-start | bytes 49156
  22.6 10.4 %copy-start.4 = (s32[1,2,256]{2,1,0:T(2,128)S(1)}, s32[1,2,256]{2,1,0:T(2,128)}, u32[]{:S(2)}) copy-start(s32[1,2,256]{2,1,0:T(2,128)} %seg_ref.1) | copy-start | bytes 6148
  27.7 6.0 %collective-permute-start.6 = (bf16[256,256]{1,0:T(8,128)(2,1)S(1)}, bf16[256,256]{1,0:T(8,128)(2,1)S(1)}, u32[]{:S(2)}, u32[]{:S(2)}) collective-permute-start(bf16[256,256]{1,0:T(8,128)(2,1)S(1)} %merge.5.refs_0_), channel_id=1, source_target_pairs={{0,2},{2,0},{4,6},{6,4},{1,3},{3,1},{5,7},{7,5},{8,10},{10,8},{12,... | collective-permute-start | bytes 393224 | tf_op jit(solution)/shard_map/ppermute | solution.py:36
  28.3 5.4 %collective-permute-start.7 = (bf16[256,256]{1,0:T(8,128)(2,1)S(1)}, bf16[256,256]{1,0:T(8,128)(2,1)S(1)}, u32[]{:S(2)}, u32[]{:S(2)}) collective-permute-start(bf16[256,256]{1,0:T(8,128)(2,1)S(1)} %merge.5.refs_0_), channel_id=1, source_target_pairs={{0,4},{2,6},{4,0},{6,2},{1,5},{3,7},{5,1},{7,3},{8,12},{10,14},{12... | collective-permute-start | bytes 393224 | tf_op jit(solution)/shard_map/ppermute | solution.py:36
  29.4 6.9 %collective-permute-start.8 = (bf16[256,256]{1,0:T(8,128)(2,1)S(1)}, bf16[256,256]{1,0:T(8,128)(2,1)S(1)}, u32[]{:S(2)}, u32[]{:S(2)}) collective-permute-start(bf16[256,256]{1,0:T(8,128)(2,1)S(1)} %merge.5.refs_0_), channel_id=1, source_target_pairs={{0,6},{2,4},{4,2},{6,0},{1,7},{3,5},{5,3},{7,1},{8,14},{10,12},{12... | collective-permute-start | bytes 393224 | tf_op jit(solution)/shard_map/ppermute | solution.py:36
  31.3 10.0 %collective-permute-start.14 = (bf16[128,1024]{1,0:T(8,128)(2,1)S(1)}, bf16[128,1024]{1,0:T(8,128)(2,1)S(1)}, u32[]{:S(2)}, u32[]{:S(2)}) collective-permute-start(bf16[128,1024]{1,0:T(8,128)(2,1)S(1)} %get-tuple-element.23), channel_id=1, source_target_pairs={{0,2},{2,0},{4,6},{6,4},{1,3},{3,1},{5,7},{7,5},{8,10},{10,8},{12,... | collective-permute-start | bytes 786440 | tf_op jit(solution)/shard_map/ppermute | solution.py:36
  31.9 9.4 %collective-permute-start.15 = (bf16[128,1024]{1,0:T(8,128)(2,1)S(1)}, bf16[128,1024]{1,0:T(8,128)(2,1)S(1)}, u32[]{:S(2)}, u32[]{:S(2)}) collective-permute-start(bf16[128,1024]{1,0:T(8,128)(2,1)S(1)} %get-tuple-element.24), channel_id=1, source_target_pairs={{0,4},{2,6},{4,0},{6,2},{1,5},{3,7},{5,1},{7,3},{8,12},{10,14},{12... | collective-permute-start | bytes 786440 | tf_op jit(solution)/shard_map/ppermute | solution.py:36
  37.8 5.0 %collective-permute-start.11 = (bf16[256,256]{1,0:T(8,128)(2,1)S(1)}, bf16[256,256]{1,0:T(8,128)(2,1)S(1)}, u32[]{:S(2)}, u32[]{:S(2)}) collective-permute-start(bf16[256,256]{1,0:T(8,128)(2,1)S(1)} %get-tuple-element.20.refs_0_), channel_id=1, source_target_pairs={{0,2},{2,0},{4,6},{6,4},{1,3},{3,1},{5,7},{7,5},{8,10},{10,8},{12,... | collective-permute-start | bytes 393224 | tf_op jit(solution)/shard_map/ppermute | solution.py:36
  38.5 6.1 %collective-permute-start.12 = (bf16[256,256]{1,0:T(8,128)(2,1)S(1)}, bf16[256,256]{1,0:T(8,128)(2,1)S(1)}, u32[]{:S(2)}, u32[]{:S(2)}) collective-permute-start(bf16[256,256]{1,0:T(8,128)(2,1)S(1)} %get-tuple-element.20.refs_0_), channel_id=1, source_target_pairs={{0,4},{2,6},{4,0},{6,2},{1,5},{3,7},{5,1},{7,3},{8,12},{10,14},{12... | collective-permute-start | bytes 393224 | tf_op jit(solution)/shard_map/ppermute | solution.py:36
  40.7 5.9 %collective-permute-start.13 = (bf16[256,256]{1,0:T(8,128)(2,1)S(1)}, bf16[256,256]{1,0:T(8,128)(2,1)S(1)}, u32[]{:S(2)}, u32[]{:S(2)}) collective-permute-start(bf16[256,256]{1,0:T(8,128)(2,1)S(1)} %get-tuple-element.20.refs_0_), channel_id=1, source_target_pairs={{0,6},{2,4},{4,2},{6,0},{1,7},{3,5},{5,3},{7,1},{8,14},{10,12},{12... | collective-permute-start | bytes 393224 | tf_op jit(solution)/shard_map/ppermute | solution.py:36
  41.3 5.2 %collective-permute-start.16 = (bf16[3,256,1024]{2,1,0:T(8,128)(2,1)S(1)}, bf16[3,256,1024]{2,1,0:T(8,128)(2,1)S(1)}, u32[]{:S(2)}, u32[]{:S(2)}) collective-permute-start(bf16[3,256,1024]{2,1,0:T(8,128)(2,1)S(1)} %get-tuple-element.22.refs_8_), channel_id=1, source_target_pairs={{0,1},{1,0},{2,3},{3,2},{4,5},{5,4},{6,7},{7,6},{8,9},{9,8},{10,11... | collective-permute-start | bytes 4718600 | tf_op jit(solution)/shard_map/ppermute | solution.py:36
  41.4 5.1 %collective-permute-start.17 = (bf16[1,256,1024]{2,1,0:T(8,128)(2,1)S(1)}, bf16[1,256,1024]{2,1,0:T(8,128)(2,1)S(1)}, u32[]{:S(2)}, u32[]{:S(2)}) collective-permute-start(bf16[1,256,1024]{2,1,0:T(8,128)(2,1)S(1)} %stack.1.refs_9_), channel_id=1, source_target_pairs={{0,1},{1,0},{2,3},{3,2},{4,5},{5,4},{6,7},{7,6},{8,9},{9,8},{10,11... | collective-permute-start | bytes 1572872 | tf_op jit(solution)/shard_map/ppermute | solution.py:36
  46.5 5.3 %copy-start.5 = (bf16[256]{0:T(256)(128)(2,1)S(1)}, bf16[256]{0:T(256)(128)(2,1)}, u32[]{:S(2)}) copy-start(bf16[256]{0:T(256)(128)(2,1)} %param.19) | copy-start | bytes 1540
  46.6 10.6 %copy-start.2 = (bf16[1024,256]{1,0:T(8,128)(2,1)S(1)}, bf16[1024,256]{1,0:T(8,128)(2,1)}, u32[]{:S(2)}) copy-start(bf16[1024,256]{1,0:T(8,128)(2,1)} %refs_6_.1) | copy-start | bytes 1572868
  48.3 6.4 %collective-permute-start.18 = (bf16[256,256]{1,0:T(8,128)(2,1)S(1)}, bf16[256,256]{1,0:T(8,128)(2,1)S(1)}, u32[]{:S(2)}, u32[]{:S(2)}) collective-permute-start(bf16[256,256]{1,0:T(8,128)(2,1)S(1)} %get-tuple-element.25.refs_0_), channel_id=1, source_target_pairs={{0,2},{2,0},{4,6},{6,4},{1,3},{3,1},{5,7},{7,5},{8,10},{10,8},{12,... | collective-permute-start | bytes 393224 | tf_op jit(solution)/shard_map/ppermute | solution.py:36
  49.3 7.8 %collective-permute-start.19 = (bf16[256,256]{1,0:T(8,128)(2,1)S(1)}, bf16[256,256]{1,0:T(8,128)(2,1)S(1)}, u32[]{:S(2)}, u32[]{:S(2)}) collective-permute-start(bf16[256,256]{1,0:T(8,128)(2,1)S(1)} %get-tuple-element.25.refs_0_), channel_id=1, source_target_pairs={{0,4},{2,6},{4,0},{6,2},{1,5},{3,7},{5,1},{7,3},{8,12},{10,14},{12... | collective-permute-start | bytes 393224 | tf_op jit(solution)/shard_map/ppermute | solution.py:36
  50.2 6.9 %collective-permute-start.20 = (bf16[256,256]{1,0:T(8,128)(2,1)S(1)}, bf16[256,256]{1,0:T(8,128)(2,1)S(1)}, u32[]{:S(2)}, u32[]{:S(2)}) collective-permute-start(bf16[256,256]{1,0:T(8,128)(2,1)S(1)} %get-tuple-element.25.refs_0_), channel_id=1, source_target_pairs={{0,6},{2,4},{4,2},{6,0},{1,7},{3,5},{5,3},{7,1},{8,14},{10,12},{12... | collective-permute-start | bytes 393224 | tf_op jit(solution)/shard_map/ppermute | solution.py:36

commit v10 on v9

--- a/solution.py
+++ b/solution.py
@@ -98,19 +98,23 @@
     )(*asked, table, *after)
 
 
-def merge_kernel(a_ref, b_ref, *refs):
-    refs[-1][...] = a_ref[...] + b_ref[...]
-
-
-def merge(a, b, after):
+def merge_kernel(count, *refs):
+    total = refs[0][...]
+    for ref in refs[1:count]:
+        total = total + ref[...]
+    refs[-1][...] = total
+
+
+def merge(a, b, more, after):
+    count = 2 + len(more)
     return pl.pallas_call(
-        merge_kernel,
+        functools.partial(merge_kernel, count),
         out_shape=jax.ShapeDtypeStruct(a.shape, BF16),
-        in_specs=[VMEM] * 2 + [HBM] * len(after),
+        in_specs=[VMEM] * count + [HBM] * len(after),
         out_specs=VMEM,
         compiler_params=params(),
         name="merge",
-    )(a, b, *after)
+    )(a, b, *more, *after)
 
 
 def hold_kernel(*refs):
@@ -166,15 +170,23 @@
     return asked
 
 
-def gather_in(blocks, first, last):
-    blocks, step = dict(enumerate(blocks)), 1
-    while step < lax.axis_size("dp"):
-        at_end = 2 * step == lax.axis_size("dp")
+def gather_in(blocks, last):
+    n = lax.axis_size("dp")
+    blocks, step, late, first = dict(enumerate(blocks)), 1, [], None
+    while step < n:
         for k in sorted((k for k in blocks if k & step), reverse=True):
-            got = exchange(blocks.pop(k), "dp", step)
-            after = last if at_end else first
-            blocks[k ^ step] = merge(blocks[k ^ step], got, after)
-            first = [blocks[k ^ step]]
+            block = blocks.pop(k)
+            if k == step and 2 * step < n:
+                late.append((block, step))
+                continue
+            got = exchange(block, "dp", step)
+            if 2 * step == n:
+                got = hold(got, [], 32 * 10**9)
+                late = [exchange(hold(b, [first] if first is not None else []), "dp", at) for b, at in late]
+                blocks[k ^ step] = merge(blocks[k ^ step], got, late, last)
+            else:
+                blocks[k ^ step] = merge(blocks[k ^ step], got, [], [])
+            first = blocks[k ^ step]
         step = 2 * step
     return blocks[0]
 
@@ -374,7 +386,7 @@
         late = fetch(asked[-1:], batches, table, part, [])
         found = fetch(asked[:-1], batches, table, part, late) + late
 
-        piece = gather_in(found, [], [w_other])
+        piece = gather_in(found, [])
     else:
         piece = fetch_rows_padded(item_owner[:, 0], item_row, table, part)
         piece = lax.dynamic_index_in_dim(

time: 59.4 us -> 64.8 us (1.091)
  starting transfers between devices: 25 us -> 29.8 us
  other arithmetic: 3.99 us -> 1.72 us
  local copies, waits for them, and re-layouts: 0.04 us -> 1.64 us
  waiting for transfers between devices: 22.6 us -> 23.8 us
    ppermute x21, starting transfers between devices: 25 us -> 29.8 us  [exchange(): return lax.ppermute(value, axis, pairs)]
    unnamed x12 -> x18, local copies, waits for them, and re-layouts: 0.03 us -> 1.63 us
    mul x1, other arithmetic: 1.9 us -> 0.31 us  [on_device(): w_own = jnp.transpose(w_in[0], (1, 0, 2)) * gains[0][None, :, None]]
    ppermute x21, waiting for transfers between devices: 22.6 us -> 23.8 us  [exchange(): return lax.ppermute(value, axis, pairs)]
    unnamed x1, other arithmetic: 0.71 us -> 0.02 us
  transfers between devices with their start and end apart: 21 -> 21, of which waited for: 10 -> 13; matrix products, arithmetic and copies ran while one was open for 4% -> 1% of each run, Pallas kernels for 5% -> 4%
where the time goes in v10:
time: 64.8 us; the launch traced here: 64.6 us
  starting transfers between devices  29.8 us (46%)
  waiting for transfers between devices  23.8 us (37%)
  Pallas kernels  6.76 us (10%)
  other arithmetic  1.72 us (3%)
  local copies, waits for them, and re-layouts  1.64 us (3%)
  between operations  0.82 us (1%)
    ppermute x21, starting transfers between devices, exchange(): return lax.ppermute(value, axis, pairs)  29.8 us
    ppermute x21, waiting for transfers between devices, exchange(): return lax.ppermute(value, axis, pairs)  23.8 us
    pallas_call x1, Pallas kernels, on_device(): pl.pallas_call(functools.partial(last_kernel, mp_count, len(o_own)), out_...  2.06 us
    pallas_call x1, Pallas kernels, on_device(): pl.pallas_call(functools.partial(middle_kernel, mp_count, len(o_own)), ou...  1.76 us
    unnamed x18, local copies, waits for them, and re-layouts  1.63 us
    pallas_call x1, Pallas kernels, on_device(): pl.pallas_call(functools.partial(first_kernel, mp_count, places), out_sha...  1.43 us
  transfers between devices with their start and end apart: 21, of which 13 were waited for; matrix products, arithmetic and copies ran while one was open for 1% of the time, Pallas kernels for 4%

profile of v10, /device:TPU:0, one launch (start us, length us, event | category | flops | bytes accessed | tf_op | source)
XLA Modules:
  0.0 64.6 jit_solution(8459778989936847500)
XLA Ops:
  0.6 0.7 %broadcast_multiply_fusion = s32[512,1]{0,1:T(1,128)S(1)} fusion(s32[512,1]{0,1:T(1,128)} %param.10), kind=kLoop, calls=%fused_computation.4 | loop fusion | flops 512 | bytes 4096 | tf_op jit(solution)/shard_map/mul | solution.py:382
  1.3 0.7 %bitcast_add_fusion.refs_0_ = s32[4,128]{1,0:T(4,128)S(1)} fusion(s32[4,128]{1,0:T(4,128)S(1)} %bitcast.19, s32[512]{0:T(512)} %param.11), kind=kLoop, calls=%fused_computation.3 | loop fusion | flops 512 | bytes 6144 | tf_op jit(solution)/shard_map/add | solution.py:382
  2.0 3.0 %collective-permute-start = (s32[4,128]{1,0:T(4,128)S(1)}, s32[4,128]{1,0:T(4,128)S(1)}, u32[]{:S(2)}, u32[]{:S(2)}) collective-permute-start(s32[4,128]{1,0:T(4,128)S(1)} %bitcast_add_fusion.refs_0_), channel_id=1, source_target_pairs={{0,8},{8,0},{16,24},{24,16},{1,9},{9,1},{17,25},{25,17},{2,10},{10... | collective-permute-start | bytes 6152 | tf_op jit(solution)/shard_map/ppermute | solution.py:36
  5.0 1.6 %collective-permute-done.refs_1_ = s32[4,128]{1,0:T(4,128)S(1)} collective-permute-done((s32[4,128]{1,0:T(4,128)S(1)}, s32[4,128]{1,0:T(4,128)S(1)}, u32[]{:S(2)}, u32[]{:S(2)}) %collective-permute-start) | collective-permute-done | bytes 2080 | tf_op jit(solution)/shard_map/ppermute | solution.py:36
  6.6 3.0 %collective-permute-start.1 = (s32[8,128]{1,0:T(8,128)S(1)}, s32[8,128]{1,0:T(8,128)S(1)}, u32[]{:S(2)}, u32[]{:S(2)}) collective-permute-start(s32[8,128]{1,0:T(8,128)S(1)} %pad_add_fusion), channel_id=1, source_target_pairs={{0,16},{8,24},{16,0},{24,8},{1,17},{9,25},{17,1},{25,9},{2,18},{10... | collective-permute-start | bytes 12296 | tf_op jit(solution)/shard_map/ppermute | solution.py:36
  9.6 1.6 %collective-permute-done.1 = s32[8,128]{1,0:T(8,128)S(1)} collective-permute-done((s32[8,128]{1,0:T(8,128)S(1)}, s32[8,128]{1,0:T(8,128)S(1)}, u32[]{:S(2)}, u32[]{:S(2)}) %collective-permute-start.1) | collective-permute-done | bytes 4128 | tf_op jit(solution)/shard_map/ppermute | solution.py:36
  11.2 1.6 %copy-done = bf16[1024,1024]{1,0:T(8,128)(2,1)S(1)} copy-done((bf16[1024,1024]{1,0:T(8,128)(2,1)S(1)}, bf16[1024,1024]{1,0:T(8,128)(2,1)}, u32[]{:S(2)}) %copy-start) | copy-done | bytes 2097176
  12.8 0.4 fetch.2.refs_4_
  13.2 2.0 %collective-permute-start.2 = (bf16[256,256]{1,0:T(8,128)(2,1)S(1)}, bf16[256,256]{1,0:T(8,128)(2,1)S(1)}, u32[]{:S(2)}, u32[]{:S(2)}) collective-permute-start(bf16[256,256]{1,0:T(8,128)(2,1)S(1)} %fetch.2.refs_4_), channel_id=1, source_target_pairs={{0,8},{8,0},{16,24},{24,16},{1,9},{9,1},{17,25},{25,17},{2,10},{10... | collective-permute-start | bytes 393224 | tf_op jit(solution)/shard_map/ppermute | solution.py:36
  15.2 1.5 %collective-permute-start.8 = (bf16[256,1024]{1,0:T(8,128)(2,1)}, bf16[256,1024]{1,0:T(8,128)(2,1)S(1)}, u32[]{:S(2)}, u32[]{:S(2)}) collective-permute-start(bf16[256,1024]{1,0:T(8,128)(2,1)} %bitcast.15), channel_id=1, source_target_pairs={{0,2},{2,0},{4,6},{6,4},{1,3},{3,1},{5,7},{7,5},{8,10},{10,8},{12,... | collective-permute-start | bytes 1572872 | tf_op jit(solution)/shard_map/ppermute | solution.py:36
  16.7 1.5 %collective-permute-start.9 = (bf16[256,1024]{1,0:T(8,128)(2,1)}, bf16[256,1024]{1,0:T(8,128)(2,1)S(1)}, u32[]{:S(2)}, u32[]{:S(2)}) collective-permute-start(bf16[256,1024]{1,0:T(8,128)(2,1)} %bitcast.16), channel_id=1, source_target_pairs={{0,4},{2,6},{4,0},{6,2},{1,5},{3,7},{5,1},{7,3},{8,12},{10,14},{12... | collective-permute-start | bytes 1572872 | tf_op jit(solution)/shard_map/ppermute | solution.py:36
  18.3 0.7 %fetch.3 = (bf16[256,256]{1,0:T(8,128)(2,1)S(1)}, bf16[256,256]{1,0:T(8,128)(2,1)S(1)}, bf16[256,256]{1,0:T(8,128)(2,1)S(1)}) custom-call(s32[4,128]{1,0:T(4,128)S(1)} %bitcast_add_fusion.refs_0_, s32[4,128]{1,0:T(4,128)S(1)} %collective-permute-done.refs_1_, s32[4,128]{1,0:T(4,128)S(1)} %get-tuple-element.31.refs_2_, bf16[1024,1024]{1,0:T(8,128)(2,1)S(1)} %copy-done.1, ...), custom_call_target="tpu_custom_call" | custom-call | flops 402653184 | bytes 524288 | tf_op jit(solution)/shard_map/fetch/pallas_call | solution.py:86
  19.0 3.4 %collective-permute-start.3 = (bf16[256,256]{1,0:T(8,128)(2,1)S(1)}, bf16[256,256]{1,0:T(8,128)(2,1)S(1)}, u32[]{:S(2)}, u32[]{:S(2)}) collective-permute-start(bf16[256,256]{1,0:T(8,128)(2,1)S(1)} %merge.2.refs_1_), channel_id=1, source_target_pairs={{0,16},{8,24},{16,0},{24,8},{1,17},{9,25},{17,1},{25,9},{2,18},{10... | collective-permute-start | bytes 393224 | tf_op jit(solution)/shard_map/ppermute | solution.py:36
  22.4 0.3 fusion.refs_0_
  22.7 0.1 collective-permute-start.10
  22.8 0.0 copy-start.4
  22.9 0.0 copy-start.2
  22.9 0.5 collective-permute-start.4
  23.4 3.4 %collective-permute-done.3.refs_0_ = bf16[256,256]{1,0:T(8,128)(2,1)S(1)} collective-permute-done((bf16[256,256]{1,0:T(8,128)(2,1)S(1)}, bf16[256,256]{1,0:T(8,128)(2,1)S(1)}, u32[]{:S(2)}, u32[]{:S(2)}) %collective-permute-start.3) | collective-permute-done | bytes 131104 | tf_op jit(solution)/shard_map/ppermute | solution.py:36
  26.9 2.7 %collective-permute-done.4.refs_2_ = bf16[256,256]{1,0:T(8,128)(2,1)S(1)} collective-permute-done((bf16[256,256]{1,0:T(8,128)(2,1)S(1)}, bf16[256,256]{1,0:T(8,128)(2,1)S(1)}, u32[]{:S(2)}, u32[]{:S(2)}) %collective-permute-start.4) | collective-permute-done | bytes 131104 | tf_op jit(solution)/shard_map/ppermute | solution.py:36
  29.6 1.6 %collective-permute-start.5 = (bf16[256,256]{1,0:T(8,128)(2,1)S(1)}, bf16[256,256]{1,0:T(8,128)(2,1)S(1)}, u32[]{:S(2)}, u32[]{:S(2)}) collective-permute-start(bf16[256,256]{1,0:T(8,128)(2,1)S(1)} %merge.3.refs_0_), channel_id=1, source_target_pairs={{0,2},{2,0},{4,6},{6,4},{1,3},{3,1},{5,7},{7,5},{8,10},{10,8},{12,... | collective-permute-start | bytes 393224 | tf_op jit(solution)/shard_map/ppermute | solution.py:36
  31.1 1.5 %collective-permute-start.6 = (bf16[256,256]{1,0:T(8,128)(2,1)S(1)}, bf16[256,256]{1,0:T(8,128)(2,1)S(1)}, u32[]{:S(2)}, u32[]{:S(2)}) collective-permute-start(bf16[256,256]{1,0:T(8,128)(2,1)S(1)} %merge.3.refs_0_), channel_id=1, source_target_pairs={{0,4},{2,6},{4,0},{6,2},{1,5},{3,7},{5,1},{7,3},{8,12},{10,14},{12... | collective-permute-start | bytes 393224 | tf_op jit(solution)/shard_map/ppermute | solution.py:36
  32.7 0.5 collective-permute-start.7
  33.2 0.1 cut.1
  33.2 1.6 %collective-permute-start.14 = (bf16[128,1024]{1,0:T(8,128)(2,1)S(1)}, bf16[128,1024]{1,0:T(8,128)(2,1)S(1)}, u32[]{:S(2)}, u32[]{:S(2)}) collective-permute-start(bf16[128,1024]{1,0:T(8,128)(2,1)S(1)} %get-tuple-element.23), channel_id=1, source_target_pairs={{0,2},{2,0},{4,6},{6,4},{1,3},{3,1},{5,7},{7,5},{8,10},{10,8},{12,... | collective-permute-start | bytes 786440 | tf_op jit(solution)/shard_map/ppermute | solution.py:36
  34.8 0.7 %collective-permute-done.5.refs_1_ = bf16[256,256]{1,0:T(8,128)(2,1)S(1)} collective-permute-done((bf16[256,256]{1,0:T(8,128)(2,1)S(1)}, bf16[256,256]{1,0:T(8,128)(2,1)S(1)}, u32[]{:S(2)}, u32[]{:S(2)}) %collective-permute-start.5) | collective-permute-done | bytes 131104 | tf_op jit(solution)/shard_map/ppermute | solution.py:36
  35.5 1.5 %collective-permute-start.15 = (bf16[128,1024]{1,0:T(8,128)(2,1)S(1)}, bf16[128,1024]{1,0:T(8,128)(2,1)S(1)}, u32[]{:S(2)}, u32[]{:S(2)}) collective-permute-start(bf16[128,1024]{1,0:T(8,128)(2,1)S(1)} %get-tuple-element.24), channel_id=1, source_target_pairs={{0,4},{2,6},{4,0},{6,2},{1,5},{3,7},{5,1},{7,3},{8,12},{10,14},{12... | collective-permute-start | bytes 786440 | tf_op jit(solution)/shard_map/ppermute | solution.py:36
  37.0 0.3 prepare.1
  37.3 2.1 %collective-permute-done.6.refs_2_ = bf16[256,256]{1,0:T(8,128)(2,1)S(1)} collective-permute-done((bf16[256,256]{1,0:T(8,128)(2,1)S(1)}, bf16[256,256]{1,0:T(8,128)(2,1)S(1)}, u32[]{:S(2)}, u32[]{:S(2)}) %collective-permute-start.6) | collective-permute-done | bytes 131104 | tf_op jit(solution)/shard_map/ppermute | solution.py:36
  39.3 0.7 %collective-permute-done.7.refs_3_ = bf16[256,256]{1,0:T(8,128)(2,1)S(1)} collective-permute-done((bf16[256,256]{1,0:T(8,128)(2,1)S(1)}, bf16[256,256]{1,0:T(8,128)(2,1)S(1)}, u32[]{:S(2)}, u32[]{:S(2)}) %collective-permute-start.7) | collective-permute-done | bytes 131104 | tf_op jit(solution)/shard_map/ppermute | solution.py:36
  40.1 1.4 %section0_front.1 = (bf16[256,256]{1,0:T(8,128)(2,1)S(1)}, bf16[256,1024]{1,0:T(8,128)(2,1)S(1)}, bf16[3,256,1024]{2,1,0:T(8,128)(2,1)S(1)}) custom-call(bf16[256,256]{1,0:T(8,128)(2,1)S(1)} %merge.3.refs_0_, bf16[256,256]{1,0:T(8,128)(2,1)S(1)} %collective-permute-done.5.refs_1_, bf16[256,256]{1,0:T(8,128)(2,1)S(1)} %collective-permute-done.6.refs_2_, ...), custom_call_target="tpu_custom_call" | custom-call | flops 603979776 | bytes 2097152 | tf_op jit(solution)/shard_map/section0_front/pallas_call | solution.py:403
  41.5 1.3 %collective-permute-start.11 = (bf16[256,256]{1,0:T(8,128)(2,1)S(1)}, bf16[256,256]{1,0:T(8,128)(2,1)S(1)}, u32[]{:S(2)}, u32[]{:S(2)}) collective-permute-start(bf16[256,256]{1,0:T(8,128)(2,1)S(1)} %get-tuple-element.20.refs_0_), channel_id=1, source_target_pairs={{0,2},{2,0},{4,6},{6,4},{1,3},{3,1},{5,7},{7,5},{8,10},{10,8},{12,... | collective-permute-start | bytes 393224 | tf_op jit(solution)/shard_map/ppermute | solution.py:36
  42.8 0.6 collective-permute-start.12
  43.4 1.6 %collective-permute-start.13 = (bf16[256,256]{1,0:T(8,128)(2,1)S(1)}, bf16[256,256]{1,0:T(8,128)(2,1)S(1)}, u32[]{:S(2)}, u32[]{:S(2)}) collective-permute-start(bf16[256,256]{1,0:T(8,128)(2,1)S(1)} %get-tuple-element.20.refs_0_), channel_id=1, source_target_pairs={{0,6},{2,4},{4,2},{6,0},{1,7},{3,5},{5,3},{7,1},{8,14},{10,12},{12... | collective-permute-start | bytes 393224 | tf_op jit(solution)/shard_map/ppermute | solution.py:36
  45.1 0.6 collective-permute-done.15.refs_1_
  45.6 0.1 stack.1.refs_9_
  45.7 0.1 collective-permute-start.17
  45.8 0.5 collective-permute-start.16
  46.3 1.5 %collective-permute-done.11.refs_1_ = bf16[256,256]{1,0:T(8,128)(2,1)S(1)} collective-permute-done((bf16[256,256]{1,0:T(8,128)(2,1)S(1)}, bf16[256,256]{1,0:T(8,128)(2,1)S(1)}, u32[]{:S(2)}, u32[]{:S(2)}) %collective-permute-start.11) | collective-permute-done | bytes 131104 | tf_op jit(solution)/shard_map/ppermute | solution.py:36
  47.8 2.6 %collective-permute-done.12.refs_2_ = bf16[256,256]{1,0:T(8,128)(2,1)S(1)} collective-permute-done((bf16[256,256]{1,0:T(8,128)(2,1)S(1)}, bf16[256,256]{1,0:T(8,128)(2,1)S(1)}, u32[]{:S(2)}, u32[]{:S(2)}) %collective-permute-start.12) | collective-permute-done | bytes 131104 | tf_op jit(solution)/shard_map/ppermute | solution.py:36
  50.4 1.8 %section0_back_section1_front.1 = (bf16[256,256]{1,0:T(8,128)(2,1)S(1)}, bf16[256,1024]{1,0:T(8,128)(2,1)S(1)}) custom-call(bf16[256,256]{1,0:T(8,128)(2,1)S(1)} %get-tuple-element.20.refs_0_, bf16[256,256]{1,0:T(8,128)(2,1)S(1)} %collective-permute-done.11.refs_1_, bf16[256,256]{1,0:T(8,128)(2,1)S(1)} %collective-permute-done.12.refs_2_, ...), custom_call_target="tpu_custom_call" | custom-call | flops 1140850688 | bytes 4194304 | tf_op jit(solution)/shard_map/section0_back_section1_front/pallas_call | solution.py:426
  52.2 1.3 %collective-permute-start.18 = (bf16[256,256]{1,0:T(8,128)(2,1)S(1)}, bf16[256,256]{1,0:T(8,128)(2,1)S(1)}, u32[]{:S(2)}, u32[]{:S(2)}) collective-permute-start(bf16[256,256]{1,0:T(8,128)(2,1)S(1)} %get-tuple-element.25.refs_0_), channel_id=1, source_target_pairs={{0,2},{2,0},{4,6},{6,4},{1,3},{3,1},{5,7},{7,5},{8,10},{10,8},{12,... | collective-permute-start | bytes 393224 | tf_op jit(solution)/shard_map/ppermute | solution.py:36
  53.5 1.3 %collective-permute-start.19 = (bf16[256,256]{1,0:T(8,128)(2,1)S(1)}, bf16[256,256]{1,0:T(8,128)(2,1)S(1)}, u32[]{:S(2)}, u32[]{:S(2)}) collective-permute-start(bf16[256,256]{1,0:T(8,128)(2,1)S(1)} %get-tuple-element.25.refs_0_), channel_id=1, source_target_pairs={{0,4},{2,6},{4,0},{6,2},{1,5},{3,7},{5,1},{7,3},{8,12},{10,14},{12... | collective-permute-start | bytes 393224 | tf_op jit(solution)/shard_map/ppermute | solution.py:36
  54.8 1.4 %collective-permute-start.20 = (bf16[256,256]{1,0:T(8,128)(2,1)S(1)}, bf16[256,256]{1,0:T(8,128)(2,1)S(1)}, u32[]{:S(2)}, u32[]{:S(2)}) collective-permute-start(bf16[256,256]{1,0:T(8,128)(2,1)S(1)} %get-tuple-element.25.refs_0_), channel_id=1, source_target_pairs={{0,6},{2,4},{4,2},{6,0},{1,7},{3,5},{5,3},{7,1},{8,14},{10,12},{12... | collective-permute-start | bytes 393224 | tf_op jit(solution)/shard_map/ppermute | solution.py:36
  56.2 1.1 %collective-permute-done.18.refs_1_ = bf16[256,256]{1,0:T(8,128)(2,1)S(1)} collective-permute-done((bf16[256,256]{1,0:T(8,128)(2,1)S(1)}, bf16[256,256]{1,0:T(8,128)(2,1)S(1)}, u32[]{:S(2)}, u32[]{:S(2)}) %collective-permute-start.18) | collective-permute-done | bytes 131104 | tf_op jit(solution)/shard_map/ppermute | solution.py:36
  57.3 3.3 %collective-permute-done.19.refs_2_ = bf16[256,256]{1,0:T(8,128)(2,1)S(1)} collective-permute-done((bf16[256,256]{1,0:T(8,128)(2,1)S(1)}, bf16[256,256]{1,0:T(8,128)(2,1)S(1)}, u32[]{:S(2)}, u32[]{:S(2)}) %collective-permute-start.19) | collective-permute-done | bytes 131104 | tf_op jit(solution)/shard_map/ppermute | solution.py:36
  60.6 1.8 %collective-permute-done.20.refs_3_ = bf16[256,256]{1,0:T(8,128)(2,1)S(1)} collective-permute-done((bf16[256,256]{1,0:T(8,128)(2,1)S(1)}, bf16[256,256]{1,0:T(8,128)(2,1)S(1)}, u32[]{:S(2)}, u32[]{:S(2)}) %collective-permute-start.20) | collective-permute-done | bytes 131104 | tf_op jit(solution)/shard_map/ppermute | solution.py:36
  62.5 2.1 %section1_back_context.1 = (bf16[256,1024]{1,0:T(8,128)(2,1)}, bf16[256,256]{1,0:T(8,128)(2,1)}) custom-call(bf16[256,256]{1,0:T(8,128)(2,1)S(1)} %get-tuple-element.25.refs_0_, bf16[256,256]{1,0:T(8,128)(2,1)S(1)} %collective-permute-done.18.refs_1_, bf16[256,256]{1,0:T(8,128)(2,1)S(1)} %collective-permute-done.19.refs_2_, ...), custom_call_target="tpu_custom_call" | custom-call | flops 805306368 | bytes 2097152 | tf_op jit(solution)/shard_map/section1_back_context/pallas_call | solution.py:440
  (33 shorter events, 0.1 us)
Async XLA Ops:
  0.6 17.6 %copy-start.7 = (bf16[1,1024]{1,0:T(2,128)(2,1)S(1)}, bf16[1,1024]{1,0:T(2,128)(2,1)}, u32[]{:S(2)}) copy-start(bf16[1,1024]{1,0:T(2,128)(2,1)} %param.15) | copy-start | bytes 6148
  2.0 4.6 %collective-permute-start = (s32[4,128]{1,0:T(4,128)S(1)}, s32[4,128]{1,0:T(4,128)S(1)}, u32[]{:S(2)}, u32[]{:S(2)}) collective-permute-start(s32[4,128]{1,0:T(4,128)S(1)} %bitcast_add_fusion.refs_0_), channel_id=1, source_target_pairs={{0,8},{8,0},{16,24},{24,16},{1,9},{9,1},{17,25},{25,17},{2,10},{10... | collective-permute-start | bytes 6152 | tf_op jit(solution)/shard_map/ppermute | solution.py:36
  6.6 4.6 %collective-permute-start.1 = (s32[8,128]{1,0:T(8,128)S(1)}, s32[8,128]{1,0:T(8,128)S(1)}, u32[]{:S(2)}, u32[]{:S(2)}) collective-permute-start(s32[8,128]{1,0:T(8,128)S(1)} %pad_add_fusion), channel_id=1, source_target_pairs={{0,16},{8,24},{16,0},{24,8},{1,17},{9,25},{17,1},{25,9},{2,18},{10... | collective-permute-start | bytes 12296 | tf_op jit(solution)/shard_map/ppermute | solution.py:36
  11.2 1.6 %copy-start = (bf16[1024,1024]{1,0:T(8,128)(2,1)S(1)}, bf16[1024,1024]{1,0:T(8,128)(2,1)}, u32[]{:S(2)}) copy-start(bf16[1024,1024]{1,0:T(8,128)(2,1)} %refs_3_.1) | copy-start | bytes 6291460
  12.8 5.4 %copy-start.1 = (bf16[1024,1024]{1,0:T(8,128)(2,1)S(1)}, bf16[1024,1024]{1,0:T(8,128)(2,1)}, u32[]{:S(2)}) copy-start(bf16[1024,1024]{1,0:T(8,128)(2,1)} %refs_3_.1) | copy-start | bytes 6291460
  13.2 5.7 %collective-permute-start.2 = (bf16[256,256]{1,0:T(8,128)(2,1)S(1)}, bf16[256,256]{1,0:T(8,128)(2,1)S(1)}, u32[]{:S(2)}, u32[]{:S(2)}) collective-permute-start(bf16[256,256]{1,0:T(8,128)(2,1)S(1)} %fetch.2.refs_4_), channel_id=1, source_target_pairs={{0,8},{8,0},{16,24},{24,16},{1,9},{9,1},{17,25},{25,17},{2,10},{10... | collective-permute-start | bytes 393224 | tf_op jit(solution)/shard_map/ppermute | solution.py:36
  15.2 17.5 %collective-permute-start.8 = (bf16[256,1024]{1,0:T(8,128)(2,1)}, bf16[256,1024]{1,0:T(8,128)(2,1)S(1)}, u32[]{:S(2)}, u32[]{:S(2)}) collective-permute-start(bf16[256,1024]{1,0:T(8,128)(2,1)} %bitcast.15), channel_id=1, source_target_pairs={{0,2},{2,0},{4,6},{6,4},{1,3},{3,1},{5,7},{7,5},{8,10},{10,8},{12,... | collective-permute-start | bytes 1572872 | tf_op jit(solution)/shard_map/ppermute | solution.py:36
  16.7 16.5 %collective-permute-start.9 = (bf16[256,1024]{1,0:T(8,128)(2,1)}, bf16[256,1024]{1,0:T(8,128)(2,1)S(1)}, u32[]{:S(2)}, u32[]{:S(2)}) collective-permute-start(bf16[256,1024]{1,0:T(8,128)(2,1)} %bitcast.16), channel_id=1, source_target_pairs={{0,4},{2,6},{4,0},{6,2},{1,5},{3,7},{5,1},{7,3},{8,12},{10,14},{12... | collective-permute-start | bytes 1572872 | tf_op jit(solution)/shard_map/ppermute | solution.py:36
  18.2 4.2 %copy-start.6 = (bf16[1,1024,4,256]{3,2,1,0:T(4,128)(2,1)S(1)}, bf16[1,1024,4,256]{3,2,1,0:T(4,128)(2,1)}, u32[]{:S(2)}) copy-start(bf16[1,1024,4,256]{3,2,1,0:T(4,128)(2,1)} %param.16) | copy-start | bytes 6291460
  19.0 7.9 %collective-permute-start.3 = (bf16[256,256]{1,0:T(8,128)(2,1)S(1)}, bf16[256,256]{1,0:T(8,128)(2,1)S(1)}, u32[]{:S(2)}, u32[]{:S(2)}) collective-permute-start(bf16[256,256]{1,0:T(8,128)(2,1)S(1)} %merge.2.refs_1_), channel_id=1, source_target_pairs={{0,16},{8,24},{16,0},{24,8},{1,17},{9,25},{17,1},{25,9},{2,18},{10... | collective-permute-start | bytes 393224 | tf_op jit(solution)/shard_map/ppermute | solution.py:36
  22.7 17.3 %collective-permute-start.10 = (bf16[4,1024,256]{2,1,0:T(8,128)(2,1)S(1)}, bf16[4,1024,256]{2,1,0:T(8,128)(2,1)S(1)}, u32[]{:S(2)}, u32[]{:S(2)}) collective-permute-start(bf16[4,1024,256]{2,1,0:T(8,128)(2,1)S(1)} %hold.6.refs_8_.refs_6_), channel_id=1, source_target_pairs={{0,1},{1,0},{2,3},{3,2},{4,5},{5,4},{6,7},{7,6},{8,9},{9,8},{10,11... | collective-permute-start | bytes 6291464 | tf_op jit(solution)/shard_map/ppermute | solution.py:36
  22.8 14.2 %copy-start.4 = (s32[1,2,256,8]{2,3,1,0:T(8,128)S(1)}, s32[1,2,256,8]{2,3,1,0:T(8,128)}, u32[]{:S(2)}) copy-start(s32[1,2,256,8]{2,3,1,0:T(8,128)} %param.13) | copy-start | bytes 49156
  22.8 14.1 %copy-start.5 = (s32[1,2,256]{2,1,0:T(2,128)S(1)}, s32[1,2,256]{2,1,0:T(2,128)}, u32[]{:S(2)}) copy-start(s32[1,2,256]{2,1,0:T(2,128)} %seg_ref.1) | copy-start | bytes 6148
  22.9 17.2 %copy-start.2 = (bf16[1,256,1024]{2,1,0:T(8,128)(2,1)S(1)}, bf16[1,256,1024]{2,1,0:T(8,128)(2,1)}, u32[]{:S(2)}) copy-start(bf16[1,256,1024]{2,1,0:T(8,128)(2,1)} %param.17) | copy-start | bytes 1572868
  22.9 6.7 %collective-permute-start.4 = (bf16[256,256]{1,0:T(8,128)(2,1)S(1)}, bf16[256,256]{1,0:T(8,128)(2,1)S(1)}, u32[]{:S(2)}, u32[]{:S(2)}) collective-permute-start(bf16[256,256]{1,0:T(8,128)(2,1)S(1)} %hold.5), channel_id=1, source_target_pairs={{0,8},{8,0},{16,24},{24,16},{1,9},{9,1},{17,25},{25,17},{2,10},{10... | collective-permute-start | bytes 393224 | tf_op jit(solution)/shard_map/ppermute | solution.py:36
  29.6 5.9 %collective-permute-start.5 = (bf16[256,256]{1,0:T(8,128)(2,1)S(1)}, bf16[256,256]{1,0:T(8,128)(2,1)S(1)}, u32[]{:S(2)}, u32[]{:S(2)}) collective-permute-start(bf16[256,256]{1,0:T(8,128)(2,1)S(1)} %merge.3.refs_0_), channel_id=1, source_target_pairs={{0,2},{2,0},{4,6},{6,4},{1,3},{3,1},{5,7},{7,5},{8,10},{10,8},{12,... | collective-permute-start | bytes 393224 | tf_op jit(solution)/shard_map/ppermute | solution.py:36
  31.1 8.2 %collective-permute-start.6 = (bf16[256,256]{1,0:T(8,128)(2,1)S(1)}, bf16[256,256]{1,0:T(8,128)(2,1)S(1)}, u32[]{:S(2)}, u32[]{:S(2)}) collective-permute-start(bf16[256,256]{1,0:T(8,128)(2,1)S(1)} %merge.3.refs_0_), channel_id=1, source_target_pairs={{0,4},{2,6},{4,0},{6,2},{1,5},{3,7},{5,1},{7,3},{8,12},{10,14},{12... | collective-permute-start | bytes 393224 | tf_op jit(solution)/shard_map/ppermute | solution.py:36
  32.7 7.4 %collective-permute-start.7 = (bf16[256,256]{1,0:T(8,128)(2,1)S(1)}, bf16[256,256]{1,0:T(8,128)(2,1)S(1)}, u32[]{:S(2)}, u32[]{:S(2)}) collective-permute-start(bf16[256,256]{1,0:T(8,128)(2,1)S(1)} %merge.3.refs_0_), channel_id=1, source_target_pairs={{0,6},{2,4},{4,2},{6,0},{1,7},{3,5},{5,3},{7,1},{8,14},{10,12},{12... | collective-permute-start | bytes 393224 | tf_op jit(solution)/shard_map/ppermute | solution.py:36
  33.2 11.8 %collective-permute-start.14 = (bf16[128,1024]{1,0:T(8,128)(2,1)S(1)}, bf16[128,1024]{1,0:T(8,128)(2,1)S(1)}, u32[]{:S(2)}, u32[]{:S(2)}) collective-permute-start(bf16[128,1024]{1,0:T(8,128)(2,1)S(1)} %get-tuple-element.23), channel_id=1, source_target_pairs={{0,2},{2,0},{4,6},{6,4},{1,3},{3,1},{5,7},{7,5},{8,10},{10,8},{12,... | collective-permute-start | bytes 786440 | tf_op jit(solution)/shard_map/ppermute | solution.py:36
  35.5 10.2 %collective-permute-start.15 = (bf16[128,1024]{1,0:T(8,128)(2,1)S(1)}, bf16[128,1024]{1,0:T(8,128)(2,1)S(1)}, u32[]{:S(2)}, u32[]{:S(2)}) collective-permute-start(bf16[128,1024]{1,0:T(8,128)(2,1)S(1)} %get-tuple-element.24), channel_id=1, source_target_pairs={{0,4},{2,6},{4,0},{6,2},{1,5},{3,7},{5,1},{7,3},{8,12},{10,14},{12... | collective-permute-start | bytes 786440 | tf_op jit(solution)/shard_map/ppermute | solution.py:36
  41.5 6.3 %collective-permute-start.11 = (bf16[256,256]{1,0:T(8,128)(2,1)S(1)}, bf16[256,256]{1,0:T(8,128)(2,1)S(1)}, u32[]{:S(2)}, u32[]{:S(2)}) collective-permute-start(bf16[256,256]{1,0:T(8,128)(2,1)S(1)} %get-tuple-element.20.refs_0_), channel_id=1, source_target_pairs={{0,2},{2,0},{4,6},{6,4},{1,3},{3,1},{5,7},{7,5},{8,10},{10,8},{12,... | collective-permute-start | bytes 393224 | tf_op jit(solution)/shard_map/ppermute | solution.py:36
  42.8 7.5 %collective-permute-start.12 = (bf16[256,256]{1,0:T(8,128)(2,1)S(1)}, bf16[256,256]{1,0:T(8,128)(2,1)S(1)}, u32[]{:S(2)}, u32[]{:S(2)}) collective-permute-start(bf16[256,256]{1,0:T(8,128)(2,1)S(1)} %get-tuple-element.20.refs_0_), channel_id=1, source_target_pairs={{0,4},{2,6},{4,0},{6,2},{1,5},{3,7},{5,1},{7,3},{8,12},{10,14},{12... | collective-permute-start | bytes 393224 | tf_op jit(solution)/shard_map/ppermute | solution.py:36
  43.4 7.0 %collective-permute-start.13 = (bf16[256,256]{1,0:T(8,128)(2,1)S(1)}, bf16[256,256]{1,0:T(8,128)(2,1)S(1)}, u32[]{:S(2)}, u32[]{:S(2)}) collective-permute-start(bf16[256,256]{1,0:T(8,128)(2,1)S(1)} %get-tuple-element.20.refs_0_), channel_id=1, source_target_pairs={{0,6},{2,4},{4,2},{6,0},{1,7},{3,5},{5,3},{7,1},{8,14},{10,12},{12... | collective-permute-start | bytes 393224 | tf_op jit(solution)/shard_map/ppermute | solution.py:36
  45.7 4.7 %collective-permute-start.17 = (bf16[1,256,1024]{2,1,0:T(8,128)(2,1)S(1)}, bf16[1,256,1024]{2,1,0:T(8,128)(2,1)S(1)}, u32[]{:S(2)}, u32[]{:S(2)}) collective-permute-start(bf16[1,256,1024]{2,1,0:T(8,128)(2,1)S(1)} %stack.1.refs_9_), channel_id=1, source_target_pairs={{0,1},{1,0},{2,3},{3,2},{4,5},{5,4},{6,7},{7,6},{8,9},{9,8},{10,11... | collective-permute-start | bytes 1572872 | tf_op jit(solution)/shard_map/ppermute | solution.py:36
  45.8 4.6 %collective-permute-start.16 = (bf16[3,256,1024]{2,1,0:T(8,128)(2,1)S(1)}, bf16[3,256,1024]{2,1,0:T(8,128)(2,1)S(1)}, u32[]{:S(2)}, u32[]{:S(2)}) collective-permute-start(bf16[3,256,1024]{2,1,0:T(8,128)(2,1)S(1)} %get-tuple-element.22.refs_8_), channel_id=1, source_target_pairs={{0,1},{1,0},{2,3},{3,2},{4,5},{5,4},{6,7},{7,6},{8,9},{9,8},{10,11... | collective-permute-start | bytes 4718600 | tf_op jit(solution)/shard_map/ppermute | solution.py:36
  50.4 5.8 %copy-start.8 = (bf16[256]{0:T(256)(128)(2,1)S(1)}, bf16[256]{0:T(256)(128)(2,1)}, u32[]{:S(2)}) copy-start(bf16[256]{0:T(256)(128)(2,1)} %param.19) | copy-start | bytes 1540
  50.4 12.1 %copy-start.3 = (bf16[1024,256]{1,0:T(8,128)(2,1)S(1)}, bf16[1024,256]{1,0:T(8,128)(2,1)}, u32[]{:S(2)}) copy-start(bf16[1024,256]{1,0:T(8,128)(2,1)} %refs_6_.1) | copy-start | bytes 1572868
  52.2 5.2 %collective-permute-start.18 = (bf16[256,256]{1,0:T(8,128)(2,1)S(1)}, bf16[256,256]{1,0:T(8,128)(2,1)S(1)}, u32[]{:S(2)}, u32[]{:S(2)}) collective-permute-start(bf16[256,256]{1,0:T(8,128)(2,1)S(1)} %get-tuple-element.25.refs_0_), channel_id=1, source_target_pairs={{0,2},{2,0},{4,6},{6,4},{1,3},{3,1},{5,7},{7,5},{8,10},{10,8},{12,... | collective-permute-start | bytes 393224 | tf_op jit(solution)/shard_map/ppermute | solution.py:36
  53.5 7.1 %collective-permute-start.19 = (bf16[256,256]{1,0:T(8,128)(2,1)S(1)}, bf16[256,256]{1,0:T(8,128)(2,1)S(1)}, u32[]{:S(2)}, u32[]{:S(2)}) collective-permute-start(bf16[256,256]{1,0:T(8,128)(2,1)S(1)} %get-tuple-element.25.refs_0_), channel_id=1, source_target_pairs={{0,4},{2,6},{4,0},{6,2},{1,5},{3,7},{5,1},{7,3},{8,12},{10,14},{12... | collective-permute-start | bytes 393224 | tf_op jit(solution)/shard_map/ppermute | solution.py:36
  54.8 7.7 %collective-permute-start.20 = (bf16[256,256]{1,0:T(8,128)(2,1)S(1)}, bf16[256,256]{1,0:T(8,128)(2,1)S(1)}, u32[]{:S(2)}, u32[]{:S(2)}) collective-permute-start(bf16[256,256]{1,0:T(8,128)(2,1)S(1)} %get-tuple-element.25.refs_0_), channel_id=1, source_target_pairs={{0,6},{2,4},{4,2},{6,0},{1,7},{3,5},{5,3},{7,1},{8,14},{10,12},{12... | collective-permute-start | bytes 393224 | tf_op jit(solution)/shard_map/ppermute | solution.py:36

commit v11 on v9

--- a/solution.py
+++ b/solution.py
@@ -50,6 +50,31 @@
 
 def silu(x):
     return x * jax.nn.sigmoid(x)
+
+
+def begin_kernel(table_rows, owner_ref, row_ref, gain_ref, wanted_ref, column_ref):
+    wanted_ref[...] = owner_ref[...] * table_rows + row_ref[...]
+    gain = gain_ref[...].astype(F32)
+    column_ref[...] = jnp.concatenate(
+        [gain[:, c : c + LANES] for c in range(0, gain.shape[1], LANES)], axis=0
+    )
+
+
+def begin(item_owner, item_row, gains, table_rows):
+    owners, at = item_owner.reshape(-1, LANES), item_row.reshape(-1, LANES)
+    width = gains.shape[1]
+    wanted, gain = pl.pallas_call(
+        functools.partial(begin_kernel, table_rows),
+        out_shape=[
+            jax.ShapeDtypeStruct(at.shape, jnp.int32),
+            jax.ShapeDtypeStruct((width // LANES, LANES), F32),
+        ],
+        in_specs=[VMEM] * 3,
+        out_specs=[VMEM] * 2,
+        compiler_params=params(),
+        name="begin",
+    )(owners, at, gains)
+    return wanted, gain.reshape(width)
 
 
 def fetch_kernel(steps, batches, *refs):
@@ -356,7 +381,9 @@
     local_cols = w_out.shape[1]
     part = width // mp_count
 
-    w_own = jnp.transpose(w_in[0], (1, 0, 2)) * gains[0][None, :, None]
+    wanted, gain = begin(item_owner, item_row, gains, table_rows)
+    w_own = jnp.transpose(w_in[0], (1, 0, 2)).astype(F32) * gain[None, :, None]
+    w_own = w_own.astype(BF16)
     relayed = mp_count == 4
     direct = range(1, 3 if relayed else mp_count)
     pieces = [w_out[0]] + [exchange(w_out[0], "mp", k) for k in direct]
@@ -367,7 +394,6 @@
     mask, share = prepare(segments, neigh)
 
     if is_pow2(dp_count) and dp_count <= 8:
-        wanted = item_owner.reshape(-1, LANES) * table_rows + item_row.reshape(-1, LANES)
         asked = ask_around(wanted)
         w_own = hold(w_own, asked[1:2])
         w_other = exchange(w_own, "phase", 1)

time: 59.4 us -> 59 us (level)
  waiting for transfers between devices: 22.6 us -> 19.1 us
  starting transfers between devices: 25 us -> 27.9 us
  local copies, waits for them, and re-layouts: 0.04 us -> 2.08 us
  other arithmetic: 3.99 us -> 2 us
    ppermute x21, waiting for transfers between devices: 22.6 us -> 19.1 us  [exchange(): return lax.ppermute(value, axis, pairs)]
    ppermute x21, starting transfers between devices: 25 us -> 27.9 us  [exchange(): return lax.ppermute(value, axis, pairs)]
    mul x2 -> x0, other arithmetic: 2.59 us -> none  [the longest x1 1.9 us: on_device(): w_own = jnp.transpose(w_in[0], (1, 0, 2)) * gains[0][None, :, None]]
    unnamed x12 -> x18, local copies, waits for them, and re-layouts: 0.03 us -> 2.07 us
    convert_element_type x0 -> x1, other arithmetic: none -> 1.99 us  [on_device(): w_own = w_own.astype(BF16)]
    unnamed x1 -> x0, other arithmetic: 0.71 us -> none
    add x1 -> x0, other arithmetic: 0.68 us -> none  [on_device(): item_owner.reshape(-1, LANES) * table_rows + item_row.reshape(-1, LANES)]
  transfers between devices with their start and end apart: 21 -> 21, of which waited for: 10 -> 9; matrix products, arithmetic and copies ran while one was open for 4% -> 3% of each run, Pallas kernels for 5% -> 5%
where the time goes in v11:
time: 59 us; the launch traced here: 58.7 us
  starting transfers between devices  27.9 us (47%)
  waiting for transfers between devices  19.1 us (32%)
  Pallas kernels  6.78 us (11%)
  local copies, waits for them, and re-layouts  2.08 us (4%)
  other arithmetic  2 us (3%)
  between operations  0.81 us (1%)
    ppermute x21, starting transfers between devices, exchange(): return lax.ppermute(value, axis, pairs)  27.9 us
    ppermute x21, waiting for transfers between devices, exchange(): return lax.ppermute(value, axis, pairs)  19.1 us
    unnamed x18, local copies, waits for them, and re-layouts  2.07 us
    pallas_call x1, Pallas kernels, on_device(): pl.pallas_call(functools.partial(last_kernel, mp_count, len(o_own)), out_...  2.06 us
    convert_element_type x1, other arithmetic, on_device(): w_own = w_own.astype(BF16)  1.99 us
    pallas_call x1, Pallas kernels, on_device(): pl.pallas_call(functools.partial(middle_kernel, mp_count, len(o_own)), ou...  1.76 us
    pallas_call x1, Pallas kernels, on_device(): pl.pallas_call(functools.partial(first_kernel, mp_count, places), out_sha...  1.43 us
  transfers between devices with their start and end apart: 21, of which 9 were waited for; matrix products, arithmetic and copies ran while one was open for 3% of the time, Pallas kernels for 5%

profile of v11, /device:TPU:0, one launch (start us, length us, event | category | flops | bytes accessed | tf_op | source)
XLA Modules:
  0.0 58.7 jit_solution(18269637851940751157)
XLA Ops:
  0.6 0.7 %copy-done.4 = bf16[1,1024]{1,0:T(2,128)(2,1)S(1)} copy-done((bf16[1,1024]{1,0:T(2,128)(2,1)S(1)}, bf16[1,1024]{1,0:T(2,128)(2,1)}, u32[]{:S(2)}) %copy-start.4) | copy-done | bytes 2072
  1.3 0.7 %copy-done.6 = s32[512,1]{0,1:T(1,128)S(1)} copy-done((s32[512,1]{0,1:T(1,128)S(1)}, s32[512,1]{0,1:T(1,128)}, u32[]{:S(2)}) %copy-start.6) | copy-done | bytes 2072
  2.0 0.7 %copy-done.7 = s32[512]{0:T(512)S(1)} copy-done((s32[512]{0:T(512)S(1)}, s32[512]{0:T(512)}, u32[]{:S(2)}) %copy-start.7) | copy-done | bytes 2072
  2.7 3.1 %collective-permute-start = (s32[4,128]{1,0:T(4,128)S(1)}, s32[4,128]{1,0:T(4,128)S(1)}, u32[]{:S(2)}, u32[]{:S(2)}) collective-permute-start(s32[4,128]{1,0:T(4,128)S(1)} %get-tuple-element.18.refs_0_), channel_id=1, source_target_pairs={{0,8},{8,0},{16,24},{24,16},{1,9},{9,1},{17,25},{25,17},{2,10},{10... | collective-permute-start | bytes 6152 | tf_op jit(solution)/shard_map/ppermute | solution.py:36
  5.8 2.0 %fusion.1.refs_0_ = bf16[4,1024,256]{2,1,0:T(8,128)(2,1)S(1)} fusion(bf16[1,1024,4,256]{3,2,1,0:T(4,128)(2,1)} %param.16, f32[1024]{0:T(1024)S(1)} %bitcast.18), kind=kLoop, calls=%fused_computation.2 | loop fusion | flops 3145728 | bytes 4198400 | tf_op jit(solution)/shard_map/convert_element_type | solution.py:386
  7.8 0.0 copy-start.1
  7.8 0.0 copy-start
  7.8 0.1 collective-permute-start.5
  7.9 2.7 %collective-permute-start.1 = (s32[8,128]{1,0:T(8,128)S(1)}, s32[8,128]{1,0:T(8,128)S(1)}, u32[]{:S(2)}, u32[]{:S(2)}) collective-permute-start(s32[8,128]{1,0:T(8,128)S(1)} %pad_add_fusion), channel_id=1, source_target_pairs={{0,16},{8,24},{16,0},{24,8},{1,17},{9,25},{17,1},{25,9},{2,18},{10... | collective-permute-start | bytes 12296 | tf_op jit(solution)/shard_map/ppermute | solution.py:36
  10.6 1.5 %collective-permute-start.10 = (bf16[256,1024]{1,0:T(8,128)(2,1)S(1)}, bf16[256,1024]{1,0:T(8,128)(2,1)S(1)}, u32[]{:S(2)}, u32[]{:S(2)}) collective-permute-start(bf16[256,1024]{1,0:T(8,128)(2,1)S(1)} %bitcast.14), channel_id=1, source_target_pairs={{0,4},{2,6},{4,0},{6,2},{1,5},{3,7},{5,1},{7,3},{8,12},{10,14},{12... | collective-permute-start | bytes 1572872 | tf_op jit(solution)/shard_map/ppermute | solution.py:36
  12.1 1.5 %collective-permute-start.9 = (bf16[256,1024]{1,0:T(8,128)(2,1)S(1)}, bf16[256,1024]{1,0:T(8,128)(2,1)S(1)}, u32[]{:S(2)}, u32[]{:S(2)}) collective-permute-start(bf16[256,1024]{1,0:T(8,128)(2,1)S(1)} %bitcast.15), channel_id=1, source_target_pairs={{0,2},{2,0},{4,6},{6,4},{1,3},{3,1},{5,7},{7,5},{8,10},{10,8},{12,... | collective-permute-start | bytes 1572872 | tf_op jit(solution)/shard_map/ppermute | solution.py:36
  13.6 0.0 collective-permute-done.1
  13.6 0.4 fetch.2.refs_4_
  14.0 1.5 %collective-permute-start.3 = (bf16[256,256]{1,0:T(8,128)(2,1)S(1)}, bf16[256,256]{1,0:T(8,128)(2,1)S(1)}, u32[]{:S(2)}, u32[]{:S(2)}) collective-permute-start(bf16[256,256]{1,0:T(8,128)(2,1)S(1)} %fetch.2.refs_4_), channel_id=1, source_target_pairs={{0,8},{8,0},{16,24},{24,16},{1,9},{9,1},{17,25},{25,17},{2,10},{10... | collective-permute-start | bytes 393224 | tf_op jit(solution)/shard_map/ppermute | solution.py:36
  15.5 0.7 %fetch.3 = (bf16[256,256]{1,0:T(8,128)(2,1)S(1)}, bf16[256,256]{1,0:T(8,128)(2,1)S(1)}, bf16[256,256]{1,0:T(8,128)(2,1)S(1)}) custom-call(s32[4,128]{1,0:T(4,128)S(1)} %get-tuple-element.18.refs_0_, s32[4,128]{1,0:T(4,128)S(1)} %collective-permute-done.refs_1_, s32[4,128]{1,0:T(4,128)S(1)} %get-tuple-element.35.refs_2_, bf16[1024,1024]{1,0:T(8,128)(2,1)S(1)} %copy-done, ...), custom_call_target="tpu_custom_call" | custom-call | flops 402653184 | bytes 524288 | tf_op jit(solution)/shard_map/fetch/pallas_call | solution.py:111
  16.2 0.6 %collective-permute-start.2 = (bf16[256,256]{1,0:T(8,128)(2,1)S(1)}, bf16[256,256]{1,0:T(8,128)(2,1)S(1)}, u32[]{:S(2)}, u32[]{:S(2)}) collective-permute-start(bf16[256,256]{1,0:T(8,128)(2,1)S(1)} %get-tuple-element.20), channel_id=1, source_target_pairs={{0,8},{8,0},{16,24},{24,16},{1,9},{9,1},{17,25},{25,17},{2,10},{10... | collective-permute-start | bytes 393224 | tf_op jit(solution)/shard_map/ppermute | solution.py:36
  16.8 3.2 %collective-permute-done.3.b_ref = bf16[256,256]{1,0:T(8,128)(2,1)S(1)} collective-permute-done((bf16[256,256]{1,0:T(8,128)(2,1)S(1)}, bf16[256,256]{1,0:T(8,128)(2,1)S(1)}, u32[]{:S(2)}, u32[]{:S(2)}) %collective-permute-start.3) | collective-permute-done | bytes 131104 | tf_op jit(solution)/shard_map/ppermute | solution.py:36
  20.0 1.8 %collective-permute-start.4 = (bf16[256,256]{1,0:T(8,128)(2,1)S(1)}, bf16[256,256]{1,0:T(8,128)(2,1)S(1)}, u32[]{:S(2)}, u32[]{:S(2)}) collective-permute-start(bf16[256,256]{1,0:T(8,128)(2,1)S(1)} %merge.3.refs_0_), channel_id=1, source_target_pairs={{0,16},{8,24},{16,0},{24,8},{1,17},{9,25},{17,1},{25,9},{2,18},{10... | collective-permute-start | bytes 393224 | tf_op jit(solution)/shard_map/ppermute | solution.py:36
  21.8 1.5 %collective-permute-done.2.b_ref = bf16[256,256]{1,0:T(8,128)(2,1)S(1)} collective-permute-done((bf16[256,256]{1,0:T(8,128)(2,1)S(1)}, bf16[256,256]{1,0:T(8,128)(2,1)S(1)}, u32[]{:S(2)}, u32[]{:S(2)}) %collective-permute-start.2) | collective-permute-done | bytes 131104 | tf_op jit(solution)/shard_map/ppermute | solution.py:36
  23.3 2.7 %collective-permute-done.4.b_ref = bf16[256,256]{1,0:T(8,128)(2,1)S(1)} collective-permute-done((bf16[256,256]{1,0:T(8,128)(2,1)S(1)}, bf16[256,256]{1,0:T(8,128)(2,1)S(1)}, u32[]{:S(2)}, u32[]{:S(2)}) %collective-permute-start.4) | collective-permute-done | bytes 131104 | tf_op jit(solution)/shard_map/ppermute | solution.py:36
  26.0 2.4 %collective-permute-start.6 = (bf16[256,256]{1,0:T(8,128)(2,1)S(1)}, bf16[256,256]{1,0:T(8,128)(2,1)S(1)}, u32[]{:S(2)}, u32[]{:S(2)}) collective-permute-start(bf16[256,256]{1,0:T(8,128)(2,1)S(1)} %merge.5.refs_0_), channel_id=1, source_target_pairs={{0,2},{2,0},{4,6},{6,4},{1,3},{3,1},{5,7},{7,5},{8,10},{10,8},{12,... | collective-permute-start | bytes 393224 | tf_op jit(solution)/shard_map/ppermute | solution.py:36
  28.4 1.5 %collective-permute-start.7 = (bf16[256,256]{1,0:T(8,128)(2,1)S(1)}, bf16[256,256]{1,0:T(8,128)(2,1)S(1)}, u32[]{:S(2)}, u32[]{:S(2)}) collective-permute-start(bf16[256,256]{1,0:T(8,128)(2,1)S(1)} %merge.5.refs_0_), channel_id=1, source_target_pairs={{0,4},{2,6},{4,0},{6,2},{1,5},{3,7},{5,1},{7,3},{8,12},{10,14},{12... | collective-permute-start | bytes 393224 | tf_op jit(solution)/shard_map/ppermute | solution.py:36
  30.0 0.0 collective-permute-start.8
  30.0 0.0 collective-permute-done.10.refs_6_.far_ref
  30.0 0.0 collective-permute-done.9.refs_5_.near_ref
  30.0 0.1 cut.1
  30.0 2.0 %collective-permute-start.14 = (bf16[128,1024]{1,0:T(8,128)(2,1)S(1)}, bf16[128,1024]{1,0:T(8,128)(2,1)S(1)}, u32[]{:S(2)}, u32[]{:S(2)}) collective-permute-start(bf16[128,1024]{1,0:T(8,128)(2,1)S(1)} %get-tuple-element.27), channel_id=1, source_target_pairs={{0,2},{2,0},{4,6},{6,4},{1,3},{3,1},{5,7},{7,5},{8,10},{10,8},{12,... | collective-permute-start | bytes 786440 | tf_op jit(solution)/shard_map/ppermute | solution.py:36
  32.1 1.5 %collective-permute-start.15 = (bf16[128,1024]{1,0:T(8,128)(2,1)S(1)}, bf16[128,1024]{1,0:T(8,128)(2,1)S(1)}, u32[]{:S(2)}, u32[]{:S(2)}) collective-permute-start(bf16[128,1024]{1,0:T(8,128)(2,1)S(1)} %get-tuple-element.28), channel_id=1, source_target_pairs={{0,4},{2,6},{4,0},{6,2},{1,5},{3,7},{5,1},{7,3},{8,12},{10,14},{12... | collective-permute-start | bytes 786440 | tf_op jit(solution)/shard_map/ppermute | solution.py:36
  33.6 0.3 prepare.1
  33.9 0.0 collective-permute-done.6.refs_1_
  33.9 2.8 %collective-permute-done.8.refs_3_ = bf16[256,256]{1,0:T(8,128)(2,1)S(1)} collective-permute-done((bf16[256,256]{1,0:T(8,128)(2,1)S(1)}, bf16[256,256]{1,0:T(8,128)(2,1)S(1)}, u32[]{:S(2)}, u32[]{:S(2)}) %collective-permute-start.8) | collective-permute-done | bytes 131104 | tf_op jit(solution)/shard_map/ppermute | solution.py:36
  36.7 1.4 %section0_front.1 = (bf16[256,256]{1,0:T(8,128)(2,1)S(1)}, bf16[256,1024]{1,0:T(8,128)(2,1)S(1)}, bf16[3,256,1024]{2,1,0:T(8,128)(2,1)S(1)}) custom-call(bf16[256,256]{1,0:T(8,128)(2,1)S(1)} %merge.5.refs_0_, bf16[256,256]{1,0:T(8,128)(2,1)S(1)} %collective-permute-done.6.refs_1_, bf16[256,256]{1,0:T(8,128)(2,1)S(1)} %collective-permute-done.7.refs_2_, ...), custom_call_target="tpu_custom_call" | custom-call | flops 603979776 | bytes 2097152 | tf_op jit(solution)/shard_map/section0_front/pallas_call | solution.py:417
  38.1 1.0 %collective-permute-start.11 = (bf16[256,256]{1,0:T(8,128)(2,1)S(1)}, bf16[256,256]{1,0:T(8,128)(2,1)S(1)}, u32[]{:S(2)}, u32[]{:S(2)}) collective-permute-start(bf16[256,256]{1,0:T(8,128)(2,1)S(1)} %get-tuple-element.24.refs_0_), channel_id=1, source_target_pairs={{0,2},{2,0},{4,6},{6,4},{1,3},{3,1},{5,7},{7,5},{8,10},{10,8},{12,... | collective-permute-start | bytes 393224 | tf_op jit(solution)/shard_map/ppermute | solution.py:36
  39.1 1.1 %collective-permute-start.12 = (bf16[256,256]{1,0:T(8,128)(2,1)S(1)}, bf16[256,256]{1,0:T(8,128)(2,1)S(1)}, u32[]{:S(2)}, u32[]{:S(2)}) collective-permute-start(bf16[256,256]{1,0:T(8,128)(2,1)S(1)} %get-tuple-element.24.refs_0_), channel_id=1, source_target_pairs={{0,4},{2,6},{4,0},{6,2},{1,5},{3,7},{5,1},{7,3},{8,12},{10,14},{12... | collective-permute-start | bytes 393224 | tf_op jit(solution)/shard_map/ppermute | solution.py:36
  40.2 1.4 %collective-permute-start.13 = (bf16[256,256]{1,0:T(8,128)(2,1)S(1)}, bf16[256,256]{1,0:T(8,128)(2,1)S(1)}, u32[]{:S(2)}, u32[]{:S(2)}) collective-permute-start(bf16[256,256]{1,0:T(8,128)(2,1)S(1)} %get-tuple-element.24.refs_0_), channel_id=1, source_target_pairs={{0,6},{2,4},{4,2},{6,0},{1,7},{3,5},{5,3},{7,1},{8,14},{10,12},{12... | collective-permute-start | bytes 393224 | tf_op jit(solution)/shard_map/ppermute | solution.py:36
  41.7 0.1 stack.1.refs_9_
  41.7 0.6 collective-permute-start.17
  42.3 0.8 %collective-permute-done.11.refs_1_ = bf16[256,256]{1,0:T(8,128)(2,1)S(1)} collective-permute-done((bf16[256,256]{1,0:T(8,128)(2,1)S(1)}, bf16[256,256]{1,0:T(8,128)(2,1)S(1)}, u32[]{:S(2)}, u32[]{:S(2)}) %collective-permute-start.11) | collective-permute-done | bytes 131104 | tf_op jit(solution)/shard_map/ppermute | solution.py:36
  43.1 1.0 %collective-permute-done.12.refs_2_ = bf16[256,256]{1,0:T(8,128)(2,1)S(1)} collective-permute-done((bf16[256,256]{1,0:T(8,128)(2,1)S(1)}, bf16[256,256]{1,0:T(8,128)(2,1)S(1)}, u32[]{:S(2)}, u32[]{:S(2)}) %collective-permute-start.12) | collective-permute-done | bytes 131104 | tf_op jit(solution)/shard_map/ppermute | solution.py:36
  44.1 2.0 %collective-permute-done.13.refs_0_ = bf16[256,256]{1,0:T(8,128)(2,1)S(1)} collective-permute-done((bf16[256,256]{1,0:T(8,128)(2,1)S(1)}, bf16[256,256]{1,0:T(8,128)(2,1)S(1)}, u32[]{:S(2)}, u32[]{:S(2)}) %collective-permute-start.13) | collective-permute-done | bytes 131104 | tf_op jit(solution)/shard_map/ppermute | solution.py:36
  46.1 0.0 copy-start.2
  46.1 1.8 %section0_back_section1_front.1 = (bf16[256,256]{1,0:T(8,128)(2,1)S(1)}, bf16[256,1024]{1,0:T(8,128)(2,1)S(1)}) custom-call(bf16[256,256]{1,0:T(8,128)(2,1)S(1)} %get-tuple-element.24.refs_0_, bf16[256,256]{1,0:T(8,128)(2,1)S(1)} %collective-permute-done.11.refs_1_, bf16[256,256]{1,0:T(8,128)(2,1)S(1)} %collective-permute-done.12.refs_2_, ...), custom_call_target="tpu_custom_call" | custom-call | flops 1140850688 | bytes 4194304 | tf_op jit(solution)/shard_map/section0_back_section1_front/pallas_call | solution.py:440
  47.9 1.0 %collective-permute-start.18 = (bf16[256,256]{1,0:T(8,128)(2,1)S(1)}, bf16[256,256]{1,0:T(8,128)(2,1)S(1)}, u32[]{:S(2)}, u32[]{:S(2)}) collective-permute-start(bf16[256,256]{1,0:T(8,128)(2,1)S(1)} %get-tuple-element.29.refs_0_), channel_id=1, source_target_pairs={{0,2},{2,0},{4,6},{6,4},{1,3},{3,1},{5,7},{7,5},{8,10},{10,8},{12,... | collective-permute-start | bytes 393224 | tf_op jit(solution)/shard_map/ppermute | solution.py:36
  48.9 1.0 %collective-permute-start.19 = (bf16[256,256]{1,0:T(8,128)(2,1)S(1)}, bf16[256,256]{1,0:T(8,128)(2,1)S(1)}, u32[]{:S(2)}, u32[]{:S(2)}) collective-permute-start(bf16[256,256]{1,0:T(8,128)(2,1)S(1)} %get-tuple-element.29.refs_0_), channel_id=1, source_target_pairs={{0,4},{2,6},{4,0},{6,2},{1,5},{3,7},{5,1},{7,3},{8,12},{10,14},{12... | collective-permute-start | bytes 393224 | tf_op jit(solution)/shard_map/ppermute | solution.py:36
  49.9 1.5 %collective-permute-start.20 = (bf16[256,256]{1,0:T(8,128)(2,1)S(1)}, bf16[256,256]{1,0:T(8,128)(2,1)S(1)}, u32[]{:S(2)}, u32[]{:S(2)}) collective-permute-start(bf16[256,256]{1,0:T(8,128)(2,1)S(1)} %get-tuple-element.29.refs_0_), channel_id=1, source_target_pairs={{0,6},{2,4},{4,2},{6,0},{1,7},{3,5},{5,3},{7,1},{8,14},{10,12},{12... | collective-permute-start | bytes 393224 | tf_op jit(solution)/shard_map/ppermute | solution.py:36
  51.4 2.7 %collective-permute-done.18.refs_1_ = bf16[256,256]{1,0:T(8,128)(2,1)S(1)} collective-permute-done((bf16[256,256]{1,0:T(8,128)(2,1)S(1)}, bf16[256,256]{1,0:T(8,128)(2,1)S(1)}, u32[]{:S(2)}, u32[]{:S(2)}) %collective-permute-start.18) | collective-permute-done | bytes 131104 | tf_op jit(solution)/shard_map/ppermute | solution.py:36
  54.1 2.5 %collective-permute-done.19.refs_2_ = bf16[256,256]{1,0:T(8,128)(2,1)S(1)} collective-permute-done((bf16[256,256]{1,0:T(8,128)(2,1)S(1)}, bf16[256,256]{1,0:T(8,128)(2,1)S(1)}, u32[]{:S(2)}, u32[]{:S(2)}) %collective-permute-start.19) | collective-permute-done | bytes 131104 | tf_op jit(solution)/shard_map/ppermute | solution.py:36
  56.7 2.1 %section1_back_context.1 = (bf16[256,1024]{1,0:T(8,128)(2,1)}, bf16[256,256]{1,0:T(8,128)(2,1)}) custom-call(bf16[256,256]{1,0:T(8,128)(2,1)S(1)} %get-tuple-element.29.refs_0_, bf16[256,256]{1,0:T(8,128)(2,1)S(1)} %collective-permute-done.18.refs_1_, bf16[256,256]{1,0:T(8,128)(2,1)S(1)} %collective-permute-done.19.refs_2_, ...), custom_call_target="tpu_custom_call" | custom-call | flops 805306368 | bytes 2097152 | tf_op jit(solution)/shard_map/section1_back_context/pallas_call | solution.py:454
  (30 shorter events, 0.1 us)
Async XLA Ops:
  0.6 0.7 %copy-start.4 = (bf16[1,1024]{1,0:T(2,128)(2,1)S(1)}, bf16[1,1024]{1,0:T(2,128)(2,1)}, u32[]{:S(2)}) copy-start(bf16[1,1024]{1,0:T(2,128)(2,1)} %gain_ref.1) | copy-start | bytes 6148
  1.3 0.7 %copy-start.6 = (s32[512,1]{0,1:T(1,128)S(1)}, s32[512,1]{0,1:T(1,128)}, u32[]{:S(2)}) copy-start(s32[512,1]{0,1:T(1,128)} %param.10) | copy-start | bytes 6148
  2.0 0.7 %copy-start.7 = (s32[512]{0:T(512)S(1)}, s32[512]{0:T(512)}, u32[]{:S(2)}) copy-start(s32[512]{0:T(512)} %param.11) | copy-start | bytes 6148
  2.7 5.1 %collective-permute-start = (s32[4,128]{1,0:T(4,128)S(1)}, s32[4,128]{1,0:T(4,128)S(1)}, u32[]{:S(2)}, u32[]{:S(2)}) collective-permute-start(s32[4,128]{1,0:T(4,128)S(1)} %get-tuple-element.18.refs_0_), channel_id=1, source_target_pairs={{0,8},{8,0},{16,24},{24,16},{1,9},{9,1},{17,25},{25,17},{2,10},{10... | collective-permute-start | bytes 6152 | tf_op jit(solution)/shard_map/ppermute | solution.py:36
  7.8 2.8 %copy-start.1 = (bf16[1,256,1024]{2,1,0:T(8,128)(2,1)S(1)}, bf16[1,256,1024]{2,1,0:T(8,128)(2,1)}, u32[]{:S(2)}) copy-start(bf16[1,256,1024]{2,1,0:T(8,128)(2,1)} %param.17) | copy-start | bytes 1572868
  7.8 5.8 %copy-start = (bf16[1024,1024]{1,0:T(8,128)(2,1)S(1)}, bf16[1024,1024]{1,0:T(8,128)(2,1)}, u32[]{:S(2)}) copy-start(bf16[1024,1024]{1,0:T(8,128)(2,1)} %refs_3_.1) | copy-start | bytes 6291460
  7.8 18.2 %collective-permute-start.5 = (bf16[4,1024,256]{2,1,0:T(8,128)(2,1)S(1)}, bf16[4,1024,256]{2,1,0:T(8,128)(2,1)S(1)}, u32[]{:S(2)}, u32[]{:S(2)}) collective-permute-start(bf16[4,1024,256]{2,1,0:T(8,128)(2,1)S(1)} %hold.2.refs_8_.refs_6_), channel_id=1, source_target_pairs={{0,1},{1,0},{2,3},{3,2},{4,5},{5,4},{6,7},{7,6},{8,9},{9,8},{10,11... | collective-permute-start | bytes 6291464 | tf_op jit(solution)/shard_map/ppermute | solution.py:36
  7.9 5.7 %collective-permute-start.1 = (s32[8,128]{1,0:T(8,128)S(1)}, s32[8,128]{1,0:T(8,128)S(1)}, u32[]{:S(2)}, u32[]{:S(2)}) collective-permute-start(s32[8,128]{1,0:T(8,128)S(1)} %pad_add_fusion), channel_id=1, source_target_pairs={{0,16},{8,24},{16,0},{24,8},{1,17},{9,25},{17,1},{25,9},{2,18},{10... | collective-permute-start | bytes 12296 | tf_op jit(solution)/shard_map/ppermute | solution.py:36
  10.6 19.4 %collective-permute-start.10 = (bf16[256,1024]{1,0:T(8,128)(2,1)S(1)}, bf16[256,1024]{1,0:T(8,128)(2,1)S(1)}, u32[]{:S(2)}, u32[]{:S(2)}) collective-permute-start(bf16[256,1024]{1,0:T(8,128)(2,1)S(1)} %bitcast.14), channel_id=1, source_target_pairs={{0,4},{2,6},{4,0},{6,2},{1,5},{3,7},{5,1},{7,3},{8,12},{10,14},{12... | collective-permute-start | bytes 1572872 | tf_op jit(solution)/shard_map/ppermute | solution.py:36
  12.1 17.9 %collective-permute-start.9 = (bf16[256,1024]{1,0:T(8,128)(2,1)S(1)}, bf16[256,1024]{1,0:T(8,128)(2,1)S(1)}, u32[]{:S(2)}, u32[]{:S(2)}) collective-permute-start(bf16[256,1024]{1,0:T(8,128)(2,1)S(1)} %bitcast.15), channel_id=1, source_target_pairs={{0,2},{2,0},{4,6},{6,4},{1,3},{3,1},{5,7},{7,5},{8,10},{10,8},{12,... | collective-permute-start | bytes 1572872 | tf_op jit(solution)/shard_map/ppermute | solution.py:36
  14.0 6.0 %collective-permute-start.3 = (bf16[256,256]{1,0:T(8,128)(2,1)S(1)}, bf16[256,256]{1,0:T(8,128)(2,1)S(1)}, u32[]{:S(2)}, u32[]{:S(2)}) collective-permute-start(bf16[256,256]{1,0:T(8,128)(2,1)S(1)} %fetch.2.refs_4_), channel_id=1, source_target_pairs={{0,8},{8,0},{16,24},{24,16},{1,9},{9,1},{17,25},{25,17},{2,10},{10... | collective-permute-start | bytes 393224 | tf_op jit(solution)/shard_map/ppermute | solution.py:36
  16.2 7.1 %collective-permute-start.2 = (bf16[256,256]{1,0:T(8,128)(2,1)S(1)}, bf16[256,256]{1,0:T(8,128)(2,1)S(1)}, u32[]{:S(2)}, u32[]{:S(2)}) collective-permute-start(bf16[256,256]{1,0:T(8,128)(2,1)S(1)} %get-tuple-element.20), channel_id=1, source_target_pairs={{0,8},{8,0},{16,24},{24,16},{1,9},{9,1},{17,25},{25,17},{2,10},{10... | collective-permute-start | bytes 393224 | tf_op jit(solution)/shard_map/ppermute | solution.py:36
  20.0 5.9 %collective-permute-start.4 = (bf16[256,256]{1,0:T(8,128)(2,1)S(1)}, bf16[256,256]{1,0:T(8,128)(2,1)S(1)}, u32[]{:S(2)}, u32[]{:S(2)}) collective-permute-start(bf16[256,256]{1,0:T(8,128)(2,1)S(1)} %merge.3.refs_0_), channel_id=1, source_target_pairs={{0,16},{8,24},{16,0},{24,8},{1,17},{9,25},{17,1},{25,9},{2,18},{10... | collective-permute-start | bytes 393224 | tf_op jit(solution)/shard_map/ppermute | solution.py:36
  23.3 10.3 %copy-start.3 = (s32[1,2,256,8]{2,3,1,0:T(8,128)S(1)}, s32[1,2,256,8]{2,3,1,0:T(8,128)}, u32[]{:S(2)}) copy-start(s32[1,2,256,8]{2,3,1,0:T(8,128)} %param.13) | copy-start | bytes 49156
  23.3 10.3 %copy-start.5 = (s32[1,2,256]{2,1,0:T(2,128)S(1)}, s32[1,2,256]{2,1,0:T(2,128)}, u32[]{:S(2)}) copy-start(s32[1,2,256]{2,1,0:T(2,128)} %seg_ref.1) | copy-start | bytes 6148
  26.0 7.9 %collective-permute-start.6 = (bf16[256,256]{1,0:T(8,128)(2,1)S(1)}, bf16[256,256]{1,0:T(8,128)(2,1)S(1)}, u32[]{:S(2)}, u32[]{:S(2)}) collective-permute-start(bf16[256,256]{1,0:T(8,128)(2,1)S(1)} %merge.5.refs_0_), channel_id=1, source_target_pairs={{0,2},{2,0},{4,6},{6,4},{1,3},{3,1},{5,7},{7,5},{8,10},{10,8},{12,... | collective-permute-start | bytes 393224 | tf_op jit(solution)/shard_map/ppermute | solution.py:36
  28.4 5.5 %collective-permute-start.7 = (bf16[256,256]{1,0:T(8,128)(2,1)S(1)}, bf16[256,256]{1,0:T(8,128)(2,1)S(1)}, u32[]{:S(2)}, u32[]{:S(2)}) collective-permute-start(bf16[256,256]{1,0:T(8,128)(2,1)S(1)} %merge.5.refs_0_), channel_id=1, source_target_pairs={{0,4},{2,6},{4,0},{6,2},{1,5},{3,7},{5,1},{7,3},{8,12},{10,14},{12... | collective-permute-start | bytes 393224 | tf_op jit(solution)/shard_map/ppermute | solution.py:36
  30.0 6.7 %collective-permute-start.8 = (bf16[256,256]{1,0:T(8,128)(2,1)S(1)}, bf16[256,256]{1,0:T(8,128)(2,1)S(1)}, u32[]{:S(2)}, u32[]{:S(2)}) collective-permute-start(bf16[256,256]{1,0:T(8,128)(2,1)S(1)} %merge.5.refs_0_), channel_id=1, source_target_pairs={{0,6},{2,4},{4,2},{6,0},{1,7},{3,5},{5,3},{7,1},{8,14},{10,12},{12... | collective-permute-start | bytes 393224 | tf_op jit(solution)/shard_map/ppermute | solution.py:36
  30.0 11.6 %collective-permute-start.14 = (bf16[128,1024]{1,0:T(8,128)(2,1)S(1)}, bf16[128,1024]{1,0:T(8,128)(2,1)S(1)}, u32[]{:S(2)}, u32[]{:S(2)}) collective-permute-start(bf16[128,1024]{1,0:T(8,128)(2,1)S(1)} %get-tuple-element.27), channel_id=1, source_target_pairs={{0,2},{2,0},{4,6},{6,4},{1,3},{3,1},{5,7},{7,5},{8,10},{10,8},{12,... | collective-permute-start | bytes 786440 | tf_op jit(solution)/shard_map/ppermute | solution.py:36
  32.1 9.6 %collective-permute-start.15 = (bf16[128,1024]{1,0:T(8,128)(2,1)S(1)}, bf16[128,1024]{1,0:T(8,128)(2,1)S(1)}, u32[]{:S(2)}, u32[]{:S(2)}) collective-permute-start(bf16[128,1024]{1,0:T(8,128)(2,1)S(1)} %get-tuple-element.28), channel_id=1, source_target_pairs={{0,4},{2,6},{4,0},{6,2},{1,5},{3,7},{5,1},{7,3},{8,12},{10,14},{12... | collective-permute-start | bytes 786440 | tf_op jit(solution)/shard_map/ppermute | solution.py:36
  38.1 5.0 %collective-permute-start.11 = (bf16[256,256]{1,0:T(8,128)(2,1)S(1)}, bf16[256,256]{1,0:T(8,128)(2,1)S(1)}, u32[]{:S(2)}, u32[]{:S(2)}) collective-permute-start(bf16[256,256]{1,0:T(8,128)(2,1)S(1)} %get-tuple-element.24.refs_0_), channel_id=1, source_target_pairs={{0,2},{2,0},{4,6},{6,4},{1,3},{3,1},{5,7},{7,5},{8,10},{10,8},{12,... | collective-permute-start | bytes 393224 | tf_op jit(solution)/shard_map/ppermute | solution.py:36
  39.1 5.0 %collective-permute-start.12 = (bf16[256,256]{1,0:T(8,128)(2,1)S(1)}, bf16[256,256]{1,0:T(8,128)(2,1)S(1)}, u32[]{:S(2)}, u32[]{:S(2)}) collective-permute-start(bf16[256,256]{1,0:T(8,128)(2,1)S(1)} %get-tuple-element.24.refs_0_), channel_id=1, source_target_pairs={{0,4},{2,6},{4,0},{6,2},{1,5},{3,7},{5,1},{7,3},{8,12},{10,14},{12... | collective-permute-start | bytes 393224 | tf_op jit(solution)/shard_map/ppermute | solution.py:36
  40.2 5.9 %collective-permute-start.13 = (bf16[256,256]{1,0:T(8,128)(2,1)S(1)}, bf16[256,256]{1,0:T(8,128)(2,1)S(1)}, u32[]{:S(2)}, u32[]{:S(2)}) collective-permute-start(bf16[256,256]{1,0:T(8,128)(2,1)S(1)} %get-tuple-element.24.refs_0_), channel_id=1, source_target_pairs={{0,6},{2,4},{4,2},{6,0},{1,7},{3,5},{5,3},{7,1},{8,14},{10,12},{12... | collective-permute-start | bytes 393224 | tf_op jit(solution)/shard_map/ppermute | solution.py:36
  41.6 4.5 %collective-permute-start.16 = (bf16[3,256,1024]{2,1,0:T(8,128)(2,1)S(1)}, bf16[3,256,1024]{2,1,0:T(8,128)(2,1)S(1)}, u32[]{:S(2)}, u32[]{:S(2)}) collective-permute-start(bf16[3,256,1024]{2,1,0:T(8,128)(2,1)S(1)} %get-tuple-element.26.refs_8_), channel_id=1, source_target_pairs={{0,1},{1,0},{2,3},{3,2},{4,5},{5,4},{6,7},{7,6},{8,9},{9,8},{10,11... | collective-permute-start | bytes 4718600 | tf_op jit(solution)/shard_map/ppermute | solution.py:36
  41.7 4.4 %collective-permute-start.17 = (bf16[1,256,1024]{2,1,0:T(8,128)(2,1)S(1)}, bf16[1,256,1024]{2,1,0:T(8,128)(2,1)S(1)}, u32[]{:S(2)}, u32[]{:S(2)}) collective-permute-start(bf16[1,256,1024]{2,1,0:T(8,128)(2,1)S(1)} %stack.1.refs_9_), channel_id=1, source_target_pairs={{0,1},{1,0},{2,3},{3,2},{4,5},{5,4},{6,7},{7,6},{8,9},{9,8},{10,11... | collective-permute-start | bytes 1572872 | tf_op jit(solution)/shard_map/ppermute | solution.py:36
  46.1 5.3 %copy-start.8 = (bf16[256]{0:T(256)(128)(2,1)S(1)}, bf16[256]{0:T(256)(128)(2,1)}, u32[]{:S(2)}) copy-start(bf16[256]{0:T(256)(128)(2,1)} %param.19) | copy-start | bytes 1540
  46.1 10.6 %copy-start.2 = (bf16[1024,256]{1,0:T(8,128)(2,1)S(1)}, bf16[1024,256]{1,0:T(8,128)(2,1)}, u32[]{:S(2)}) copy-start(bf16[1024,256]{1,0:T(8,128)(2,1)} %refs_6_.1) | copy-start | bytes 1572868
  47.9 6.2 %collective-permute-start.18 = (bf16[256,256]{1,0:T(8,128)(2,1)S(1)}, bf16[256,256]{1,0:T(8,128)(2,1)S(1)}, u32[]{:S(2)}, u32[]{:S(2)}) collective-permute-start(bf16[256,256]{1,0:T(8,128)(2,1)S(1)} %get-tuple-element.29.refs_0_), channel_id=1, source_target_pairs={{0,2},{2,0},{4,6},{6,4},{1,3},{3,1},{5,7},{7,5},{8,10},{10,8},{12,... | collective-permute-start | bytes 393224 | tf_op jit(solution)/shard_map/ppermute | solution.py:36
  48.9 7.8 %collective-permute-start.19 = (bf16[256,256]{1,0:T(8,128)(2,1)S(1)}, bf16[256,256]{1,0:T(8,128)(2,1)S(1)}, u32[]{:S(2)}, u32[]{:S(2)}) collective-permute-start(bf16[256,256]{1,0:T(8,128)(2,1)S(1)} %get-tuple-element.29.refs_0_), channel_id=1, source_target_pairs={{0,4},{2,6},{4,0},{6,2},{1,5},{3,7},{5,1},{7,3},{8,12},{10,14},{12... | collective-permute-start | bytes 393224 | tf_op jit(solution)/shard_map/ppermute | solution.py:36
  49.9 6.7 %collective-permute-start.20 = (bf16[256,256]{1,0:T(8,128)(2,1)S(1)}, bf16[256,256]{1,0:T(8,128)(2,1)S(1)}, u32[]{:S(2)}, u32[]{:S(2)}) collective-permute-start(bf16[256,256]{1,0:T(8,128)(2,1)S(1)} %get-tuple-element.29.refs_0_), channel_id=1, source_target_pairs={{0,6},{2,4},{4,2},{6,0},{1,7},{3,5},{5,3},{7,1},{8,14},{10,12},{12... | collective-permute-start | bytes 393224 | tf_op jit(solution)/shard_map/ppermute | solution.py:36

commit v12 on v9

--- a/solution.py
+++ b/solution.py
@@ -55,17 +55,19 @@
 def fetch_kernel(steps, batches, *refs):
     asked_refs, table_ref = refs[:steps], refs[steps]
     out_refs, width = refs[-steps:], refs[-1].shape[1]
-    first = lax.axis_index("dp") * table_ref.shape[0]
+    me = lax.axis_index("dp")
     phase = lax.axis_index("phase")
     hots = []
     for asked_ref in asked_refs:
-        per = asked_ref.shape[0] // batches
-        cols = jnp.concatenate(
-            [
-                columns_of(asked_ref[pl.ds(phase * per + n, 1), :] - first, LANES)
-                for n in range(per)
-            ]
-        )
+        half = asked_ref.shape[0] // 2
+        per = half // batches
+        cols = []
+        for n in range(per):
+            at = phase * per + n
+            mine = asked_ref[pl.ds(at, 1), :] == me
+            row = jnp.where(mine, asked_ref[pl.ds(half + at, 1), :], -1)
+            cols.append(columns_of(row, LANES))
+        cols = jnp.concatenate(cols)
         lane = lax.broadcasted_iota(jnp.int32, cols.shape, 1)
         hots.append(
             jnp.concatenate(
@@ -82,7 +84,7 @@
 
 
 def fetch(asked, batches, table, width, after):
-    steps, rows = len(asked), asked[0].size // batches
+    steps, rows = len(asked), asked[0].size // (2 * batches)
     return pl.pallas_call(
         functools.partial(fetch_kernel, steps, batches),
         out_shape=[jax.ShapeDtypeStruct((rows, width), BF16)] * steps,
@@ -367,7 +369,7 @@
     mask, share = prepare(segments, neigh)
 
     if is_pow2(dp_count) and dp_count <= 8:
-        wanted = item_owner.reshape(-1, LANES) * table_rows + item_row.reshape(-1, LANES)
+        wanted = jnp.concatenate([item_owner.reshape(-1, LANES), item_row.reshape(-1, LANES)])
         asked = ask_around(wanted)
         w_own = hold(w_own, asked[1:2])
         w_other = exchange(w_own, "phase", 1)

time: 59.4 us -> 58.6 us (0.987)
  waiting for transfers between devices: 22.6 us -> 21.2 us
  other arithmetic: 3.99 us -> 3.33 us
  starting transfers between devices: 25 us -> 25.6 us
    ppermute x21, waiting for transfers between devices: 22.6 us -> 21.2 us  [exchange(): return lax.ppermute(value, axis, pairs)]
    concatenate x0 -> x1, other arithmetic: none -> 0.71 us  [on_device(): jnp.concatenate([item_owner.reshape(-1, LANES), item_row.reshape(-1, LANE...]
    mul x1 -> x0, other arithmetic: 0.69 us -> none  [on_device(): item_owner.reshape(-1, LANES) * table_rows + item_row.reshape(-1, LANES)]
    add x1 -> x0, other arithmetic: 0.68 us -> none  [on_device(): item_owner.reshape(-1, LANES) * table_rows + item_row.reshape(-1, LANES)]
  transfers between devices with their start and end apart: 21 -> 21, of which waited for: 10 -> 9; matrix products, arithmetic and copies ran while one was open for 4% -> 5% of each run, Pallas kernels for 5% -> 5%
where the time goes in v12:
time: 58.6 us; the launch traced here: 58.3 us
  starting transfers between devices  25.6 us (44%)
  waiting for transfers between devices  21.2 us (36%)
  Pallas kernels  6.77 us (12%)
  other arithmetic  3.33 us (6%)
  between operations  0.81 us (1%)
  local copies, waits for them, and re-layouts  0.6 us (1%)
    ppermute x21, starting transfers between devices, exchange(): return lax.ppermute(value, axis, pairs)  25.6 us
    ppermute x21, waiting for transfers between devices, exchange(): return lax.ppermute(value, axis, pairs)  21.2 us
    pallas_call x1, Pallas kernels, on_device(): pl.pallas_call(functools.partial(last_kernel, mp_count, len(o_own)), out_...  2.06 us
    mul x1, other arithmetic, on_device(): w_own = jnp.transpose(w_in[0], (1, 0, 2)) * gains[0][None, :, None]  1.9 us
    pallas_call x1, Pallas kernels, on_device(): pl.pallas_call(functools.partial(middle_kernel, mp_count, len(o_own)), ou...  1.76 us
    pallas_call x1, Pallas kernels, on_device(): pl.pallas_call(functools.partial(first_kernel, mp_count, places), out_sha...  1.43 us
  transfers between devices with their start and end apart: 21, of which 9 were waited for; matrix products, arithmetic and copies ran while one was open for 5% of the time, Pallas kernels for 5%

profile of v12, /device:TPU:0, one launch (start us, length us, event | category | flops | bytes accessed | tf_op | source)
XLA Modules:
  0.0 58.3 jit_solution(2181078631142203108)
XLA Ops:
  0.6 0.7 %pad_add_fusion.1.refs_0_ = s32[8,128]{1,0:T(8,128)S(1)} fusion(s32[4,128]{1,0:T(4,128)} %bitcast.18, s32[4,128]{1,0:T(4,128)} %bitcast.20), kind=kLoop, calls=%fused_computation.3 | loop fusion | flops 1024 | bytes 8192 | tf_op jit(solution)/shard_map/concatenate | solution.py:372
  1.3 3.0 %collective-permute-start = (s32[8,128]{1,0:T(8,128)S(1)}, s32[8,128]{1,0:T(8,128)S(1)}, u32[]{:S(2)}, u32[]{:S(2)}) collective-permute-start(s32[8,128]{1,0:T(8,128)S(1)} %pad_add_fusion.1.refs_0_), channel_id=1, source_target_pairs={{0,8},{8,0},{16,24},{24,16},{1,9},{9,1},{17,25},{25,17},{2,10},{10... | collective-permute-start | bytes 12296 | tf_op jit(solution)/shard_map/ppermute | solution.py:36
  4.4 0.7 %reduce = bf16[1024]{0:T(1024)(128)(2,1)S(1)} reduce(bf16[1,1024]{1,0:T(2,128)(2,1)} %param.15, bf16[]{:T(256)} %constant.5), dimensions={0}, to_apply=%param.15.reduce_sub_computation | reduce | bytes 4098 | tf_op args[5]
  5.1 1.9 %fusion.refs_0_ = bf16[4,1024,256]{2,1,0:T(8,128)(2,1)S(1)} fusion(bf16[1,1024,4,256]{3,2,1,0:T(4,128)(2,1)} %param.16, bf16[1024]{0:T(1024)(128)(2,1)S(1)} %reduce), kind=kLoop, calls=%fused_computation.1 | loop fusion | flops 1048576 | bytes 4196352 | tf_op jit(solution)/shard_map/mul | solution.py:361
  7.0 0.0 copy-start.5
  7.0 0.0 copy-start.6
  7.0 0.0 copy-start.1
  7.0 0.0 copy-start
  7.0 0.0 collective-permute-done.refs_1_
  7.0 0.1 collective-permute-start.5
  7.1 0.5 copy-done.5
  7.7 0.0 copy-done.6
  7.7 2.6 %collective-permute-start.1 = (s32[16,128]{1,0:T(8,128)S(1)}, s32[16,128]{1,0:T(8,128)S(1)}, u32[]{:S(2)}, u32[]{:S(2)}) collective-permute-start(s32[16,128]{1,0:T(8,128)S(1)} %pad_add_fusion), channel_id=1, source_target_pairs={{0,16},{8,24},{16,0},{24,8},{1,17},{9,25},{17,1},{25,9},{2,18},{10... | collective-permute-start | bytes 24584 | tf_op jit(solution)/shard_map/ppermute | solution.py:36
  10.3 1.5 %collective-permute-start.10 = (bf16[256,1024]{1,0:T(8,128)(2,1)S(1)}, bf16[256,1024]{1,0:T(8,128)(2,1)S(1)}, u32[]{:S(2)}, u32[]{:S(2)}) collective-permute-start(bf16[256,1024]{1,0:T(8,128)(2,1)S(1)} %bitcast.14), channel_id=1, source_target_pairs={{0,4},{2,6},{4,0},{6,2},{1,5},{3,7},{5,1},{7,3},{8,12},{10,14},{12... | collective-permute-start | bytes 1572872 | tf_op jit(solution)/shard_map/ppermute | solution.py:36
  11.9 1.5 %collective-permute-start.9 = (bf16[256,1024]{1,0:T(8,128)(2,1)S(1)}, bf16[256,1024]{1,0:T(8,128)(2,1)S(1)}, u32[]{:S(2)}, u32[]{:S(2)}) collective-permute-start(bf16[256,1024]{1,0:T(8,128)(2,1)S(1)} %bitcast.15), channel_id=1, source_target_pairs={{0,2},{2,0},{4,6},{6,4},{1,3},{3,1},{5,7},{7,5},{8,10},{10,8},{12,... | collective-permute-start | bytes 1572872 | tf_op jit(solution)/shard_map/ppermute | solution.py:36
  13.4 0.4 fetch.2.refs_4_
  13.8 0.5 collective-permute-start.3
  14.3 0.7 %fetch.3 = (bf16[256,256]{1,0:T(8,128)(2,1)S(1)}, bf16[256,256]{1,0:T(8,128)(2,1)S(1)}, bf16[256,256]{1,0:T(8,128)(2,1)S(1)}) custom-call(s32[8,128]{1,0:T(8,128)S(1)} %pad_add_fusion.1.refs_0_, s32[8,128]{1,0:T(8,128)S(1)} %collective-permute-done.refs_1_, s32[8,128]{1,0:T(8,128)S(1)} %get-tuple-element.31.refs_2_, bf16[1024,1024]{1,0:T(8,128)(2,1)S(1)} %copy-done, ...), custom_call_target="tpu_custom_call" | custom-call | flops 402653184 | bytes 524288 | tf_op jit(solution)/shard_map/fetch/pallas_call | solution.py:88
  15.0 1.6 %collective-permute-start.2 = (bf16[256,256]{1,0:T(8,128)(2,1)S(1)}, bf16[256,256]{1,0:T(8,128)(2,1)S(1)}, u32[]{:S(2)}, u32[]{:S(2)}) collective-permute-start(bf16[256,256]{1,0:T(8,128)(2,1)S(1)} %get-tuple-element.17), channel_id=1, source_target_pairs={{0,8},{8,0},{16,24},{24,16},{1,9},{9,1},{17,25},{25,17},{2,10},{10... | collective-permute-start | bytes 393224 | tf_op jit(solution)/shard_map/ppermute | solution.py:36
  16.6 3.2 %collective-permute-done.3.b_ref = bf16[256,256]{1,0:T(8,128)(2,1)S(1)} collective-permute-done((bf16[256,256]{1,0:T(8,128)(2,1)S(1)}, bf16[256,256]{1,0:T(8,128)(2,1)S(1)}, u32[]{:S(2)}, u32[]{:S(2)}) %collective-permute-start.3) | collective-permute-done | bytes 131104 | tf_op jit(solution)/shard_map/ppermute | solution.py:36
  19.8 1.3 %collective-permute-start.4 = (bf16[256,256]{1,0:T(8,128)(2,1)S(1)}, bf16[256,256]{1,0:T(8,128)(2,1)S(1)}, u32[]{:S(2)}, u32[]{:S(2)}) collective-permute-start(bf16[256,256]{1,0:T(8,128)(2,1)S(1)} %merge.3.refs_0_), channel_id=1, source_target_pairs={{0,16},{8,24},{16,0},{24,8},{1,17},{9,25},{17,1},{25,9},{2,18},{10... | collective-permute-start | bytes 393224 | tf_op jit(solution)/shard_map/ppermute | solution.py:36
  21.1 1.0 %collective-permute-done.2.b_ref = bf16[256,256]{1,0:T(8,128)(2,1)S(1)} collective-permute-done((bf16[256,256]{1,0:T(8,128)(2,1)S(1)}, bf16[256,256]{1,0:T(8,128)(2,1)S(1)}, u32[]{:S(2)}, u32[]{:S(2)}) %collective-permute-start.2) | collective-permute-done | bytes 131104 | tf_op jit(solution)/shard_map/ppermute | solution.py:36
  22.1 5.0 %collective-permute-done.4.b_ref = bf16[256,256]{1,0:T(8,128)(2,1)S(1)} collective-permute-done((bf16[256,256]{1,0:T(8,128)(2,1)S(1)}, bf16[256,256]{1,0:T(8,128)(2,1)S(1)}, u32[]{:S(2)}, u32[]{:S(2)}) %collective-permute-start.4) | collective-permute-done | bytes 131104 | tf_op jit(solution)/shard_map/ppermute | solution.py:36
  27.1 0.6 %collective-permute-start.6 = (bf16[256,256]{1,0:T(8,128)(2,1)S(1)}, bf16[256,256]{1,0:T(8,128)(2,1)S(1)}, u32[]{:S(2)}, u32[]{:S(2)}) collective-permute-start(bf16[256,256]{1,0:T(8,128)(2,1)S(1)} %merge.5.refs_0_), channel_id=1, source_target_pairs={{0,2},{2,0},{4,6},{6,4},{1,3},{3,1},{5,7},{7,5},{8,10},{10,8},{12,... | collective-permute-start | bytes 393224 | tf_op jit(solution)/shard_map/ppermute | solution.py:36
  27.7 1.6 %collective-permute-start.7 = (bf16[256,256]{1,0:T(8,128)(2,1)S(1)}, bf16[256,256]{1,0:T(8,128)(2,1)S(1)}, u32[]{:S(2)}, u32[]{:S(2)}) collective-permute-start(bf16[256,256]{1,0:T(8,128)(2,1)S(1)} %merge.5.refs_0_), channel_id=1, source_target_pairs={{0,4},{2,6},{4,0},{6,2},{1,5},{3,7},{5,1},{7,3},{8,12},{10,14},{12... | collective-permute-start | bytes 393224 | tf_op jit(solution)/shard_map/ppermute | solution.py:36
  29.3 1.4 %collective-permute-start.8 = (bf16[256,256]{1,0:T(8,128)(2,1)S(1)}, bf16[256,256]{1,0:T(8,128)(2,1)S(1)}, u32[]{:S(2)}, u32[]{:S(2)}) collective-permute-start(bf16[256,256]{1,0:T(8,128)(2,1)S(1)} %merge.5.refs_0_), channel_id=1, source_target_pairs={{0,6},{2,4},{4,2},{6,0},{1,7},{3,5},{5,3},{7,1},{8,14},{10,12},{12... | collective-permute-start | bytes 393224 | tf_op jit(solution)/shard_map/ppermute | solution.py:36
  30.7 0.1 cut.1
  30.8 0.6 %collective-permute-start.14 = (bf16[128,1024]{1,0:T(8,128)(2,1)S(1)}, bf16[128,1024]{1,0:T(8,128)(2,1)S(1)}, u32[]{:S(2)}, u32[]{:S(2)}) collective-permute-start(bf16[128,1024]{1,0:T(8,128)(2,1)S(1)} %get-tuple-element.23), channel_id=1, source_target_pairs={{0,2},{2,0},{4,6},{6,4},{1,3},{3,1},{5,7},{7,5},{8,10},{10,8},{12,... | collective-permute-start | bytes 786440 | tf_op jit(solution)/shard_map/ppermute | solution.py:36
  31.4 1.6 %collective-permute-start.15 = (bf16[128,1024]{1,0:T(8,128)(2,1)S(1)}, bf16[128,1024]{1,0:T(8,128)(2,1)S(1)}, u32[]{:S(2)}, u32[]{:S(2)}) collective-permute-start(bf16[128,1024]{1,0:T(8,128)(2,1)S(1)} %get-tuple-element.24), channel_id=1, source_target_pairs={{0,4},{2,6},{4,0},{6,2},{1,5},{3,7},{5,1},{7,3},{8,12},{10,14},{12... | collective-permute-start | bytes 786440 | tf_op jit(solution)/shard_map/ppermute | solution.py:36
  33.0 0.3 prepare.1
  33.3 3.4 %collective-permute-done.8.refs_3_ = bf16[256,256]{1,0:T(8,128)(2,1)S(1)} collective-permute-done((bf16[256,256]{1,0:T(8,128)(2,1)S(1)}, bf16[256,256]{1,0:T(8,128)(2,1)S(1)}, u32[]{:S(2)}, u32[]{:S(2)}) %collective-permute-start.8) | collective-permute-done | bytes 131104 | tf_op jit(solution)/shard_map/ppermute | solution.py:36
  36.7 1.4 %section0_front.1 = (bf16[256,256]{1,0:T(8,128)(2,1)S(1)}, bf16[256,1024]{1,0:T(8,128)(2,1)S(1)}, bf16[3,256,1024]{2,1,0:T(8,128)(2,1)S(1)}) custom-call(bf16[256,256]{1,0:T(8,128)(2,1)S(1)} %merge.5.refs_0_, bf16[256,256]{1,0:T(8,128)(2,1)S(1)} %collective-permute-done.6.refs_1_, bf16[256,256]{1,0:T(8,128)(2,1)S(1)} %collective-permute-done.7.refs_2_, ...), custom_call_target="tpu_custom_call" | custom-call | flops 603979776 | bytes 2097152 | tf_op jit(solution)/shard_map/section0_front/pallas_call | solution.py:393
  38.1 0.1 collective-permute-start.11
  38.2 1.9 %collective-permute-start.12 = (bf16[256,256]{1,0:T(8,128)(2,1)S(1)}, bf16[256,256]{1,0:T(8,128)(2,1)S(1)}, u32[]{:S(2)}, u32[]{:S(2)}) collective-permute-start(bf16[256,256]{1,0:T(8,128)(2,1)S(1)} %get-tuple-element.20.refs_0_), channel_id=1, source_target_pairs={{0,4},{2,6},{4,0},{6,2},{1,5},{3,7},{5,1},{7,3},{8,12},{10,14},{12... | collective-permute-start | bytes 393224 | tf_op jit(solution)/shard_map/ppermute | solution.py:36
  40.1 1.6 %collective-permute-start.13 = (bf16[256,256]{1,0:T(8,128)(2,1)S(1)}, bf16[256,256]{1,0:T(8,128)(2,1)S(1)}, u32[]{:S(2)}, u32[]{:S(2)}) collective-permute-start(bf16[256,256]{1,0:T(8,128)(2,1)S(1)} %get-tuple-element.20.refs_0_), channel_id=1, source_target_pairs={{0,6},{2,4},{4,2},{6,0},{1,7},{3,5},{5,3},{7,1},{8,14},{10,12},{12... | collective-permute-start | bytes 393224 | tf_op jit(solution)/shard_map/ppermute | solution.py:36
  41.7 0.1 stack.1.refs_9_
  41.8 0.6 collective-permute-start.17
  42.3 0.8 %collective-permute-done.11.refs_1_ = bf16[256,256]{1,0:T(8,128)(2,1)S(1)} collective-permute-done((bf16[256,256]{1,0:T(8,128)(2,1)S(1)}, bf16[256,256]{1,0:T(8,128)(2,1)S(1)}, u32[]{:S(2)}, u32[]{:S(2)}) %collective-permute-start.11) | collective-permute-done | bytes 131104 | tf_op jit(solution)/shard_map/ppermute | solution.py:36
  43.2 0.8 %collective-permute-done.12.refs_2_ = bf16[256,256]{1,0:T(8,128)(2,1)S(1)} collective-permute-done((bf16[256,256]{1,0:T(8,128)(2,1)S(1)}, bf16[256,256]{1,0:T(8,128)(2,1)S(1)}, u32[]{:S(2)}, u32[]{:S(2)}) %collective-permute-start.12) | collective-permute-done | bytes 131104 | tf_op jit(solution)/shard_map/ppermute | solution.py:36
  44.0 1.9 %collective-permute-done.13.refs_0_ = bf16[256,256]{1,0:T(8,128)(2,1)S(1)} collective-permute-done((bf16[256,256]{1,0:T(8,128)(2,1)S(1)}, bf16[256,256]{1,0:T(8,128)(2,1)S(1)}, u32[]{:S(2)}, u32[]{:S(2)}) %collective-permute-start.13) | collective-permute-done | bytes 131104 | tf_op jit(solution)/shard_map/ppermute | solution.py:36
  46.0 0.0 copy-start.2
  46.0 1.8 %section0_back_section1_front.1 = (bf16[256,256]{1,0:T(8,128)(2,1)S(1)}, bf16[256,1024]{1,0:T(8,128)(2,1)S(1)}) custom-call(bf16[256,256]{1,0:T(8,128)(2,1)S(1)} %get-tuple-element.20.refs_0_, bf16[256,256]{1,0:T(8,128)(2,1)S(1)} %collective-permute-done.11.refs_1_, bf16[256,256]{1,0:T(8,128)(2,1)S(1)} %collective-permute-done.12.refs_2_, ...), custom_call_target="tpu_custom_call" | custom-call | flops 1140850688 | bytes 4194304 | tf_op jit(solution)/shard_map/section0_back_section1_front/pallas_call | solution.py:416
  47.7 0.7 %collective-permute-start.18 = (bf16[256,256]{1,0:T(8,128)(2,1)S(1)}, bf16[256,256]{1,0:T(8,128)(2,1)S(1)}, u32[]{:S(2)}, u32[]{:S(2)}) collective-permute-start(bf16[256,256]{1,0:T(8,128)(2,1)S(1)} %get-tuple-element.25.refs_0_), channel_id=1, source_target_pairs={{0,2},{2,0},{4,6},{6,4},{1,3},{3,1},{5,7},{7,5},{8,10},{10,8},{12,... | collective-permute-start | bytes 393224 | tf_op jit(solution)/shard_map/ppermute | solution.py:36
  48.5 1.5 %collective-permute-start.19 = (bf16[256,256]{1,0:T(8,128)(2,1)S(1)}, bf16[256,256]{1,0:T(8,128)(2,1)S(1)}, u32[]{:S(2)}, u32[]{:S(2)}) collective-permute-start(bf16[256,256]{1,0:T(8,128)(2,1)S(1)} %get-tuple-element.25.refs_0_), channel_id=1, source_target_pairs={{0,4},{2,6},{4,0},{6,2},{1,5},{3,7},{5,1},{7,3},{8,12},{10,14},{12... | collective-permute-start | bytes 393224 | tf_op jit(solution)/shard_map/ppermute | solution.py:36
  50.0 1.3 %collective-permute-start.20 = (bf16[256,256]{1,0:T(8,128)(2,1)S(1)}, bf16[256,256]{1,0:T(8,128)(2,1)S(1)}, u32[]{:S(2)}, u32[]{:S(2)}) collective-permute-start(bf16[256,256]{1,0:T(8,128)(2,1)S(1)} %get-tuple-element.25.refs_0_), channel_id=1, source_target_pairs={{0,6},{2,4},{4,2},{6,0},{1,7},{3,5},{5,3},{7,1},{8,14},{10,12},{12... | collective-permute-start | bytes 393224 | tf_op jit(solution)/shard_map/ppermute | solution.py:36
  51.3 2.9 %collective-permute-done.18.refs_1_ = bf16[256,256]{1,0:T(8,128)(2,1)S(1)} collective-permute-done((bf16[256,256]{1,0:T(8,128)(2,1)S(1)}, bf16[256,256]{1,0:T(8,128)(2,1)S(1)}, u32[]{:S(2)}, u32[]{:S(2)}) %collective-permute-start.18) | collective-permute-done | bytes 131104 | tf_op jit(solution)/shard_map/ppermute | solution.py:36
  54.2 2.1 %collective-permute-done.19.refs_2_ = bf16[256,256]{1,0:T(8,128)(2,1)S(1)} collective-permute-done((bf16[256,256]{1,0:T(8,128)(2,1)S(1)}, bf16[256,256]{1,0:T(8,128)(2,1)S(1)}, u32[]{:S(2)}, u32[]{:S(2)}) %collective-permute-start.19) | collective-permute-done | bytes 131104 | tf_op jit(solution)/shard_map/ppermute | solution.py:36
  56.2 2.1 %section1_back_context.1 = (bf16[256,1024]{1,0:T(8,128)(2,1)}, bf16[256,256]{1,0:T(8,128)(2,1)}) custom-call(bf16[256,256]{1,0:T(8,128)(2,1)S(1)} %get-tuple-element.25.refs_0_, bf16[256,256]{1,0:T(8,128)(2,1)S(1)} %collective-permute-done.18.refs_1_, bf16[256,256]{1,0:T(8,128)(2,1)S(1)} %collective-permute-done.19.refs_2_, ...), custom_call_target="tpu_custom_call" | custom-call | flops 805306368 | bytes 2097152 | tf_op jit(solution)/shard_map/section1_back_context/pallas_call | solution.py:430
  (29 shorter events, 0.1 us)
Async XLA Ops:
  1.3 5.7 %collective-permute-start = (s32[8,128]{1,0:T(8,128)S(1)}, s32[8,128]{1,0:T(8,128)S(1)}, u32[]{:S(2)}, u32[]{:S(2)}) collective-permute-start(s32[8,128]{1,0:T(8,128)S(1)} %pad_add_fusion.1.refs_0_), channel_id=1, source_target_pairs={{0,8},{8,0},{16,24},{24,16},{1,9},{9,1},{17,25},{25,17},{2,10},{10... | collective-permute-start | bytes 12296 | tf_op jit(solution)/shard_map/ppermute | solution.py:36
  7.0 0.7 %copy-start.5 = (s32[512]{0:T(512)S(1)}, s32[512]{0:T(512)}, u32[]{:S(2)}) copy-start(s32[512]{0:T(512)} %param.11) | copy-start | bytes 6148
  7.0 0.7 %copy-start.6 = (s32[512,1]{0,1:T(1,128)S(1)}, s32[512,1]{0,1:T(1,128)}, u32[]{:S(2)}) copy-start(s32[512,1]{0,1:T(1,128)} %param.10) | copy-start | bytes 6148
  7.0 3.3 %copy-start.1 = (bf16[1,256,1024]{2,1,0:T(8,128)(2,1)S(1)}, bf16[1,256,1024]{2,1,0:T(8,128)(2,1)}, u32[]{:S(2)}) copy-start(bf16[1,256,1024]{2,1,0:T(8,128)(2,1)} %param.17) | copy-start | bytes 1572868
  7.0 6.3 %copy-start = (bf16[1024,1024]{1,0:T(8,128)(2,1)S(1)}, bf16[1024,1024]{1,0:T(8,128)(2,1)}, u32[]{:S(2)}) copy-start(bf16[1024,1024]{1,0:T(8,128)(2,1)} %refs_3_.1) | copy-start | bytes 6291460
  7.0 20.1 %collective-permute-start.5 = (bf16[4,1024,256]{2,1,0:T(8,128)(2,1)S(1)}, bf16[4,1024,256]{2,1,0:T(8,128)(2,1)S(1)}, u32[]{:S(2)}, u32[]{:S(2)}) collective-permute-start(bf16[4,1024,256]{2,1,0:T(8,128)(2,1)S(1)} %hold.2.refs_8_.refs_6_), channel_id=1, source_target_pairs={{0,1},{1,0},{2,3},{3,2},{4,5},{5,4},{6,7},{7,6},{8,9},{9,8},{10,11... | collective-permute-start | bytes 6291464 | tf_op jit(solution)/shard_map/ppermute | solution.py:36
  7.7 5.7 %collective-permute-start.1 = (s32[16,128]{1,0:T(8,128)S(1)}, s32[16,128]{1,0:T(8,128)S(1)}, u32[]{:S(2)}, u32[]{:S(2)}) collective-permute-start(s32[16,128]{1,0:T(8,128)S(1)} %pad_add_fusion), channel_id=1, source_target_pairs={{0,16},{8,24},{16,0},{24,8},{1,17},{9,25},{17,1},{25,9},{2,18},{10... | collective-permute-start | bytes 24584 | tf_op jit(solution)/shard_map/ppermute | solution.py:36
  10.3 20.4 %collective-permute-start.10 = (bf16[256,1024]{1,0:T(8,128)(2,1)S(1)}, bf16[256,1024]{1,0:T(8,128)(2,1)S(1)}, u32[]{:S(2)}, u32[]{:S(2)}) collective-permute-start(bf16[256,1024]{1,0:T(8,128)(2,1)S(1)} %bitcast.14), channel_id=1, source_target_pairs={{0,4},{2,6},{4,0},{6,2},{1,5},{3,7},{5,1},{7,3},{8,12},{10,14},{12... | collective-permute-start | bytes 1572872 | tf_op jit(solution)/shard_map/ppermute | solution.py:36
  11.9 18.8 %collective-permute-start.9 = (bf16[256,1024]{1,0:T(8,128)(2,1)S(1)}, bf16[256,1024]{1,0:T(8,128)(2,1)S(1)}, u32[]{:S(2)}, u32[]{:S(2)}) collective-permute-start(bf16[256,1024]{1,0:T(8,128)(2,1)S(1)} %bitcast.15), channel_id=1, source_target_pairs={{0,2},{2,0},{4,6},{6,4},{1,3},{3,1},{5,7},{7,5},{8,10},{10,8},{12,... | collective-permute-start | bytes 1572872 | tf_op jit(solution)/shard_map/ppermute | solution.py:36
  13.8 6.0 %collective-permute-start.3 = (bf16[256,256]{1,0:T(8,128)(2,1)S(1)}, bf16[256,256]{1,0:T(8,128)(2,1)S(1)}, u32[]{:S(2)}, u32[]{:S(2)}) collective-permute-start(bf16[256,256]{1,0:T(8,128)(2,1)S(1)} %fetch.2.refs_4_), channel_id=1, source_target_pairs={{0,8},{8,0},{16,24},{24,16},{1,9},{9,1},{17,25},{25,17},{2,10},{10... | collective-permute-start | bytes 393224 | tf_op jit(solution)/shard_map/ppermute | solution.py:36
  15.0 7.1 %collective-permute-start.2 = (bf16[256,256]{1,0:T(8,128)(2,1)S(1)}, bf16[256,256]{1,0:T(8,128)(2,1)S(1)}, u32[]{:S(2)}, u32[]{:S(2)}) collective-permute-start(bf16[256,256]{1,0:T(8,128)(2,1)S(1)} %get-tuple-element.17), channel_id=1, source_target_pairs={{0,8},{8,0},{16,24},{24,16},{1,9},{9,1},{17,25},{25,17},{2,10},{10... | collective-permute-start | bytes 393224 | tf_op jit(solution)/shard_map/ppermute | solution.py:36
  19.8 7.3 %collective-permute-start.4 = (bf16[256,256]{1,0:T(8,128)(2,1)S(1)}, bf16[256,256]{1,0:T(8,128)(2,1)S(1)}, u32[]{:S(2)}, u32[]{:S(2)}) collective-permute-start(bf16[256,256]{1,0:T(8,128)(2,1)S(1)} %merge.3.refs_0_), channel_id=1, source_target_pairs={{0,16},{8,24},{16,0},{24,8},{1,17},{9,25},{17,1},{25,9},{2,18},{10... | collective-permute-start | bytes 393224 | tf_op jit(solution)/shard_map/ppermute | solution.py:36
  22.0 10.9 %copy-start.3 = (s32[1,2,256,8]{2,3,1,0:T(8,128)S(1)}, s32[1,2,256,8]{2,3,1,0:T(8,128)}, u32[]{:S(2)}) copy-start(s32[1,2,256,8]{2,3,1,0:T(8,128)} %param.13) | copy-start | bytes 49156
  22.0 10.9 %copy-start.4 = (s32[1,2,256]{2,1,0:T(2,128)S(1)}, s32[1,2,256]{2,1,0:T(2,128)}, u32[]{:S(2)}) copy-start(s32[1,2,256]{2,1,0:T(2,128)} %seg_ref.1) | copy-start | bytes 6148
  27.1 6.1 %collective-permute-start.6 = (bf16[256,256]{1,0:T(8,128)(2,1)S(1)}, bf16[256,256]{1,0:T(8,128)(2,1)S(1)}, u32[]{:S(2)}, u32[]{:S(2)}) collective-permute-start(bf16[256,256]{1,0:T(8,128)(2,1)S(1)} %merge.5.refs_0_), channel_id=1, source_target_pairs={{0,2},{2,0},{4,6},{6,4},{1,3},{3,1},{5,7},{7,5},{8,10},{10,8},{12,... | collective-permute-start | bytes 393224 | tf_op jit(solution)/shard_map/ppermute | solution.py:36
  27.7 5.5 %collective-permute-start.7 = (bf16[256,256]{1,0:T(8,128)(2,1)S(1)}, bf16[256,256]{1,0:T(8,128)(2,1)S(1)}, u32[]{:S(2)}, u32[]{:S(2)}) collective-permute-start(bf16[256,256]{1,0:T(8,128)(2,1)S(1)} %merge.5.refs_0_), channel_id=1, source_target_pairs={{0,4},{2,6},{4,0},{6,2},{1,5},{3,7},{5,1},{7,3},{8,12},{10,14},{12... | collective-permute-start | bytes 393224 | tf_op jit(solution)/shard_map/ppermute | solution.py:36
  29.3 7.4 %collective-permute-start.8 = (bf16[256,256]{1,0:T(8,128)(2,1)S(1)}, bf16[256,256]{1,0:T(8,128)(2,1)S(1)}, u32[]{:S(2)}, u32[]{:S(2)}) collective-permute-start(bf16[256,256]{1,0:T(8,128)(2,1)S(1)} %merge.5.refs_0_), channel_id=1, source_target_pairs={{0,6},{2,4},{4,2},{6,0},{1,7},{3,5},{5,3},{7,1},{8,14},{10,12},{12... | collective-permute-start | bytes 393224 | tf_op jit(solution)/shard_map/ppermute | solution.py:36
  30.8 10.9 %collective-permute-start.14 = (bf16[128,1024]{1,0:T(8,128)(2,1)S(1)}, bf16[128,1024]{1,0:T(8,128)(2,1)S(1)}, u32[]{:S(2)}, u32[]{:S(2)}) collective-permute-start(bf16[128,1024]{1,0:T(8,128)(2,1)S(1)} %get-tuple-element.23), channel_id=1, source_target_pairs={{0,2},{2,0},{4,6},{6,4},{1,3},{3,1},{5,7},{7,5},{8,10},{10,8},{12,... | collective-permute-start | bytes 786440 | tf_op jit(solution)/shard_map/ppermute | solution.py:36
  31.4 10.3 %collective-permute-start.15 = (bf16[128,1024]{1,0:T(8,128)(2,1)S(1)}, bf16[128,1024]{1,0:T(8,128)(2,1)S(1)}, u32[]{:S(2)}, u32[]{:S(2)}) collective-permute-start(bf16[128,1024]{1,0:T(8,128)(2,1)S(1)} %get-tuple-element.24), channel_id=1, source_target_pairs={{0,4},{2,6},{4,0},{6,2},{1,5},{3,7},{5,1},{7,3},{8,12},{10,14},{12... | collective-permute-start | bytes 786440 | tf_op jit(solution)/shard_map/ppermute | solution.py:36
  38.1 5.0 %collective-permute-start.11 = (bf16[256,256]{1,0:T(8,128)(2,1)S(1)}, bf16[256,256]{1,0:T(8,128)(2,1)S(1)}, u32[]{:S(2)}, u32[]{:S(2)}) collective-permute-start(bf16[256,256]{1,0:T(8,128)(2,1)S(1)} %get-tuple-element.20.refs_0_), channel_id=1, source_target_pairs={{0,2},{2,0},{4,6},{6,4},{1,3},{3,1},{5,7},{7,5},{8,10},{10,8},{12,... | collective-permute-start | bytes 393224 | tf_op jit(solution)/shard_map/ppermute | solution.py:36
  38.2 5.8 %collective-permute-start.12 = (bf16[256,256]{1,0:T(8,128)(2,1)S(1)}, bf16[256,256]{1,0:T(8,128)(2,1)S(1)}, u32[]{:S(2)}, u32[]{:S(2)}) collective-permute-start(bf16[256,256]{1,0:T(8,128)(2,1)S(1)} %get-tuple-element.20.refs_0_), channel_id=1, source_target_pairs={{0,4},{2,6},{4,0},{6,2},{1,5},{3,7},{5,1},{7,3},{8,12},{10,14},{12... | collective-permute-start | bytes 393224 | tf_op jit(solution)/shard_map/ppermute | solution.py:36
  40.1 5.9 %collective-permute-start.13 = (bf16[256,256]{1,0:T(8,128)(2,1)S(1)}, bf16[256,256]{1,0:T(8,128)(2,1)S(1)}, u32[]{:S(2)}, u32[]{:S(2)}) collective-permute-start(bf16[256,256]{1,0:T(8,128)(2,1)S(1)} %get-tuple-element.20.refs_0_), channel_id=1, source_target_pairs={{0,6},{2,4},{4,2},{6,0},{1,7},{3,5},{5,3},{7,1},{8,14},{10,12},{12... | collective-permute-start | bytes 393224 | tf_op jit(solution)/shard_map/ppermute | solution.py:36
  41.7 4.3 %collective-permute-start.16 = (bf16[3,256,1024]{2,1,0:T(8,128)(2,1)S(1)}, bf16[3,256,1024]{2,1,0:T(8,128)(2,1)S(1)}, u32[]{:S(2)}, u32[]{:S(2)}) collective-permute-start(bf16[3,256,1024]{2,1,0:T(8,128)(2,1)S(1)} %get-tuple-element.22.refs_8_), channel_id=1, source_target_pairs={{0,1},{1,0},{2,3},{3,2},{4,5},{5,4},{6,7},{7,6},{8,9},{9,8},{10,11... | collective-permute-start | bytes 4718600 | tf_op jit(solution)/shard_map/ppermute | solution.py:36
  41.8 4.2 %collective-permute-start.17 = (bf16[1,256,1024]{2,1,0:T(8,128)(2,1)S(1)}, bf16[1,256,1024]{2,1,0:T(8,128)(2,1)S(1)}, u32[]{:S(2)}, u32[]{:S(2)}) collective-permute-start(bf16[1,256,1024]{2,1,0:T(8,128)(2,1)S(1)} %stack.1.refs_9_), channel_id=1, source_target_pairs={{0,1},{1,0},{2,3},{3,2},{4,5},{5,4},{6,7},{7,6},{8,9},{9,8},{10,11... | collective-permute-start | bytes 1572872 | tf_op jit(solution)/shard_map/ppermute | solution.py:36
  46.0 5.3 %copy-start.7 = (bf16[256]{0:T(256)(128)(2,1)S(1)}, bf16[256]{0:T(256)(128)(2,1)}, u32[]{:S(2)}) copy-start(bf16[256]{0:T(256)(128)(2,1)} %param.19) | copy-start | bytes 1540
  46.0 10.3 %copy-start.2 = (bf16[1024,256]{1,0:T(8,128)(2,1)S(1)}, bf16[1024,256]{1,0:T(8,128)(2,1)}, u32[]{:S(2)}) copy-start(bf16[1024,256]{1,0:T(8,128)(2,1)} %refs_6_.1) | copy-start | bytes 1572868
  47.7 6.4 %collective-permute-start.18 = (bf16[256,256]{1,0:T(8,128)(2,1)S(1)}, bf16[256,256]{1,0:T(8,128)(2,1)S(1)}, u32[]{:S(2)}, u32[]{:S(2)}) collective-permute-start(bf16[256,256]{1,0:T(8,128)(2,1)S(1)} %get-tuple-element.25.refs_0_), channel_id=1, source_target_pairs={{0,2},{2,0},{4,6},{6,4},{1,3},{3,1},{5,7},{7,5},{8,10},{10,8},{12,... | collective-permute-start | bytes 393224 | tf_op jit(solution)/shard_map/ppermute | solution.py:36
  48.5 7.8 %collective-permute-start.19 = (bf16[256,256]{1,0:T(8,128)(2,1)S(1)}, bf16[256,256]{1,0:T(8,128)(2,1)S(1)}, u32[]{:S(2)}, u32[]{:S(2)}) collective-permute-start(bf16[256,256]{1,0:T(8,128)(2,1)S(1)} %get-tuple-element.25.refs_0_), channel_id=1, source_target_pairs={{0,4},{2,6},{4,0},{6,2},{1,5},{3,7},{5,1},{7,3},{8,12},{10,14},{12... | collective-permute-start | bytes 393224 | tf_op jit(solution)/shard_map/ppermute | solution.py:36
  50.0 6.3 %collective-permute-start.20 = (bf16[256,256]{1,0:T(8,128)(2,1)S(1)}, bf16[256,256]{1,0:T(8,128)(2,1)S(1)}, u32[]{:S(2)}, u32[]{:S(2)}) collective-permute-start(bf16[256,256]{1,0:T(8,128)(2,1)S(1)} %get-tuple-element.25.refs_0_), channel_id=1, source_target_pairs={{0,6},{2,4},{4,2},{6,0},{1,7},{3,5},{5,3},{7,1},{8,14},{10,12},{12... | collective-permute-start | bytes 393224 | tf_op jit(solution)/shard_map/ppermute | solution.py:36

commit v13 on v12

--- a/solution.py
+++ b/solution.py
@@ -318,16 +318,18 @@
     gated_refs, refs = refs[:steps], refs[steps:]
     x_ref, share_ref, w_ref, bias_ref = refs[:4]
     o_own, o_other = refs[4 : 4 + parts], refs[4 + parts : 4 + 2 * parts]
-    states_ref, ctx_ref = refs[-2:]
+    out_ref, ctx_ref, states_ref, sem = refs[-4:]
+    copy = pltpu.make_async_copy(states_ref, out_ref, sem)
 
     def body(*o_refs):
-        states = back(x_ref[...], gated_refs, o_refs)
-        states_ref[...] = states
-        context = jnp.dot(share_ref[...], states, preferred_element_type=F32).astype(BF16)
-        summed = jnp.dot(context, w_ref[...], preferred_element_type=F32)
-        ctx_ref[...] = silu(summed + bias_ref[...].astype(F32)).astype(BF16)
+        states_ref[...] = back(x_ref[...], gated_refs, o_refs)
 
     by_phase(body, o_other, o_own)
+    copy.start()
+    context = jnp.dot(share_ref[...], states_ref[...], preferred_element_type=F32).astype(BF16)
+    summed = jnp.dot(context, w_ref[...], preferred_element_type=F32)
+    ctx_ref[...] = silu(summed + bias_ref[...].astype(F32)).astype(BF16)
+    copy.wait()
 
 
 def section_flops(rows, width, local_cols):
@@ -431,7 +433,8 @@
         functools.partial(last_kernel, mp_count, len(o_own)),
         out_shape=[x_shape, jax.ShapeDtypeStruct((imps, w_ctx.shape[1]), BF16)],
         in_specs=[VMEM] * (mp_count + 4 + 2 * len(o_own)),
-        out_specs=[VMEM] * 2,
+        out_specs=[HBM, VMEM],
+        scratch_shapes=[pltpu.VMEM((rows, width), BF16), pltpu.SemaphoreType.DMA],
         compiler_params=params(),
         cost_estimate=pl.CostEstimate(
             flops=back_flops + 2 * imps * width * (rows + w_ctx.shape[1]),

time: 58.6 us -> 59 us (level)
  transfers between devices with their start and end apart: 21 -> 21, of which waited for: 9 -> 9; matrix products, arithmetic and copies ran while one was open for 5% -> 4% of each run, Pallas kernels for 5% -> 5%
where the time goes in v13:
time: 59 us; the launch traced here: 58.8 us
  starting transfers between devices  25.6 us (43%)
  waiting for transfers between devices  21.2 us (36%)
  Pallas kernels  7.25 us (12%)
  other arithmetic  3.33 us (6%)
  between operations  0.81 us (1%)
  local copies, waits for them, and re-layouts  0.6 us (1%)
    ppermute x21, starting transfers between devices, exchange(): return lax.ppermute(value, axis, pairs)  25.6 us
    ppermute x21, waiting for transfers between devices, exchange(): return lax.ppermute(value, axis, pairs)  21.2 us
    pallas_call x1, Pallas kernels, on_device(): pl.pallas_call(functools.partial(last_kernel, mp_count, len(o_own)), out_...  2.55 us
    mul x1, other arithmetic, on_device(): w_own = jnp.transpose(w_in[0], (1, 0, 2)) * gains[0][None, :, None]  1.9 us
    pallas_call x1, Pallas kernels, on_device(): pl.pallas_call(functools.partial(middle_kernel, mp_count, len(o_own)), ou...  1.76 us
    pallas_call x1, Pallas kernels, on_device(): pl.pallas_call(functools.partial(first_kernel, mp_count, places), out_sha...  1.43 us
  transfers between devices with their start and end apart: 21, of which 9 were waited for; matrix products, arithmetic and copies ran while one was open for 4% of the time, Pallas kernels for 5%

profile of v13, /device:TPU:0, one launch (start us, length us, event | category | flops | bytes accessed | tf_op | source)
XLA Modules:
  0.0 58.8 jit_solution(211909035240550467)
XLA Ops:
  0.6 0.7 %pad_add_fusion.1.refs_0_ = s32[8,128]{1,0:T(8,128)S(1)} fusion(s32[4,128]{1,0:T(4,128)} %bitcast.18, s32[4,128]{1,0:T(4,128)} %bitcast.20), kind=kLoop, calls=%fused_computation.3 | loop fusion | flops 1024 | bytes 8192 | tf_op jit(solution)/shard_map/concatenate | solution.py:374
  1.3 3.0 %collective-permute-start = (s32[8,128]{1,0:T(8,128)S(1)}, s32[8,128]{1,0:T(8,128)S(1)}, u32[]{:S(2)}, u32[]{:S(2)}) collective-permute-start(s32[8,128]{1,0:T(8,128)S(1)} %pad_add_fusion.1.refs_0_), channel_id=1, source_target_pairs={{0,8},{8,0},{16,24},{24,16},{1,9},{9,1},{17,25},{25,17},{2,10},{10... | collective-permute-start | bytes 12296 | tf_op jit(solution)/shard_map/ppermute | solution.py:36
  4.4 0.7 %reduce = bf16[1024]{0:T(1024)(128)(2,1)S(1)} reduce(bf16[1,1024]{1,0:T(2,128)(2,1)} %param.15, bf16[]{:T(256)} %constant.5), dimensions={0}, to_apply=%param.15.reduce_sub_computation | reduce | bytes 4098 | tf_op args[5]
  5.1 1.9 %fusion.refs_0_ = bf16[4,1024,256]{2,1,0:T(8,128)(2,1)S(1)} fusion(bf16[1,1024,4,256]{3,2,1,0:T(4,128)(2,1)} %param.16, bf16[1024]{0:T(1024)(128)(2,1)S(1)} %reduce), kind=kLoop, calls=%fused_computation.1 | loop fusion | flops 1048576 | bytes 4196352 | tf_op jit(solution)/shard_map/mul | solution.py:363
  7.0 0.0 copy-start.5
  7.0 0.0 copy-start.6
  7.0 0.0 copy-start.1
  7.0 0.0 copy-start
  7.0 0.0 collective-permute-done.refs_1_
  7.0 0.1 collective-permute-start.5
  7.1 0.5 copy-done.5
  7.7 0.0 copy-done.6
  7.7 2.6 %collective-permute-start.1 = (s32[16,128]{1,0:T(8,128)S(1)}, s32[16,128]{1,0:T(8,128)S(1)}, u32[]{:S(2)}, u32[]{:S(2)}) collective-permute-start(s32[16,128]{1,0:T(8,128)S(1)} %pad_add_fusion), channel_id=1, source_target_pairs={{0,16},{8,24},{16,0},{24,8},{1,17},{9,25},{17,1},{25,9},{2,18},{10... | collective-permute-start | bytes 24584 | tf_op jit(solution)/shard_map/ppermute | solution.py:36
  10.3 1.5 %collective-permute-start.10 = (bf16[256,1024]{1,0:T(8,128)(2,1)S(1)}, bf16[256,1024]{1,0:T(8,128)(2,1)S(1)}, u32[]{:S(2)}, u32[]{:S(2)}) collective-permute-start(bf16[256,1024]{1,0:T(8,128)(2,1)S(1)} %bitcast.14), channel_id=1, source_target_pairs={{0,4},{2,6},{4,0},{6,2},{1,5},{3,7},{5,1},{7,3},{8,12},{10,14},{12... | collective-permute-start | bytes 1572872 | tf_op jit(solution)/shard_map/ppermute | solution.py:36
  11.9 1.5 %collective-permute-start.9 = (bf16[256,1024]{1,0:T(8,128)(2,1)S(1)}, bf16[256,1024]{1,0:T(8,128)(2,1)S(1)}, u32[]{:S(2)}, u32[]{:S(2)}) collective-permute-start(bf16[256,1024]{1,0:T(8,128)(2,1)S(1)} %bitcast.15), channel_id=1, source_target_pairs={{0,2},{2,0},{4,6},{6,4},{1,3},{3,1},{5,7},{7,5},{8,10},{10,8},{12,... | collective-permute-start | bytes 1572872 | tf_op jit(solution)/shard_map/ppermute | solution.py:36
  13.4 0.4 fetch.2.refs_4_
  13.8 0.5 collective-permute-start.3
  14.3 0.7 %fetch.3 = (bf16[256,256]{1,0:T(8,128)(2,1)S(1)}, bf16[256,256]{1,0:T(8,128)(2,1)S(1)}, bf16[256,256]{1,0:T(8,128)(2,1)S(1)}) custom-call(s32[8,128]{1,0:T(8,128)S(1)} %pad_add_fusion.1.refs_0_, s32[8,128]{1,0:T(8,128)S(1)} %collective-permute-done.refs_1_, s32[8,128]{1,0:T(8,128)S(1)} %get-tuple-element.31.refs_2_, bf16[1024,1024]{1,0:T(8,128)(2,1)S(1)} %copy-done, ...), custom_call_target="tpu_custom_call" | custom-call | flops 402653184 | bytes 524288 | tf_op jit(solution)/shard_map/fetch/pallas_call | solution.py:88
  15.0 1.6 %collective-permute-start.2 = (bf16[256,256]{1,0:T(8,128)(2,1)S(1)}, bf16[256,256]{1,0:T(8,128)(2,1)S(1)}, u32[]{:S(2)}, u32[]{:S(2)}) collective-permute-start(bf16[256,256]{1,0:T(8,128)(2,1)S(1)} %get-tuple-element.17), channel_id=1, source_target_pairs={{0,8},{8,0},{16,24},{24,16},{1,9},{9,1},{17,25},{25,17},{2,10},{10... | collective-permute-start | bytes 393224 | tf_op jit(solution)/shard_map/ppermute | solution.py:36
  16.6 3.2 %collective-permute-done.3.b_ref = bf16[256,256]{1,0:T(8,128)(2,1)S(1)} collective-permute-done((bf16[256,256]{1,0:T(8,128)(2,1)S(1)}, bf16[256,256]{1,0:T(8,128)(2,1)S(1)}, u32[]{:S(2)}, u32[]{:S(2)}) %collective-permute-start.3) | collective-permute-done | bytes 131104 | tf_op jit(solution)/shard_map/ppermute | solution.py:36
  19.8 1.3 %collective-permute-start.4 = (bf16[256,256]{1,0:T(8,128)(2,1)S(1)}, bf16[256,256]{1,0:T(8,128)(2,1)S(1)}, u32[]{:S(2)}, u32[]{:S(2)}) collective-permute-start(bf16[256,256]{1,0:T(8,128)(2,1)S(1)} %merge.3.refs_0_), channel_id=1, source_target_pairs={{0,16},{8,24},{16,0},{24,8},{1,17},{9,25},{17,1},{25,9},{2,18},{10... | collective-permute-start | bytes 393224 | tf_op jit(solution)/shard_map/ppermute | solution.py:36
  21.1 1.0 %collective-permute-done.2.b_ref = bf16[256,256]{1,0:T(8,128)(2,1)S(1)} collective-permute-done((bf16[256,256]{1,0:T(8,128)(2,1)S(1)}, bf16[256,256]{1,0:T(8,128)(2,1)S(1)}, u32[]{:S(2)}, u32[]{:S(2)}) %collective-permute-start.2) | collective-permute-done | bytes 131104 | tf_op jit(solution)/shard_map/ppermute | solution.py:36
  22.1 5.0 %collective-permute-done.4.b_ref = bf16[256,256]{1,0:T(8,128)(2,1)S(1)} collective-permute-done((bf16[256,256]{1,0:T(8,128)(2,1)S(1)}, bf16[256,256]{1,0:T(8,128)(2,1)S(1)}, u32[]{:S(2)}, u32[]{:S(2)}) %collective-permute-start.4) | collective-permute-done | bytes 131104 | tf_op jit(solution)/shard_map/ppermute | solution.py:36
  27.1 0.6 %collective-permute-start.6 = (bf16[256,256]{1,0:T(8,128)(2,1)S(1)}, bf16[256,256]{1,0:T(8,128)(2,1)S(1)}, u32[]{:S(2)}, u32[]{:S(2)}) collective-permute-start(bf16[256,256]{1,0:T(8,128)(2,1)S(1)} %merge.5.refs_0_), channel_id=1, source_target_pairs={{0,2},{2,0},{4,6},{6,4},{1,3},{3,1},{5,7},{7,5},{8,10},{10,8},{12,... | collective-permute-start | bytes 393224 | tf_op jit(solution)/shard_map/ppermute | solution.py:36
  27.7 1.6 %collective-permute-start.7 = (bf16[256,256]{1,0:T(8,128)(2,1)S(1)}, bf16[256,256]{1,0:T(8,128)(2,1)S(1)}, u32[]{:S(2)}, u32[]{:S(2)}) collective-permute-start(bf16[256,256]{1,0:T(8,128)(2,1)S(1)} %merge.5.refs_0_), channel_id=1, source_target_pairs={{0,4},{2,6},{4,0},{6,2},{1,5},{3,7},{5,1},{7,3},{8,12},{10,14},{12... | collective-permute-start | bytes 393224 | tf_op jit(solution)/shard_map/ppermute | solution.py:36
  29.3 1.4 %collective-permute-start.8 = (bf16[256,256]{1,0:T(8,128)(2,1)S(1)}, bf16[256,256]{1,0:T(8,128)(2,1)S(1)}, u32[]{:S(2)}, u32[]{:S(2)}) collective-permute-start(bf16[256,256]{1,0:T(8,128)(2,1)S(1)} %merge.5.refs_0_), channel_id=1, source_target_pairs={{0,6},{2,4},{4,2},{6,0},{1,7},{3,5},{5,3},{7,1},{8,14},{10,12},{12... | collective-permute-start | bytes 393224 | tf_op jit(solution)/shard_map/ppermute | solution.py:36
  30.7 0.1 cut.1
  30.8 0.6 %collective-permute-start.14 = (bf16[128,1024]{1,0:T(8,128)(2,1)S(1)}, bf16[128,1024]{1,0:T(8,128)(2,1)S(1)}, u32[]{:S(2)}, u32[]{:S(2)}) collective-permute-start(bf16[128,1024]{1,0:T(8,128)(2,1)S(1)} %get-tuple-element.23), channel_id=1, source_target_pairs={{0,2},{2,0},{4,6},{6,4},{1,3},{3,1},{5,7},{7,5},{8,10},{10,8},{12,... | collective-permute-start | bytes 786440 | tf_op jit(solution)/shard_map/ppermute | solution.py:36
  31.4 1.6 %collective-permute-start.15 = (bf16[128,1024]{1,0:T(8,128)(2,1)S(1)}, bf16[128,1024]{1,0:T(8,128)(2,1)S(1)}, u32[]{:S(2)}, u32[]{:S(2)}) collective-permute-start(bf16[128,1024]{1,0:T(8,128)(2,1)S(1)} %get-tuple-element.24), channel_id=1, source_target_pairs={{0,4},{2,6},{4,0},{6,2},{1,5},{3,7},{5,1},{7,3},{8,12},{10,14},{12... | collective-permute-start | bytes 786440 | tf_op jit(solution)/shard_map/ppermute | solution.py:36
  33.0 0.3 prepare.1
  33.3 3.4 %collective-permute-done.8.refs_3_ = bf16[256,256]{1,0:T(8,128)(2,1)S(1)} collective-permute-done((bf16[256,256]{1,0:T(8,128)(2,1)S(1)}, bf16[256,256]{1,0:T(8,128)(2,1)S(1)}, u32[]{:S(2)}, u32[]{:S(2)}) %collective-permute-start.8) | collective-permute-done | bytes 131104 | tf_op jit(solution)/shard_map/ppermute | solution.py:36
  36.7 1.4 %section0_front.1 = (bf16[256,256]{1,0:T(8,128)(2,1)S(1)}, bf16[256,1024]{1,0:T(8,128)(2,1)S(1)}, bf16[3,256,1024]{2,1,0:T(8,128)(2,1)S(1)}) custom-call(bf16[256,256]{1,0:T(8,128)(2,1)S(1)} %merge.5.refs_0_, bf16[256,256]{1,0:T(8,128)(2,1)S(1)} %collective-permute-done.6.refs_1_, bf16[256,256]{1,0:T(8,128)(2,1)S(1)} %collective-permute-done.7.refs_2_, ...), custom_call_target="tpu_custom_call" | custom-call | flops 603979776 | bytes 2097152 | tf_op jit(solution)/shard_map/section0_front/pallas_call | solution.py:395
  38.1 0.1 collective-permute-start.11
  38.2 1.9 %collective-permute-start.12 = (bf16[256,256]{1,0:T(8,128)(2,1)S(1)}, bf16[256,256]{1,0:T(8,128)(2,1)S(1)}, u32[]{:S(2)}, u32[]{:S(2)}) collective-permute-start(bf16[256,256]{1,0:T(8,128)(2,1)S(1)} %get-tuple-element.20.refs_0_), channel_id=1, source_target_pairs={{0,4},{2,6},{4,0},{6,2},{1,5},{3,7},{5,1},{7,3},{8,12},{10,14},{12... | collective-permute-start | bytes 393224 | tf_op jit(solution)/shard_map/ppermute | solution.py:36
  40.1 1.6 %collective-permute-start.13 = (bf16[256,256]{1,0:T(8,128)(2,1)S(1)}, bf16[256,256]{1,0:T(8,128)(2,1)S(1)}, u32[]{:S(2)}, u32[]{:S(2)}) collective-permute-start(bf16[256,256]{1,0:T(8,128)(2,1)S(1)} %get-tuple-element.20.refs_0_), channel_id=1, source_target_pairs={{0,6},{2,4},{4,2},{6,0},{1,7},{3,5},{5,3},{7,1},{8,14},{10,12},{12... | collective-permute-start | bytes 393224 | tf_op jit(solution)/shard_map/ppermute | solution.py:36
  41.7 0.1 stack.1.refs_9_
  41.8 0.6 collective-permute-start.17
  42.3 0.8 %collective-permute-done.11.refs_1_ = bf16[256,256]{1,0:T(8,128)(2,1)S(1)} collective-permute-done((bf16[256,256]{1,0:T(8,128)(2,1)S(1)}, bf16[256,256]{1,0:T(8,128)(2,1)S(1)}, u32[]{:S(2)}, u32[]{:S(2)}) %collective-permute-start.11) | collective-permute-done | bytes 131104 | tf_op jit(solution)/shard_map/ppermute | solution.py:36
  43.2 0.8 %collective-permute-done.12.refs_2_ = bf16[256,256]{1,0:T(8,128)(2,1)S(1)} collective-permute-done((bf16[256,256]{1,0:T(8,128)(2,1)S(1)}, bf16[256,256]{1,0:T(8,128)(2,1)S(1)}, u32[]{:S(2)}, u32[]{:S(2)}) %collective-permute-start.12) | collective-permute-done | bytes 131104 | tf_op jit(solution)/shard_map/ppermute | solution.py:36
  44.0 1.9 %collective-permute-done.13.refs_0_ = bf16[256,256]{1,0:T(8,128)(2,1)S(1)} collective-permute-done((bf16[256,256]{1,0:T(8,128)(2,1)S(1)}, bf16[256,256]{1,0:T(8,128)(2,1)S(1)}, u32[]{:S(2)}, u32[]{:S(2)}) %collective-permute-start.13) | collective-permute-done | bytes 131104 | tf_op jit(solution)/shard_map/ppermute | solution.py:36
  46.0 0.0 copy-start.2
  46.0 1.8 %section0_back_section1_front.1 = (bf16[256,256]{1,0:T(8,128)(2,1)S(1)}, bf16[256,1024]{1,0:T(8,128)(2,1)S(1)}) custom-call(bf16[256,256]{1,0:T(8,128)(2,1)S(1)} %get-tuple-element.20.refs_0_, bf16[256,256]{1,0:T(8,128)(2,1)S(1)} %collective-permute-done.11.refs_1_, bf16[256,256]{1,0:T(8,128)(2,1)S(1)} %collective-permute-done.12.refs_2_, ...), custom_call_target="tpu_custom_call" | custom-call | flops 1140850688 | bytes 4194304 | tf_op jit(solution)/shard_map/section0_back_section1_front/pallas_call | solution.py:418
  47.7 0.7 %collective-permute-start.18 = (bf16[256,256]{1,0:T(8,128)(2,1)S(1)}, bf16[256,256]{1,0:T(8,128)(2,1)S(1)}, u32[]{:S(2)}, u32[]{:S(2)}) collective-permute-start(bf16[256,256]{1,0:T(8,128)(2,1)S(1)} %get-tuple-element.25.refs_0_), channel_id=1, source_target_pairs={{0,2},{2,0},{4,6},{6,4},{1,3},{3,1},{5,7},{7,5},{8,10},{10,8},{12,... | collective-permute-start | bytes 393224 | tf_op jit(solution)/shard_map/ppermute | solution.py:36
  48.5 1.5 %collective-permute-start.19 = (bf16[256,256]{1,0:T(8,128)(2,1)S(1)}, bf16[256,256]{1,0:T(8,128)(2,1)S(1)}, u32[]{:S(2)}, u32[]{:S(2)}) collective-permute-start(bf16[256,256]{1,0:T(8,128)(2,1)S(1)} %get-tuple-element.25.refs_0_), channel_id=1, source_target_pairs={{0,4},{2,6},{4,0},{6,2},{1,5},{3,7},{5,1},{7,3},{8,12},{10,14},{12... | collective-permute-start | bytes 393224 | tf_op jit(solution)/shard_map/ppermute | solution.py:36
  50.0 1.3 %collective-permute-start.20 = (bf16[256,256]{1,0:T(8,128)(2,1)S(1)}, bf16[256,256]{1,0:T(8,128)(2,1)S(1)}, u32[]{:S(2)}, u32[]{:S(2)}) collective-permute-start(bf16[256,256]{1,0:T(8,128)(2,1)S(1)} %get-tuple-element.25.refs_0_), channel_id=1, source_target_pairs={{0,6},{2,4},{4,2},{6,0},{1,7},{3,5},{5,3},{7,1},{8,14},{10,12},{12... | collective-permute-start | bytes 393224 | tf_op jit(solution)/shard_map/ppermute | solution.py:36
  51.3 2.9 %collective-permute-done.18.refs_1_ = bf16[256,256]{1,0:T(8,128)(2,1)S(1)} collective-permute-done((bf16[256,256]{1,0:T(8,128)(2,1)S(1)}, bf16[256,256]{1,0:T(8,128)(2,1)S(1)}, u32[]{:S(2)}, u32[]{:S(2)}) %collective-permute-start.18) | collective-permute-done | bytes 131104 | tf_op jit(solution)/shard_map/ppermute | solution.py:36
  54.2 2.1 %collective-permute-done.19.refs_2_ = bf16[256,256]{1,0:T(8,128)(2,1)S(1)} collective-permute-done((bf16[256,256]{1,0:T(8,128)(2,1)S(1)}, bf16[256,256]{1,0:T(8,128)(2,1)S(1)}, u32[]{:S(2)}, u32[]{:S(2)}) %collective-permute-start.19) | collective-permute-done | bytes 131104 | tf_op jit(solution)/shard_map/ppermute | solution.py:36
  56.2 2.6 %section1_back_context.1 = (bf16[256,1024]{1,0:T(8,128)(2,1)}, bf16[256,256]{1,0:T(8,128)(2,1)}) custom-call(bf16[256,256]{1,0:T(8,128)(2,1)S(1)} %get-tuple-element.25.refs_0_, bf16[256,256]{1,0:T(8,128)(2,1)S(1)} %collective-permute-done.18.refs_1_, bf16[256,256]{1,0:T(8,128)(2,1)S(1)} %collective-permute-done.19.refs_2_, ...), custom_call_target="tpu_custom_call" | custom-call | flops 805306368 | bytes 2097152 | tf_op jit(solution)/shard_map/section1_back_context/pallas_call | solution.py:432
  (29 shorter events, 0.1 us)
Async XLA Ops:
  1.3 5.7 %collective-permute-start = (s32[8,128]{1,0:T(8,128)S(1)}, s32[8,128]{1,0:T(8,128)S(1)}, u32[]{:S(2)}, u32[]{:S(2)}) collective-permute-start(s32[8,128]{1,0:T(8,128)S(1)} %pad_add_fusion.1.refs_0_), channel_id=1, source_target_pairs={{0,8},{8,0},{16,24},{24,16},{1,9},{9,1},{17,25},{25,17},{2,10},{10... | collective-permute-start | bytes 12296 | tf_op jit(solution)/shard_map/ppermute | solution.py:36
  7.0 0.7 %copy-start.5 = (s32[512]{0:T(512)S(1)}, s32[512]{0:T(512)}, u32[]{:S(2)}) copy-start(s32[512]{0:T(512)} %param.11) | copy-start | bytes 6148
  7.0 0.7 %copy-start.6 = (s32[512,1]{0,1:T(1,128)S(1)}, s32[512,1]{0,1:T(1,128)}, u32[]{:S(2)}) copy-start(s32[512,1]{0,1:T(1,128)} %param.10) | copy-start | bytes 6148
  7.0 3.3 %copy-start.1 = (bf16[1,256,1024]{2,1,0:T(8,128)(2,1)S(1)}, bf16[1,256,1024]{2,1,0:T(8,128)(2,1)}, u32[]{:S(2)}) copy-start(bf16[1,256,1024]{2,1,0:T(8,128)(2,1)} %param.17) | copy-start | bytes 1572868
  7.0 6.3 %copy-start = (bf16[1024,1024]{1,0:T(8,128)(2,1)S(1)}, bf16[1024,1024]{1,0:T(8,128)(2,1)}, u32[]{:S(2)}) copy-start(bf16[1024,1024]{1,0:T(8,128)(2,1)} %refs_3_.1) | copy-start | bytes 6291460
  7.0 20.1 %collective-permute-start.5 = (bf16[4,1024,256]{2,1,0:T(8,128)(2,1)S(1)}, bf16[4,1024,256]{2,1,0:T(8,128)(2,1)S(1)}, u32[]{:S(2)}, u32[]{:S(2)}) collective-permute-start(bf16[4,1024,256]{2,1,0:T(8,128)(2,1)S(1)} %hold.2.refs_8_.refs_6_), channel_id=1, source_target_pairs={{0,1},{1,0},{2,3},{3,2},{4,5},{5,4},{6,7},{7,6},{8,9},{9,8},{10,11... | collective-permute-start | bytes 6291464 | tf_op jit(solution)/shard_map/ppermute | solution.py:36
  7.7 5.7 %collective-permute-start.1 = (s32[16,128]{1,0:T(8,128)S(1)}, s32[16,128]{1,0:T(8,128)S(1)}, u32[]{:S(2)}, u32[]{:S(2)}) collective-permute-start(s32[16,128]{1,0:T(8,128)S(1)} %pad_add_fusion), channel_id=1, source_target_pairs={{0,16},{8,24},{16,0},{24,8},{1,17},{9,25},{17,1},{25,9},{2,18},{10... | collective-permute-start | bytes 24584 | tf_op jit(solution)/shard_map/ppermute | solution.py:36
  10.3 20.4 %collective-permute-start.10 = (bf16[256,1024]{1,0:T(8,128)(2,1)S(1)}, bf16[256,1024]{1,0:T(8,128)(2,1)S(1)}, u32[]{:S(2)}, u32[]{:S(2)}) collective-permute-start(bf16[256,1024]{1,0:T(8,128)(2,1)S(1)} %bitcast.14), channel_id=1, source_target_pairs={{0,4},{2,6},{4,0},{6,2},{1,5},{3,7},{5,1},{7,3},{8,12},{10,14},{12... | collective-permute-start | bytes 1572872 | tf_op jit(solution)/shard_map/ppermute | solution.py:36
  11.9 18.8 %collective-permute-start.9 = (bf16[256,1024]{1,0:T(8,128)(2,1)S(1)}, bf16[256,1024]{1,0:T(8,128)(2,1)S(1)}, u32[]{:S(2)}, u32[]{:S(2)}) collective-permute-start(bf16[256,1024]{1,0:T(8,128)(2,1)S(1)} %bitcast.15), channel_id=1, source_target_pairs={{0,2},{2,0},{4,6},{6,4},{1,3},{3,1},{5,7},{7,5},{8,10},{10,8},{12,... | collective-permute-start | bytes 1572872 | tf_op jit(solution)/shard_map/ppermute | solution.py:36
  13.8 6.0 %collective-permute-start.3 = (bf16[256,256]{1,0:T(8,128)(2,1)S(1)}, bf16[256,256]{1,0:T(8,128)(2,1)S(1)}, u32[]{:S(2)}, u32[]{:S(2)}) collective-permute-start(bf16[256,256]{1,0:T(8,128)(2,1)S(1)} %fetch.2.refs_4_), channel_id=1, source_target_pairs={{0,8},{8,0},{16,24},{24,16},{1,9},{9,1},{17,25},{25,17},{2,10},{10... | collective-permute-start | bytes 393224 | tf_op jit(solution)/shard_map/ppermute | solution.py:36
  15.0 7.1 %collective-permute-start.2 = (bf16[256,256]{1,0:T(8,128)(2,1)S(1)}, bf16[256,256]{1,0:T(8,128)(2,1)S(1)}, u32[]{:S(2)}, u32[]{:S(2)}) collective-permute-start(bf16[256,256]{1,0:T(8,128)(2,1)S(1)} %get-tuple-element.17), channel_id=1, source_target_pairs={{0,8},{8,0},{16,24},{24,16},{1,9},{9,1},{17,25},{25,17},{2,10},{10... | collective-permute-start | bytes 393224 | tf_op jit(solution)/shard_map/ppermute | solution.py:36
  19.8 7.3 %collective-permute-start.4 = (bf16[256,256]{1,0:T(8,128)(2,1)S(1)}, bf16[256,256]{1,0:T(8,128)(2,1)S(1)}, u32[]{:S(2)}, u32[]{:S(2)}) collective-permute-start(bf16[256,256]{1,0:T(8,128)(2,1)S(1)} %merge.3.refs_0_), channel_id=1, source_target_pairs={{0,16},{8,24},{16,0},{24,8},{1,17},{9,25},{17,1},{25,9},{2,18},{10... | collective-permute-start | bytes 393224 | tf_op jit(solution)/shard_map/ppermute | solution.py:36
  22.0 10.9 %copy-start.3 = (s32[1,2,256,8]{2,3,1,0:T(8,128)S(1)}, s32[1,2,256,8]{2,3,1,0:T(8,128)}, u32[]{:S(2)}) copy-start(s32[1,2,256,8]{2,3,1,0:T(8,128)} %param.13) | copy-start | bytes 49156
  22.0 10.9 %copy-start.4 = (s32[1,2,256]{2,1,0:T(2,128)S(1)}, s32[1,2,256]{2,1,0:T(2,128)}, u32[]{:S(2)}) copy-start(s32[1,2,256]{2,1,0:T(2,128)} %seg_ref.1) | copy-start | bytes 6148
  27.1 6.1 %collective-permute-start.6 = (bf16[256,256]{1,0:T(8,128)(2,1)S(1)}, bf16[256,256]{1,0:T(8,128)(2,1)S(1)}, u32[]{:S(2)}, u32[]{:S(2)}) collective-permute-start(bf16[256,256]{1,0:T(8,128)(2,1)S(1)} %merge.5.refs_0_), channel_id=1, source_target_pairs={{0,2},{2,0},{4,6},{6,4},{1,3},{3,1},{5,7},{7,5},{8,10},{10,8},{12,... | collective-permute-start | bytes 393224 | tf_op jit(solution)/shard_map/ppermute | solution.py:36
  27.7 5.5 %collective-permute-start.7 = (bf16[256,256]{1,0:T(8,128)(2,1)S(1)}, bf16[256,256]{1,0:T(8,128)(2,1)S(1)}, u32[]{:S(2)}, u32[]{:S(2)}) collective-permute-start(bf16[256,256]{1,0:T(8,128)(2,1)S(1)} %merge.5.refs_0_), channel_id=1, source_target_pairs={{0,4},{2,6},{4,0},{6,2},{1,5},{3,7},{5,1},{7,3},{8,12},{10,14},{12... | collective-permute-start | bytes 393224 | tf_op jit(solution)/shard_map/ppermute | solution.py:36
  29.3 7.4 %collective-permute-start.8 = (bf16[256,256]{1,0:T(8,128)(2,1)S(1)}, bf16[256,256]{1,0:T(8,128)(2,1)S(1)}, u32[]{:S(2)}, u32[]{:S(2)}) collective-permute-start(bf16[256,256]{1,0:T(8,128)(2,1)S(1)} %merge.5.refs_0_), channel_id=1, source_target_pairs={{0,6},{2,4},{4,2},{6,0},{1,7},{3,5},{5,3},{7,1},{8,14},{10,12},{12... | collective-permute-start | bytes 393224 | tf_op jit(solution)/shard_map/ppermute | solution.py:36
  30.8 10.9 %collective-permute-start.14 = (bf16[128,1024]{1,0:T(8,128)(2,1)S(1)}, bf16[128,1024]{1,0:T(8,128)(2,1)S(1)}, u32[]{:S(2)}, u32[]{:S(2)}) collective-permute-start(bf16[128,1024]{1,0:T(8,128)(2,1)S(1)} %get-tuple-element.23), channel_id=1, source_target_pairs={{0,2},{2,0},{4,6},{6,4},{1,3},{3,1},{5,7},{7,5},{8,10},{10,8},{12,... | collective-permute-start | bytes 786440 | tf_op jit(solution)/shard_map/ppermute | solution.py:36
  31.4 10.3 %collective-permute-start.15 = (bf16[128,1024]{1,0:T(8,128)(2,1)S(1)}, bf16[128,1024]{1,0:T(8,128)(2,1)S(1)}, u32[]{:S(2)}, u32[]{:S(2)}) collective-permute-start(bf16[128,1024]{1,0:T(8,128)(2,1)S(1)} %get-tuple-element.24), channel_id=1, source_target_pairs={{0,4},{2,6},{4,0},{6,2},{1,5},{3,7},{5,1},{7,3},{8,12},{10,14},{12... | collective-permute-start | bytes 786440 | tf_op jit(solution)/shard_map/ppermute | solution.py:36
  38.1 5.0 %collective-permute-start.11 = (bf16[256,256]{1,0:T(8,128)(2,1)S(1)}, bf16[256,256]{1,0:T(8,128)(2,1)S(1)}, u32[]{:S(2)}, u32[]{:S(2)}) collective-permute-start(bf16[256,256]{1,0:T(8,128)(2,1)S(1)} %get-tuple-element.20.refs_0_), channel_id=1, source_target_pairs={{0,2},{2,0},{4,6},{6,4},{1,3},{3,1},{5,7},{7,5},{8,10},{10,8},{12,... | collective-permute-start | bytes 393224 | tf_op jit(solution)/shard_map/ppermute | solution.py:36
  38.2 5.8 %collective-permute-start.12 = (bf16[256,256]{1,0:T(8,128)(2,1)S(1)}, bf16[256,256]{1,0:T(8,128)(2,1)S(1)}, u32[]{:S(2)}, u32[]{:S(2)}) collective-permute-start(bf16[256,256]{1,0:T(8,128)(2,1)S(1)} %get-tuple-element.20.refs_0_), channel_id=1, source_target_pairs={{0,4},{2,6},{4,0},{6,2},{1,5},{3,7},{5,1},{7,3},{8,12},{10,14},{12... | collective-permute-start | bytes 393224 | tf_op jit(solution)/shard_map/ppermute | solution.py:36
  40.1 5.9 %collective-permute-start.13 = (bf16[256,256]{1,0:T(8,128)(2,1)S(1)}, bf16[256,256]{1,0:T(8,128)(2,1)S(1)}, u32[]{:S(2)}, u32[]{:S(2)}) collective-permute-start(bf16[256,256]{1,0:T(8,128)(2,1)S(1)} %get-tuple-element.20.refs_0_), channel_id=1, source_target_pairs={{0,6},{2,4},{4,2},{6,0},{1,7},{3,5},{5,3},{7,1},{8,14},{10,12},{12... | collective-permute-start | bytes 393224 | tf_op jit(solution)/shard_map/ppermute | solution.py:36
  41.7 4.3 %collective-permute-start.16 = (bf16[3,256,1024]{2,1,0:T(8,128)(2,1)S(1)}, bf16[3,256,1024]{2,1,0:T(8,128)(2,1)S(1)}, u32[]{:S(2)}, u32[]{:S(2)}) collective-permute-start(bf16[3,256,1024]{2,1,0:T(8,128)(2,1)S(1)} %get-tuple-element.22.refs_8_), channel_id=1, source_target_pairs={{0,1},{1,0},{2,3},{3,2},{4,5},{5,4},{6,7},{7,6},{8,9},{9,8},{10,11... | collective-permute-start | bytes 4718600 | tf_op jit(solution)/shard_map/ppermute | solution.py:36
  41.8 4.2 %collective-permute-start.17 = (bf16[1,256,1024]{2,1,0:T(8,128)(2,1)S(1)}, bf16[1,256,1024]{2,1,0:T(8,128)(2,1)S(1)}, u32[]{:S(2)}, u32[]{:S(2)}) collective-permute-start(bf16[1,256,1024]{2,1,0:T(8,128)(2,1)S(1)} %stack.1.refs_9_), channel_id=1, source_target_pairs={{0,1},{1,0},{2,3},{3,2},{4,5},{5,4},{6,7},{7,6},{8,9},{9,8},{10,11... | collective-permute-start | bytes 1572872 | tf_op jit(solution)/shard_map/ppermute | solution.py:36
  46.0 5.3 %copy-start.7 = (bf16[256]{0:T(256)(128)(2,1)S(1)}, bf16[256]{0:T(256)(128)(2,1)}, u32[]{:S(2)}) copy-start(bf16[256]{0:T(256)(128)(2,1)} %param.19) | copy-start | bytes 1540
  46.0 10.3 %copy-start.2 = (bf16[1024,256]{1,0:T(8,128)(2,1)S(1)}, bf16[1024,256]{1,0:T(8,128)(2,1)}, u32[]{:S(2)}) copy-start(bf16[1024,256]{1,0:T(8,128)(2,1)} %refs_6_.1) | copy-start | bytes 1572868
  47.7 6.4 %collective-permute-start.18 = (bf16[256,256]{1,0:T(8,128)(2,1)S(1)}, bf16[256,256]{1,0:T(8,128)(2,1)S(1)}, u32[]{:S(2)}, u32[]{:S(2)}) collective-permute-start(bf16[256,256]{1,0:T(8,128)(2,1)S(1)} %get-tuple-element.25.refs_0_), channel_id=1, source_target_pairs={{0,2},{2,0},{4,6},{6,4},{1,3},{3,1},{5,7},{7,5},{8,10},{10,8},{12,... | collective-permute-start | bytes 393224 | tf_op jit(solution)/shard_map/ppermute | solution.py:36
  48.5 7.8 %collective-permute-start.19 = (bf16[256,256]{1,0:T(8,128)(2,1)S(1)}, bf16[256,256]{1,0:T(8,128)(2,1)S(1)}, u32[]{:S(2)}, u32[]{:S(2)}) collective-permute-start(bf16[256,256]{1,0:T(8,128)(2,1)S(1)} %get-tuple-element.25.refs_0_), channel_id=1, source_target_pairs={{0,4},{2,6},{4,0},{6,2},{1,5},{3,7},{5,1},{7,3},{8,12},{10,14},{12... | collective-permute-start | bytes 393224 | tf_op jit(solution)/shard_map/ppermute | solution.py:36
  50.0 6.3 %collective-permute-start.20 = (bf16[256,256]{1,0:T(8,128)(2,1)S(1)}, bf16[256,256]{1,0:T(8,128)(2,1)S(1)}, u32[]{:S(2)}, u32[]{:S(2)}) collective-permute-start(bf16[256,256]{1,0:T(8,128)(2,1)S(1)} %get-tuple-element.25.refs_0_), channel_id=1, source_target_pairs={{0,6},{2,4},{4,2},{6,0},{1,7},{3,5},{5,3},{7,1},{8,14},{10,12},{12... | collective-permute-start | bytes 393224 | tf_op jit(solution)/shard_map/ppermute | solution.py:36

commit v14 on v12

--- a/solution.py
+++ b/solution.py
@@ -408,7 +408,7 @@
     )(*x_pieces, *pieces, mask, w_own, w_other)
     o_own = [o_own]
     if relayed:
-        o_own.append(stack(relay(*pieces[1:], [piece]), corner, 1, []))
+        o_own.append(stack(relay(*pieces[1:], x_pieces[1:2]), corner, 1, []))
     o_other = [exchange(block, "phase", 1) for block in o_own]
 
     arrived = spread(gated, "mp")

time: 58.6 us -> 59.4 us (1.014)
  waiting for transfers between devices: 21.2 us -> 22 us
    ppermute x21, waiting for transfers between devices: 21.2 us -> 22 us  [exchange(): return lax.ppermute(value, axis, pairs)]
  transfers between devices with their start and end apart: 21 -> 21, of which waited for: 9 -> 10; matrix products, arithmetic and copies ran while one was open for 5% -> 4% of each run, Pallas kernels for 5% -> 5%
where the time goes in v14:
time: 59.4 us; the launch traced here: 59.2 us
  starting transfers between devices  25.7 us (43%)
  waiting for transfers between devices  22 us (37%)
  Pallas kernels  6.77 us (11%)
  other arithmetic  3.33 us (6%)
  between operations  0.8 us (1%)
  local copies, waits for them, and re-layouts  0.6 us (1%)
    ppermute x21, starting transfers between devices, exchange(): return lax.ppermute(value, axis, pairs)  25.7 us
    ppermute x21, waiting for transfers between devices, exchange(): return lax.ppermute(value, axis, pairs)  22 us
    pallas_call x1, Pallas kernels, on_device(): pl.pallas_call(functools.partial(last_kernel, mp_count, len(o_own)), out_...  2.06 us
    mul x1, other arithmetic, on_device(): w_own = jnp.transpose(w_in[0], (1, 0, 2)) * gains[0][None, :, None]  1.9 us
    pallas_call x1, Pallas kernels, on_device(): pl.pallas_call(functools.partial(middle_kernel, mp_count, len(o_own)), ou...  1.76 us
    pallas_call x1, Pallas kernels, on_device(): pl.pallas_call(functools.partial(first_kernel, mp_count, places), out_sha...  1.43 us
  transfers between devices with their start and end apart: 21, of which 10 were waited for; matrix products, arithmetic and copies ran while one was open for 4% of the time, Pallas kernels for 5%

profile of v14, /device:TPU:0, one launch (start us, length us, event | category | flops | bytes accessed | tf_op | source)
XLA Modules:
  0.0 59.2 jit_solution(6663211954632465692)
XLA Ops:
  0.6 0.7 %pad_add_fusion.1.refs_0_ = s32[8,128]{1,0:T(8,128)S(1)} fusion(s32[4,128]{1,0:T(4,128)} %bitcast.18, s32[4,128]{1,0:T(4,128)} %bitcast.20), kind=kLoop, calls=%fused_computation.3 | loop fusion | flops 1024 | bytes 8192 | tf_op jit(solution)/shard_map/concatenate | solution.py:372
  1.3 3.0 %collective-permute-start = (s32[8,128]{1,0:T(8,128)S(1)}, s32[8,128]{1,0:T(8,128)S(1)}, u32[]{:S(2)}, u32[]{:S(2)}) collective-permute-start(s32[8,128]{1,0:T(8,128)S(1)} %pad_add_fusion.1.refs_0_), channel_id=1, source_target_pairs={{0,8},{8,0},{16,24},{24,16},{1,9},{9,1},{17,25},{25,17},{2,10},{10... | collective-permute-start | bytes 12296 | tf_op jit(solution)/shard_map/ppermute | solution.py:36
  4.4 0.7 %reduce = bf16[1024]{0:T(1024)(128)(2,1)S(1)} reduce(bf16[1,1024]{1,0:T(2,128)(2,1)} %param.15, bf16[]{:T(256)} %constant.5), dimensions={0}, to_apply=%param.15.reduce_sub_computation | reduce | bytes 4098 | tf_op args[5]
  5.1 1.9 %fusion.refs_0_ = bf16[4,1024,256]{2,1,0:T(8,128)(2,1)S(1)} fusion(bf16[1,1024,4,256]{3,2,1,0:T(4,128)(2,1)} %param.16, bf16[1024]{0:T(1024)(128)(2,1)S(1)} %reduce), kind=kLoop, calls=%fused_computation.1 | loop fusion | flops 1048576 | bytes 4196352 | tf_op jit(solution)/shard_map/mul | solution.py:361
  7.0 0.0 copy-start.5
  7.0 0.0 copy-start.6
  7.0 0.0 copy-start.1
  7.0 0.0 copy-start
  7.0 0.1 collective-permute-start.5
  7.1 0.5 copy-done.5
  7.7 0.0 copy-done.6
  7.7 2.6 %collective-permute-start.1 = (s32[16,128]{1,0:T(8,128)S(1)}, s32[16,128]{1,0:T(8,128)S(1)}, u32[]{:S(2)}, u32[]{:S(2)}) collective-permute-start(s32[16,128]{1,0:T(8,128)S(1)} %pad_add_fusion), channel_id=1, source_target_pairs={{0,16},{8,24},{16,0},{24,8},{1,17},{9,25},{17,1},{25,9},{2,18},{10... | collective-permute-start | bytes 24584 | tf_op jit(solution)/shard_map/ppermute | solution.py:36
  10.3 1.5 %collective-permute-start.10 = (bf16[256,1024]{1,0:T(8,128)(2,1)S(1)}, bf16[256,1024]{1,0:T(8,128)(2,1)S(1)}, u32[]{:S(2)}, u32[]{:S(2)}) collective-permute-start(bf16[256,1024]{1,0:T(8,128)(2,1)S(1)} %bitcast.14), channel_id=1, source_target_pairs={{0,4},{2,6},{4,0},{6,2},{1,5},{3,7},{5,1},{7,3},{8,12},{10,14},{12... | collective-permute-start | bytes 1572872 | tf_op jit(solution)/shard_map/ppermute | solution.py:36
  11.9 1.5 %collective-permute-start.9 = (bf16[256,1024]{1,0:T(8,128)(2,1)S(1)}, bf16[256,1024]{1,0:T(8,128)(2,1)S(1)}, u32[]{:S(2)}, u32[]{:S(2)}) collective-permute-start(bf16[256,1024]{1,0:T(8,128)(2,1)S(1)} %bitcast.15), channel_id=1, source_target_pairs={{0,2},{2,0},{4,6},{6,4},{1,3},{3,1},{5,7},{7,5},{8,10},{10,8},{12,... | collective-permute-start | bytes 1572872 | tf_op jit(solution)/shard_map/ppermute | solution.py:36
  13.4 0.4 fetch.2.refs_4_
  13.8 0.5 collective-permute-start.3
  14.3 0.7 %fetch.3 = (bf16[256,256]{1,0:T(8,128)(2,1)S(1)}, bf16[256,256]{1,0:T(8,128)(2,1)S(1)}, bf16[256,256]{1,0:T(8,128)(2,1)S(1)}) custom-call(s32[8,128]{1,0:T(8,128)S(1)} %pad_add_fusion.1.refs_0_, s32[8,128]{1,0:T(8,128)S(1)} %collective-permute-done.refs_1_, s32[8,128]{1,0:T(8,128)S(1)} %get-tuple-element.31.refs_2_, bf16[1024,1024]{1,0:T(8,128)(2,1)S(1)} %copy-done, ...), custom_call_target="tpu_custom_call" | custom-call | flops 402653184 | bytes 524288 | tf_op jit(solution)/shard_map/fetch/pallas_call | solution.py:88
  15.0 1.6 %collective-permute-start.2 = (bf16[256,256]{1,0:T(8,128)(2,1)S(1)}, bf16[256,256]{1,0:T(8,128)(2,1)S(1)}, u32[]{:S(2)}, u32[]{:S(2)}) collective-permute-start(bf16[256,256]{1,0:T(8,128)(2,1)S(1)} %get-tuple-element.17), channel_id=1, source_target_pairs={{0,8},{8,0},{16,24},{24,16},{1,9},{9,1},{17,25},{25,17},{2,10},{10... | collective-permute-start | bytes 393224 | tf_op jit(solution)/shard_map/ppermute | solution.py:36
  16.6 3.2 %collective-permute-done.3.b_ref = bf16[256,256]{1,0:T(8,128)(2,1)S(1)} collective-permute-done((bf16[256,256]{1,0:T(8,128)(2,1)S(1)}, bf16[256,256]{1,0:T(8,128)(2,1)S(1)}, u32[]{:S(2)}, u32[]{:S(2)}) %collective-permute-start.3) | collective-permute-done | bytes 131104 | tf_op jit(solution)/shard_map/ppermute | solution.py:36
  19.8 1.3 %collective-permute-start.4 = (bf16[256,256]{1,0:T(8,128)(2,1)S(1)}, bf16[256,256]{1,0:T(8,128)(2,1)S(1)}, u32[]{:S(2)}, u32[]{:S(2)}) collective-permute-start(bf16[256,256]{1,0:T(8,128)(2,1)S(1)} %merge.3.refs_0_), channel_id=1, source_target_pairs={{0,16},{8,24},{16,0},{24,8},{1,17},{9,25},{17,1},{25,9},{2,18},{10... | collective-permute-start | bytes 393224 | tf_op jit(solution)/shard_map/ppermute | solution.py:36
  21.1 1.0 %collective-permute-done.2.b_ref = bf16[256,256]{1,0:T(8,128)(2,1)S(1)} collective-permute-done((bf16[256,256]{1,0:T(8,128)(2,1)S(1)}, bf16[256,256]{1,0:T(8,128)(2,1)S(1)}, u32[]{:S(2)}, u32[]{:S(2)}) %collective-permute-start.2) | collective-permute-done | bytes 131104 | tf_op jit(solution)/shard_map/ppermute | solution.py:36
  22.1 5.0 %collective-permute-done.4.b_ref = bf16[256,256]{1,0:T(8,128)(2,1)S(1)} collective-permute-done((bf16[256,256]{1,0:T(8,128)(2,1)S(1)}, bf16[256,256]{1,0:T(8,128)(2,1)S(1)}, u32[]{:S(2)}, u32[]{:S(2)}) %collective-permute-start.4) | collective-permute-done | bytes 131104 | tf_op jit(solution)/shard_map/ppermute | solution.py:36
  27.1 0.6 %collective-permute-start.6 = (bf16[256,256]{1,0:T(8,128)(2,1)S(1)}, bf16[256,256]{1,0:T(8,128)(2,1)S(1)}, u32[]{:S(2)}, u32[]{:S(2)}) collective-permute-start(bf16[256,256]{1,0:T(8,128)(2,1)S(1)} %merge.5.refs_0_), channel_id=1, source_target_pairs={{0,2},{2,0},{4,6},{6,4},{1,3},{3,1},{5,7},{7,5},{8,10},{10,8},{12,... | collective-permute-start | bytes 393224 | tf_op jit(solution)/shard_map/ppermute | solution.py:36
  27.7 1.6 %collective-permute-start.7 = (bf16[256,256]{1,0:T(8,128)(2,1)S(1)}, bf16[256,256]{1,0:T(8,128)(2,1)S(1)}, u32[]{:S(2)}, u32[]{:S(2)}) collective-permute-start(bf16[256,256]{1,0:T(8,128)(2,1)S(1)} %merge.5.refs_0_), channel_id=1, source_target_pairs={{0,4},{2,6},{4,0},{6,2},{1,5},{3,7},{5,1},{7,3},{8,12},{10,14},{12... | collective-permute-start | bytes 393224 | tf_op jit(solution)/shard_map/ppermute | solution.py:36
  29.3 1.4 %collective-permute-start.8 = (bf16[256,256]{1,0:T(8,128)(2,1)S(1)}, bf16[256,256]{1,0:T(8,128)(2,1)S(1)}, u32[]{:S(2)}, u32[]{:S(2)}) collective-permute-start(bf16[256,256]{1,0:T(8,128)(2,1)S(1)} %merge.5.refs_0_), channel_id=1, source_target_pairs={{0,6},{2,4},{4,2},{6,0},{1,7},{3,5},{5,3},{7,1},{8,14},{10,12},{12... | collective-permute-start | bytes 393224 | tf_op jit(solution)/shard_map/ppermute | solution.py:36
  30.7 2.8 %collective-permute-done.6.refs_1_.refs_0_ = bf16[256,256]{1,0:T(8,128)(2,1)S(1)} collective-permute-done((bf16[256,256]{1,0:T(8,128)(2,1)S(1)}, bf16[256,256]{1,0:T(8,128)(2,1)S(1)}, u32[]{:S(2)}, u32[]{:S(2)}) %collective-permute-start.6) | collective-permute-done | bytes 131104 | tf_op jit(solution)/shard_map/ppermute | solution.py:36
  33.5 0.1 cut.1
  33.6 0.6 collective-permute-start.14
  34.2 1.7 %collective-permute-start.15 = (bf16[128,1024]{1,0:T(8,128)(2,1)S(1)}, bf16[128,1024]{1,0:T(8,128)(2,1)S(1)}, u32[]{:S(2)}, u32[]{:S(2)}) collective-permute-start(bf16[128,1024]{1,0:T(8,128)(2,1)S(1)} %get-tuple-element.24), channel_id=1, source_target_pairs={{0,4},{2,6},{4,0},{6,2},{1,5},{3,7},{5,1},{7,3},{8,12},{10,14},{12... | collective-permute-start | bytes 786440 | tf_op jit(solution)/shard_map/ppermute | solution.py:36
  35.9 0.3 prepare.1
  36.2 0.5 collective-permute-done.8.refs_3_
  36.7 1.4 %section0_front.1 = (bf16[256,256]{1,0:T(8,128)(2,1)S(1)}, bf16[256,1024]{1,0:T(8,128)(2,1)S(1)}, bf16[3,256,1024]{2,1,0:T(8,128)(2,1)S(1)}) custom-call(bf16[256,256]{1,0:T(8,128)(2,1)S(1)} %merge.5.refs_0_, bf16[256,256]{1,0:T(8,128)(2,1)S(1)} %collective-permute-done.6.refs_1_.refs_0_, bf16[256,256]{1,0:T(8,128)(2,1)S(1)} %collective-permute-done.7.refs_2_, ...), custom_call_target="tpu_custom_call" | custom-call | flops 603979776 | bytes 2097152 | tf_op jit(solution)/shard_map/section0_front/pallas_call | solution.py:393
  38.1 1.5 %collective-permute-start.11 = (bf16[256,256]{1,0:T(8,128)(2,1)S(1)}, bf16[256,256]{1,0:T(8,128)(2,1)S(1)}, u32[]{:S(2)}, u32[]{:S(2)}) collective-permute-start(bf16[256,256]{1,0:T(8,128)(2,1)S(1)} %get-tuple-element.20.refs_0_), channel_id=1, source_target_pairs={{0,2},{2,0},{4,6},{6,4},{1,3},{3,1},{5,7},{7,5},{8,10},{10,8},{12,... | collective-permute-start | bytes 393224 | tf_op jit(solution)/shard_map/ppermute | solution.py:36
  39.6 0.5 collective-permute-start.12
  40.1 1.6 %collective-permute-start.13 = (bf16[256,256]{1,0:T(8,128)(2,1)S(1)}, bf16[256,256]{1,0:T(8,128)(2,1)S(1)}, u32[]{:S(2)}, u32[]{:S(2)}) collective-permute-start(bf16[256,256]{1,0:T(8,128)(2,1)S(1)} %get-tuple-element.20.refs_0_), channel_id=1, source_target_pairs={{0,6},{2,4},{4,2},{6,0},{1,7},{3,5},{5,3},{7,1},{8,14},{10,12},{12... | collective-permute-start | bytes 393224 | tf_op jit(solution)/shard_map/ppermute | solution.py:36
  41.7 0.1 stack.1.refs_9_
  41.7 0.6 collective-permute-start.17
  42.3 0.8 %collective-permute-done.11.refs_1_ = bf16[256,256]{1,0:T(8,128)(2,1)S(1)} collective-permute-done((bf16[256,256]{1,0:T(8,128)(2,1)S(1)}, bf16[256,256]{1,0:T(8,128)(2,1)S(1)}, u32[]{:S(2)}, u32[]{:S(2)}) %collective-permute-start.11) | collective-permute-done | bytes 131104 | tf_op jit(solution)/shard_map/ppermute | solution.py:36
  43.1 1.4 %collective-permute-done.12.refs_2_ = bf16[256,256]{1,0:T(8,128)(2,1)S(1)} collective-permute-done((bf16[256,256]{1,0:T(8,128)(2,1)S(1)}, bf16[256,256]{1,0:T(8,128)(2,1)S(1)}, u32[]{:S(2)}, u32[]{:S(2)}) %collective-permute-start.12) | collective-permute-done | bytes 131104 | tf_op jit(solution)/shard_map/ppermute | solution.py:36
  44.6 1.4 %collective-permute-done.13.refs_0_ = bf16[256,256]{1,0:T(8,128)(2,1)S(1)} collective-permute-done((bf16[256,256]{1,0:T(8,128)(2,1)S(1)}, bf16[256,256]{1,0:T(8,128)(2,1)S(1)}, u32[]{:S(2)}, u32[]{:S(2)}) %collective-permute-start.13) | collective-permute-done | bytes 131104 | tf_op jit(solution)/shard_map/ppermute | solution.py:36
  46.0 0.0 copy-start.2
  46.0 1.8 %section0_back_section1_front.1 = (bf16[256,256]{1,0:T(8,128)(2,1)S(1)}, bf16[256,1024]{1,0:T(8,128)(2,1)S(1)}) custom-call(bf16[256,256]{1,0:T(8,128)(2,1)S(1)} %get-tuple-element.20.refs_0_, bf16[256,256]{1,0:T(8,128)(2,1)S(1)} %collective-permute-done.11.refs_1_, bf16[256,256]{1,0:T(8,128)(2,1)S(1)} %collective-permute-done.12.refs_2_, ...), custom_call_target="tpu_custom_call" | custom-call | flops 1140850688 | bytes 4194304 | tf_op jit(solution)/shard_map/section0_back_section1_front/pallas_call | solution.py:416
  47.8 1.3 %collective-permute-start.18 = (bf16[256,256]{1,0:T(8,128)(2,1)S(1)}, bf16[256,256]{1,0:T(8,128)(2,1)S(1)}, u32[]{:S(2)}, u32[]{:S(2)}) collective-permute-start(bf16[256,256]{1,0:T(8,128)(2,1)S(1)} %get-tuple-element.25.refs_0_), channel_id=1, source_target_pairs={{0,2},{2,0},{4,6},{6,4},{1,3},{3,1},{5,7},{7,5},{8,10},{10,8},{12,... | collective-permute-start | bytes 393224 | tf_op jit(solution)/shard_map/ppermute | solution.py:36
  49.1 0.9 %collective-permute-start.19 = (bf16[256,256]{1,0:T(8,128)(2,1)S(1)}, bf16[256,256]{1,0:T(8,128)(2,1)S(1)}, u32[]{:S(2)}, u32[]{:S(2)}) collective-permute-start(bf16[256,256]{1,0:T(8,128)(2,1)S(1)} %get-tuple-element.25.refs_0_), channel_id=1, source_target_pairs={{0,4},{2,6},{4,0},{6,2},{1,5},{3,7},{5,1},{7,3},{8,12},{10,14},{12... | collective-permute-start | bytes 393224 | tf_op jit(solution)/shard_map/ppermute | solution.py:36
  49.9 1.4 %collective-permute-start.20 = (bf16[256,256]{1,0:T(8,128)(2,1)S(1)}, bf16[256,256]{1,0:T(8,128)(2,1)S(1)}, u32[]{:S(2)}, u32[]{:S(2)}) collective-permute-start(bf16[256,256]{1,0:T(8,128)(2,1)S(1)} %get-tuple-element.25.refs_0_), channel_id=1, source_target_pairs={{0,6},{2,4},{4,2},{6,0},{1,7},{3,5},{5,3},{7,1},{8,14},{10,12},{12... | collective-permute-start | bytes 393224 | tf_op jit(solution)/shard_map/ppermute | solution.py:36
  51.3 2.3 %collective-permute-done.18.refs_1_ = bf16[256,256]{1,0:T(8,128)(2,1)S(1)} collective-permute-done((bf16[256,256]{1,0:T(8,128)(2,1)S(1)}, bf16[256,256]{1,0:T(8,128)(2,1)S(1)}, u32[]{:S(2)}, u32[]{:S(2)}) %collective-permute-start.18) | collective-permute-done | bytes 131104 | tf_op jit(solution)/shard_map/ppermute | solution.py:36
  53.6 3.5 %collective-permute-done.19.refs_2_ = bf16[256,256]{1,0:T(8,128)(2,1)S(1)} collective-permute-done((bf16[256,256]{1,0:T(8,128)(2,1)S(1)}, bf16[256,256]{1,0:T(8,128)(2,1)S(1)}, u32[]{:S(2)}, u32[]{:S(2)}) %collective-permute-start.19) | collective-permute-done | bytes 131104 | tf_op jit(solution)/shard_map/ppermute | solution.py:36
  57.1 2.1 %section1_back_context.1 = (bf16[256,1024]{1,0:T(8,128)(2,1)}, bf16[256,256]{1,0:T(8,128)(2,1)}) custom-call(bf16[256,256]{1,0:T(8,128)(2,1)S(1)} %get-tuple-element.25.refs_0_, bf16[256,256]{1,0:T(8,128)(2,1)S(1)} %collective-permute-done.18.refs_1_, bf16[256,256]{1,0:T(8,128)(2,1)S(1)} %collective-permute-done.19.refs_2_, ...), custom_call_target="tpu_custom_call" | custom-call | flops 805306368 | bytes 2097152 | tf_op jit(solution)/shard_map/section1_back_context/pallas_call | solution.py:430
  (29 shorter events, 0.1 us)
Async XLA Ops:
  1.3 5.7 %collective-permute-start = (s32[8,128]{1,0:T(8,128)S(1)}, s32[8,128]{1,0:T(8,128)S(1)}, u32[]{:S(2)}, u32[]{:S(2)}) collective-permute-start(s32[8,128]{1,0:T(8,128)S(1)} %pad_add_fusion.1.refs_0_), channel_id=1, source_target_pairs={{0,8},{8,0},{16,24},{24,16},{1,9},{9,1},{17,25},{25,17},{2,10},{10... | collective-permute-start | bytes 12296 | tf_op jit(solution)/shard_map/ppermute | solution.py:36
  7.0 0.7 %copy-start.5 = (s32[512]{0:T(512)S(1)}, s32[512]{0:T(512)}, u32[]{:S(2)}) copy-start(s32[512]{0:T(512)} %param.11) | copy-start | bytes 6148
  7.0 0.7 %copy-start.6 = (s32[512,1]{0,1:T(1,128)S(1)}, s32[512,1]{0,1:T(1,128)}, u32[]{:S(2)}) copy-start(s32[512,1]{0,1:T(1,128)} %param.10) | copy-start | bytes 6148
  7.0 3.3 %copy-start.1 = (bf16[1,256,1024]{2,1,0:T(8,128)(2,1)S(1)}, bf16[1,256,1024]{2,1,0:T(8,128)(2,1)}, u32[]{:S(2)}) copy-start(bf16[1,256,1024]{2,1,0:T(8,128)(2,1)} %param.17) | copy-start | bytes 1572868
  7.0 6.3 %copy-start = (bf16[1024,1024]{1,0:T(8,128)(2,1)S(1)}, bf16[1024,1024]{1,0:T(8,128)(2,1)}, u32[]{:S(2)}) copy-start(bf16[1024,1024]{1,0:T(8,128)(2,1)} %refs_3_.1) | copy-start | bytes 6291460
  7.0 20.1 %collective-permute-start.5 = (bf16[4,1024,256]{2,1,0:T(8,128)(2,1)S(1)}, bf16[4,1024,256]{2,1,0:T(8,128)(2,1)S(1)}, u32[]{:S(2)}, u32[]{:S(2)}) collective-permute-start(bf16[4,1024,256]{2,1,0:T(8,128)(2,1)S(1)} %hold.2.refs_8_.refs_6_), channel_id=1, source_target_pairs={{0,1},{1,0},{2,3},{3,2},{4,5},{5,4},{6,7},{7,6},{8,9},{9,8},{10,11... | collective-permute-start | bytes 6291464 | tf_op jit(solution)/shard_map/ppermute | solution.py:36
  7.7 5.7 %collective-permute-start.1 = (s32[16,128]{1,0:T(8,128)S(1)}, s32[16,128]{1,0:T(8,128)S(1)}, u32[]{:S(2)}, u32[]{:S(2)}) collective-permute-start(s32[16,128]{1,0:T(8,128)S(1)} %pad_add_fusion), channel_id=1, source_target_pairs={{0,16},{8,24},{16,0},{24,8},{1,17},{9,25},{17,1},{25,9},{2,18},{10... | collective-permute-start | bytes 24584 | tf_op jit(solution)/shard_map/ppermute | solution.py:36
  10.3 20.4 %collective-permute-start.10 = (bf16[256,1024]{1,0:T(8,128)(2,1)S(1)}, bf16[256,1024]{1,0:T(8,128)(2,1)S(1)}, u32[]{:S(2)}, u32[]{:S(2)}) collective-permute-start(bf16[256,1024]{1,0:T(8,128)(2,1)S(1)} %bitcast.14), channel_id=1, source_target_pairs={{0,4},{2,6},{4,0},{6,2},{1,5},{3,7},{5,1},{7,3},{8,12},{10,14},{12... | collective-permute-start | bytes 1572872 | tf_op jit(solution)/shard_map/ppermute | solution.py:36
  11.9 18.8 %collective-permute-start.9 = (bf16[256,1024]{1,0:T(8,128)(2,1)S(1)}, bf16[256,1024]{1,0:T(8,128)(2,1)S(1)}, u32[]{:S(2)}, u32[]{:S(2)}) collective-permute-start(bf16[256,1024]{1,0:T(8,128)(2,1)S(1)} %bitcast.15), channel_id=1, source_target_pairs={{0,2},{2,0},{4,6},{6,4},{1,3},{3,1},{5,7},{7,5},{8,10},{10,8},{12,... | collective-permute-start | bytes 1572872 | tf_op jit(solution)/shard_map/ppermute | solution.py:36
  13.8 6.0 %collective-permute-start.3 = (bf16[256,256]{1,0:T(8,128)(2,1)S(1)}, bf16[256,256]{1,0:T(8,128)(2,1)S(1)}, u32[]{:S(2)}, u32[]{:S(2)}) collective-permute-start(bf16[256,256]{1,0:T(8,128)(2,1)S(1)} %fetch.2.refs_4_), channel_id=1, source_target_pairs={{0,8},{8,0},{16,24},{24,16},{1,9},{9,1},{17,25},{25,17},{2,10},{10... | collective-permute-start | bytes 393224 | tf_op jit(solution)/shard_map/ppermute | solution.py:36
  15.0 7.1 %collective-permute-start.2 = (bf16[256,256]{1,0:T(8,128)(2,1)S(1)}, bf16[256,256]{1,0:T(8,128)(2,1)S(1)}, u32[]{:S(2)}, u32[]{:S(2)}) collective-permute-start(bf16[256,256]{1,0:T(8,128)(2,1)S(1)} %get-tuple-element.17), channel_id=1, source_target_pairs={{0,8},{8,0},{16,24},{24,16},{1,9},{9,1},{17,25},{25,17},{2,10},{10... | collective-permute-start | bytes 393224 | tf_op jit(solution)/shard_map/ppermute | solution.py:36
  19.8 7.3 %collective-permute-start.4 = (bf16[256,256]{1,0:T(8,128)(2,1)S(1)}, bf16[256,256]{1,0:T(8,128)(2,1)S(1)}, u32[]{:S(2)}, u32[]{:S(2)}) collective-permute-start(bf16[256,256]{1,0:T(8,128)(2,1)S(1)} %merge.3.refs_0_), channel_id=1, source_target_pairs={{0,16},{8,24},{16,0},{24,8},{1,17},{9,25},{17,1},{25,9},{2,18},{10... | collective-permute-start | bytes 393224 | tf_op jit(solution)/shard_map/ppermute | solution.py:36
  22.0 13.8 %copy-start.3 = (s32[1,2,256,8]{2,3,1,0:T(8,128)S(1)}, s32[1,2,256,8]{2,3,1,0:T(8,128)}, u32[]{:S(2)}) copy-start(s32[1,2,256,8]{2,3,1,0:T(8,128)} %param.13) | copy-start | bytes 49156
  22.0 13.8 %copy-start.4 = (s32[1,2,256]{2,1,0:T(2,128)S(1)}, s32[1,2,256]{2,1,0:T(2,128)}, u32[]{:S(2)}) copy-start(s32[1,2,256]{2,1,0:T(2,128)} %seg_ref.1) | copy-start | bytes 6148
  27.1 6.4 %collective-permute-start.6 = (bf16[256,256]{1,0:T(8,128)(2,1)S(1)}, bf16[256,256]{1,0:T(8,128)(2,1)S(1)}, u32[]{:S(2)}, u32[]{:S(2)}) collective-permute-start(bf16[256,256]{1,0:T(8,128)(2,1)S(1)} %merge.5.refs_0_), channel_id=1, source_target_pairs={{0,2},{2,0},{4,6},{6,4},{1,3},{3,1},{5,7},{7,5},{8,10},{10,8},{12,... | collective-permute-start | bytes 393224 | tf_op jit(solution)/shard_map/ppermute | solution.py:36
  27.7 8.4 %collective-permute-start.7 = (bf16[256,256]{1,0:T(8,128)(2,1)S(1)}, bf16[256,256]{1,0:T(8,128)(2,1)S(1)}, u32[]{:S(2)}, u32[]{:S(2)}) collective-permute-start(bf16[256,256]{1,0:T(8,128)(2,1)S(1)} %merge.5.refs_0_), channel_id=1, source_target_pairs={{0,4},{2,6},{4,0},{6,2},{1,5},{3,7},{5,1},{7,3},{8,12},{10,14},{12... | collective-permute-start | bytes 393224 | tf_op jit(solution)/shard_map/ppermute | solution.py:36
  29.3 7.3 %collective-permute-start.8 = (bf16[256,256]{1,0:T(8,128)(2,1)S(1)}, bf16[256,256]{1,0:T(8,128)(2,1)S(1)}, u32[]{:S(2)}, u32[]{:S(2)}) collective-permute-start(bf16[256,256]{1,0:T(8,128)(2,1)S(1)} %merge.5.refs_0_), channel_id=1, source_target_pairs={{0,6},{2,4},{4,2},{6,0},{1,7},{3,5},{5,3},{7,1},{8,14},{10,12},{12... | collective-permute-start | bytes 393224 | tf_op jit(solution)/shard_map/ppermute | solution.py:36
  33.6 8.0 %collective-permute-start.14 = (bf16[128,1024]{1,0:T(8,128)(2,1)S(1)}, bf16[128,1024]{1,0:T(8,128)(2,1)S(1)}, u32[]{:S(2)}, u32[]{:S(2)}) collective-permute-start(bf16[128,1024]{1,0:T(8,128)(2,1)S(1)} %get-tuple-element.23), channel_id=1, source_target_pairs={{0,2},{2,0},{4,6},{6,4},{1,3},{3,1},{5,7},{7,5},{8,10},{10,8},{12,... | collective-permute-start | bytes 786440 | tf_op jit(solution)/shard_map/ppermute | solution.py:36
  34.2 7.5 %collective-permute-start.15 = (bf16[128,1024]{1,0:T(8,128)(2,1)S(1)}, bf16[128,1024]{1,0:T(8,128)(2,1)S(1)}, u32[]{:S(2)}, u32[]{:S(2)}) collective-permute-start(bf16[128,1024]{1,0:T(8,128)(2,1)S(1)} %get-tuple-element.24), channel_id=1, source_target_pairs={{0,4},{2,6},{4,0},{6,2},{1,5},{3,7},{5,1},{7,3},{8,12},{10,14},{12... | collective-permute-start | bytes 786440 | tf_op jit(solution)/shard_map/ppermute | solution.py:36
  38.1 5.0 %collective-permute-start.11 = (bf16[256,256]{1,0:T(8,128)(2,1)S(1)}, bf16[256,256]{1,0:T(8,128)(2,1)S(1)}, u32[]{:S(2)}, u32[]{:S(2)}) collective-permute-start(bf16[256,256]{1,0:T(8,128)(2,1)S(1)} %get-tuple-element.20.refs_0_), channel_id=1, source_target_pairs={{0,2},{2,0},{4,6},{6,4},{1,3},{3,1},{5,7},{7,5},{8,10},{10,8},{12,... | collective-permute-start | bytes 393224 | tf_op jit(solution)/shard_map/ppermute | solution.py:36
  39.6 5.0 %collective-permute-start.12 = (bf16[256,256]{1,0:T(8,128)(2,1)S(1)}, bf16[256,256]{1,0:T(8,128)(2,1)S(1)}, u32[]{:S(2)}, u32[]{:S(2)}) collective-permute-start(bf16[256,256]{1,0:T(8,128)(2,1)S(1)} %get-tuple-element.20.refs_0_), channel_id=1, source_target_pairs={{0,4},{2,6},{4,0},{6,2},{1,5},{3,7},{5,1},{7,3},{8,12},{10,14},{12... | collective-permute-start | bytes 393224 | tf_op jit(solution)/shard_map/ppermute | solution.py:36
  40.1 5.9 %collective-permute-start.13 = (bf16[256,256]{1,0:T(8,128)(2,1)S(1)}, bf16[256,256]{1,0:T(8,128)(2,1)S(1)}, u32[]{:S(2)}, u32[]{:S(2)}) collective-permute-start(bf16[256,256]{1,0:T(8,128)(2,1)S(1)} %get-tuple-element.20.refs_0_), channel_id=1, source_target_pairs={{0,6},{2,4},{4,2},{6,0},{1,7},{3,5},{5,3},{7,1},{8,14},{10,12},{12... | collective-permute-start | bytes 393224 | tf_op jit(solution)/shard_map/ppermute | solution.py:36
  41.7 4.3 %collective-permute-start.16 = (bf16[3,256,1024]{2,1,0:T(8,128)(2,1)S(1)}, bf16[3,256,1024]{2,1,0:T(8,128)(2,1)S(1)}, u32[]{:S(2)}, u32[]{:S(2)}) collective-permute-start(bf16[3,256,1024]{2,1,0:T(8,128)(2,1)S(1)} %get-tuple-element.22.refs_8_), channel_id=1, source_target_pairs={{0,1},{1,0},{2,3},{3,2},{4,5},{5,4},{6,7},{7,6},{8,9},{9,8},{10,11... | collective-permute-start | bytes 4718600 | tf_op jit(solution)/shard_map/ppermute | solution.py:36
  41.7 4.2 %collective-permute-start.17 = (bf16[1,256,1024]{2,1,0:T(8,128)(2,1)S(1)}, bf16[1,256,1024]{2,1,0:T(8,128)(2,1)S(1)}, u32[]{:S(2)}, u32[]{:S(2)}) collective-permute-start(bf16[1,256,1024]{2,1,0:T(8,128)(2,1)S(1)} %stack.1.refs_9_), channel_id=1, source_target_pairs={{0,1},{1,0},{2,3},{3,2},{4,5},{5,4},{6,7},{7,6},{8,9},{9,8},{10,11... | collective-permute-start | bytes 1572872 | tf_op jit(solution)/shard_map/ppermute | solution.py:36
  46.0 5.3 %copy-start.7 = (bf16[256]{0:T(256)(128)(2,1)S(1)}, bf16[256]{0:T(256)(128)(2,1)}, u32[]{:S(2)}) copy-start(bf16[256]{0:T(256)(128)(2,1)} %param.19) | copy-start | bytes 1540
  46.0 11.2 %copy-start.2 = (bf16[1024,256]{1,0:T(8,128)(2,1)S(1)}, bf16[1024,256]{1,0:T(8,128)(2,1)}, u32[]{:S(2)}) copy-start(bf16[1024,256]{1,0:T(8,128)(2,1)} %refs_6_.1) | copy-start | bytes 1572868
  47.8 5.8 %collective-permute-start.18 = (bf16[256,256]{1,0:T(8,128)(2,1)S(1)}, bf16[256,256]{1,0:T(8,128)(2,1)S(1)}, u32[]{:S(2)}, u32[]{:S(2)}) collective-permute-start(bf16[256,256]{1,0:T(8,128)(2,1)S(1)} %get-tuple-element.25.refs_0_), channel_id=1, source_target_pairs={{0,2},{2,0},{4,6},{6,4},{1,3},{3,1},{5,7},{7,5},{8,10},{10,8},{12,... | collective-permute-start | bytes 393224 | tf_op jit(solution)/shard_map/ppermute | solution.py:36
  49.1 8.1 %collective-permute-start.19 = (bf16[256,256]{1,0:T(8,128)(2,1)S(1)}, bf16[256,256]{1,0:T(8,128)(2,1)S(1)}, u32[]{:S(2)}, u32[]{:S(2)}) collective-permute-start(bf16[256,256]{1,0:T(8,128)(2,1)S(1)} %get-tuple-element.25.refs_0_), channel_id=1, source_target_pairs={{0,4},{2,6},{4,0},{6,2},{1,5},{3,7},{5,1},{7,3},{8,12},{10,14},{12... | collective-permute-start | bytes 393224 | tf_op jit(solution)/shard_map/ppermute | solution.py:36
  49.9 7.2 %collective-permute-start.20 = (bf16[256,256]{1,0:T(8,128)(2,1)S(1)}, bf16[256,256]{1,0:T(8,128)(2,1)S(1)}, u32[]{:S(2)}, u32[]{:S(2)}) collective-permute-start(bf16[256,256]{1,0:T(8,128)(2,1)S(1)} %get-tuple-element.25.refs_0_), channel_id=1, source_target_pairs={{0,6},{2,4},{4,2},{6,0},{1,7},{3,5},{5,3},{7,1},{8,14},{10,12},{12... | collective-permute-start | bytes 393224 | tf_op jit(solution)/shard_map/ppermute | solution.py:36
